TPU v7x, 32 devices: a whole 2x2x4 slice. The times are simulated.
32 devices in a mesh: members: 2 (over y), lon: 16 (over z, x, core).
Axes of the slice: x: 2, y: 2, z: 4, core: 2. Of those that a mesh axis runs over, the one named last changes fastest.
Arguments:
- source: float32 [1024, 2240], P(('members', 'lon')), parts along dimension 0, may hold values from -6 to 6
- diagonal: float32 [1024, 2240], P(('members', 'lon')), parts along dimension 0, may hold values from 0.02 to 0.5
- u_vel: float32 [6, 1024, 2240], P(None, ('members', 'lon')), parts along dimension 1, may hold values from -6 to 6
- v_vel: float32 [6, 1024, 2240], P(None, ('members', 'lon')), parts along dimension 1, may hold values from -6 to 6
- bottom: int32 [1024, 2240], P(('members', 'lon')), parts along dimension 0, may hold values from 0 to 6
Outputs:
- surface: float32 [1024, 2240], P(('members', 'lon')), parts along dimension 0
- u_new: float32 [6, 1024, 2240], P(None, ('members', 'lon')), parts along dimension 1
- v_new: float32 [6, 1024, 2240], P(None, ('members', 'lon')), parts along dimension 1
- w_vel: float32 [6, 1024, 2240], P(None, ('members', 'lon')), parts along dimension 1
There are 2 independent parts, one for each index of `members`. A program takes and returns all parts, laid end to end along the dimension named above; each array names one. Nothing has to cross between parts.
All inputs are finite; a program needn't handle non-finite values.
Results may differ from a plain program's by a relative error of at most 0.0001.
Values sent between devices are 32-bit elements; how exact they have to be, the bound alone decides.
No kernel may reach another device: no remote copies, remote signals or barrier semaphores. Data moves between devices by JAX's collectives and lax.ppermute only.
A program may use at most 64 MiB of HBM per device.

v0:
```python
import math

import jax
import jax.numpy as jnp
from jax import lax
from jax.sharding import PartitionSpec as P

LT = 112
OV = 8
KL = 6
ITERS = 2


tile_shift = 0.1
gravity_step = 0.5


def extended_2(x, sides, width):
    for axis, dim in sides:
        devices, length = (lax.axis_size(axis), x.shape[dim])
        up = [(i, (i + 1) % devices) for i in range(devices)]
        down = [(j, i) for i, j in up]
        last = lax.slice_in_dim(x, length - width, length, axis=dim)
        first = lax.slice_in_dim(x, 0, width, axis=dim)
        before = lax.ppermute(last, axis, up)
        after = lax.ppermute(first, axis, down)
        x = jnp.concatenate([before, x, after], axis=dim)
    return x


def from_behind(block, axis, distance):
    devices = range(lax.axis_size(axis))
    route = [((i - distance) % len(devices), i) for i in devices]
    return lax.ppermute(block, axis, route)


def sine_basis(length):
    ordinal = jnp.arange(length, dtype=jnp.float32) + 1.0
    angles = math.pi * ordinal[:, None] * ordinal[None, :] / (length + 1)
    basis_matrix = jnp.sqrt(2.0 / (length + 1)) * jnp.sin(angles)
    eigen_value = 2.0 - 2.0 * jnp.cos(math.pi * ordinal / (length + 1))
    return (basis_matrix, eigen_value)


def split_windows(padded, block_len, blocks, margin):
    leading = padded.shape[:-1]
    extra_cols = block_len * (blocks + 1) - padded.shape[-1]
    padded = jnp.pad(padded, [(0, 0)] * len(leading) + [(0, extra_cols)])
    main_part = padded[..., : block_len * blocks].reshape(leading + (blocks, block_len))
    tail_part = padded[..., block_len : block_len * (blocks + 1)].reshape(
        leading + (blocks, block_len)
    )[..., : 2 * margin]
    return jnp.concatenate([main_part, tail_part], axis=-1)


def join_windows(windows, block_len, blocks, margin):
    leading = windows.shape[:-2]
    main_part = windows[..., :block_len].reshape(leading + (blocks * block_len,))
    tail_part = jnp.pad(
        windows[..., block_len:], [(0, 0)] * (len(leading) + 1) + [(0, block_len - 2 * margin)]
    )
    tail_part = tail_part.reshape(leading + (blocks * block_len,))
    widths = [(0, 0)] * len(leading)
    summed = jnp.pad(main_part, widths + [(0, block_len)]) + jnp.pad(
        tail_part, widths + [(block_len, 0)]
    )
    return summed[..., : block_len * blocks + 2 * margin]


def residual_sum(residue, precond):
    return lax.psum(jnp.sum(residue * precond), "lon")


def body(source, diagonal, u_vel, v_vel, bottom):
    highest = lax.Precision.HIGHEST
    wet_mask = (bottom > 0).astype(jnp.float32)
    depths = bottom.astype(jnp.float32)
    cells = source.shape[0]
    lat_cells = source.shape[1]
    tiles = lat_cells // LT
    lon_basis, lon_value = sine_basis(cells + 2 * OV)
    lat_basis, lat_value = sine_basis(LT + 2 * OV)

    def precondition(residue):
        masked = wet_mask * residue
        extended = extended_2(masked, (("lon", 0),), OV)
        padded = jnp.pad(extended, ((0, 0), (OV, OV)))
        windows = split_windows(padded, LT, tiles, OV)
        spectral = jnp.einsum("atb,ac->ctb", windows, lon_basis, precision=highest)
        spectral = jnp.einsum("ctb,bd->ctd", spectral, lat_basis, precision=highest)
        spectral = spectral / (lon_value[:, None, None] + lat_value[None, None, :] + tile_shift)
        restored = jnp.einsum("ctd,bd->ctb", spectral, lat_basis, precision=highest)
        restored = jnp.einsum("ctb,ac->atb", restored, lon_basis, precision=highest)
        full_rows = join_windows(restored, LT, tiles, OV)[:, OV : OV + lat_cells]
        centre = full_rows[OV : OV + cells]
        from_east = from_behind(full_rows[:OV], "lon", -1)
        from_west = from_behind(full_rows[cells + OV :], "lon", 1)
        sides = None
        centre = centre + jnp.pad(from_east, ((cells - OV, 0), (0, 0)))
        centre = centre + jnp.pad(from_west, ((0, cells - OV), (0, 0)))
        return (wet_mask * centre + (1.0 - wet_mask) * residue, sides)

    solution = jnp.zeros_like(source)
    residue = source
    precond, sides = precondition(residue)
    norm_now = residual_sum(residue, precond)
    direction = precond
    for iteration in range(ITERS):
        operate_masked = wet_mask * direction
        haloed = extended_2(operate_masked, (("lon", 0),), 1)
        beside = haloed[:-2] + haloed[2:]
        operate_padded = jnp.pad(operate_masked, ((0, 0), (1, 1)))
        beside = beside + operate_padded[:, 2:] + operate_padded[:, :-2]
        image = wet_mask * ((4.0 + diagonal) * direction - beside) + (1.0 - wet_mask) * direction
        step_length = norm_now / lax.psum(jnp.sum(direction * image), "lon")
        solution = solution + step_length * direction
        residue = residue - step_length * image
        if iteration + 1 < ITERS:
            precond, sides = precondition(residue)
            norm_next = residual_sum(residue, precond)
            beta_ratio = norm_next / norm_now
            direction = precond + beta_ratio * direction
            norm_now = norm_next
    levels = jnp.arange(KL, dtype=jnp.float32).reshape(KL, 1, 1)
    edge = jnp.stack([solution[:1], depths[:1]])
    arrived = from_behind(edge, "lon", -1)
    east_surface = jnp.concatenate([solution[1:], arrived[0]], axis=0)
    east_depth = jnp.concatenate([depths[1:], arrived[1]], axis=0)
    u_face = (levels < jnp.minimum(depths, east_depth)[None]).astype(jnp.float32)
    u_new = u_face * (u_vel - gravity_step * (east_surface - solution)[None])
    u_left = from_behind(u_new[:, -1:, :], "lon", 1)
    west_u = jnp.concatenate([u_left, u_new[:, :-1, :]], axis=1)
    north_depth = jnp.concatenate([depths[:, 1:], jnp.zeros_like(depths[:, :1])], axis=1)
    north_surface = jnp.concatenate([solution[:, 1:], jnp.zeros_like(solution[:, :1])], axis=1)
    v_face = (levels < jnp.minimum(depths, north_depth)[None]).astype(jnp.float32)
    v_new = v_face * (v_vel - gravity_step * (north_surface - solution)[None])
    wet_levels = (levels < depths[None]).astype(jnp.float32)
    south_v = jnp.pad(v_new[:, :, :-1], ((0, 0), (0, 0), (1, 0)))
    divergence = wet_levels * (u_new - west_u + (v_new - south_v))
    w_vel = jnp.cumsum(divergence[::-1], axis=0)[::-1]
    return (solution, u_new, v_new, w_vel)


def solution(mesh):
    return jax.shard_map(
        body,
        mesh=mesh,
        in_specs=(
            P(("members", "lon"), None),
            P(("members", "lon"), None),
            P(None, ("members", "lon"), None),
            P(None, ("members", "lon"), None),
            P(("members", "lon"), None),
        ),
        out_specs=(
            P(("members", "lon"), None),
            P(None, ("members", "lon"), None),
            P(None, ("members", "lon"), None),
            P(None, ("members", "lon"), None),
        ),
        check_vma=False,
    )
```

profile of v0, /device:TPU:0, one launch (start us, length us, event | category | flops | bytes accessed | tf_op | source)
XLA Modules:
  0.0 181.6 jit_solution(17057000450216667745)
XLA Ops:
  0.6 1.1 broadcast_select_fusion.3
  1.8 0.5 collective-permute-start
  2.3 5.0 %collective-permute-start.1 = (f32[8,2240]{1,0:T(8,128)S(1)}, f32[8,2240]{1,0:T(8,128)S(1)}, u32[]{:S(2)}, u32[]{:S(2)}) collective-permute-start(f32[8,2240]{1,0:T(8,128)S(1)} %get-tuple-element.36), channel_id=1, source_target_pairs={{1,0},{2,1},{3,2},{4,3},{5,4},{6,5},{7,6},{8,7},{9,8},{10,9},{11,1... | collective-permute-start | bytes 215048 | tf_op jit(solution)/shard_map/ppermute | solution.py:26
  7.5 1.9 %collective-permute-done = f32[8,2240]{1,0:T(8,128)S(1)} collective-permute-done((f32[8,2240]{1,0:T(8,128)S(1)}, f32[8,2240]{1,0:T(8,128)S(1)}, u32[]{:S(2)}, u32[]{:S(2)}) %collective-permute-start) | collective-permute-done | bytes 71712 | tf_op jit(solution)/shard_map/ppermute | solution.py:25
  9.6 0.2 fusion.102
  9.7 0.3 reshape.108
  10.1 0.3 reshape.109
  10.4 0.2 pad_maximum_fusion
  10.6 0.7 fusion.8
  11.3 0.8 fusion.42
  12.4 0.8 fusion.6
  13.2 0.7 fusion.63
  13.9 0.2 slice.195
  15.1 4.4 %collective-permute-start.2 = (f32[8,2240]{1,0:T(8,128)S(1)}, f32[8,2240]{1,0:T(8,128)S(1)}, u32[]{:S(2)}, u32[]{:S(2)}) collective-permute-start(f32[8,2240]{1,0:T(8,128)S(1)} %get-tuple-element.19), channel_id=1, source_target_pairs={{1,0},{2,1},{3,2},{4,3},{5,4},{6,5},{7,6},{8,7},{9,8},{10,9},{11,1... | collective-permute-start | bytes 215048 | tf_op jit(solution)/shard_map/ppermute | solution.py:34
  19.5 2.0 %collective-permute-done.2 = f32[8,2240]{1,0:T(8,128)S(1)} collective-permute-done((f32[8,2240]{1,0:T(8,128)S(1)}, f32[8,2240]{1,0:T(8,128)S(1)}, u32[]{:S(2)}, u32[]{:S(2)}) %collective-permute-start.2) | collective-permute-done | bytes 71712 | tf_op jit(solution)/shard_map/ppermute | solution.py:34
  21.5 4.5 %collective-permute-done.3 = f32[8,2240]{1,0:T(8,128)S(1)} collective-permute-done((f32[8,2240]{1,0:T(8,128)S(1)}, f32[8,2240]{1,0:T(8,128)S(1)}, u32[]{:S(2)}, u32[]{:S(2)}) %collective-permute-start.3) | collective-permute-done | bytes 71712 | tf_op jit(solution)/shard_map/ppermute | solution.py:34
  26.0 0.2 broadcast_select_fusion.2
  26.3 4.4 %collective-permute-start.5 = (f32[1,2240]{1,0:T(1,128)S(1)}, f32[1,2240]{1,0:T(1,128)S(1)}, u32[]{:S(2)}, u32[]{:S(2)}) collective-permute-start(f32[1,2240]{1,0:T(1,128)S(1)} %get-tuple-element.34), channel_id=1, source_target_pairs={{1,0},{2,1},{3,2},{4,3},{5,4},{6,5},{7,6},{8,7},{9,8},{10,9},{11,1... | collective-permute-start | bytes 26888 | tf_op jit(solution)/shard_map/ppermute | solution.py:26
  30.7 1.3 collective-permute-done.4
  32.1 0.9 multiply_reduce_fusion.1
  33.0 34.5 %all-reduce.19 = (f32[]{:T(128)}, f32[]{:T(128)}) all-reduce(f32[]{:T(128)} %get-tuple-element.5, f32[]{:T(128)} %get-tuple-element.4), channel_id=1, replica_groups=mesh['members'=2,'lon'=16] {'lon'}, use_global_device_ids=true, to_apply=%region_1.2 | all-reduce | flops 2 | bytes 16 | tf_op jit(solution)/shard_map/psum | solution.py:71
  69.0 4.4 %collective-permute-start.7 = (f32[8,2240]{1,0:T(8,128)S(1)}, f32[8,2240]{1,0:T(8,128)S(1)}, u32[]{:S(2)}, u32[]{:S(2)}) collective-permute-start(f32[8,2240]{1,0:T(8,128)S(1)} %get-tuple-element.32), channel_id=1, source_target_pairs={{1,0},{2,1},{3,2},{4,3},{5,4},{6,5},{7,6},{8,7},{9,8},{10,9},{11,1... | collective-permute-start | bytes 215048 | tf_op jit(solution)/shard_map/ppermute | solution.py:26
  73.4 2.0 %collective-permute-done.6 = f32[8,2240]{1,0:T(8,128)S(1)} collective-permute-done((f32[8,2240]{1,0:T(8,128)S(1)}, f32[8,2240]{1,0:T(8,128)S(1)}, u32[]{:S(2)}, u32[]{:S(2)}) %collective-permute-start.6) | collective-permute-done | bytes 71712 | tf_op jit(solution)/shard_map/ppermute | solution.py:25
  75.6 0.2 fusion.101
  75.8 0.3 reshape.112
  76.1 0.3 reshape.113
  76.4 0.2 pad_maximum_fusion.1
  76.7 0.7 fusion.4
  77.4 0.8 fusion.39
  78.4 0.8 fusion.2
  79.3 0.7 fusion.60
  80.0 0.2 slice.207
  81.1 4.7 %collective-permute-start.8 = (f32[8,2240]{1,0:T(8,128)S(1)}, f32[8,2240]{1,0:T(8,128)S(1)}, u32[]{:S(2)}, u32[]{:S(2)}) collective-permute-start(f32[8,2240]{1,0:T(8,128)S(1)} %get-tuple-element.17), channel_id=1, source_target_pairs={{1,0},{2,1},{3,2},{4,3},{5,4},{6,5},{7,6},{8,7},{9,8},{10,9},{11,1... | collective-permute-start | bytes 215048 | tf_op jit(solution)/shard_map/ppermute | solution.py:34
  85.8 2.0 %collective-permute-done.8 = f32[8,2240]{1,0:T(8,128)S(1)} collective-permute-done((f32[8,2240]{1,0:T(8,128)S(1)}, f32[8,2240]{1,0:T(8,128)S(1)}, u32[]{:S(2)}, u32[]{:S(2)}) %collective-permute-start.8) | collective-permute-done | bytes 71712 | tf_op jit(solution)/shard_map/ppermute | solution.py:34
  87.8 4.5 %collective-permute-done.9 = f32[8,2240]{1,0:T(8,128)S(1)} collective-permute-done((f32[8,2240]{1,0:T(8,128)S(1)}, f32[8,2240]{1,0:T(8,128)S(1)}, u32[]{:S(2)}, u32[]{:S(2)}) %collective-permute-start.9) | collective-permute-done | bytes 71712 | tf_op jit(solution)/shard_map/ppermute | solution.py:34
  92.3 0.8 multiply_reduce_fusion
  93.1 30.1 %psum.30 = f32[]{:T(128)} all-reduce(f32[]{:T(128)} %get-tuple-element.8), channel_id=1, replica_groups=mesh['members'=2,'lon'=16] {'lon'}, use_global_device_ids=true, to_apply=%region_5.6 | all-reduce | flops 1 | bytes 8 | tf_op jit(solution)/shard_map/psum | solution.py:71
  124.7 4.4 %collective-permute-start.11 = (f32[1,2240]{1,0:T(1,128)S(1)}, f32[1,2240]{1,0:T(1,128)S(1)}, u32[]{:S(2)}, u32[]{:S(2)}) collective-permute-start(f32[1,2240]{1,0:T(1,128)S(1)} %get-tuple-element.30), channel_id=1, source_target_pairs={{1,0},{2,1},{3,2},{4,3},{5,4},{6,5},{7,6},{8,7},{9,8},{10,9},{11,1... | collective-permute-start | bytes 26888 | tf_op jit(solution)/shard_map/ppermute | solution.py:26
  129.2 1.3 collective-permute-done.10
  130.5 0.9 fusion.35
  131.4 34.5 %psum.31 = f32[]{:T(128)} all-reduce(f32[]{:T(128)} %fusion.35), channel_id=1, replica_groups=mesh['members'=2,'lon'=16] {'lon'}, use_global_device_ids=true, to_apply=%region_7.8 | all-reduce | flops 1 | bytes 8 | tf_op jit(solution)/shard_map/psum | solution.py:115
  167.8 1.1 collective-permute-done.12
  169.5 0.5 collective-permute-start.13
  170.1 1.3 copy-done.2
  171.6 4.3 %collective-permute-done.13 = f32[6,1,2240]{2,1,0:T(1,128)S(1)} collective-permute-done((f32[6,1,2240]{2,1,0:T(1,128)S(1)}, f32[6,1,2240]{2,1,0:T(1,128)S(1)}, u32[]{:S(2)}, u32[]{:S(2)}) %collective-permute-start.13) | collective-permute-done | bytes 53792 | tf_op jit(solution)/shard_map/ppermute | solution.py:34
  175.9 0.9 fusion.1
  176.9 3.3 %fusion.107 = f32[6,32,2240]{2,1,0:T(8,128)S(1)} fusion(f32[6,32,2240]{2,1,0:T(8,128)S(1)} %rev.6), kind=kOutput, calls=%fused_computation.166 | output fusion | flops 2150400 | bytes 3440640 | tf_op jit(solution)/shard_map/jit(cumsum)/reduce_window_sum | solution.py:140
  180.2 1.3 rev.7
  (72 shorter events, 4.5 us)
Async XLA Ops:
  1.8 7.6 %collective-permute-start = (f32[8,2240]{1,0:T(8,128)S(1)}, f32[8,2240]{1,0:T(8,128)S(1)}, u32[]{:S(2)}, u32[]{:S(2)}) collective-permute-start(f32[8,2240]{1,0:T(8,128)S(1)} %get-tuple-element.35), channel_id=1, source_target_pairs={{0,1},{1,2},{2,3},{3,4},{4,5},{5,6},{6,7},{7,8},{8,9},{9,10},{10,1... | collective-permute-start | bytes 215048 | tf_op jit(solution)/shard_map/ppermute | solution.py:25
  2.3 7.1 %collective-permute-start.1 = (f32[8,2240]{1,0:T(8,128)S(1)}, f32[8,2240]{1,0:T(8,128)S(1)}, u32[]{:S(2)}, u32[]{:S(2)}) collective-permute-start(f32[8,2240]{1,0:T(8,128)S(1)} %get-tuple-element.36), channel_id=1, source_target_pairs={{1,0},{2,1},{3,2},{4,3},{5,4},{6,5},{7,6},{8,7},{9,8},{10,9},{11,1... | collective-permute-start | bytes 215048 | tf_op jit(solution)/shard_map/ppermute | solution.py:26
  14.5 11.5 %copy-start.7 = (f32[32,2240]{1,0:T(8,128)S(1)}, f32[32,2240]{1,0:T(8,128)}, u32[]{:S(2)}) copy-start(f32[32,2240]{1,0:T(8,128)} %param.5) | copy-start | bytes 860164
  14.9 17.2 %copy-start.9 = (f32[32,2240]{1,0:T(8,128)S(1)}, f32[32,2240]{1,0:T(8,128)}, u32[]{:S(2)}) copy-start(f32[32,2240]{1,0:T(8,128)} %param.6) | copy-start | bytes 860164
  15.1 6.4 %collective-permute-start.2 = (f32[8,2240]{1,0:T(8,128)S(1)}, f32[8,2240]{1,0:T(8,128)S(1)}, u32[]{:S(2)}, u32[]{:S(2)}) collective-permute-start(f32[8,2240]{1,0:T(8,128)S(1)} %get-tuple-element.19), channel_id=1, source_target_pairs={{1,0},{2,1},{3,2},{4,3},{5,4},{6,5},{7,6},{8,7},{9,8},{10,9},{11,1... | collective-permute-start | bytes 215048 | tf_op jit(solution)/shard_map/ppermute | solution.py:34
  19.5 6.5 %collective-permute-start.3 = (f32[8,2240]{1,0:T(8,128)S(1)}, f32[8,2240]{1,0:T(8,128)S(1)}, u32[]{:S(2)}, u32[]{:S(2)}) collective-permute-start(f32[8,2240]{1,0:T(8,128)S(1)} %get-tuple-element.20), channel_id=1, source_target_pairs={{15,0},{0,1},{1,2},{2,3},{3,4},{4,5},{5,6},{6,7},{7,8},{8,9},{9,10... | collective-permute-start | bytes 215048 | tf_op jit(solution)/shard_map/ppermute | solution.py:34
  26.2 5.8 %collective-permute-start.4 = (f32[1,2240]{1,0:T(1,128)S(1)}, f32[1,2240]{1,0:T(1,128)S(1)}, u32[]{:S(2)}, u32[]{:S(2)}) collective-permute-start(f32[1,2240]{1,0:T(1,128)S(1)} %get-tuple-element.33), channel_id=1, source_target_pairs={{0,1},{1,2},{2,3},{3,4},{4,5},{5,6},{6,7},{7,8},{8,9},{9,10},{10,1... | collective-permute-start | bytes 26888 | tf_op jit(solution)/shard_map/ppermute | solution.py:25
  26.3 5.8 %collective-permute-start.5 = (f32[1,2240]{1,0:T(1,128)S(1)}, f32[1,2240]{1,0:T(1,128)S(1)}, u32[]{:S(2)}, u32[]{:S(2)}) collective-permute-start(f32[1,2240]{1,0:T(1,128)S(1)} %get-tuple-element.34), channel_id=1, source_target_pairs={{1,0},{2,1},{3,2},{4,3},{5,4},{6,5},{7,6},{8,7},{9,8},{10,9},{11,1... | collective-permute-start | bytes 26888 | tf_op jit(solution)/shard_map/ppermute | solution.py:26
  68.9 6.5 %collective-permute-start.6 = (f32[8,2240]{1,0:T(8,128)S(1)}, f32[8,2240]{1,0:T(8,128)S(1)}, u32[]{:S(2)}, u32[]{:S(2)}) collective-permute-start(f32[8,2240]{1,0:T(8,128)S(1)} %get-tuple-element.31), channel_id=1, source_target_pairs={{0,1},{1,2},{2,3},{3,4},{4,5},{5,6},{6,7},{7,8},{8,9},{9,10},{10,1... | collective-permute-start | bytes 215048 | tf_op jit(solution)/shard_map/ppermute | solution.py:25
  69.0 6.5 %collective-permute-start.7 = (f32[8,2240]{1,0:T(8,128)S(1)}, f32[8,2240]{1,0:T(8,128)S(1)}, u32[]{:S(2)}, u32[]{:S(2)}) collective-permute-start(f32[8,2240]{1,0:T(8,128)S(1)} %get-tuple-element.32), channel_id=1, source_target_pairs={{1,0},{2,1},{3,2},{4,3},{5,4},{6,5},{7,6},{8,7},{9,8},{10,9},{11,1... | collective-permute-start | bytes 215048 | tf_op jit(solution)/shard_map/ppermute | solution.py:26
  81.0 48.2 %copy-start.8 = (s32[32,2240]{1,0:T(8,128)S(1)}, s32[32,2240]{1,0:T(8,128)}, u32[]{:S(2)}) copy-start(s32[32,2240]{1,0:T(8,128)} %param.9) | copy-start | bytes 860164
  81.1 6.7 %collective-permute-start.8 = (f32[8,2240]{1,0:T(8,128)S(1)}, f32[8,2240]{1,0:T(8,128)S(1)}, u32[]{:S(2)}, u32[]{:S(2)}) collective-permute-start(f32[8,2240]{1,0:T(8,128)S(1)} %get-tuple-element.17), channel_id=1, source_target_pairs={{1,0},{2,1},{3,2},{4,3},{5,4},{6,5},{7,6},{8,7},{9,8},{10,9},{11,1... | collective-permute-start | bytes 215048 | tf_op jit(solution)/shard_map/ppermute | solution.py:34
  85.8 6.5 %collective-permute-start.9 = (f32[8,2240]{1,0:T(8,128)S(1)}, f32[8,2240]{1,0:T(8,128)S(1)}, u32[]{:S(2)}, u32[]{:S(2)}) collective-permute-start(f32[8,2240]{1,0:T(8,128)S(1)} %get-tuple-element.18), channel_id=1, source_target_pairs={{15,0},{0,1},{1,2},{2,3},{3,4},{4,5},{5,6},{6,7},{7,8},{8,9},{9,10... | collective-permute-start | bytes 215048 | tf_op jit(solution)/shard_map/ppermute | solution.py:34
  124.7 5.8 %collective-permute-start.10 = (f32[1,2240]{1,0:T(1,128)S(1)}, f32[1,2240]{1,0:T(1,128)S(1)}, u32[]{:S(2)}, u32[]{:S(2)}) collective-permute-start(f32[1,2240]{1,0:T(1,128)S(1)} %get-tuple-element.29), channel_id=1, source_target_pairs={{0,1},{1,2},{2,3},{3,4},{4,5},{5,6},{6,7},{7,8},{8,9},{9,10},{10,1... | collective-permute-start | bytes 26888 | tf_op jit(solution)/shard_map/ppermute | solution.py:25
  124.7 5.8 %collective-permute-start.11 = (f32[1,2240]{1,0:T(1,128)S(1)}, f32[1,2240]{1,0:T(1,128)S(1)}, u32[]{:S(2)}, u32[]{:S(2)}) collective-permute-start(f32[1,2240]{1,0:T(1,128)S(1)} %get-tuple-element.30), channel_id=1, source_target_pairs={{1,0},{2,1},{3,2},{4,3},{5,4},{6,5},{7,6},{8,7},{9,8},{10,9},{11,1... | collective-permute-start | bytes 26888 | tf_op jit(solution)/shard_map/ppermute | solution.py:26
  129.2 38.6 %copy-start.5 = (f32[32,2240]{1,0:T(8,128)}, f32[32,2240]{1,0:T(8,128)S(1)}, u32[]{:S(2)}) copy-start(f32[32,2240]{1,0:T(8,128)S(1)} %convert_element_type.36) | copy-start | bytes 860164
  167.3 1.7 copy-start.4
  167.4 1.5 collective-permute-start.12
  167.8 1.5 copy-start.1
  169.3 2.1 %copy-start.2 = (f32[6,32,2240]{2,1,0:T(8,128)S(1)}, f32[6,32,2240]{2,1,0:T(8,128)}, u32[]{:S(2)}) copy-start(f32[6,32,2240]{2,1,0:T(8,128)} %param.8) | copy-start | bytes 5160964
  169.4 6.4 %copy-start = (f32[6,32,2240]{2,1,0:T(8,128)}, f32[6,32,2240]{2,1,0:T(8,128)S(1)}, u32[]{:S(2)}) copy-start(f32[6,32,2240]{2,1,0:T(8,128)S(1)} %subtract_select_fusion.1) | copy-start | bytes 5160964
  169.5 6.3 %collective-permute-start.13 = (f32[6,1,2240]{2,1,0:T(1,128)S(1)}, f32[6,1,2240]{2,1,0:T(1,128)S(1)}, u32[]{:S(2)}, u32[]{:S(2)}) collective-permute-start(f32[6,1,2240]{2,1,0:T(1,128)S(1)} %slice.222), channel_id=1, source_target_pairs={{15,0},{0,1},{1,2},{2,3},{3,4},{4,5},{5,6},{6,7},{7,8},{8,9},{9,10... | collective-permute-start | bytes 161288 | tf_op jit(solution)/shard_map/ppermute | solution.py:34
  171.4 4.5 %copy-start.6 = (f32[32,2240]{1,0:T(8,128)S(1)}, f32[32,2240]{1,0:T(8,128)}, u32[]{:S(2)}) copy-start(f32[32,2240]{1,0:T(8,128)} %copy-done.5) | copy-start | bytes 860164
  171.6 4.3 %copy-start.3 = (f32[6,32,2240]{2,1,0:T(8,128)}, f32[6,32,2240]{2,1,0:T(8,128)S(1)}, u32[]{:S(2)}) copy-start(f32[6,32,2240]{2,1,0:T(8,128)S(1)} %subtract_select_fusion) | copy-start | bytes 5160964
where the time goes:
time: 182 us
  blocking collectives  99.2 us (55%)
  starting transfers between devices  28.7 us (16%)
  waiting for transfers between devices  24.9 us (14%)
  other arithmetic  10.5 us (6%)
  local copies, waits for them, and re-layouts  6.86 us (4%)
  matrix products  6.24 us (3%)
  between operations  5.15 us (3%)
    psum x2, blocking collectives, residual_sum(): return lax.psum(jnp.sum(residue * precond), 'lon')  64.7 us
    psum x1, blocking collectives, body(): step_length = norm_now / lax.psum(jnp.sum(direction * image), 'lon')  34.5 us
    ppermute x4, starting transfers between devices, extended_2(): after = lax.ppermute(first, axis, down)  18.3 us
    ppermute x6, waiting for transfers between devices, from_behind(): return lax.ppermute(block, axis, route)  18.3 us
    ppermute x6, starting transfers between devices, from_behind(): return lax.ppermute(block, axis, route)  9.72 us
    ppermute x4, waiting for transfers between devices, extended_2(): before = lax.ppermute(last, axis, up)  6.55 us
  transfers between devices with their start and end apart: 14, of which 10 were waited for; matrix products, arithmetic and copies ran while one was open for 0% of the time, Pallas kernels for 0%

commit v1 on v0

v1 whole, which is shorter than its diff:
```python
import math

import jax
import jax.numpy as jnp
from jax import lax
from jax.sharding import PartitionSpec as P

LT = 112
OV = 8
KL = 6
ITERS = 2


tile_shift = 0.1
gravity_step = 0.5


def sine_basis(length):
    ordinal = jnp.arange(length, dtype=jnp.float32) + 1.0
    angles = math.pi * ordinal[:, None] * ordinal[None, :] / (length + 1)
    basis_matrix = jnp.sqrt(2.0 / (length + 1)) * jnp.sin(angles)
    eigen_value = 2.0 - 2.0 * jnp.cos(math.pi * ordinal / (length + 1))
    return (basis_matrix, eigen_value)


def split_windows(padded, block_len, blocks, margin):
    leading = padded.shape[:-1]
    extra_cols = block_len * (blocks + 1) - padded.shape[-1]
    padded = jnp.pad(padded, [(0, 0)] * len(leading) + [(0, extra_cols)])
    main_part = padded[..., : block_len * blocks].reshape(leading + (blocks, block_len))
    tail_part = padded[..., block_len : block_len * (blocks + 1)].reshape(
        leading + (blocks, block_len)
    )[..., : 2 * margin]
    return jnp.concatenate([main_part, tail_part], axis=-1)


def join_windows(windows, block_len, blocks, margin):
    leading = windows.shape[:-2]
    main_part = windows[..., :block_len].reshape(leading + (blocks * block_len,))
    tail_part = jnp.pad(
        windows[..., block_len:], [(0, 0)] * (len(leading) + 1) + [(0, block_len - 2 * margin)]
    )
    tail_part = tail_part.reshape(leading + (blocks * block_len,))
    widths = [(0, 0)] * len(leading)
    summed = jnp.pad(main_part, widths + [(0, block_len)]) + jnp.pad(
        tail_part, widths + [(block_len, 0)]
    )
    return summed[..., : block_len * blocks + 2 * margin]


def swap_pairs(block, outward):
    devices = lax.axis_size("lon")
    if outward:
        route = [(i, (i - 1 if i % 2 == 0 else i + 1) % devices) for i in range(devices)]
    else:
        route = [(i, i ^ 1) for i in range(devices)]
    return lax.ppermute(block, "lon", route)


def exchange(to_west, to_east):
    even = lax.axis_index("lon") % 2 == 0
    inner = swap_pairs(jnp.where(even, to_east, to_west), False)
    outer = swap_pairs(jnp.where(even, to_west, to_east), True)
    return jnp.where(even, outer, inner), jnp.where(even, inner, outer)


def total(parts):
    devices = lax.axis_size("lon")
    sent = jnp.broadcast_to(parts[None], (devices,) + parts.shape)
    return jnp.sum(lax.all_to_all(sent, "lon", 0, 0), axis=0)


def body(source, diagonal, u_vel, v_vel, bottom):
    highest = lax.Precision.HIGHEST
    cells, lat_cells = source.shape
    tiles = lat_cells // LT
    depths = bottom.astype(jnp.float32)
    wet = (bottom > 0).astype(jnp.float32)
    coef = wet * (4.0 + diagonal)
    masked = wet * source
    lon_basis, lon_value = sine_basis(cells + 2 * OV)
    lat_basis, lat_value = sine_basis(LT + 2 * OV)

    def tile_solve(rows):
        padded = jnp.pad(rows, ((0, 0), (OV, OV)))
        windows = split_windows(padded, LT, tiles, OV)
        spectral = jnp.einsum("atb,ac->ctb", windows, lon_basis, precision=highest)
        spectral = jnp.einsum("ctb,bd->ctd", spectral, lat_basis, precision=highest)
        spectral = spectral / (lon_value[:, None, None] + lat_value[None, None, :] + tile_shift)
        restored = jnp.einsum("ctd,bd->ctb", spectral, lat_basis, precision=highest)
        restored = jnp.einsum("ctb,ac->atb", restored, lon_basis, precision=highest)
        return join_windows(restored, LT, tiles, OV)[:, OV : OV + lat_cells]

    def lat_beside(x):
        p = jnp.pad(x, ((0, 0), (1, 1)))
        return p[:, 2:] + p[:, :-2]

    west, east = exchange(masked[:OV], masked[cells - OV :])
    first = tile_solve(jnp.concatenate([west, masked, east], axis=0))
    edge = OV + 1
    west, east = exchange(
        jnp.concatenate([first[: 2 * OV + 1], coef[:edge]], axis=0),
        jnp.concatenate([first[cells - 1 :], coef[cells - edge :]], axis=0),
    )
    wide = 2 * OV + 1
    z = jnp.pad(first, ((1, 1), (0, 0)))
    z = z + jnp.concatenate(
        [west[:wide], jnp.zeros((cells + 2 * edge - 2 * wide, lat_cells)), east[:wide]], axis=0
    )
    coef_wide = jnp.concatenate([west[wide:], coef, east[wide:]], axis=0)
    z = jnp.where(coef_wide > 0, z, 0.0)
    inner = coef_wide[1:-1]
    y = jnp.where(inner > 0, inner * z[1:-1] - (z[:-2] + z[2:] + lat_beside(z[1:-1])), 0.0)

    second = tile_solve(y)
    west, east = exchange(
        jnp.concatenate([second[: OV + 1], depths[:1], jnp.zeros((KL, lat_cells))], axis=0),
        jnp.concatenate([second[cells + OV - 1 :], depths[-1:], u_vel[:, cells - 1]], axis=0),
    )
    w = second[OV - 1 : cells + OV + 1]
    w = w + jnp.concatenate(
        [west[: OV + 1], jnp.zeros((cells + 2 - 2 * edge, lat_cells)), east[: OV + 1]], axis=0
    )
    near = coef_wide[OV : cells + OV + 2]
    w = jnp.where(near > 0, w, 0.0)
    z_near = z[OV : cells + OV + 2]
    wet_own = wet > 0
    x = jnp.where(wet_own, coef * w[1:-1] - (w[:-2] + w[2:] + lat_beside(w[1:-1])), 0.0)
    z_own, w_own, y_own = z_near[1:-1], w[1:-1], y[OV : cells + OV]
    land = source - masked

    def partial(a, b):
        return jnp.sum(a * b, axis=0)

    sums = total(
        jnp.stack(
            [
                partial(masked, z_own),
                partial(z_own, y_own),
                partial(masked, w_own),
                partial(y_own, w_own),
                partial(z_own, x),
                partial(w_own, x),
                partial(land, land),
            ]
        ).reshape(7, -1, LT).sum(axis=1)
    )
    rz, zy, rw, yw, zx, wx, ll = [jnp.sum(sums[i]) for i in range(7)]
    step0 = (rz + ll) / (zy + ll)
    rest = (zy - rz) / (zy + ll)
    new = rz - step0 * (zy + rw) + step0 * step0 * yw + rest * rest * ll
    beta = new / (rz + ll)
    grown = 1.0 + beta
    bent = grown * grown * zy - grown * step0 * (zx + yw) + step0 * step0 * wx
    step1 = new / (bent + (rest + beta) * (rest + beta) * ll)
    of_z = step0 + step1 * grown
    of_w = -step1 * step0
    of_land = step0 + step1 * (rest + beta)

    surface = of_z * z_near + of_w * w
    solution = surface[1:-1] + of_land * land
    levels = jnp.arange(KL, dtype=jnp.float32).reshape(KL, 1, 1)
    depth = jnp.concatenate([west[edge : edge + 1], depths, east[edge : edge + 1]], axis=0)
    u_wide = jnp.concatenate([west[edge + 1 :][:, None], u_vel], axis=1)
    u_face = levels < jnp.minimum(depth[:-1], depth[1:])[None]
    slope = gravity_step * (surface[1:] - surface[:-1])
    u_wide = jnp.where(u_face, u_wide - slope[None], 0.0)
    north_depth = jnp.pad(depths[:, 1:], ((0, 0), (0, 1)))
    north_surface = jnp.pad(solution[:, 1:], ((0, 0), (0, 1)))
    v_face = levels < jnp.minimum(depths, north_depth)[None]
    v_new = jnp.where(v_face, v_vel - gravity_step * (north_surface - solution)[None], 0.0)
    south_v = jnp.pad(v_new[:, :, :-1], ((0, 0), (0, 0), (1, 0)))
    u_new = u_wide[:, 1:]
    divergence = u_new - u_wide[:, :-1] + (v_new - south_v)
    divergence = jnp.where(levels < depths[None], divergence, 0.0)
    w_vel = [divergence[KL - 1]]
    for level in range(KL - 2, -1, -1):
        w_vel.append(w_vel[-1] + divergence[level])
    return solution, u_new, v_new, jnp.stack(w_vel[::-1])


def solution(mesh):
    return jax.shard_map(
        body,
        mesh=mesh,
        in_specs=(
            P(("members", "lon"), None),
            P(("members", "lon"), None),
            P(None, ("members", "lon"), None),
            P(None, ("members", "lon"), None),
            P(("members", "lon"), None),
        ),
        out_specs=(
            P(("members", "lon"), None),
            P(None, ("members", "lon"), None),
            P(None, ("members", "lon"), None),
            P(None, ("members", "lon"), None),
        ),
        check_vma=False,
    )
```

time: 182 us -> 81.8 us (0.45)
  blocking collectives: 99.2 us -> 0 us
  local copies, waits for them, and re-layouts: 6.86 us -> 21 us
  starting transfers between devices: 28.7 us -> 18 us
  waiting for transfers between devices: 24.9 us -> 15.3 us
  between operations: 5.15 us -> 11.7 us
    psum x3 -> x0, blocking collectives: 99.2 us -> none  [the longest x2 64.7 us: residual_sum(): return lax.psum(jnp.sum(residue * precond), 'lon')]
    ppermute x14 -> x6, waiting for transfers between devices: 24.9 us -> 8.52 us  [swap_pairs(): return lax.ppermute(block, 'lon', route)]
    ppermute x14 -> x6, starting transfers between devices: 28.7 us -> 13 us  [swap_pairs(): return lax.ppermute(block, 'lon', route)]
    all_to_all x0 -> x1, waiting for transfers between devices: none -> 6.75 us  [total(): return jnp.sum(lax.all_to_all(sent, 'lon', 0, 0), axis=0)]
    all_to_all x0 -> x1, starting transfers between devices: none -> 5.03 us  [total(): return jnp.sum(lax.all_to_all(sent, 'lon', 0, 0), axis=0)]
    slice x9 -> x14, local copies, waits for them, and re-layouts: 0.42 us -> 4.06 us  [the longest x1 1.96 us: split_windows(): padded[..., block_len:block_len * (blocks + 1)]]
    select_n x0 -> x12, other arithmetic: none -> 3.56 us  [the longest x1 1.93 us: body(): divergence = jnp.where(levels < depths[None], divergence, 0.0)]
    unnamed x22 -> x50, local copies, waits for them, and re-layouts: 1.88 us -> 5.36 us
  transfers between devices with their start and end apart: 14 -> 7, of which waited for: 10 -> 3; matrix products, arithmetic and copies ran while one was open for 0% -> 4% of each run, Pallas kernels for 0% -> 0%
where the time goes in v1:
time: 81.8 us; the launch traced here: 81.1 us
  local copies, waits for them, and re-layouts  21 us (26%)
  starting transfers between devices  18 us (22%)
  waiting for transfers between devices  15.3 us (19%)
  between operations  11.7 us (14%)
  other arithmetic  8.81 us (11%)
  matrix products  6.29 us (8%)
    ppermute x6, starting transfers between devices, swap_pairs(): return lax.ppermute(block, 'lon', route)  13 us
    ppermute x6, waiting for transfers between devices, swap_pairs(): return lax.ppermute(block, 'lon', route)  8.52 us
    all_to_all x1, waiting for transfers between devices, total(): return jnp.sum(lax.all_to_all(sent, 'lon', 0, 0), axis=0)  6.75 us
    unnamed x50, local copies, waits for them, and re-layouts  5.36 us
    all_to_all x1, starting transfers between devices, total(): return jnp.sum(lax.all_to_all(sent, 'lon', 0, 0), axis=0)  5.03 us
    slice x1, local copies, waits for them, and re-layouts, split_windows(): padded[..., block_len:block_len * (blocks + 1)]  1.96 us
    select_n x1, other arithmetic, body(): divergence = jnp.where(levels < depths[None], divergence, 0.0)  1.93 us
    dot_general x2, matrix products, tile_solve(): restored = jnp.einsum('ctd,bd->ctb', spectral, lat_basis, precision=highest)  1.68 us
  transfers between devices with their start and end apart: 7, of which 3 were waited for; matrix products, arithmetic and copies ran while one was open for 4% of the time, Pallas kernels for 0%

profile of v1, /device:TPU:0, one launch (start us, length us, event | category | flops | bytes accessed | tf_op | source)
XLA Modules:
  0.0 81.1 jit_solution(13343007831432647834)
XLA Ops:
  0.7 1.0 %convert_element_type.32 = f32[32,2240]{1,0:T(8,128)S(1)} convert(s32[32,2240]{1,0:T(8,128)} %param.9) | non-fusion elementwise | flops 71680 | bytes 573440 | tf_op jit(solution)/shard_map/convert_element_type | solution.py:77
  1.8 1.3 %broadcast_select_fusion = (f32[32,2240]{1,0:T(8,128)S(1)}, pred[32,2240]{1,0:T(8,128)(4,1)S(1)}, f32[32,2240]{1,0:T(8,128)S(1)}) fusion(f32[32,2240]{1,0:T(8,128)} %param.5, s32[32,2240]{1,0:T(8,128)} %param.9, f32[32,2239]{1,0:T(8,128)S(1)} %slice.337), kind=kLoop, calls=%fused_computation.84 | loop fusion | flops 286720 | bytes 1505152 | tf_op jit(solution)/shard_map/mul | solution.py:80
  3.1 5.5 %collective-permute-start = (f32[8,2240]{1,0:T(8,128)S(1)}, f32[8,2240]{1,0:T(8,128)S(1)}, u32[]{:S(2)}, u32[]{:S(2)}) collective-permute-start(f32[8,2240]{1,0:T(8,128)S(1)} %get-tuple-element.45), channel_id=1, source_target_pairs={{0,15},{1,2},{2,1},{3,4},{4,3},{5,6},{6,5},{7,8},{8,7},{9,10},{10,... | collective-permute-start | bytes 215048 | tf_op jit(solution)/shard_map/ppermute | solution.py:57
  8.7 1.1 %slice.259 = f32[6,1,2240]{2,1,0:T(1,128)S(1)} slice(f32[6,32,2240]{2,1,0:T(8,128)} %param.7), slice={[0:6], [31:32], [0:2240]} | slice | bytes 107520 | tf_op jit(solution)/shard_map/slice | solution.py:118
  9.8 0.6 copy.59
  10.5 0.7 pad.88.clone
  11.7 0.3 reshape.123
  12.1 0.3 reshape.124
  12.5 0.8 fusion.4
  13.3 0.8 %convolution_divide_fusion.1 = f32[48,20,128]{2,0,1:T(8,128)S(1)} fusion(f32[48,20,128]{2,0,1:T(8,128)S(1)} %fusion.4, f32[48,128]{1,0:T(8,128)S(1)} %add_add_fusion, f32[128]{0:T(128)S(1)} %get-tuple-element.51, f32[128]{0:T(128)S(1)} %get-tuple-element.52), kind=kOutput, calls=%fused_computation.10 | convolution fusion | flops 188915712 | bytes 1008640 | tf_op jit(solution)/shard_map/ctb,bd->ctd/dot_general | solution.py:88
  14.2 0.8 %fusion.37 = f32[48,20,128]{2,0,1:T(8,128)S(1)} fusion(f32[48,20,128]{2,0,1:T(8,128)S(1)} %convolution_divide_fusion.1, f32[128]{0:T(128)S(1)} %get-tuple-element.51, f32[128]{0:T(128)S(1)} %get-tuple-element.52), kind=kOutput, calls=%fused_computation.101 | convolution fusion | flops 188792832 | bytes 984064 | tf_op jit(solution)/shard_map/ctd,bd->ctb/dot_general | solution.py:90
  15.0 0.7 fusion.60
  15.7 0.2 slice.297
  16.7 0.3 fusion.26
  17.1 3.8 %collective-permute-start.2 = (f32[26,2240]{1,0:T(8,128)S(1)}, f32[26,2240]{1,0:T(8,128)S(1)}, u32[]{:S(2)}, u32[]{:S(2)}) collective-permute-start(f32[26,2240]{1,0:T(8,128)S(1)} %get-tuple-element.30), channel_id=1, source_target_pairs={{0,15},{1,2},{2,1},{3,4},{4,3},{5,6},{6,5},{7,8},{8,7},{9,10},{10,... | collective-permute-start | bytes 698888 | tf_op jit(solution)/shard_map/ppermute | solution.py:57
  20.9 0.3 pad_add_fusion
  21.2 4.9 %collective-permute-done.2 = f32[26,2240]{1,0:T(8,128)S(1)} collective-permute-done((f32[26,2240]{1,0:T(8,128)S(1)}, f32[26,2240]{1,0:T(8,128)S(1)}, u32[]{:S(2)}, u32[]{:S(2)}) %collective-permute-start.2) | collective-permute-done | bytes 232992 | tf_op jit(solution)/shard_map/ppermute | solution.py:57
  26.5 0.4 copy-done.6
  26.9 0.3 fusion.14
  27.4 0.9 %pad.65 = f32[48,2256]{1,0:T(8,128)} pad(f32[48,2240]{1,0:T(8,128)S(1)} %fusion.14, f32[]{:T(128)} %constant.22.clone.1), padding=0_0x8_8 | pad | bytes 863236 | tf_op jit(solution)/shard_map/jit(_pad)/pad | solution.py:85
  28.4 0.3 reshape.127
  28.8 2.0 %pad_slice_fusion = f32[48,2240]{1,0:T(8,128)} fusion(f32[48,2256]{1,0:T(8,128)} %pad.65), kind=kLoop, calls=%fused_computation.24 | loop fusion | bytes 863232 | tf_op jit(solution)/shard_map/slice | solution.py:31
  30.7 1.3 %reshape.128 = f32[48,20,112]{2,1,0:T(8,128)S(1)} reshape(f32[48,2240]{1,0:T(8,128)} %pad_slice_fusion) | data formatting | bytes 860160 | tf_op jit(solution)/shard_map/reshape | solution.py:31
  32.1 0.8 fusion.8
  32.9 0.8 %convolution_divide_fusion = f32[48,20,128]{2,0,1:T(8,128)S(1)} fusion(f32[48,20,128]{2,0,1:T(8,128)S(1)} %fusion.8, f32[48,128]{1,0:T(8,128)S(1)} %copy-done.17, f32[128]{0:T(128)S(1)} %get-tuple-element.51, f32[128]{0:T(128)S(1)} %get-tuple-element.52), kind=kOutput, calls=%fused_computation.9 | convolution fusion | flops 188915712 | bytes 1008640 | tf_op jit(solution)/shard_map/ctb,bd->ctd/dot_general | solution.py:88
  33.8 0.8 %fusion.34 = f32[48,20,128]{2,0,1:T(8,128)S(1)} fusion(f32[48,20,128]{2,0,1:T(8,128)S(1)} %convolution_divide_fusion, f32[128]{0:T(128)S(1)} %get-tuple-element.51, f32[128]{0:T(128)S(1)} %get-tuple-element.52), kind=kOutput, calls=%fused_computation.98 | convolution fusion | flops 188792832 | bytes 984064 | tf_op jit(solution)/shard_map/ctd,bd->ctb/dot_general | solution.py:90
  34.6 0.7 fusion.58
  35.7 0.9 %pad.68.clone = f32[48,20,112]{2,1,0:T(8,128)} pad(f32[48,20,16]{2,1,0:T(8,128)S(1)} %copy.57, f32[]{:T(128)} %constant.22.clone.1), padding=0_0x0_0x0_96 | pad | bytes 491524 | tf_op jit(solution)/shard_map/jit(_pad)/pad | solution.py:40
  36.6 1.2 %reshape.130 = f32[48,2240]{1,0:T(8,128)S(1)} reshape(f32[48,20,112]{2,1,0:T(8,128)} %pad.68.clone) | data formatting | bytes 860160 | tf_op jit(solution)/shard_map/reshape | solution.py:43
  37.8 1.0 %copy.36 = f32[48,20,112]{2,1,0:T(8,128)} copy(f32[48,20,112]{2,0,1:T(8,128)S(1)} %bitcast.39) | data formatting | bytes 860160 | tf_op jit(solution)/shard_map/slice | solution.py:39
  38.8 1.3 %reshape.129 = f32[48,2240]{1,0:T(8,128)S(1)} reshape(f32[48,20,112]{2,1,0:T(8,128)} %copy.36) | data formatting | bytes 860160 | tf_op jit(solution)/shard_map/reshape | solution.py:39
  40.1 0.2 pad_add_fusion.1
  40.6 3.7 %collective-permute-start.4 = (f32[16,2240]{1,0:T(8,128)S(1)}, f32[16,2240]{1,0:T(8,128)S(1)}, u32[]{:S(2)}, u32[]{:S(2)}) collective-permute-start(f32[16,2240]{1,0:T(8,128)S(1)} %get-tuple-element.36), channel_id=1, source_target_pairs={{0,15},{1,2},{2,1},{3,4},{4,3},{5,6},{6,5},{7,8},{8,7},{9,10},{10,... | collective-permute-start | bytes 430088 | tf_op jit(solution)/shard_map/ppermute | solution.py:57
  44.4 3.6 %collective-permute-done.4 = f32[16,2240]{1,0:T(8,128)S(1)} collective-permute-done((f32[16,2240]{1,0:T(8,128)S(1)}, f32[16,2240]{1,0:T(8,128)S(1)}, u32[]{:S(2)}, u32[]{:S(2)}) %collective-permute-start.4) | collective-permute-done | bytes 143392 | tf_op jit(solution)/shard_map/ppermute | solution.py:57
  48.0 0.6 slice_bitcast_fusion
  48.7 0.6 slice.332
  49.3 0.3 fusion.18
  49.6 0.5 multiply_reduce_fusion.2
  50.8 0.6 broadcast_in_dim.22
  51.4 5.0 %all-to-all-start = ((f32[16,7,112]{2,1,0:T(8,128)}), f32[16,7,112]{2,1,0:T(8,128)S(1)}, u32[]{:S(2)}, u32[]{:S(2)}) async-start(f32[16,7,112]{2,1,0:T(8,128)} %broadcast_in_dim.22), calls=%async_computation | async-start | bytes 131072 | tf_op jit(solution)/shard_map/all_to_all | solution.py:70
  56.6 6.8 %all-to-all-done = f32[16,7,112]{2,1,0:T(8,128)S(1)} async-done(((f32[16,7,112]{2,1,0:T(8,128)}), f32[16,7,112]{2,1,0:T(8,128)S(1)}, u32[]{:S(2)}, u32[]{:S(2)}) %all-to-all-start) | async-done | bytes 50208 | tf_op jit(solution)/shard_map/all_to_all | solution.py:70
  63.4 0.7 slice_reduce_fusion
  74.8 1.2 %copy-done.5 = f32[6,32,2240]{2,1,0:T(8,128)S(1)} copy-done((f32[6,32,2240]{2,1,0:T(8,128)S(1)}, f32[6,32,2240]{2,1,0:T(8,128)}, u32[]{:S(2)}) %copy-start.5) | copy-done | bytes 1720344
  76.0 0.4 fusion
  76.4 1.1 %copy-done = f32[6,32,2240]{2,1,0:T(8,128)S(1)} copy-done((f32[6,32,2240]{2,1,0:T(8,128)S(1)}, f32[6,32,2240]{2,1,0:T(8,128)}, u32[]{:S(2)}) %copy-start) | copy-done | bytes 1720344
  77.5 0.2 subtract_select_fusion
  77.7 1.9 %fusion.2 = (f32[6,32,2240]{2,1,0:T(8,128)S(1)}, f32[6,32,2240]{2,1,0:T(8,128)}) fusion(f32[6,33,2240]{2,1,0:T(8,128)S(1)} %fusion, f32[6,32,2239]{2,1,0:T(8,128)S(1)} %bitcast.38, f32[32,2240]{1,0:T(8,128)S(1)} %convert_element_type.32, f32[6,32,2240]{2,1,0:T(8,128)S(1)} %copy-done, f32[32,2240]{1,0:T(8,128)S(1)} %subtract_multiply_fusion, ...), kind=kLoop, calls=%fused_computation.5 | loop fusion | flops 3440640 | bytes 11181312 | tf_op jit(solution)/shard_map/jit(_where)/select_n | solution.py:175
  79.9 1.2 %copy-done.14 = f32[6,32,2240]{2,1,0:T(8,128)} copy-done((f32[6,32,2240]{2,1,0:T(8,128)}, f32[6,32,2240]{2,1,0:T(8,128)S(1)}, u32[]{:S(2)}) %copy-start.14) | copy-done | bytes 1720344
  (109 shorter events, 4.7 us)
Async XLA Ops:
  0.6 9.8 %copy-start.10 = (f32[32,2240]{1,0:T(8,128)S(1)}, f32[32,2240]{1,0:T(8,128)}, u32[]{:S(2)}) copy-start(f32[32,2240]{1,0:T(8,128)} %param.6) | copy-start | bytes 860164
  3.1 8.3 %copy-start.8 = (pred[32,2240]{1,0:T(8,128)(4,1)}, pred[32,2240]{1,0:T(8,128)(4,1)S(1)}, u32[]{:S(2)}) copy-start(pred[32,2240]{1,0:T(8,128)(4,1)S(1)} %get-tuple-element.25) | copy-start | bytes 215044
  3.1 8.2 %collective-permute-start = (f32[8,2240]{1,0:T(8,128)S(1)}, f32[8,2240]{1,0:T(8,128)S(1)}, u32[]{:S(2)}, u32[]{:S(2)}) collective-permute-start(f32[8,2240]{1,0:T(8,128)S(1)} %get-tuple-element.45), channel_id=1, source_target_pairs={{0,15},{1,2},{2,1},{3,4},{4,3},{5,6},{6,5},{7,8},{8,7},{9,10},{10,... | collective-permute-start | bytes 215048 | tf_op jit(solution)/shard_map/ppermute | solution.py:57
  8.6 2.7 %collective-permute-start.1 = (f32[8,2240]{1,0:T(8,128)S(1)}, f32[8,2240]{1,0:T(8,128)S(1)}, u32[]{:S(2)}, u32[]{:S(2)}) collective-permute-start(f32[8,2240]{1,0:T(8,128)S(1)} %get-tuple-element.46), channel_id=1, source_target_pairs={{0,1},{1,0},{2,3},{3,2},{4,5},{5,4},{6,7},{7,6},{8,9},{9,8},{10,11... | collective-permute-start | bytes 215048 | tf_op jit(solution)/shard_map/ppermute | solution.py:57
  11.3 2.0 %copy-start.16 = (f32[48,128]{1,0:T(8,128)}, f32[48,128]{1,0:T(8,128)S(1)}, u32[]{:S(2)}) copy-start(f32[48,128]{1,0:T(8,128)S(1)} %add_add_fusion) | copy-start | bytes 73732
  17.1 9.0 %collective-permute-start.2 = (f32[26,2240]{1,0:T(8,128)S(1)}, f32[26,2240]{1,0:T(8,128)S(1)}, u32[]{:S(2)}, u32[]{:S(2)}) collective-permute-start(f32[26,2240]{1,0:T(8,128)S(1)} %get-tuple-element.30), channel_id=1, source_target_pairs={{0,15},{1,2},{2,1},{3,4},{4,3},{5,6},{6,5},{7,8},{8,7},{9,10},{10,... | collective-permute-start | bytes 698888 | tf_op jit(solution)/shard_map/ppermute | solution.py:57
  20.9 5.2 %collective-permute-start.3 = (f32[26,2240]{1,0:T(8,128)S(1)}, f32[26,2240]{1,0:T(8,128)S(1)}, u32[]{:S(2)}, u32[]{:S(2)}) collective-permute-start(f32[26,2240]{1,0:T(8,128)S(1)} %get-tuple-element.31), channel_id=1, source_target_pairs={{0,1},{1,0},{2,3},{3,2},{4,5},{5,4},{6,7},{7,6},{8,9},{9,8},{10,11... | collective-permute-start | bytes 698888 | tf_op jit(solution)/shard_map/ppermute | solution.py:57
  26.2 0.7 copy-start.6
  30.7 2.2 %copy-start.17 = (f32[48,128]{1,0:T(8,128)S(1)}, f32[48,128]{1,0:T(8,128)}, u32[]{:S(2)}) copy-start(f32[48,128]{1,0:T(8,128)} %copy-done.16) | copy-start | bytes 73732
  37.8 2.7 %copy-start.13 = (f32[6,1,2240]{2,0,1:T(8,128)S(1)}, f32[6,1,2240]{2,0,1:T(8,128)}, u32[]{:S(2)}) copy-start(f32[6,1,2240]{2,0,1:T(8,128)} %copy.59) | copy-start | bytes 161284
  37.8 2.7 %copy-start.18 = (f32[16]{0:T(128)S(1)}, f32[16]{0:T(128)}, u32[]{:S(2)}) copy-start(f32[16]{0:T(128)} %pad.88.clone) | copy-start | bytes 196
  38.8 10.5 %copy-start.7 = (f32[16,2240]{1,0:T(8,128)S(1)}, f32[16,2240]{1,0:T(8,128)}, u32[]{:S(2)}) copy-start(f32[16,2240]{1,0:T(8,128)} %copy-done.6) | copy-start | bytes 430084
  40.6 9.0 %copy-start.2 = (f32[32,2240]{1,0:T(8,128)S(1)}, f32[32,2240]{1,0:T(8,128)}, u32[]{:S(2)}) copy-start(f32[32,2240]{1,0:T(8,128)} %param.5) | copy-start | bytes 860164
  40.6 9.0 %copy-start.9 = (pred[32,2240]{1,0:T(8,128)(4,1)S(1)}, pred[32,2240]{1,0:T(8,128)(4,1)}, u32[]{:S(2)}) copy-start(pred[32,2240]{1,0:T(8,128)(4,1)} %copy-done.8) | copy-start | bytes 215044
  40.6 9.0 %copy-start.11 = (f32[32,2240]{1,0:T(8,128)S(1)}, f32[32,2240]{1,0:T(8,128)}, u32[]{:S(2)}) copy-start(f32[32,2240]{1,0:T(8,128)} %param.6) | copy-start | bytes 860164
  40.6 7.3 %collective-permute-start.4 = (f32[16,2240]{1,0:T(8,128)S(1)}, f32[16,2240]{1,0:T(8,128)S(1)}, u32[]{:S(2)}, u32[]{:S(2)}) collective-permute-start(f32[16,2240]{1,0:T(8,128)S(1)} %get-tuple-element.36), channel_id=1, source_target_pairs={{0,15},{1,2},{2,1},{3,4},{4,3},{5,6},{6,5},{7,8},{8,7},{9,10},{10,... | collective-permute-start | bytes 430088 | tf_op jit(solution)/shard_map/ppermute | solution.py:57
  44.3 3.6 %collective-permute-start.5 = (f32[16,2240]{1,0:T(8,128)S(1)}, f32[16,2240]{1,0:T(8,128)S(1)}, u32[]{:S(2)}, u32[]{:S(2)}) collective-permute-start(f32[16,2240]{1,0:T(8,128)S(1)} %get-tuple-element.37), channel_id=1, source_target_pairs={{0,1},{1,0},{2,3},{3,2},{4,5},{5,4},{6,7},{7,6},{8,9},{9,8},{10,11... | collective-permute-start | bytes 430088 | tf_op jit(solution)/shard_map/ppermute | solution.py:57
  49.5 6.9 %copy-start.15 = (f32[1,2240]{1,0:T(1,128)S(1)}, f32[1,2240]{1,0:T(1,128)}, u32[]{:S(2)}) copy-start(f32[1,2240]{1,0:T(1,128)} %slice.332) | copy-start | bytes 26884
  49.6 6.9 %copy-start.12 = (f32[6,1,2240]{2,0,1:T(8,128)S(1)}, f32[6,1,2240]{2,0,1:T(8,128)}, u32[]{:S(2)}) copy-start(f32[6,1,2240]{2,0,1:T(8,128)} %slice_bitcast_fusion) | copy-start | bytes 161284
  50.7 23.8 %copy-start.3 = (f32[32,2240]{1,0:T(8,128)S(1)}, f32[32,2240]{1,0:T(8,128)}, u32[]{:S(2)}) copy-start(f32[32,2240]{1,0:T(8,128)} %param.5) | copy-start | bytes 860164
  51.4 11.9 %all-to-all-start = ((f32[16,7,112]{2,1,0:T(8,128)}), f32[16,7,112]{2,1,0:T(8,128)S(1)}, u32[]{:S(2)}, u32[]{:S(2)}) async-start(f32[16,7,112]{2,1,0:T(8,128)} %broadcast_in_dim.22), calls=%async_computation | async-start | bytes 131072 | tf_op jit(solution)/shard_map/all_to_all | solution.py:70
  74.4 1.6 %copy-start.5 = (f32[6,32,2240]{2,1,0:T(8,128)S(1)}, f32[6,32,2240]{2,1,0:T(8,128)}, u32[]{:S(2)}) copy-start(f32[6,32,2240]{2,1,0:T(8,128)} %param.7) | copy-start | bytes 5160964
  74.6 1.8 %copy-start.4 = (f32[32,2240]{1,0:T(8,128)}, f32[32,2240]{1,0:T(8,128)S(1)}, u32[]{:S(2)}) copy-start(f32[32,2240]{1,0:T(8,128)S(1)} %slice_add_fusion.6) | copy-start | bytes 860164
  76.0 1.5 %copy-start = (f32[6,32,2240]{2,1,0:T(8,128)S(1)}, f32[6,32,2240]{2,1,0:T(8,128)}, u32[]{:S(2)}) copy-start(f32[6,32,2240]{2,1,0:T(8,128)} %param.8) | copy-start | bytes 5160964
  77.7 1.9 %copy-start.1 = (f32[6,32,2240]{2,1,0:T(8,128)}, f32[6,32,2240]{2,1,0:T(8,128)S(1)}, u32[]{:S(2)}) copy-start(f32[6,32,2240]{2,1,0:T(8,128)S(1)} %subtract_select_fusion) | copy-start | bytes 5160964
  79.9 1.2 %copy-start.14 = (f32[6,32,2240]{2,1,0:T(8,128)}, f32[6,32,2240]{2,1,0:T(8,128)S(1)}, u32[]{:S(2)}) copy-start(f32[6,32,2240]{2,1,0:T(8,128)S(1)} %slice_dynamic-update-slice_fusion) | copy-start | bytes 5160964

commit v2 on v0

v2 whole, which is shorter than its diff:
```python
import math

import jax
import jax.numpy as jnp
import ml_dtypes
import numpy as np
from jax import lax
from jax.experimental import pallas as pl
from jax.experimental.pallas import tpu as pltpu
from jax.sharding import PartitionSpec as P

LT = 112
OV = 8
KL = 6
LANE = 128

tile_shift = 0.1
gravity_step = 0.5

F32 = jnp.float32
BF16 = jnp.bfloat16
VM = pl.BlockSpec(memory_space=pltpu.VMEM)
SM = pl.BlockSpec(memory_space=pltpu.SMEM)
HB = pl.BlockSpec(memory_space=pl.ANY)
PARAMS = pltpu.CompilerParams(vmem_limit_bytes=40 * 1024 * 1024)


def sine_basis(length):
    ordinal = np.arange(length, dtype=np.float64) + 1.0
    angles = math.pi * ordinal[:, None] * ordinal[None, :] / (length + 1)
    basis_matrix = np.sqrt(2.0 / (length + 1)) * np.sin(angles)
    eigen_value = 2.0 - 2.0 * np.cos(math.pi * ordinal / (length + 1))
    return basis_matrix, eigen_value


def halves(matrix):
    high = matrix.astype(ml_dtypes.bfloat16)
    low = (matrix - high.astype(np.float64)).astype(ml_dtypes.bfloat16)
    return high, low


def window_at(tile):
    return divmod(tile * LT - OV + LANE, LANE)


def tables(span):
    lon_basis, lon_value = sine_basis(span)
    lat_basis, lat_value = sine_basis(LT + 2 * OV)
    high, low = halves(lat_basis)
    forward = np.zeros((8, 2 * LANE, 2 * LANE), ml_dtypes.bfloat16)
    inverse = np.zeros((8, 2 * LANE, 2 * LANE), ml_dtypes.bfloat16)
    for kind in range(8):
        lane = window_at(kind)[1]
        forward[kind, lane : lane + LANE, :LANE] = high
        forward[kind, lane : lane + LANE, LANE:] = low
        inverse[kind, :LANE, lane : lane + LANE] = high.T
        inverse[kind, LANE:, lane : lane + LANE] = low.T
    high, low = halves(lon_basis)
    lon = np.concatenate([high, low, high], axis=1)
    scale = 1.0 / (lon_value[:, None] + lat_value[None, :] + tile_shift)
    return forward, inverse, lon, scale.astype(np.float32)


def split(x):
    high = x.astype(BF16)
    return high, (x - high.astype(F32)).astype(BF16)


def tile_solve(x, forward, inverse, lon, scale, wide, spectral, restored, out):
    span, lat = x.shape
    tiles = lat // LT
    high, low = split(x)
    wide[:, :LANE] = jnp.zeros((2 * span, LANE), BF16)
    wide[:, LANE + lat :] = jnp.zeros((2 * span, wide.shape[1] - LANE - lat), BF16)
    wide[:span, LANE : LANE + lat] = high
    wide[span:, LANE : LANE + lat] = low
    for kind in range(8):
        group = range(kind, tiles, 8)
        starts = [window_at(t)[0] * LANE for t in group]
        rows = jnp.concatenate([wide[:, s : s + 2 * LANE] for s in starts], axis=0)
        product = jnp.dot(rows, forward[kind], preferred_element_type=F32)
        for i, t in enumerate(group):
            part = product[2 * span * i : 2 * span * (i + 1)]
            part = part[:, :LANE] + part[:, LANE:]
            high, low = split(part[:span] + part[span:])
            at = pl.ds(t * LANE, LANE)
            spectral[:span, at] = high
            spectral[span : 2 * span, at] = high
            spectral[2 * span :, at] = low
    chunk = 4
    for first in range(0, tiles, chunk):
        n = min(chunk, tiles - first)
        c = jnp.dot(lon[...], spectral[:, pl.ds(first * LANE, n * LANE)], preferred_element_type=F32)
        c = c * jnp.concatenate([scale[...]] * n, axis=1)
        high, low = split(c)
        c = jnp.concatenate([high, high, low], axis=0)
        c = jnp.dot(lon[...], c, preferred_element_type=F32)
        high, low = split(c)
        for i in range(n):
            for side in range(2):
                at = pl.ds((2 * (first + i) + side) * LANE, LANE)
                restored[:span, at] = high[:, i * LANE : (i + 1) * LANE]
                restored[span:, at] = low[:, i * LANE : (i + 1) * LANE]
    out[...] = jnp.zeros(out.shape, F32)
    for kind in range(8):
        group = range(kind, tiles, 8)
        rows = jnp.concatenate(
            [restored[:, pl.ds(2 * t * LANE, 2 * LANE)] for t in group], axis=0
        )
        product = jnp.dot(rows, inverse[kind], preferred_element_type=F32)
        for i, t in enumerate(group):
            part = product[2 * span * i : 2 * span * (i + 1)]
            at = pl.ds(window_at(t)[0] * LANE, 2 * LANE)
            out[:, at] += part[:span] + part[span:]


def solve_scratch(span, lat):
    tiles = lat // LT
    lanes = (window_at(tiles - 1)[0] + 2) * LANE
    return [
        pltpu.VMEM((2 * span, lanes), BF16),
        pltpu.VMEM((3 * span, tiles * LANE), BF16),
        pltpu.VMEM((2 * span, 2 * tiles * LANE), BF16),
        pltpu.VMEM((span, lanes), F32),
    ]


def is_even(parity, shape):
    return jnp.full(shape, parity[0], jnp.int32) == 0


def lat_beside(m):
    zero = jnp.zeros((m.shape[0], 1), m.dtype)
    return jnp.concatenate([m[:, 1:], zero], axis=1) + jnp.concatenate([zero, m[:, :-1]], axis=1)


def first_edges(parity, source_w, bottom_w, source_e, bottom_e, inner, outer):
    even = is_even(parity, inner.shape)
    west = jnp.where(bottom_w[...] > 0, source_w[...], 0.0)
    east = jnp.where(bottom_e[...] > 0, source_e[...], 0.0)
    inner[...] = jnp.where(even, east, west)
    outer[...] = jnp.where(even, west, east)


def first_solve(parity, inner_in, outer_in, source, diagonal, bottom, forward, inverse, lon, scale,
                first, inner, outer, wide, spectral, restored, out):
    cells, lat = source.shape
    even = is_even(parity, inner_in.shape)
    west = jnp.where(even, outer_in[...], inner_in[...])
    east = jnp.where(even, inner_in[...], outer_in[...])
    wet = bottom[...] > 0
    masked = jnp.where(wet, source[...], 0.0)
    x = jnp.concatenate([west, masked, east], axis=0)
    tile_solve(x, forward, inverse, lon, scale, wide, spectral, restored, out)
    first[...] = out[:, LANE : LANE + lat]
    coef = jnp.where(wet, 4.0 + diagonal[...], 0.0)
    blank = jnp.zeros((6, lat), F32)
    span = cells + 2 * OV
    to_west = jnp.concatenate(
        [first[2 * OV : 2 * OV + 1], coef[OV : OV + 1], blank, first[: 2 * OV], coef[:OV]], axis=0
    )
    to_east = jnp.concatenate(
        [blank, coef[cells - OV - 1 : cells - OV], first[cells - 1 : cells], first[cells:span],
         coef[cells - OV :]], axis=0
    )
    even = is_even(parity, inner.shape)
    inner[...] = jnp.where(even, to_east, to_west)
    outer[...] = jnp.where(even, to_west, to_east)


def second_solve(parity, inner_in, outer_in, first, diagonal, bottom, u_hbm, v_hbm, forward, inverse, lon, scale,
                 z, y, coef, second, inner, outer, u_vmem, v_vmem, wide, spectral, restored, out, m_rows, sems):
    cells, lat = diagonal.shape
    span = cells + 2 * OV
    fetch_u = pltpu.make_async_copy(u_hbm, u_vmem, sems.at[0])
    fetch_v = pltpu.make_async_copy(v_hbm, v_vmem, sems.at[1])
    fetch_u.start()
    fetch_v.start()
    even = is_even(parity, inner_in.shape)
    west = jnp.where(even, outer_in[...], inner_in[...])
    east = jnp.where(even, inner_in[...], outer_in[...])
    wet = bottom[...] > 0
    coef[:OV] = west[3 * OV :]
    coef[OV : OV + cells] = jnp.where(wet, 4.0 + diagonal[...], 0.0)
    coef[OV + cells :] = east[3 * OV :]
    m_rows[: 2 * OV] = jnp.where(coef[: 2 * OV] > 0, first[: 2 * OV] + west[OV : 3 * OV], 0.0)
    m_rows[cells:span] = jnp.where(coef[cells:] > 0, first[cells:] + east[OV : 3 * OV], 0.0)
    m_rows[2 * OV : cells] = jnp.where(coef[2 * OV : cells] > 0, first[2 * OV : cells], 0.0)
    m = m_rows[:span]
    z[...] = m
    row_w = jnp.where(west[OV - 2 : OV - 1] > 0, west[OV - 1 : OV], 0.0)
    row_e = jnp.where(east[1:2] > 0, east[0:1], 0.0)
    beside = jnp.concatenate([row_w, m[:-1]], axis=0) + jnp.concatenate([m[1:], row_e], axis=0)
    c = coef[...]
    image = jnp.where(c > 0, c * m - (beside + lat_beside(m)), 0.0)
    y[...] = image
    tile_solve(image, forward, inverse, lon, scale, wide, spectral, restored, out)
    second[...] = out[:, LANE : LANE + lat]
    depth = bottom[...].astype(F32)
    blank = jnp.zeros((6, lat), F32)
    fetch_u.wait()
    fetch_v.wait()
    to_west = jnp.concatenate([second[OV : OV + 1], depth[:1], blank, second[:OV]], axis=0)
    u_rows = [u_vmem[level, cells - 1 : cells] for level in range(KL)]
    to_east = jnp.concatenate(
        [depth[cells - 1 :]] + u_rows + [second[span - OV - 1 : span - OV], second[span - OV :]], axis=0
    )
    even = is_even(parity, inner.shape)
    inner[...] = jnp.where(even, to_east, to_west)
    outer[...] = jnp.where(even, to_west, to_east)


def sums(parity, inner_in, outer_in, second, z, y, coef, source, w, edges, sent):
    cells, lat = source.shape
    even = is_even(parity, inner_in.shape)
    west = jnp.where(even, outer_in[...], inner_in[...])
    east = jnp.where(even, inner_in[...], outer_in[...])
    own = slice(OV, OV + cells)
    full = second[own] + jnp.concatenate(
        [west[OV:], jnp.zeros((cells - 2 * OV, lat), F32), east[OV:]], axis=0
    )
    wet = coef[own] > 0
    m = jnp.where(wet, full, 0.0)
    row_w = second[OV - 1 : OV] + west[OV - 1 : OV]
    row_w = jnp.where(coef[OV - 1 : OV] > 0, row_w, 0.0)
    row_e = second[OV + cells : OV + cells + 1] + east[0:1]
    row_e = jnp.where(coef[OV + cells : OV + cells + 1] > 0, row_e, 0.0)
    w[:OV] = jnp.broadcast_to(row_w, (OV, lat))
    w[own] = m
    w[OV + cells :] = jnp.broadcast_to(row_e, (OV, lat))
    edges[: OV] = west[:OV]
    edges[OV :] = east[:OV]
    beside = jnp.concatenate([row_w, m[:-1]], axis=0) + jnp.concatenate([m[1:], row_e], axis=0)
    x = jnp.where(wet, coef[own] * m - (beside + lat_beside(m)), 0.0)
    masked = jnp.where(wet, source[...], 0.0)
    land = jnp.where(wet, 0.0, source[...])
    z_own, y_own = z[own], y[own]

    def partial(a, b):
        rows = jnp.sum(a * b, axis=0, keepdims=True)
        whole = lat // LANE * LANE
        total = rows[:, :LANE]
        for at in range(LANE, whole, LANE):
            total = total + rows[:, at : at + LANE]
        if whole < lat:
            rest = jnp.concatenate([rows[:, whole:], jnp.zeros((1, LANE - lat + whole), F32)], axis=1)
            total = total + rest
        return total

    parts = [
        partial(masked, z_own),
        partial(z_own, y_own),
        partial(masked, m),
        partial(y_own, m),
        partial(z_own, x),
        partial(m, x),
        partial(land, land),
        jnp.zeros((1, LANE), F32),
    ]
    sent[...] = jnp.broadcast_to(jnp.concatenate(parts, axis=0)[None], sent.shape)


def finish(came, z, w, edges, source, bottom, u_vel, v_vel, solution, u_new, v_new, w_vel,
           s_rows, d_rows, u_rows, v_out, w_out, s_out, sems):
    cells, lat = source.shape
    total = jnp.sum(jnp.sum(came[...], axis=0), axis=1, keepdims=True)
    rz, zy, rw, yw, zx, wx, ll = [total[i : i + 1] for i in range(7)]
    step0 = (rz + ll) / (zy + ll)
    rest = (zy - rz) / (zy + ll)
    new = rz - step0 * (zy + rw) + step0 * step0 * yw + rest * rest * ll
    beta = new / (rz + ll)
    grown = 1.0 + beta
    bent = grown * grown * zy - grown * step0 * (zx + yw) + step0 * step0 * wx
    step1 = new / (bent + (rest + beta) * (rest + beta) * ll)
    of_z = jnp.broadcast_to(step0 + step1 * grown, (OV, lat))
    of_w = jnp.broadcast_to(-step1 * step0, (OV, lat))
    of_land = jnp.broadcast_to(step0 + step1 * (rest + beta), (OV, lat))

    copies = []
    d_rows[:OV] = jnp.broadcast_to(edges[:1], (OV, lat))
    d_rows[OV : OV + cells] = bottom[...].astype(F32)
    d_rows[OV + cells :] = jnp.broadcast_to(edges[OV + 1 : OV + 2], (OV, lat))
    for at in range(0, cells + 2 * OV, OV):
        s = of_z * z[at : at + OV] + of_w * w[at : at + OV]
        if OV <= at < OV + cells:
            d = d_rows[at : at + OV]
            s = jnp.where(d > 0, s, of_land * source[at - OV : at])
            s_out[at - OV : at] = s
        s_rows[at : at + OV] = s
    copies.append(pltpu.make_async_copy(s_out, solution, sems.at[0]))
    copies[-1].start()

    s_west = s_rows[OV - 1 : OV]
    s_first = s_rows[OV : OV + 1]
    d_west = jnp.minimum(d_rows[OV - 1 : OV], d_rows[OV : OV + 1])
    for level in range(KL):
        left = edges[level + 1 : level + 2] - gravity_step * (s_first - s_west)
        u_rows[level, :OV] = jnp.broadcast_to(jnp.where(d_west > level, left, 0.0), (OV, lat))
    zero = jnp.zeros((OV, 1), F32)
    for block in range(cells // OV):
        at = OV + block * OV
        own = slice(at - OV, at)
        s = s_rows[at : at + OV]
        d = d_rows[at : at + OV]
        slope_e = gravity_step * (s_rows[at + 1 : at + OV + 1] - s)
        depth_e = jnp.minimum(d, d_rows[at + 1 : at + OV + 1])
        slope_n = gravity_step * (jnp.concatenate([s[:, 1:], zero], axis=1) - s)
        depth_n = jnp.minimum(d, jnp.concatenate([d[:, 1:], zero], axis=1))
        w_sum = jnp.zeros((OV, lat), F32)
        for level in range(KL - 1, -1, -1):
            u = jnp.where(depth_e > level, u_vel[level, own] - slope_e, 0.0)
            u_rows[level, at : at + OV] = u
            v = jnp.where(depth_n > level, v_vel[level, own] - slope_n, 0.0)
            v_out[level, own] = v
            south = jnp.concatenate([zero, v[:, :-1]], axis=1)
            flow = (u - u_rows[level, at - 1 : at + OV - 1]) + (v - south)
            w_sum = w_sum + jnp.where(d > level, flow, 0.0)
            w_out[level, own] = w_sum
        for i, (held, result) in enumerate(
            [(u_rows.at[:, at : at + OV], u_new), (v_out.at[:, own], v_new), (w_out.at[:, own], w_vel)]
        ):
            copies.append(pltpu.make_async_copy(held, result.at[:, own], sems.at[1 + 3 * block + i]))
            copies[-1].start()
    for copy in copies:
        copy.wait()


def swap_pairs(block, outward):
    devices = lax.axis_size("lon")
    if outward:
        route = [(i, (i - 1 if i % 2 == 0 else i + 1) % devices) for i in range(devices)]
    else:
        route = [(i, i ^ 1) for i in range(devices)]
    return lax.ppermute(block, "lon", route)


def shape(*dims):
    return jax.ShapeDtypeStruct(dims, F32)


def body(source, diagonal, u_vel, v_vel, bottom):
    cells, lat = source.shape
    span = cells + 2 * OV
    devices = lax.axis_size("lon")
    parity = (lax.axis_index("lon") % 2).astype(jnp.int32).reshape(1)
    consts = [jnp.asarray(table) for table in tables(span)]
    last = cells // OV - 1

    row_w = pl.BlockSpec((OV, lat), lambda i: (0, 0))
    row_e = pl.BlockSpec((OV, lat), lambda i: (last, 0))
    inner, outer = pl.pallas_call(
        first_edges,
        grid=(1,),
        in_specs=[SM, row_w, row_w, row_e, row_e],
        out_specs=[row_w, row_w],
        out_shape=[shape(OV, lat)] * 2,
        name="first_edges",
    )(parity, source, bottom, source, bottom)
    inner, outer = swap_pairs(inner, False), swap_pairs(outer, True)

    first, inner, outer = pl.pallas_call(
        first_solve,
        in_specs=[SM] + [VM] * 9,
        out_specs=[VM] * 3,
        out_shape=[shape(span, lat), shape(4 * OV, lat), shape(4 * OV, lat)],
        scratch_shapes=solve_scratch(span, lat),
        compiler_params=PARAMS,
        name="first_solve",
    )(parity, inner, outer, source, diagonal, bottom, *consts)
    inner, outer = swap_pairs(inner, False), swap_pairs(outer, True)

    z, y, coef, second, inner, outer, u_near, v_near = pl.pallas_call(
        second_solve,
        in_specs=[SM] + [VM] * 5 + [HB] * 2 + [VM] * 4,
        out_specs=[VM] * 8,
        out_shape=[shape(span, lat)] * 4 + [shape(2 * OV, lat)] * 2 + [shape(KL, cells, lat)] * 2,
        scratch_shapes=solve_scratch(span, lat)
        + [pltpu.VMEM((span, lat), F32), pltpu.SemaphoreType.DMA((2,))],
        compiler_params=PARAMS,
        name="second_solve",
    )(parity, inner, outer, first, diagonal, bottom, u_vel, v_vel, *consts)
    inner, outer = swap_pairs(inner, False), swap_pairs(outer, True)

    w, edges, sent = pl.pallas_call(
        sums,
        in_specs=[SM] + [VM] * 7,
        out_specs=[VM] * 3,
        out_shape=[shape(span, lat), shape(2 * OV, lat), shape(devices, 8, LANE)],
        compiler_params=PARAMS,
        name="sums",
    )(parity, inner, outer, second, z, y, coef, source)
    came = lax.all_to_all(sent, "lon", 0, 0)

    return pl.pallas_call(
        finish,
        in_specs=[VM] * 8,
        out_specs=[HB] * 4,
        out_shape=[shape(cells, lat)] + [shape(KL, cells, lat)] * 3,
        scratch_shapes=[
            pltpu.VMEM((span, lat), F32),
            pltpu.VMEM((span, lat), F32),
            pltpu.VMEM((KL, OV + cells, lat), F32),
            pltpu.VMEM((KL, cells, lat), F32),
            pltpu.VMEM((KL, cells, lat), F32),
            pltpu.VMEM((cells, lat), F32),
            pltpu.SemaphoreType.DMA((1 + 3 * (cells // OV),)),
        ],
        compiler_params=PARAMS,
        name="finish",
    )(came, z, w, edges, source, bottom, u_near, v_near)


def solution(mesh):
    return jax.shard_map(
        body,
        mesh=mesh,
        in_specs=(
            P(("members", "lon"), None),
            P(("members", "lon"), None),
            P(None, ("members", "lon"), None),
            P(None, ("members", "lon"), None),
            P(("members", "lon"), None),
        ),
        out_specs=(
            P(("members", "lon"), None),
            P(None, ("members", "lon"), None),
            P(None, ("members", "lon"), None),
            P(None, ("members", "lon"), None),
        ),
        check_vma=False,
    )
```

time: 182 us -> 57.2 us (0.31)
  blocking collectives: 99.2 us -> 12.5 us
  waiting for transfers between devices: 24.9 us -> 9.74 us
  starting transfers between devices: 28.7 us -> 15.8 us
  other arithmetic: 10.5 us -> 0 us
  Pallas kernels: 0 us -> 9.59 us
  matrix products: 6.24 us -> 0 us
  between operations: 5.15 us -> 0.74 us
    psum x3 -> x0, blocking collectives: 99.2 us -> none  [the longest x2 64.7 us: residual_sum(): return lax.psum(jnp.sum(residue * precond), 'lon')]
    ppermute x14 -> x6, waiting for transfers between devices: 24.9 us -> 9.74 us  [swap_pairs(): return lax.ppermute(block, 'lon', route)]
    ppermute x14 -> x6, starting transfers between devices: 28.7 us -> 15.8 us  [swap_pairs(): return lax.ppermute(block, 'lon', route)]
    all_to_all x0 -> x1, blocking collectives: none -> 12.5 us  [body(): came = lax.all_to_all(sent, 'lon', 0, 0)]
    pallas_call x0 -> x5, Pallas kernels: none -> 9.59 us  [the longest x1 2.98 us: body(): pl.pallas_call(finish, in_specs=[VM] * 8, out_specs=[HB] * 4, out_shape=[...]
    unnamed x22 -> x28, local copies, waits for them, and re-layouts: 1.88 us -> 8.31 us
    dot_general x8 -> x0, matrix products: 6.24 us -> none  [the longest x2 1.68 us: precondition(): spectral = jnp.einsum('ctb,bd->ctd', spectral, lat_basis, precision=highest)]
    another operation x2 -> x0, other arithmetic: 3.3 us -> none  [the longest x1 3.28 us: body(): w_vel = jnp.cumsum(divergence[::-1], axis=0)[::-1]]
  transfers between devices with their start and end apart: 14 -> 6, of which waited for: 10 -> 3; matrix products, arithmetic and copies ran while one was open for 0% -> 0% of each run, Pallas kernels for 0% -> 0%
where the time goes in v2:
time: 57.2 us; the launch traced here: 56.7 us
  starting transfers between devices  15.8 us (28%)
  blocking collectives  12.5 us (22%)
  waiting for transfers between devices  9.74 us (17%)
  Pallas kernels  9.59 us (17%)
  local copies, waits for them, and re-layouts  8.31 us (15%)
  between operations  0.74 us (1%)
    ppermute x6, starting transfers between devices, swap_pairs(): return lax.ppermute(block, 'lon', route)  15.8 us
    all_to_all x1, blocking collectives, body(): came = lax.all_to_all(sent, 'lon', 0, 0)  12.5 us
    ppermute x6, waiting for transfers between devices, swap_pairs(): return lax.ppermute(block, 'lon', route)  9.74 us
    unnamed x28, local copies, waits for them, and re-layouts  8.31 us
    pallas_call x1, Pallas kernels, body(): pl.pallas_call(finish, in_specs=[VM] * 8, out_specs=[HB] * 4, out_shape=[...  2.98 us
    pallas_call x1, Pallas kernels, body(): pl.pallas_call(second_solve, in_specs=[SM] + [VM] * 5 + [HB] * 2 + [VM] *...  2.7 us
    pallas_call x1, Pallas kernels, body(): pl.pallas_call(first_edges, grid=(1,), in_specs=[SM, row_w, row_w, row_e,...  1.71 us
    pallas_call x1, Pallas kernels, body(): pl.pallas_call(first_solve, in_specs=[SM] + [VM] * 9, out_specs=[VM] * 3,...  1.66 us
  transfers between devices with their start and end apart: 6, of which 3 were waited for; matrix products, arithmetic and copies ran while one was open for 0% of the time, Pallas kernels for 0%

profile of v2, /device:TPU:0, one launch (start us, length us, event | category | flops | bytes accessed | tf_op | source)
XLA Modules:
  0.0 56.7 jit_solution(3618962102133538629)
XLA Ops:
  0.6 0.0 copy-start.3
  0.7 0.0 copy-start.11
  0.7 0.0 copy-start.13
  0.7 1.7 %first_edges.1 = (f32[8,2240]{1,0:T(8,128)}, f32[8,2240]{1,0:T(8,128)}) custom-call(s32[1]{0:T(128)} %bitcast.parity, f32[32,2240]{1,0:T(8,128)} %source.5, s32[32,2240]{1,0:T(8,128)} %bottom.5, f32[32,2240]{1,0:T(8,128)} %source.5, s32[32,2240]{1,0:T(8,128)} %bottom.5), custom_call_target="tpu_custom_call" | custom-call | tf_op jit(solution)/shard_map/first_edges/pallas_call | solution.py:351
  2.4 0.5 collective-permute-start
  2.8 5.6 %collective-permute-start.1 = (f32[8,2240]{1,0:T(8,128)}, f32[8,2240]{1,0:T(8,128)S(1)}, u32[]{:S(2)}, u32[]{:S(2)}) collective-permute-start(f32[8,2240]{1,0:T(8,128)} %get-tuple-element.21), channel_id=1, source_target_pairs={{0,15},{1,2},{2,1},{3,4},{4,3},{5,6},{6,5},{7,8},{8,7},{9,10},{10,... | collective-permute-start | bytes 215048 | tf_op jit(solution)/shard_map/ppermute | solution.py:334
  8.5 0.0 collective-permute-done.inner_in
  8.5 2.3 %collective-permute-done.1.outer_in = f32[8,2240]{1,0:T(8,128)S(1)} collective-permute-done((f32[8,2240]{1,0:T(8,128)}, f32[8,2240]{1,0:T(8,128)S(1)}, u32[]{:S(2)}, u32[]{:S(2)}) %collective-permute-start.1) | collective-permute-done | bytes 71712 | tf_op jit(solution)/shard_map/ppermute | solution.py:334
  10.8 0.0 copy-start
  10.8 1.0 %copy-done = f32[32,2240]{1,0:T(8,128)S(1)} copy-done((f32[32,2240]{1,0:T(8,128)S(1)}, f32[32,2240]{1,0:T(8,128)}, u32[]{:S(2)}) %copy-start) | copy-done | bytes 286744
  11.7 0.0 copy-start.2
  11.7 1.0 %copy-done.2 = s32[32,2240]{1,0:T(8,128)S(1)} copy-done((s32[32,2240]{1,0:T(8,128)S(1)}, s32[32,2240]{1,0:T(8,128)}, u32[]{:S(2)}) %copy-start.2) | copy-done | bytes 286744
  12.7 0.0 copy-start.4
  12.7 1.2 %copy-done.4 = bf16[8,256,256]{2,1,0:T(8,128)(2,1)S(1)} copy-done((bf16[8,256,256]{2,1,0:T(8,128)(2,1)S(1)}, bf16[8,256,256]{2,1,0:T(8,128)(2,1)}, u32[]{:S(2)}) %copy-start.4) | copy-done | bytes 1048600
  13.9 0.0 copy-start.6
  13.9 1.2 %copy-done.6 = bf16[8,256,256]{2,1,0:T(8,128)(2,1)S(1)} copy-done((bf16[8,256,256]{2,1,0:T(8,128)(2,1)S(1)}, bf16[8,256,256]{2,1,0:T(8,128)(2,1)}, u32[]{:S(2)}) %copy-start.6) | copy-done | bytes 1048600
  15.2 0.0 copy-start.9
  15.2 1.0 %copy-done.9 = f32[32,2240]{1,0:T(8,128)S(1)} copy-done((f32[32,2240]{1,0:T(8,128)S(1)}, f32[32,2240]{1,0:T(8,128)}, u32[]{:S(2)}) %copy-start.9) | copy-done | bytes 286744
  16.1 0.0 copy-start.10
  16.1 0.7 %copy-done.10 = f32[48,128]{1,0:T(8,128)S(1)} copy-done((f32[48,128]{1,0:T(8,128)S(1)}, f32[48,128]{1,0:T(8,128)}, u32[]{:S(2)}) %copy-start.10) | copy-done | bytes 24600
  16.9 0.0 copy-start.12
  16.9 0.7 %copy-done.12 = bf16[48,144]{1,0:T(8,128)(2,1)S(1)} copy-done((bf16[48,144]{1,0:T(8,128)(2,1)S(1)}, bf16[48,144]{1,0:T(8,128)(2,1)}, u32[]{:S(2)}) %copy-start.12) | copy-done | bytes 13848
  17.6 0.0 copy-start.5
  17.6 0.0 copy-start.7
  17.6 1.7 %first_solve.1 = (f32[48,2240]{1,0:T(8,128)S(1)}, f32[32,2240]{1,0:T(8,128)S(1)}, f32[32,2240]{1,0:T(8,128)S(1)}) custom-call(s32[1]{0:T(128)} %bitcast.parity, f32[8,2240]{1,0:T(8,128)S(1)} %collective-permute-done.inner_in, f32[8,2240]{1,0:T(8,128)S(1)} %collective-permute-done.1.outer_in, f32[32,2240]{1,0:T(8,128)S(1)} %copy-done, ...), custom_call_target="tpu_custom_call" | custom-call | tf_op jit(solution)/shard_map/first_solve/pallas_call | solution.py:361
  19.3 0.1 collective-permute-start.2
  19.3 4.5 %collective-permute-start.3 = (f32[32,2240]{1,0:T(8,128)S(1)}, f32[32,2240]{1,0:T(8,128)S(1)}, u32[]{:S(2)}, u32[]{:S(2)}) collective-permute-start(f32[32,2240]{1,0:T(8,128)S(1)} %get-tuple-element.23), channel_id=1, source_target_pairs={{0,15},{1,2},{2,1},{3,4},{4,3},{5,6},{6,5},{7,8},{8,7},{9,10},{10,... | collective-permute-start | bytes 860168 | tf_op jit(solution)/shard_map/ppermute | solution.py:334
  23.8 0.0 collective-permute-done.2.inner_in
  23.8 4.6 %collective-permute-done.3.outer_in = f32[32,2240]{1,0:T(8,128)S(1)} collective-permute-done((f32[32,2240]{1,0:T(8,128)S(1)}, f32[32,2240]{1,0:T(8,128)S(1)}, u32[]{:S(2)}, u32[]{:S(2)}) %collective-permute-start.3) | collective-permute-done | bytes 286752 | tf_op jit(solution)/shard_map/ppermute | solution.py:334
  28.4 0.0 copy-done.3
  28.4 0.0 copy-done.11
  28.4 0.0 copy-done.13
  28.4 0.0 copy-done.5
  28.4 0.0 copy-done.7
  28.4 0.0 copy-start.8
  28.4 1.5 %copy-done.8 = f32[6,32,2240]{2,1,0:T(8,128)S(1)} copy-done((f32[6,32,2240]{2,1,0:T(8,128)S(1)}, f32[6,32,2240]{2,1,0:T(8,128)}, u32[]{:S(2)}) %copy-start.8) | copy-done | bytes 1720344
  29.9 0.0 copy-start.1
  29.9 2.7 %second_solve.1 = (f32[48,2240]{1,0:T(8,128)S(1)}, f32[48,2240]{1,0:T(8,128)S(1)}, f32[48,2240]{1,0:T(8,128)S(1)}, f32[48,2240]{1,0:T(8,128)S(1)}, f32[16,2240]{...) custom-call(s32[1]{0:T(128)} %bitcast.parity, ...), custom_call_target="tpu_custom_call" | custom-call | tf_op jit(solution)/shard_map/second_solve/pallas_call | solution.py:372
  32.6 0.8 %collective-permute-start.4 = (f32[16,2240]{1,0:T(8,128)S(1)}, f32[16,2240]{1,0:T(8,128)S(1)}, u32[]{:S(2)}, u32[]{:S(2)}) collective-permute-start(f32[16,2240]{1,0:T(8,128)S(1)} %get-tuple-element.25), channel_id=1, source_target_pairs={{0,1},{1,0},{2,3},{3,2},{4,5},{5,4},{6,7},{7,6},{8,9},{9,8},{10,11... | collective-permute-start | bytes 430088 | tf_op jit(solution)/shard_map/ppermute | solution.py:334
  33.4 4.4 %collective-permute-start.5 = (f32[16,2240]{1,0:T(8,128)S(1)}, f32[16,2240]{1,0:T(8,128)S(1)}, u32[]{:S(2)}, u32[]{:S(2)}) collective-permute-start(f32[16,2240]{1,0:T(8,128)S(1)} %get-tuple-element.26), channel_id=1, source_target_pairs={{0,15},{1,2},{2,1},{3,4},{4,3},{5,6},{6,5},{7,8},{8,7},{9,10},{10,... | collective-permute-start | bytes 430088 | tf_op jit(solution)/shard_map/ppermute | solution.py:334
  37.8 0.0 collective-permute-done.4.inner_in
  37.8 2.9 %collective-permute-done.5.outer_in = f32[16,2240]{1,0:T(8,128)S(1)} collective-permute-done((f32[16,2240]{1,0:T(8,128)S(1)}, f32[16,2240]{1,0:T(8,128)S(1)}, u32[]{:S(2)}, u32[]{:S(2)}) %collective-permute-start.5) | collective-permute-done | bytes 143392 | tf_op jit(solution)/shard_map/ppermute | solution.py:334
  40.7 0.0 copy-done.1
  40.7 0.5 sums.1
  41.2 12.5 %all_to_all.5.came = f32[16,8,128]{2,1,0:T(8,128)S(1)} all-to-all(f32[16,8,128]{2,1,0:T(8,128)S(1)} %get-tuple-element.31), channel_id=1, replica_groups=mesh['members'=2,'lon'=16] {'lon'}, dimensions={0} | all-to-all | bytes 131072 | tf_op jit(solution)/shard_map/all_to_all | solution.py:392
  53.7 3.0 %finish.1 = (f32[32,2240]{1,0:T(8,128)}, f32[6,32,2240]{2,1,0:T(8,128)}, f32[6,32,2240]{2,1,0:T(8,128)}, f32[6,32,2240]{2,1,0:T(8,128)}) custom-call(f32[16,8,128]{2,1,0:T(8,128)S(1)} %all_to_all.5.came, f32[48,2240]{1,0:T(8,128)S(1)} %get-tuple-element.28.z, f32[48,2240]{1,0:T(8,128)S(1)} %get-tuple-element.32.w, f32[16,2240]{1,0:T(8,128)S(1)} %get-tuple-element.33.edges, ...), custom_call_target="tpu_custom_call" | custom-call | tf_op jit(solution)/shard_map/finish/pallas_call | solution.py:394
Async XLA Ops:
  0.6 27.7 %copy-start.3 = (s32[32,2240]{1,0:T(8,128)S(1)}, s32[32,2240]{1,0:T(8,128)}, u32[]{:S(2)}) copy-start(s32[32,2240]{1,0:T(8,128)} %bottom.5) | copy-start | bytes 860164
  0.7 27.7 %copy-start.11 = (f32[48,128]{1,0:T(8,128)S(1)}, f32[48,128]{1,0:T(8,128)}, u32[]{:S(2)}) copy-start(f32[48,128]{1,0:T(8,128)} %constant.28.clone.scale) | copy-start | bytes 73732
  0.7 27.7 %copy-start.13 = (bf16[48,144]{1,0:T(8,128)(2,1)S(1)}, bf16[48,144]{1,0:T(8,128)(2,1)}, u32[]{:S(2)}) copy-start(bf16[48,144]{1,0:T(8,128)(2,1)} %constant.27.clone.lon) | copy-start | bytes 41476
  2.4 6.1 %collective-permute-start = (f32[8,2240]{1,0:T(8,128)}, f32[8,2240]{1,0:T(8,128)S(1)}, u32[]{:S(2)}, u32[]{:S(2)}) collective-permute-start(f32[8,2240]{1,0:T(8,128)} %get-tuple-element.20), channel_id=1, source_target_pairs={{0,1},{1,0},{2,3},{3,2},{4,5},{5,4},{6,7},{7,6},{8,9},{9,8},{10,11... | collective-permute-start | bytes 215048 | tf_op jit(solution)/shard_map/ppermute | solution.py:334
  2.8 7.9 %collective-permute-start.1 = (f32[8,2240]{1,0:T(8,128)}, f32[8,2240]{1,0:T(8,128)S(1)}, u32[]{:S(2)}, u32[]{:S(2)}) collective-permute-start(f32[8,2240]{1,0:T(8,128)} %get-tuple-element.21), channel_id=1, source_target_pairs={{0,15},{1,2},{2,1},{3,4},{4,3},{5,6},{6,5},{7,8},{8,7},{9,10},{10,... | collective-permute-start | bytes 215048 | tf_op jit(solution)/shard_map/ppermute | solution.py:334
  10.8 1.0 %copy-start = (f32[32,2240]{1,0:T(8,128)S(1)}, f32[32,2240]{1,0:T(8,128)}, u32[]{:S(2)}) copy-start(f32[32,2240]{1,0:T(8,128)} %source.5) | copy-start | bytes 860164
  11.7 1.0 %copy-start.2 = (s32[32,2240]{1,0:T(8,128)S(1)}, s32[32,2240]{1,0:T(8,128)}, u32[]{:S(2)}) copy-start(s32[32,2240]{1,0:T(8,128)} %bottom.5) | copy-start | bytes 860164
  12.7 1.2 %copy-start.4 = (bf16[8,256,256]{2,1,0:T(8,128)(2,1)S(1)}, bf16[8,256,256]{2,1,0:T(8,128)(2,1)}, u32[]{:S(2)}) copy-start(bf16[8,256,256]{2,1,0:T(8,128)(2,1)} %constant.26.clone.inverse) | copy-start | bytes 3145732
  13.9 1.2 %copy-start.6 = (bf16[8,256,256]{2,1,0:T(8,128)(2,1)S(1)}, bf16[8,256,256]{2,1,0:T(8,128)(2,1)}, u32[]{:S(2)}) copy-start(bf16[8,256,256]{2,1,0:T(8,128)(2,1)} %constant.25.clone.forward) | copy-start | bytes 3145732
  15.2 1.0 %copy-start.9 = (f32[32,2240]{1,0:T(8,128)S(1)}, f32[32,2240]{1,0:T(8,128)}, u32[]{:S(2)}) copy-start(f32[32,2240]{1,0:T(8,128)} %diagonal.3) | copy-start | bytes 860164
  16.1 0.7 %copy-start.10 = (f32[48,128]{1,0:T(8,128)S(1)}, f32[48,128]{1,0:T(8,128)}, u32[]{:S(2)}) copy-start(f32[48,128]{1,0:T(8,128)} %constant.28.clone.scale) | copy-start | bytes 73732
  16.9 0.7 %copy-start.12 = (bf16[48,144]{1,0:T(8,128)(2,1)S(1)}, bf16[48,144]{1,0:T(8,128)(2,1)}, u32[]{:S(2)}) copy-start(bf16[48,144]{1,0:T(8,128)(2,1)} %constant.27.clone.lon) | copy-start | bytes 41476
  17.6 10.8 %copy-start.5 = (bf16[8,256,256]{2,1,0:T(8,128)(2,1)S(1)}, bf16[8,256,256]{2,1,0:T(8,128)(2,1)}, u32[]{:S(2)}) copy-start(bf16[8,256,256]{2,1,0:T(8,128)(2,1)} %constant.26.clone.inverse) | copy-start | bytes 3145732
  17.6 10.8 %copy-start.7 = (f32[6,32,2240]{2,1,0:T(8,128)S(1)}, f32[6,32,2240]{2,1,0:T(8,128)}, u32[]{:S(2)}) copy-start(f32[6,32,2240]{2,1,0:T(8,128)} %u_hbm.1) | copy-start | bytes 5160964
  19.3 4.5 %collective-permute-start.2 = (f32[32,2240]{1,0:T(8,128)S(1)}, f32[32,2240]{1,0:T(8,128)S(1)}, u32[]{:S(2)}, u32[]{:S(2)}) collective-permute-start(f32[32,2240]{1,0:T(8,128)S(1)} %get-tuple-element.22), channel_id=1, source_target_pairs={{0,1},{1,0},{2,3},{3,2},{4,5},{5,4},{6,7},{7,6},{8,9},{9,8},{10,11... | collective-permute-start | bytes 860168 | tf_op jit(solution)/shard_map/ppermute | solution.py:334
  19.3 9.0 %collective-permute-start.3 = (f32[32,2240]{1,0:T(8,128)S(1)}, f32[32,2240]{1,0:T(8,128)S(1)}, u32[]{:S(2)}, u32[]{:S(2)}) collective-permute-start(f32[32,2240]{1,0:T(8,128)S(1)} %get-tuple-element.23), channel_id=1, source_target_pairs={{0,15},{1,2},{2,1},{3,4},{4,3},{5,6},{6,5},{7,8},{8,7},{9,10},{10,... | collective-permute-start | bytes 860168 | tf_op jit(solution)/shard_map/ppermute | solution.py:334
  28.4 1.5 %copy-start.8 = (f32[6,32,2240]{2,1,0:T(8,128)S(1)}, f32[6,32,2240]{2,1,0:T(8,128)}, u32[]{:S(2)}) copy-start(f32[6,32,2240]{2,1,0:T(8,128)} %v_hbm.1) | copy-start | bytes 5160964
  29.9 10.8 %copy-start.1 = (f32[32,2240]{1,0:T(8,128)S(1)}, f32[32,2240]{1,0:T(8,128)}, u32[]{:S(2)}) copy-start(f32[32,2240]{1,0:T(8,128)} %source.5) | copy-start | bytes 860164
  32.6 5.2 %collective-permute-start.4 = (f32[16,2240]{1,0:T(8,128)S(1)}, f32[16,2240]{1,0:T(8,128)S(1)}, u32[]{:S(2)}, u32[]{:S(2)}) collective-permute-start(f32[16,2240]{1,0:T(8,128)S(1)} %get-tuple-element.25), channel_id=1, source_target_pairs={{0,1},{1,0},{2,3},{3,2},{4,5},{5,4},{6,7},{7,6},{8,9},{9,8},{10,11... | collective-permute-start | bytes 430088 | tf_op jit(solution)/shard_map/ppermute | solution.py:334
  33.4 7.3 %collective-permute-start.5 = (f32[16,2240]{1,0:T(8,128)S(1)}, f32[16,2240]{1,0:T(8,128)S(1)}, u32[]{:S(2)}, u32[]{:S(2)}) collective-permute-start(f32[16,2240]{1,0:T(8,128)S(1)} %get-tuple-element.26), channel_id=1, source_target_pairs={{0,15},{1,2},{2,1},{3,4},{4,3},{5,6},{6,5},{7,8},{8,7},{9,10},{10,... | collective-permute-start | bytes 430088 | tf_op jit(solution)/shard_map/ppermute | solution.py:334

commit v3 on v2

--- a/solution.py
+++ b/solution.py
@@ -22,7 +22,7 @@
 VM = pl.BlockSpec(memory_space=pltpu.VMEM)
 SM = pl.BlockSpec(memory_space=pltpu.SMEM)
 HB = pl.BlockSpec(memory_space=pl.ANY)
-PARAMS = pltpu.CompilerParams(vmem_limit_bytes=40 * 1024 * 1024)
+PARAMS = pltpu.CompilerParams(vmem_limit_bytes=32 * 1024 * 1024)
 
 
 def sine_basis(length):
@@ -125,8 +125,9 @@
     ]
 
 
-def is_even(parity, shape):
-    return jnp.full(shape, parity[0], jnp.int32) == 0
+def pick(parity, inner, outer):
+    even = jnp.full(inner.shape, parity[0], jnp.int32) == 0
+    return jnp.where(even, outer, inner), jnp.where(even, inner, outer)
 
 
 def lat_beside(m):
@@ -134,104 +135,110 @@
     return jnp.concatenate([m[:, 1:], zero], axis=1) + jnp.concatenate([zero, m[:, :-1]], axis=1)
 
 
+def pack(message, rows):
+    n, lat = rows.shape
+    for block, at in enumerate(range(0, lat, LANE)):
+        width = min(LANE, lat - at)
+        message[block * n : (block + 1) * n, :width] = rows[:, at : at + width]
+
+
+def unpack(message, n, lat):
+    blocks = [message[i * n : (i + 1) * n] for i in range(-(-lat // LANE))]
+    return jnp.concatenate(blocks, axis=1)[:, :lat]
+
+
 def first_edges(parity, source_w, bottom_w, source_e, bottom_e, inner, outer):
-    even = is_even(parity, inner.shape)
     west = jnp.where(bottom_w[...] > 0, source_w[...], 0.0)
     east = jnp.where(bottom_e[...] > 0, source_e[...], 0.0)
-    inner[...] = jnp.where(even, east, west)
-    outer[...] = jnp.where(even, west, east)
-
-
-def first_solve(parity, inner_in, outer_in, source, diagonal, bottom, forward, inverse, lon, scale,
+    outer[...], inner[...] = pick(parity, east, west)
+
+
+def prepare(parity, inner_w, outer_w, source_h, diagonal_h, bottom_h, u_h, v_h, *refs):
+    tables_h, refs = refs[:4], refs[4:]
+    inner, outer, masked, coef, depth, source, u, v = refs[:8]
+    held, (diagonal, bottom, sems) = refs[8:12], refs[12:]
+    pairs = [(source_h, source), (bottom_h, bottom), (diagonal_h, diagonal), (u_h, u)]
+    pairs += list(zip(tables_h, held)) + [(v_h, v)]
+    copies = [pltpu.make_async_copy(a, b, sems.at[i]) for i, (a, b) in enumerate(pairs)]
+    for copy in copies:
+        copy.start()
+    for copy in copies[:3]:
+        copy.wait()
+    cells, lat = source.shape
+    wet = bottom[...] > 0
+    masked[...] = jnp.where(wet, source[...], 0.0)
+    coef[...] = jnp.where(wet, 4.0 + diagonal[...], 0.0)
+    depth[...] = bottom[...].astype(F32)
+    copies[3].wait()
+    edge = OV + 1
+    to_west = jnp.concatenate(
+        [coef[:edge], jnp.zeros((2 * OV - edge - 1, lat), F32), depth[:1]], axis=0
+    )
+    u_rows = [u[level, cells - 1 : cells] for level in range(KL)]
+    to_east = jnp.concatenate(u_rows + [depth[cells - 1 :], coef[cells - edge :]], axis=0)
+    outer[...], inner[...] = pick(parity, to_east, to_west)
+    for copy in copies[4:]:
+        copy.wait()
+
+
+def first_solve(parity, inner_in, outer_in, masked, forward, inverse, lon, scale,
                 first, inner, outer, wide, spectral, restored, out):
-    cells, lat = source.shape
-    even = is_even(parity, inner_in.shape)
-    west = jnp.where(even, outer_in[...], inner_in[...])
-    east = jnp.where(even, inner_in[...], outer_in[...])
-    wet = bottom[...] > 0
-    masked = jnp.where(wet, source[...], 0.0)
-    x = jnp.concatenate([west, masked, east], axis=0)
+    cells, lat = masked.shape
+    west, east = pick(parity, inner_in[...], outer_in[...])
+    x = jnp.concatenate([west, masked[...], east], axis=0)
     tile_solve(x, forward, inverse, lon, scale, wide, spectral, restored, out)
     first[...] = out[:, LANE : LANE + lat]
-    coef = jnp.where(wet, 4.0 + diagonal[...], 0.0)
-    blank = jnp.zeros((6, lat), F32)
+    reach = 2 * OV + 1
+    to_outer, to_inner = pick(parity, first[cells - 1 :], first[:reach])
+    pack(inner, to_inner)
+    pack(outer, to_outer)
+
+
+def second_solve(parity, inner_in, outer_in, inner_far, outer_far, first, coef_own, forward, inverse, lon, scale,
+                 z, y, coef, second, edges, inner, outer, wide, spectral, restored, out, m_rows, c_rows):
+    cells, lat = coef_own.shape
     span = cells + 2 * OV
-    to_west = jnp.concatenate(
-        [first[2 * OV : 2 * OV + 1], coef[OV : OV + 1], blank, first[: 2 * OV], coef[:OV]], axis=0
-    )
-    to_east = jnp.concatenate(
-        [blank, coef[cells - OV - 1 : cells - OV], first[cells - 1 : cells], first[cells:span],
-         coef[cells - OV :]], axis=0
-    )
-    even = is_even(parity, inner.shape)
-    inner[...] = jnp.where(even, to_east, to_west)
-    outer[...] = jnp.where(even, to_west, to_east)
-
-
-def second_solve(parity, inner_in, outer_in, first, diagonal, bottom, u_hbm, v_hbm, forward, inverse, lon, scale,
-                 z, y, coef, second, inner, outer, u_vmem, v_vmem, wide, spectral, restored, out, m_rows, sems):
-    cells, lat = diagonal.shape
-    span = cells + 2 * OV
-    fetch_u = pltpu.make_async_copy(u_hbm, u_vmem, sems.at[0])
-    fetch_v = pltpu.make_async_copy(v_hbm, v_vmem, sems.at[1])
-    fetch_u.start()
-    fetch_v.start()
-    even = is_even(parity, inner_in.shape)
-    west = jnp.where(even, outer_in[...], inner_in[...])
-    east = jnp.where(even, inner_in[...], outer_in[...])
-    wet = bottom[...] > 0
-    coef[:OV] = west[3 * OV :]
-    coef[OV : OV + cells] = jnp.where(wet, 4.0 + diagonal[...], 0.0)
-    coef[OV + cells :] = east[3 * OV :]
-    m_rows[: 2 * OV] = jnp.where(coef[: 2 * OV] > 0, first[: 2 * OV] + west[OV : 3 * OV], 0.0)
-    m_rows[cells:span] = jnp.where(coef[cells:] > 0, first[cells:] + east[OV : 3 * OV], 0.0)
-    m_rows[2 * OV : cells] = jnp.where(coef[2 * OV : cells] > 0, first[2 * OV : cells], 0.0)
-    m = m_rows[:span]
+    reach = 2 * OV + 1
+    far_w, far_e = pick(parity, inner_far[...], outer_far[...])
+    edges[:OV] = far_w[:OV]
+    edges[OV:] = far_e[OV:]
+    c_rows[: 2 * OV] = far_w
+    c_rows[: OV - 1] = jnp.zeros((OV - 1, lat), F32)
+    c_rows[2 * OV : 2 * OV + cells] = coef_own[...]
+    c_rows[2 * OV + cells :] = far_e
+    west, east = pick(parity, unpack(inner_in, reach, lat), unpack(outer_in, reach, lat))
+    m_rows[:OV] = jnp.zeros((OV, lat), F32)
+    m_rows[OV : OV + span] = first[...]
+    m_rows[OV + span :] = jnp.zeros((OV, lat), F32)
+    m_rows[OV - 1 : OV - 1 + reach] += west
+    m_rows[OV + cells : OV + cells + reach] += east
+    m_rows[...] = jnp.where(c_rows[...] > 0, m_rows[...], 0.0)
+    inside = slice(OV, OV + span)
+    c, m = c_rows[inside], m_rows[inside]
+    coef[...] = c
     z[...] = m
-    row_w = jnp.where(west[OV - 2 : OV - 1] > 0, west[OV - 1 : OV], 0.0)
-    row_e = jnp.where(east[1:2] > 0, east[0:1], 0.0)
-    beside = jnp.concatenate([row_w, m[:-1]], axis=0) + jnp.concatenate([m[1:], row_e], axis=0)
-    c = coef[...]
+    beside = m_rows[OV - 1 : OV - 1 + span] + m_rows[OV + 1 : OV + 1 + span]
     image = jnp.where(c > 0, c * m - (beside + lat_beside(m)), 0.0)
     y[...] = image
     tile_solve(image, forward, inverse, lon, scale, wide, spectral, restored, out)
     second[...] = out[:, LANE : LANE + lat]
-    depth = bottom[...].astype(F32)
-    blank = jnp.zeros((6, lat), F32)
-    fetch_u.wait()
-    fetch_v.wait()
-    to_west = jnp.concatenate([second[OV : OV + 1], depth[:1], blank, second[:OV]], axis=0)
-    u_rows = [u_vmem[level, cells - 1 : cells] for level in range(KL)]
-    to_east = jnp.concatenate(
-        [depth[cells - 1 :]] + u_rows + [second[span - OV - 1 : span - OV], second[span - OV :]], axis=0
-    )
-    even = is_even(parity, inner.shape)
-    inner[...] = jnp.where(even, to_east, to_west)
-    outer[...] = jnp.where(even, to_west, to_east)
-
-
-def sums(parity, inner_in, outer_in, second, z, y, coef, source, w, edges, sent):
+    to_outer, to_inner = pick(parity, second[span - OV - 1 :], second[: OV + 1])
+    pack(inner, to_inner)
+    pack(outer, to_outer)
+
+
+def sums(parity, inner_in, outer_in, second, z, y, coef, source, w, sent):
     cells, lat = source.shape
-    even = is_even(parity, inner_in.shape)
-    west = jnp.where(even, outer_in[...], inner_in[...])
-    east = jnp.where(even, inner_in[...], outer_in[...])
+    west, east = pick(parity, unpack(inner_in, OV + 1, lat), unpack(outer_in, OV + 1, lat))
+    w[...] = second[...]
+    w[OV - 1 : 2 * OV] += west
+    w[cells : cells + OV + 1] += east
+    w[...] = jnp.where(coef[...] > 0, w[...], 0.0)
     own = slice(OV, OV + cells)
-    full = second[own] + jnp.concatenate(
-        [west[OV:], jnp.zeros((cells - 2 * OV, lat), F32), east[OV:]], axis=0
-    )
-    wet = coef[own] > 0
-    m = jnp.where(wet, full, 0.0)
-    row_w = second[OV - 1 : OV] + west[OV - 1 : OV]
-    row_w = jnp.where(coef[OV - 1 : OV] > 0, row_w, 0.0)
-    row_e = second[OV + cells : OV + cells + 1] + east[0:1]
-    row_e = jnp.where(coef[OV + cells : OV + cells + 1] > 0, row_e, 0.0)
-    w[:OV] = jnp.broadcast_to(row_w, (OV, lat))
-    w[own] = m
-    w[OV + cells :] = jnp.broadcast_to(row_e, (OV, lat))
-    edges[: OV] = west[:OV]
-    edges[OV :] = east[:OV]
-    beside = jnp.concatenate([row_w, m[:-1]], axis=0) + jnp.concatenate([m[1:], row_e], axis=0)
-    x = jnp.where(wet, coef[own] * m - (beside + lat_beside(m)), 0.0)
+    c, m = coef[own], w[own]
+    wet = c > 0
+    beside = w[OV - 1 : OV - 1 + cells] + w[OV + 1 : OV + 1 + cells]
+    x = jnp.where(wet, c * m - (beside + lat_beside(m)), 0.0)
     masked = jnp.where(wet, source[...], 0.0)
     land = jnp.where(wet, 0.0, source[...])
     z_own, y_own = z[own], y[own]
@@ -260,7 +267,7 @@
     sent[...] = jnp.broadcast_to(jnp.concatenate(parts, axis=0)[None], sent.shape)
 
 
-def finish(came, z, w, edges, source, bottom, u_vel, v_vel, solution, u_new, v_new, w_vel,
+def finish(came, z, w, edges, source, depth, u_vel, v_vel, solution, u_new, v_new, w_vel,
            s_rows, d_rows, u_rows, v_out, w_out, s_out, sems):
     cells, lat = source.shape
     total = jnp.sum(jnp.sum(came[...], axis=0), axis=1, keepdims=True)
@@ -277,9 +284,9 @@
     of_land = jnp.broadcast_to(step0 + step1 * (rest + beta), (OV, lat))
 
     copies = []
-    d_rows[:OV] = jnp.broadcast_to(edges[:1], (OV, lat))
-    d_rows[OV : OV + cells] = bottom[...].astype(F32)
-    d_rows[OV + cells :] = jnp.broadcast_to(edges[OV + 1 : OV + 2], (OV, lat))
+    d_rows[:OV] = jnp.broadcast_to(edges[KL : KL + 1], (OV, lat))
+    d_rows[OV : OV + cells] = depth[...]
+    d_rows[OV + cells :] = jnp.broadcast_to(edges[2 * OV - 1 :], (OV, lat))
     for at in range(0, cells + 2 * OV, OV):
         s = of_z * z[at : at + OV] + of_w * w[at : at + OV]
         if OV <= at < OV + cells:
@@ -294,7 +301,7 @@
     s_first = s_rows[OV : OV + 1]
     d_west = jnp.minimum(d_rows[OV - 1 : OV], d_rows[OV : OV + 1])
     for level in range(KL):
-        left = edges[level + 1 : level + 2] - gravity_step * (s_first - s_west)
+        left = edges[level : level + 1] - gravity_step * (s_first - s_west)
         u_rows[level, :OV] = jnp.broadcast_to(jnp.where(d_west > level, left, 0.0), (OV, lat))
     zero = jnp.zeros((OV, 1), F32)
     for block in range(cells // OV):
@@ -334,6 +341,10 @@
     return lax.ppermute(block, "lon", route)
 
 
+def in_hbm(x):
+    return pltpu.with_memory_space_constraint(x, pltpu.HBM)
+
+
 def shape(*dims):
     return jax.ShapeDtypeStruct(dims, F32)
 
@@ -356,39 +367,59 @@
         out_shape=[shape(OV, lat)] * 2,
         name="first_edges",
     )(parity, source, bottom, source, bottom)
-    inner, outer = swap_pairs(inner, False), swap_pairs(outer, True)
-
+    near = swap_pairs(inner, False), swap_pairs(outer, True)
+
+    inner, outer, masked, coef_own, depth, source_v, u_v, v_v, *held = pl.pallas_call(
+        prepare,
+        in_specs=[SM] + [HB] * 11,
+        out_specs=[VM] * 12,
+        out_shape=[pltpu.VMEM((2 * OV, lat), F32)] * 2
+        + [pltpu.VMEM((cells, lat), F32)] * 4
+        + [pltpu.VMEM((KL, cells, lat), F32)] * 2
+        + [pltpu.VMEM(table.shape, table.dtype) for table in consts],
+        scratch_shapes=[
+            pltpu.VMEM((cells, lat), F32),
+            pltpu.VMEM((cells, lat), jnp.int32),
+            pltpu.SemaphoreType.DMA((9,)),
+        ],
+        compiler_params=pltpu.CompilerParams(vmem_limit_bytes=16 * 1024 * 1024),
+        cost_estimate=pl.CostEstimate(flops=10**6, bytes_accessed=7 * 10**6, transcendentals=0),
+        name="prepare",
+    )(parity, inner, outer, *[in_hbm(x) for x in (source, diagonal, bottom, u_vel, v_vel, *consts)])
+    far = swap_pairs(inner, False), swap_pairs(outer, True)
+
+    blocks = -(-lat // LANE)
     first, inner, outer = pl.pallas_call(
         first_solve,
-        in_specs=[SM] + [VM] * 9,
+        in_specs=[SM] + [VM] * 7,
         out_specs=[VM] * 3,
-        out_shape=[shape(span, lat), shape(4 * OV, lat), shape(4 * OV, lat)],
+        out_shape=[shape(span, lat)] + [shape((2 * OV + 1) * blocks, LANE)] * 2,
         scratch_shapes=solve_scratch(span, lat),
         compiler_params=PARAMS,
+        cost_estimate=pl.CostEstimate(flops=10**6, bytes_accessed=10**6, transcendentals=0),
         name="first_solve",
-    )(parity, inner, outer, source, diagonal, bottom, *consts)
-    inner, outer = swap_pairs(inner, False), swap_pairs(outer, True)
-
-    z, y, coef, second, inner, outer, u_near, v_near = pl.pallas_call(
+    )(parity, *near, masked, *held)
+    near = swap_pairs(inner, False), swap_pairs(outer, True)
+
+    z, y, coef, second, edges, inner, outer = pl.pallas_call(
         second_solve,
-        in_specs=[SM] + [VM] * 5 + [HB] * 2 + [VM] * 4,
-        out_specs=[VM] * 8,
-        out_shape=[shape(span, lat)] * 4 + [shape(2 * OV, lat)] * 2 + [shape(KL, cells, lat)] * 2,
-        scratch_shapes=solve_scratch(span, lat)
-        + [pltpu.VMEM((span, lat), F32), pltpu.SemaphoreType.DMA((2,))],
+        in_specs=[SM] + [VM] * 10,
+        out_specs=[VM] * 7,
+        out_shape=[shape(span, lat)] * 4 + [shape(2 * OV, lat)] + [shape((OV + 1) * blocks, LANE)] * 2,
+        scratch_shapes=solve_scratch(span, lat) + [pltpu.VMEM((span + 2 * OV, lat), F32)] * 2,
         compiler_params=PARAMS,
         name="second_solve",
-    )(parity, inner, outer, first, diagonal, bottom, u_vel, v_vel, *consts)
-    inner, outer = swap_pairs(inner, False), swap_pairs(outer, True)
-
-    w, edges, sent = pl.pallas_call(
+    )(parity, *near, *far, first, coef_own, *held)
+    near = swap_pairs(inner, False), swap_pairs(outer, True)
+
+    w, sent = pl.pallas_call(
         sums,
         in_specs=[SM] + [VM] * 7,
-        out_specs=[VM] * 3,
-        out_shape=[shape(span, lat), shape(2 * OV, lat), shape(devices, 8, LANE)],
+        out_specs=[VM] * 2,
+        out_shape=[shape(span, lat), shape(devices, 8, LANE)],
         compiler_params=PARAMS,
         name="sums",
-    )(parity, inner, outer, second, z, y, coef, source)
+    )(parity, *near, second, z, y, coef, source_v)
     came = lax.all_to_all(sent, "lon", 0, 0)
 
     return pl.pallas_call(
@@ -407,7 +438,7 @@
         ],
         compiler_params=PARAMS,
         name="finish",
-    )(came, z, w, edges, source, bottom, u_near, v_near)
+    )(came, z, w, edges, source_v, depth, u_v, v_v)
 
 
 def solution(mesh):

time: 57.2 us -> 48.6 us (0.85)
  local copies, waits for them, and re-layouts: 8.31 us -> 1.8 us
  Pallas kernels: 9.59 us -> 12 us
  blocking collectives: 12.5 us -> 10.7 us
  starting transfers between devices: 15.8 us -> 14.4 us
  waiting for transfers between devices: 9.74 us -> 8.68 us
    unnamed x28 -> x4, local copies, waits for them, and re-layouts: 8.31 us -> 1.8 us
    pallas_call x3 -> x4, Pallas kernels: 4.9 us -> 7.31 us  [the longest x1 3.04 us: body(): pl.pallas_call(prepare, in_specs=[SM] + [HB] * 11, out_specs=[VM] * 12, o...]
    all_to_all x1, blocking collectives: 12.5 us -> 10.7 us  [body(): came = lax.all_to_all(sent, 'lon', 0, 0)]
    ppermute x6 -> x8, starting transfers between devices: 15.8 us -> 14.4 us  [swap_pairs(): return lax.ppermute(block, 'lon', route)]
    ppermute x6 -> x8, waiting for transfers between devices: 9.74 us -> 8.68 us  [swap_pairs(): return lax.ppermute(block, 'lon', route)]
  transfers between devices with their start and end apart: 6 -> 8, of which waited for: 3 -> 2; matrix products, arithmetic and copies ran while one was open for 0% -> 0% of each run, Pallas kernels for 0% -> 6%
where the time goes in v3:
time: 48.6 us; the launch traced here: 48.3 us
  starting transfers between devices  14.4 us (30%)
  Pallas kernels  12 us (25%)
  blocking collectives  10.7 us (22%)
  waiting for transfers between devices  8.68 us (18%)
  local copies, waits for them, and re-layouts  1.8 us (4%)
  between operations  0.7 us (1%)
    ppermute x8, starting transfers between devices, swap_pairs(): return lax.ppermute(block, 'lon', route)  14.4 us
    all_to_all x1, blocking collectives, body(): came = lax.all_to_all(sent, 'lon', 0, 0)  10.7 us
    ppermute x8, waiting for transfers between devices, swap_pairs(): return lax.ppermute(block, 'lon', route)  8.68 us
    pallas_call x1, Pallas kernels, body(): pl.pallas_call(prepare, in_specs=[SM] + [HB] * 11, out_specs=[VM] * 12, o...  3.04 us
    pallas_call x1, Pallas kernels, body(): pl.pallas_call(finish, in_specs=[VM] * 8, out_specs=[HB] * 4, out_shape=[...  3 us
    pallas_call x1, Pallas kernels, body(): pl.pallas_call(second_solve, in_specs=[SM] + [VM] * 10, out_specs=[VM] *...  1.98 us
    unnamed x4, local copies, waits for them, and re-layouts  1.8 us
    pallas_call x1, Pallas kernels, body(): pl.pallas_call(first_edges, grid=(1,), in_specs=[SM, row_w, row_w, row_e,...  1.68 us
  transfers between devices with their start and end apart: 8, of which 2 were waited for; matrix products, arithmetic and copies ran while one was open for 0% of the time, Pallas kernels for 6%

profile of v3, /device:TPU:0, one launch (start us, length us, event | category | flops | bytes accessed | tf_op | source)
XLA Modules:
  0.0 48.3 jit_solution(16707472002409160610)
XLA Ops:
  0.6 1.7 %first_edges.1 = (f32[8,2240]{1,0:T(8,128)}, f32[8,2240]{1,0:T(8,128)}) custom-call(s32[1]{0:T(128)} %bitcast.parity, f32[32,2240]{1,0:T(8,128)} %source_h.1, s32[32,2240]{1,0:T(8,128)} %bottom_h.1, f32[32,2240]{1,0:T(8,128)} %source_h.1, s32[32,2240]{1,0:T(8,128)} %bottom_h.1), custom_call_target="tpu_custom_call" | custom-call | tf_op jit(solution)/shard_map/first_edges/pallas_call | solution.py:362
  2.3 0.5 collective-permute-start
  2.8 5.6 %collective-permute-start.1 = (f32[8,2240]{1,0:T(8,128)}, f32[8,2240]{1,0:T(8,128)S(1)}, u32[]{:S(2)}, u32[]{:S(2)}) collective-permute-start(f32[8,2240]{1,0:T(8,128)} %get-tuple-element.31.outer_w), channel_id=1, source_target_pairs={{0,15},{1,2},{2,1},{3,4},{4,3},{5,6},{6,5},{7,8},{8,7},{9,10},{10,... | collective-permute-start | bytes 215048 | tf_op jit(solution)/shard_map/ppermute | solution.py:341
  8.4 0.0 copy-start
  8.4 0.9 %copy-done = f32[8,2240]{1,0:T(8,128)S(1)} copy-done((f32[8,2240]{1,0:T(8,128)S(1)}, f32[8,2240]{1,0:T(8,128)}, u32[]{:S(2)}) %copy-start) | copy-done | bytes 71704
  9.3 0.0 copy-start.1
  9.3 0.9 %copy-done.1 = f32[8,2240]{1,0:T(8,128)S(1)} copy-done((f32[8,2240]{1,0:T(8,128)S(1)}, f32[8,2240]{1,0:T(8,128)}, u32[]{:S(2)}) %copy-start.1) | copy-done | bytes 71704
  10.2 3.0 %prepare.1 = (f32[16,2240]{1,0:T(8,128)S(1)}, f32[16,2240]{1,0:T(8,128)S(1)}, f32[32,2240]{1,0:T(8,128)S(1)}, f32[32,2240]{1,0:T(8,128)S(1)}, f32[32,2240]{1,0:T...) custom-call(s32[1]{0:T(128)} %bitcast.parity, ...), custom_call_target="tpu_custom_call" | custom-call | flops 1000000 | bytes 7000000 | tf_op jit(solution)/shard_map/prepare/pallas_call | solution.py:372
  13.3 0.0 collective-permute-done.inner_in
  13.3 0.0 collective-permute-done.1.outer_in
  13.3 1.6 %first_solve.1 = (f32[48,2240]{1,0:T(8,128)S(1)}, f32[306,128]{1,0:T(8,128)S(1)}, f32[306,128]{1,0:T(8,128)S(1)}) custom-call(s32[1]{0:T(128)} %bitcast.parity, f32[8,2240]{1,0:T(8,128)S(1)} %collective-permute-done.inner_in, f32[8,2240]{1,0:T(8,128)S(1)} %collective-permute-done.1.outer_in, f32[32,2240]{1,0:T(8,128)S(1)} %get-tuple-element.32.masked, ...), custom_call_target="tpu_custom_call" | custom-call | flops 1000000 | bytes 1000000 | tf_op jit(solution)/shard_map/first_solve/pallas_call | solution.py:392
  14.9 0.1 collective-permute-start.2
  15.0 1.9 %collective-permute-start.3 = (f32[306,128]{1,0:T(8,128)S(1)}, f32[306,128]{1,0:T(8,128)S(1)}, u32[]{:S(2)}, u32[]{:S(2)}) collective-permute-start(f32[306,128]{1,0:T(8,128)S(1)} %get-tuple-element.38), channel_id=1, source_target_pairs={{0,15},{1,2},{2,1},{3,4},{4,3},{5,6},{6,5},{7,8},{8,7},{9,10},{10,... | collective-permute-start | bytes 470024 | tf_op jit(solution)/shard_map/ppermute | solution.py:341
  16.9 0.0 collective-permute-start.4
  16.9 2.6 %collective-permute-start.5 = (f32[16,2240]{1,0:T(8,128)S(1)}, f32[16,2240]{1,0:T(8,128)S(1)}, u32[]{:S(2)}, u32[]{:S(2)}) collective-permute-start(f32[16,2240]{1,0:T(8,128)S(1)} %get-tuple-element.40), channel_id=1, source_target_pairs={{0,15},{1,2},{2,1},{3,4},{4,3},{5,6},{6,5},{7,8},{8,7},{9,10},{10,... | collective-permute-start | bytes 430088 | tf_op jit(solution)/shard_map/ppermute | solution.py:341
  19.5 0.0 collective-permute-done.4.inner_far
  19.5 4.7 %collective-permute-done.5.outer_far = f32[16,2240]{1,0:T(8,128)S(1)} collective-permute-done((f32[16,2240]{1,0:T(8,128)S(1)}, f32[16,2240]{1,0:T(8,128)S(1)}, u32[]{:S(2)}, u32[]{:S(2)}) %collective-permute-start.5) | collective-permute-done | bytes 143392 | tf_op jit(solution)/shard_map/ppermute | solution.py:341
  24.2 0.0 collective-permute-done.2.inner_in
  24.2 0.0 collective-permute-done.3.outer_in
  24.2 2.0 %second_solve.1 = (f32[48,2240]{1,0:T(8,128)S(1)}, f32[48,2240]{1,0:T(8,128)S(1)}, f32[48,2240]{1,0:T(8,128)S(1)}, f32[48,2240]{1,0:T(8,128)S(1)}, f32[16,2240]{...) custom-call(s32[1]{0:T(128)} %bitcast.parity, f32[306,128]{1,0:T(8,128)S(1)} %collective-permute-done.2.inner_in, ...), custom_call_target="tpu_custom_call" | custom-call | tf_op jit(solution)/shard_map/second_solve/pallas_call | solution.py:404
  26.2 1.1 %collective-permute-start.6 = (f32[162,128]{1,0:T(8,128)S(1)}, f32[162,128]{1,0:T(8,128)S(1)}, u32[]{:S(2)}, u32[]{:S(2)}) collective-permute-start(f32[162,128]{1,0:T(8,128)S(1)} %get-tuple-element.43), channel_id=1, source_target_pairs={{0,1},{1,0},{2,3},{3,2},{4,5},{5,4},{6,7},{7,6},{8,9},{9,8},{10,11... | collective-permute-start | bytes 248840 | tf_op jit(solution)/shard_map/ppermute | solution.py:341
  27.3 2.6 %collective-permute-start.7 = (f32[162,128]{1,0:T(8,128)S(1)}, f32[162,128]{1,0:T(8,128)S(1)}, u32[]{:S(2)}, u32[]{:S(2)}) collective-permute-start(f32[162,128]{1,0:T(8,128)S(1)} %get-tuple-element.44), channel_id=1, source_target_pairs={{0,15},{1,2},{2,1},{3,4},{4,3},{5,6},{6,5},{7,8},{8,7},{9,10},{10,... | collective-permute-start | bytes 248840 | tf_op jit(solution)/shard_map/ppermute | solution.py:341
  29.9 0.0 collective-permute-done.6.inner_in
  29.9 4.0 %collective-permute-done.7.outer_in = f32[162,128]{1,0:T(8,128)S(1)} collective-permute-done((f32[162,128]{1,0:T(8,128)S(1)}, f32[162,128]{1,0:T(8,128)S(1)}, u32[]{:S(2)}, u32[]{:S(2)}) %collective-permute-start.7) | collective-permute-done | bytes 82976 | tf_op jit(solution)/shard_map/ppermute | solution.py:341
  33.9 0.6 %sums.1 = (f32[48,2240]{1,0:T(8,128)S(1)}, f32[16,8,128]{2,1,0:T(8,128)S(1)}) custom-call(s32[1]{0:T(128)} %bitcast.parity, f32[162,128]{1,0:T(8,128)S(1)} %collective-permute-done.6.inner_in, f32[162,128]{1,0:T(8,128)S(1)} %collective-permute-done.7.outer_in, f32[48,2240]{1,0:T(8,128)S(1)} %get-tuple-element.45.second, f32[48,2240]{1,0:T(8,128)S(1)} %get-tuple-element.46.z, ...), custom_call_target="tpu_custom_call" | custom-call | tf_op jit(solution)/shard_map/sums/pallas_call | solution.py:415
  34.6 10.7 %all_to_all.5.came = f32[16,8,128]{2,1,0:T(8,128)S(1)} all-to-all(f32[16,8,128]{2,1,0:T(8,128)S(1)} %get-tuple-element.50), channel_id=1, replica_groups=mesh['members'=2,'lon'=16] {'lon'}, dimensions={0} | all-to-all | bytes 131072 | tf_op jit(solution)/shard_map/all_to_all | solution.py:423
  45.3 3.0 %finish.1 = (f32[32,2240]{1,0:T(8,128)}, f32[6,32,2240]{2,1,0:T(8,128)}, f32[6,32,2240]{2,1,0:T(8,128)}, f32[6,32,2240]{2,1,0:T(8,128)}) custom-call(f32[16,8,128]{2,1,0:T(8,128)S(1)} %all_to_all.5.came, f32[48,2240]{1,0:T(8,128)S(1)} %get-tuple-element.46.z, f32[48,2240]{1,0:T(8,128)S(1)} %get-tuple-element.51.w, f32[16,2240]{1,0:T(8,128)S(1)} %get-tuple-element.52.edges, ...), custom_call_target="tpu_custom_call" | custom-call | tf_op jit(solution)/shard_map/finish/pallas_call | solution.py:425
Async XLA Ops:
  2.3 10.9 %collective-permute-start = (f32[8,2240]{1,0:T(8,128)}, f32[8,2240]{1,0:T(8,128)S(1)}, u32[]{:S(2)}, u32[]{:S(2)}) collective-permute-start(f32[8,2240]{1,0:T(8,128)} %get-tuple-element.30.inner_w), channel_id=1, source_target_pairs={{0,1},{1,0},{2,3},{3,2},{4,5},{5,4},{6,7},{7,6},{8,9},{9,8},{10,11... | collective-permute-start | bytes 215048 | tf_op jit(solution)/shard_map/ppermute | solution.py:341
  2.8 10.5 %collective-permute-start.1 = (f32[8,2240]{1,0:T(8,128)}, f32[8,2240]{1,0:T(8,128)S(1)}, u32[]{:S(2)}, u32[]{:S(2)}) collective-permute-start(f32[8,2240]{1,0:T(8,128)} %get-tuple-element.31.outer_w), channel_id=1, source_target_pairs={{0,15},{1,2},{2,1},{3,4},{4,3},{5,6},{6,5},{7,8},{8,7},{9,10},{10,... | collective-permute-start | bytes 215048 | tf_op jit(solution)/shard_map/ppermute | solution.py:341
  8.4 0.9 %copy-start = (f32[8,2240]{1,0:T(8,128)S(1)}, f32[8,2240]{1,0:T(8,128)}, u32[]{:S(2)}) copy-start(f32[8,2240]{1,0:T(8,128)} %get-tuple-element.31.outer_w) | copy-start | bytes 215044
  9.3 0.9 %copy-start.1 = (f32[8,2240]{1,0:T(8,128)S(1)}, f32[8,2240]{1,0:T(8,128)}, u32[]{:S(2)}) copy-start(f32[8,2240]{1,0:T(8,128)} %get-tuple-element.30.inner_w) | copy-start | bytes 215044
  14.9 9.3 %collective-permute-start.2 = (f32[306,128]{1,0:T(8,128)S(1)}, f32[306,128]{1,0:T(8,128)S(1)}, u32[]{:S(2)}, u32[]{:S(2)}) collective-permute-start(f32[306,128]{1,0:T(8,128)S(1)} %get-tuple-element.37), channel_id=1, source_target_pairs={{0,1},{1,0},{2,3},{3,2},{4,5},{5,4},{6,7},{7,6},{8,9},{9,8},{10,11... | collective-permute-start | bytes 470024 | tf_op jit(solution)/shard_map/ppermute | solution.py:341
  15.0 9.2 %collective-permute-start.3 = (f32[306,128]{1,0:T(8,128)S(1)}, f32[306,128]{1,0:T(8,128)S(1)}, u32[]{:S(2)}, u32[]{:S(2)}) collective-permute-start(f32[306,128]{1,0:T(8,128)S(1)} %get-tuple-element.38), channel_id=1, source_target_pairs={{0,15},{1,2},{2,1},{3,4},{4,3},{5,6},{6,5},{7,8},{8,7},{9,10},{10,... | collective-permute-start | bytes 470024 | tf_op jit(solution)/shard_map/ppermute | solution.py:341
  16.9 2.6 %collective-permute-start.4 = (f32[16,2240]{1,0:T(8,128)S(1)}, f32[16,2240]{1,0:T(8,128)S(1)}, u32[]{:S(2)}, u32[]{:S(2)}) collective-permute-start(f32[16,2240]{1,0:T(8,128)S(1)} %get-tuple-element.39), channel_id=1, source_target_pairs={{0,1},{1,0},{2,3},{3,2},{4,5},{5,4},{6,7},{7,6},{8,9},{9,8},{10,11... | collective-permute-start | bytes 430088 | tf_op jit(solution)/shard_map/ppermute | solution.py:341
  16.9 7.3 %collective-permute-start.5 = (f32[16,2240]{1,0:T(8,128)S(1)}, f32[16,2240]{1,0:T(8,128)S(1)}, u32[]{:S(2)}, u32[]{:S(2)}) collective-permute-start(f32[16,2240]{1,0:T(8,128)S(1)} %get-tuple-element.40), channel_id=1, source_target_pairs={{0,15},{1,2},{2,1},{3,4},{4,3},{5,6},{6,5},{7,8},{8,7},{9,10},{10,... | collective-permute-start | bytes 430088 | tf_op jit(solution)/shard_map/ppermute | solution.py:341
  26.2 3.7 %collective-permute-start.6 = (f32[162,128]{1,0:T(8,128)S(1)}, f32[162,128]{1,0:T(8,128)S(1)}, u32[]{:S(2)}, u32[]{:S(2)}) collective-permute-start(f32[162,128]{1,0:T(8,128)S(1)} %get-tuple-element.43), channel_id=1, source_target_pairs={{0,1},{1,0},{2,3},{3,2},{4,5},{5,4},{6,7},{7,6},{8,9},{9,8},{10,11... | collective-permute-start | bytes 248840 | tf_op jit(solution)/shard_map/ppermute | solution.py:341
  27.3 6.6 %collective-permute-start.7 = (f32[162,128]{1,0:T(8,128)S(1)}, f32[162,128]{1,0:T(8,128)S(1)}, u32[]{:S(2)}, u32[]{:S(2)}) collective-permute-start(f32[162,128]{1,0:T(8,128)S(1)} %get-tuple-element.44), channel_id=1, source_target_pairs={{0,15},{1,2},{2,1},{3,4},{4,3},{5,6},{6,5},{7,8},{8,7},{9,10},{10,... | collective-permute-start | bytes 248840 | tf_op jit(solution)/shard_map/ppermute | solution.py:341

commit v4 on v3

--- a/solution.py
+++ b/solution.py
@@ -147,71 +147,78 @@
     return jnp.concatenate(blocks, axis=1)[:, :lat]
 
 
-def first_edges(parity, source_w, bottom_w, source_e, bottom_e, inner, outer):
+def first_edges(parity, source, bottom, inner, outer, source_w, source_e, bottom_w, bottom_e, sems):
+    last = source.shape[0] - OV
+    pairs = [(source, 0, source_w), (bottom, 0, bottom_w), (source, last, source_e), (bottom, last, bottom_e)]
+    copies = [
+        pltpu.make_async_copy(held.at[pl.ds(at, OV)], block, sems.at[i])
+        for i, (held, at, block) in enumerate(pairs)
+    ]
+    for copy in copies:
+        copy.start()
+    for copy in copies:
+        copy.wait()
     west = jnp.where(bottom_w[...] > 0, source_w[...], 0.0)
     east = jnp.where(bottom_e[...] > 0, source_e[...], 0.0)
     outer[...], inner[...] = pick(parity, east, west)
 
 
-def prepare(parity, inner_w, outer_w, source_h, diagonal_h, bottom_h, u_h, v_h, *refs):
-    tables_h, refs = refs[:4], refs[4:]
-    inner, outer, masked, coef, depth, source, u, v = refs[:8]
-    held, (diagonal, bottom, sems) = refs[8:12], refs[12:]
-    pairs = [(source_h, source), (bottom_h, bottom), (diagonal_h, diagonal), (u_h, u)]
-    pairs += list(zip(tables_h, held)) + [(v_h, v)]
+def prepare(inner, outer, source_h, diagonal_h, bottom_h, *refs):
+    tables_h, (masked, coef, depth, source), held = refs[:4], refs[4:8], refs[8:12]
+    diagonal, bottom, sems = refs[12:]
+    pairs = [(source_h, source), (bottom_h, bottom), (diagonal_h, diagonal)]
+    pairs += list(zip(tables_h, held))
     copies = [pltpu.make_async_copy(a, b, sems.at[i]) for i, (a, b) in enumerate(pairs)]
     for copy in copies:
         copy.start()
     for copy in copies[:3]:
         copy.wait()
-    cells, lat = source.shape
     wet = bottom[...] > 0
     masked[...] = jnp.where(wet, source[...], 0.0)
     coef[...] = jnp.where(wet, 4.0 + diagonal[...], 0.0)
     depth[...] = bottom[...].astype(F32)
-    copies[3].wait()
-    edge = OV + 1
-    to_west = jnp.concatenate(
-        [coef[:edge], jnp.zeros((2 * OV - edge - 1, lat), F32), depth[:1]], axis=0
-    )
-    u_rows = [u[level, cells - 1 : cells] for level in range(KL)]
-    to_east = jnp.concatenate(u_rows + [depth[cells - 1 :], coef[cells - edge :]], axis=0)
-    outer[...], inner[...] = pick(parity, to_east, to_west)
-    for copy in copies[4:]:
+    for copy in copies[3:]:
         copy.wait()
 
 
-def first_solve(parity, inner_in, outer_in, masked, forward, inverse, lon, scale,
-                first, inner, outer, wide, spectral, restored, out):
+def first_solve(parity, inner_in, outer_in, masked, coef, u_h, v_h, forward, inverse, lon, scale,
+                first, inner, outer, u, v, wide, spectral, restored, out, sems):
     cells, lat = masked.shape
+    copies = [pltpu.make_async_copy(a, b, sems.at[i]) for i, (a, b) in enumerate([(u_h, u), (v_h, v)])]
+    for copy in copies:
+        copy.start()
     west, east = pick(parity, inner_in[...], outer_in[...])
     x = jnp.concatenate([west, masked[...], east], axis=0)
     tile_solve(x, forward, inverse, lon, scale, wide, spectral, restored, out)
     first[...] = out[:, LANE : LANE + lat]
-    reach = 2 * OV + 1
-    to_outer, to_inner = pick(parity, first[cells - 1 :], first[:reach])
+    reach, edge = 2 * OV + 1, OV + 1
+    to_west = jnp.concatenate([first[:reach], coef[:edge]], axis=0)
+    to_east = jnp.concatenate([first[cells - 1 :], coef[cells - edge :]], axis=0)
+    to_outer, to_inner = pick(parity, to_east, to_west)
     pack(inner, to_inner)
     pack(outer, to_outer)
-
-
-def second_solve(parity, inner_in, outer_in, inner_far, outer_far, first, coef_own, forward, inverse, lon, scale,
-                 z, y, coef, second, edges, inner, outer, wide, spectral, restored, out, m_rows, c_rows):
+    for copy in copies:
+        copy.wait()
+
+
+def second_solve(parity, inner_in, outer_in, first, coef_own, depth, u, forward, inverse, lon, scale,
+                 z, y, coef, second, inner, outer, wide, spectral, restored, out, m_rows, c_rows):
     cells, lat = coef_own.shape
     span = cells + 2 * OV
-    reach = 2 * OV + 1
-    far_w, far_e = pick(parity, inner_far[...], outer_far[...])
-    edges[:OV] = far_w[:OV]
-    edges[OV:] = far_e[OV:]
-    c_rows[: 2 * OV] = far_w
-    c_rows[: OV - 1] = jnp.zeros((OV - 1, lat), F32)
+    reach, edge = 2 * OV + 1, OV + 1
+    west, east = pick(
+        parity, unpack(inner_in, reach + edge, lat), unpack(outer_in, reach + edge, lat)
+    )
+    c_rows[:OV] = jnp.zeros((OV, lat), F32)
+    c_rows[OV - 1 : 2 * OV] = west[reach:]
     c_rows[2 * OV : 2 * OV + cells] = coef_own[...]
-    c_rows[2 * OV + cells :] = far_e
-    west, east = pick(parity, unpack(inner_in, reach, lat), unpack(outer_in, reach, lat))
+    c_rows[2 * OV + cells + OV :] = jnp.zeros((OV, lat), F32)
+    c_rows[2 * OV + cells : 2 * OV + cells + edge] = east[reach:]
     m_rows[:OV] = jnp.zeros((OV, lat), F32)
     m_rows[OV : OV + span] = first[...]
     m_rows[OV + span :] = jnp.zeros((OV, lat), F32)
-    m_rows[OV - 1 : OV - 1 + reach] += west
-    m_rows[OV + cells : OV + cells + reach] += east
+    m_rows[OV - 1 : OV - 1 + reach] += west[:reach]
+    m_rows[OV + cells : OV + cells + reach] += east[:reach]
     m_rows[...] = jnp.where(c_rows[...] > 0, m_rows[...], 0.0)
     inside = slice(OV, OV + span)
     c, m = c_rows[inside], m_rows[inside]
@@ -222,17 +229,20 @@
     y[...] = image
     tile_solve(image, forward, inverse, lon, scale, wide, spectral, restored, out)
     second[...] = out[:, LANE : LANE + lat]
-    to_outer, to_inner = pick(parity, second[span - OV - 1 :], second[: OV + 1])
-    pack(inner, to_inner)
-    pack(outer, to_outer)
-
-
-def sums(parity, inner_in, outer_in, second, z, y, coef, source, w, sent):
+    to_west = jnp.concatenate([second[:edge], depth[:1], jnp.zeros((KL, lat), F32)], axis=0)
+    u_rows = [u[level, cells - 1 : cells] for level in range(KL)]
+    to_east = jnp.concatenate([second[span - edge :], depth[cells - 1 :]] + u_rows, axis=0)
+    outer[...], inner[...] = pick(parity, to_east, to_west)
+
+
+def sums(parity, inner_in, outer_in, second, z, y, coef, source, w, edges, sent):
     cells, lat = source.shape
-    west, east = pick(parity, unpack(inner_in, OV + 1, lat), unpack(outer_in, OV + 1, lat))
+    west, east = pick(parity, inner_in[...], outer_in[...])
+    edges[:OV] = west[OV:]
+    edges[OV:] = east[OV:]
     w[...] = second[...]
-    w[OV - 1 : 2 * OV] += west
-    w[cells : cells + OV + 1] += east
+    w[OV - 1 : 2 * OV] += west[: OV + 1]
+    w[cells : cells + OV + 1] += east[: OV + 1]
     w[...] = jnp.where(coef[...] > 0, w[...], 0.0)
     own = slice(OV, OV + cells)
     c, m = coef[own], w[own]
@@ -244,15 +254,18 @@
     z_own, y_own = z[own], y[own]
 
     def partial(a, b):
-        rows = jnp.sum(a * b, axis=0, keepdims=True)
+        product = a * b
+        rows = product[:OV]
+        for at in range(OV, cells, OV):
+            rows = rows + product[at : at + OV]
         whole = lat // LANE * LANE
         total = rows[:, :LANE]
         for at in range(LANE, whole, LANE):
             total = total + rows[:, at : at + LANE]
         if whole < lat:
-            rest = jnp.concatenate([rows[:, whole:], jnp.zeros((1, LANE - lat + whole), F32)], axis=1)
-            total = total + rest
-        return total
+            blank = jnp.zeros((OV, LANE - lat + whole), F32)
+            total = total + jnp.concatenate([rows[:, whole:], blank], axis=1)
+        return jnp.sum(total, axis=0, keepdims=True)
 
     parts = [
         partial(masked, z_own),
@@ -265,6 +278,15 @@
         jnp.zeros((1, LANE), F32),
     ]
     sent[...] = jnp.broadcast_to(jnp.concatenate(parts, axis=0)[None], sent.shape)
+
+
+def send(copies, level, at, u_rows, v_out, w_out, u_new, v_new, w_vel, sems):
+    own = slice(at - OV, at)
+    for held, rows, result in ((u_rows, slice(at, at + OV), u_new), (v_out, own, v_new), (w_out, own, w_vel)):
+        copies.append(
+            pltpu.make_async_copy(held.at[level, rows], result.at[level, own], sems.at[len(copies)])
+        )
+        copies[-1].start()
 
 
 def finish(came, z, w, edges, source, depth, u_vel, v_vel, solution, u_new, v_new, w_vel,
@@ -284,9 +306,9 @@
     of_land = jnp.broadcast_to(step0 + step1 * (rest + beta), (OV, lat))
 
     copies = []
-    d_rows[:OV] = jnp.broadcast_to(edges[KL : KL + 1], (OV, lat))
+    d_rows[:OV] = jnp.broadcast_to(edges[1:2], (OV, lat))
     d_rows[OV : OV + cells] = depth[...]
-    d_rows[OV + cells :] = jnp.broadcast_to(edges[2 * OV - 1 :], (OV, lat))
+    d_rows[OV + cells :] = jnp.broadcast_to(edges[OV + 1 : OV + 2], (OV, lat))
     for at in range(0, cells + 2 * OV, OV):
         s = of_z * z[at : at + OV] + of_w * w[at : at + OV]
         if OV <= at < OV + cells:
@@ -301,7 +323,7 @@
     s_first = s_rows[OV : OV + 1]
     d_west = jnp.minimum(d_rows[OV - 1 : OV], d_rows[OV : OV + 1])
     for level in range(KL):
-        left = edges[level : level + 1] - gravity_step * (s_first - s_west)
+        left = edges[level + 2 : level + 3] - gravity_step * (s_first - s_west)
         u_rows[level, :OV] = jnp.broadcast_to(jnp.where(d_west > level, left, 0.0), (OV, lat))
     zero = jnp.zeros((OV, 1), F32)
     for block in range(cells // OV):
@@ -323,11 +345,10 @@
             flow = (u - u_rows[level, at - 1 : at + OV - 1]) + (v - south)
             w_sum = w_sum + jnp.where(d > level, flow, 0.0)
             w_out[level, own] = w_sum
-        for i, (held, result) in enumerate(
-            [(u_rows.at[:, at : at + OV], u_new), (v_out.at[:, own], v_new), (w_out.at[:, own], w_vel)]
-        ):
-            copies.append(pltpu.make_async_copy(held, result.at[:, own], sems.at[1 + 3 * block + i]))
-            copies[-1].start()
+            if block == 0:
+                send(copies, level, at, u_rows, v_out, w_out, u_new, v_new, w_vel, sems)
+        if block > 0:
+            send(copies, slice(None), at, u_rows, v_out, w_out, u_new, v_new, w_vel, sems)
     for copy in copies:
         copy.wait()
 
@@ -341,10 +362,6 @@
     return lax.ppermute(block, "lon", route)
 
 
-def in_hbm(x):
-    return pltpu.with_memory_space_constraint(x, pltpu.HBM)
-
-
 def shape(*dims):
     return jax.ShapeDtypeStruct(dims, F32)
 
@@ -355,68 +372,70 @@
     devices = lax.axis_size("lon")
     parity = (lax.axis_index("lon") % 2).astype(jnp.int32).reshape(1)
     consts = [jnp.asarray(table) for table in tables(span)]
-    last = cells // OV - 1
-
-    row_w = pl.BlockSpec((OV, lat), lambda i: (0, 0))
-    row_e = pl.BlockSpec((OV, lat), lambda i: (last, 0))
+    hbm = {name: pltpu.with_memory_space_constraint(x, pltpu.HBM) for name, x in (
+        ("source", source), ("diagonal", diagonal), ("u", u_vel), ("v", v_vel), ("bottom", bottom))}
+    consts = [pltpu.with_memory_space_constraint(x, pltpu.HBM) for x in consts]
+
     inner, outer = pl.pallas_call(
         first_edges,
-        grid=(1,),
-        in_specs=[SM, row_w, row_w, row_e, row_e],
-        out_specs=[row_w, row_w],
-        out_shape=[shape(OV, lat)] * 2,
+        in_specs=[SM, HB, HB],
+        out_specs=[VM] * 2,
+        out_shape=[pltpu.VMEM((OV, lat), F32)] * 2,
+        scratch_shapes=[pltpu.VMEM((OV, lat), F32)] * 2
+        + [pltpu.VMEM((OV, lat), jnp.int32)] * 2
+        + [pltpu.SemaphoreType.DMA((4,))],
+        compiler_params=PARAMS,
         name="first_edges",
-    )(parity, source, bottom, source, bottom)
+    )(parity, hbm["source"], hbm["bottom"])
     near = swap_pairs(inner, False), swap_pairs(outer, True)
 
-    inner, outer, masked, coef_own, depth, source_v, u_v, v_v, *held = pl.pallas_call(
+    masked, coef_own, depth, source_v, *held = pl.pallas_call(
         prepare,
-        in_specs=[SM] + [HB] * 11,
-        out_specs=[VM] * 12,
-        out_shape=[pltpu.VMEM((2 * OV, lat), F32)] * 2
-        + [pltpu.VMEM((cells, lat), F32)] * 4
-        + [pltpu.VMEM((KL, cells, lat), F32)] * 2
+        in_specs=[HB] * 9,
+        out_specs=[VM] * 8,
+        out_shape=[pltpu.VMEM((cells, lat), F32)] * 4
         + [pltpu.VMEM(table.shape, table.dtype) for table in consts],
         scratch_shapes=[
             pltpu.VMEM((cells, lat), F32),
             pltpu.VMEM((cells, lat), jnp.int32),
-            pltpu.SemaphoreType.DMA((9,)),
+            pltpu.SemaphoreType.DMA((7,)),
         ],
-        compiler_params=pltpu.CompilerParams(vmem_limit_bytes=16 * 1024 * 1024),
+        compiler_params=PARAMS,
         cost_estimate=pl.CostEstimate(flops=10**6, bytes_accessed=7 * 10**6, transcendentals=0),
         name="prepare",
-    )(parity, inner, outer, *[in_hbm(x) for x in (source, diagonal, bottom, u_vel, v_vel, *consts)])
-    far = swap_pairs(inner, False), swap_pairs(outer, True)
+    )(inner, outer, hbm["source"], hbm["diagonal"], hbm["bottom"], *consts)
 
     blocks = -(-lat // LANE)
-    first, inner, outer = pl.pallas_call(
+    first, inner, outer, u_v, v_v = pl.pallas_call(
         first_solve,
+        in_specs=[SM] + [VM] * 4 + [HB] * 2 + [VM] * 4,
+        out_specs=[VM] * 5,
+        out_shape=[pltpu.VMEM((span, lat), F32)]
+        + [pltpu.VMEM(((3 * OV + 2) * blocks, LANE), F32)] * 2
+        + [pltpu.VMEM((KL, cells, lat), F32)] * 2,
+        scratch_shapes=solve_scratch(span, lat) + [pltpu.SemaphoreType.DMA((2,))],
+        compiler_params=PARAMS,
+        name="first_solve",
+    )(parity, *near, masked, coef_own, hbm["u"], hbm["v"], *held)
+    near = swap_pairs(inner, False), swap_pairs(outer, True)
+
+    z, y, coef, second, inner, outer = pl.pallas_call(
+        second_solve,
+        in_specs=[SM] + [VM] * 10,
+        out_specs=[VM] * 6,
+        out_shape=[pltpu.VMEM((span, lat), F32)] * 4 + [pltpu.VMEM((2 * OV, lat), F32)] * 2,
+        scratch_shapes=solve_scratch(span, lat) + [pltpu.VMEM((span + 2 * OV, lat), F32)] * 2,
+        compiler_params=PARAMS,
+        name="second_solve",
+    )(parity, *near, first, coef_own, depth, u_v, *held)
+    near = swap_pairs(inner, False), swap_pairs(outer, True)
+
+    w, edges, sent = pl.pallas_call(
+        sums,
         in_specs=[SM] + [VM] * 7,
         out_specs=[VM] * 3,
-        out_shape=[shape(span, lat)] + [shape((2 * OV + 1) * blocks, LANE)] * 2,
-        scratch_shapes=solve_scratch(span, lat),
-        compiler_params=PARAMS,
-        cost_estimate=pl.CostEstimate(flops=10**6, bytes_accessed=10**6, transcendentals=0),
-        name="first_solve",
-    )(parity, *near, masked, *held)
-    near = swap_pairs(inner, False), swap_pairs(outer, True)
-
-    z, y, coef, second, edges, inner, outer = pl.pallas_call(
-        second_solve,
-        in_specs=[SM] + [VM] * 10,
-        out_specs=[VM] * 7,
-        out_shape=[shape(span, lat)] * 4 + [shape(2 * OV, lat)] + [shape((OV + 1) * blocks, LANE)] * 2,
-        scratch_shapes=solve_scratch(span, lat) + [pltpu.VMEM((span + 2 * OV, lat), F32)] * 2,
-        compiler_params=PARAMS,
-        name="second_solve",
-    )(parity, *near, *far, first, coef_own, *held)
-    near = swap_pairs(inner, False), swap_pairs(outer, True)
-
-    w, sent = pl.pallas_call(
-        sums,
-        in_specs=[SM] + [VM] * 7,
-        out_specs=[VM] * 2,
-        out_shape=[shape(span, lat), shape(devices, 8, LANE)],
+        out_shape=[pltpu.VMEM((span, lat), F32), pltpu.VMEM((2 * OV, lat), F32),
+                   pltpu.VMEM((devices, 8, LANE), F32)],
         compiler_params=PARAMS,
         name="sums",
     )(parity, *near, second, z, y, coef, source_v)
@@ -434,7 +453,7 @@
             pltpu.VMEM((KL, cells, lat), F32),
             pltpu.VMEM((KL, cells, lat), F32),
             pltpu.VMEM((cells, lat), F32),
-            pltpu.SemaphoreType.DMA((1 + 3 * (cells // OV),)),
+            pltpu.SemaphoreType.DMA((1 + 3 * (KL + cells // OV - 1),)),
         ],
         compiler_params=PARAMS,
         name="finish",

time: 48.6 us -> 46.4 us (0.955)
  local copies, waits for them, and re-layouts: 1.8 us -> 0 us
  blocking collectives: 10.7 us -> 12.3 us
  waiting for transfers between devices: 8.68 us -> 7.15 us
  Pallas kernels: 12 us -> 10.8 us
  starting transfers between devices: 14.4 us -> 15.2 us
    unnamed x4 -> x0, local copies, waits for them, and re-layouts: 1.8 us -> none
    all_to_all x1, blocking collectives: 10.7 us -> 12.3 us  [body(): came = lax.all_to_all(sent, 'lon', 0, 0)]
    ppermute x8 -> x6, waiting for transfers between devices: 8.68 us -> 7.15 us  [swap_pairs(): return lax.ppermute(block, 'lon', route)]
    pallas_call x4, Pallas kernels: 7 us -> 5.66 us  [the longest x1 2.19 us: body(): pl.pallas_call(first_solve, in_specs=[SM] + [VM] * 4 + [HB] * 2 + [VM] *...]
    ppermute x8 -> x6, starting transfers between devices: 14.4 us -> 15.2 us  [swap_pairs(): return lax.ppermute(block, 'lon', route)]
  transfers between devices with their start and end apart: 8 -> 6, of which waited for: 2 -> 3; matrix products, arithmetic and copies ran while one was open for 0% -> 0% of each run, Pallas kernels for 6% -> 4%
where the time goes in v4:
time: 46.4 us; the launch traced here: 46.1 us
  starting transfers between devices  15.2 us (33%)
  blocking collectives  12.3 us (27%)
  Pallas kernels  10.8 us (23%)
  waiting for transfers between devices  7.15 us (15%)
  between operations  0.7 us (2%)
    ppermute x6, starting transfers between devices, swap_pairs(): return lax.ppermute(block, 'lon', route)  15.2 us
    all_to_all x1, blocking collectives, body(): came = lax.all_to_all(sent, 'lon', 0, 0)  12.3 us
    ppermute x6, waiting for transfers between devices, swap_pairs(): return lax.ppermute(block, 'lon', route)  7.15 us
    pallas_call x1, Pallas kernels, body(): pl.pallas_call(finish, in_specs=[VM] * 8, out_specs=[HB] * 4, out_shape=[...  3.16 us
    pallas_call x1, Pallas kernels, body(): pl.pallas_call(first_solve, in_specs=[SM] + [VM] * 4 + [HB] * 2 + [VM] *...  2.19 us
    pallas_call x1, Pallas kernels, body(): pl.pallas_call(second_solve, in_specs=[SM] + [VM] * 10, out_specs=[VM] *...  1.99 us
    pallas_call x1, Pallas kernels, body(): pl.pallas_call(prepare, in_specs=[HB] * 9, out_specs=[VM] * 8, out_shape=...  1.88 us
    pallas_call x1, Pallas kernels, body(): pl.pallas_call(first_edges, in_specs=[SM, HB, HB], out_specs=[VM] * 2, ou...  1.05 us
  transfers between devices with their start and end apart: 6, of which 3 were waited for; matrix products, arithmetic and copies ran while one was open for 0% of the time, Pallas kernels for 4%

profile of v4, /device:TPU:0, one launch (start us, length us, event | category | flops | bytes accessed | tf_op | source)
XLA Modules:
  0.0 46.1 jit_solution(17122053728918932336)
XLA Ops:
  0.6 1.0 %first_edges.1 = (f32[8,2240]{1,0:T(8,128)S(1)}, f32[8,2240]{1,0:T(8,128)S(1)}) custom-call(s32[1]{0:T(128)} %bitcast.parity, f32[32,2240]{1,0:T(8,128)} %source_h.1, s32[32,2240]{1,0:T(8,128)} %bottom_h.1), custom_call_target="tpu_custom_call" | custom-call | tf_op jit(solution)/shard_map/first_edges/pallas_call | solution.py:379
  1.7 0.5 %collective-permute-start = (f32[8,2240]{1,0:T(8,128)S(1)}, f32[8,2240]{1,0:T(8,128)S(1)}, u32[]{:S(2)}, u32[]{:S(2)}) collective-permute-start(f32[8,2240]{1,0:T(8,128)S(1)} %get-tuple-element.28.inner), channel_id=1, source_target_pairs={{0,1},{1,0},{2,3},{3,2},{4,5},{5,4},{6,7},{7,6},{8,9},{9,8},{10,11... | collective-permute-start | bytes 215048 | tf_op jit(solution)/shard_map/ppermute | solution.py:362
  2.2 5.6 %collective-permute-start.1 = (f32[8,2240]{1,0:T(8,128)S(1)}, f32[8,2240]{1,0:T(8,128)S(1)}, u32[]{:S(2)}, u32[]{:S(2)}) collective-permute-start(f32[8,2240]{1,0:T(8,128)S(1)} %get-tuple-element.29.outer), channel_id=1, source_target_pairs={{0,15},{1,2},{2,1},{3,4},{4,3},{5,6},{6,5},{7,8},{8,7},{9,10},{10,... | collective-permute-start | bytes 215048 | tf_op jit(solution)/shard_map/ppermute | solution.py:362
  7.9 1.9 %prepare.1 = (f32[32,2240]{1,0:T(8,128)S(1)}, f32[32,2240]{1,0:T(8,128)S(1)}, f32[32,2240]{1,0:T(8,128)S(1)}, f32[32,2240]{1,0:T(8,128)S(1)}, bf16[8,256,256]{2,...) custom-call(f32[8,2240]{1,0:T(8,128)S(1)} %get-tuple-element.28.inner, ...), custom_call_target="tpu_custom_call" | custom-call | flops 1000000 | bytes 7000000 | tf_op jit(solution)/shard_map/prepare/pallas_call | solution.py:392
  9.7 0.0 collective-permute-done.inner_in
  9.8 0.1 collective-permute-done.1.outer_in
  9.9 2.2 %first_solve.1 = (f32[48,2240]{1,0:T(8,128)S(1)}, f32[468,128]{1,0:T(8,128)S(1)}, f32[468,128]{1,0:T(8,128)S(1)}, f32[6,32,2240]{2,1,0:T(8,128)S(1)}, f32[6,32,2240]{2,1,0:T(8,128)S(1)}) custom-call(s32[1]{0:T(128)} %bitcast.parity, f32[8,2240]{1,0:T(8,128)S(1)} %collective-permute-done.inner_in, f32[8,2240]{1,0:T(8,128)S(1)} %collective-permute-done.1.outer_in, ...), custom_call_target="tpu_custom_call" | custom-call | tf_op jit(solution)/shard_map/first_solve/pallas_call | solution.py:409
  12.1 0.1 collective-permute-start.2
  12.2 4.5 %collective-permute-start.3 = (f32[468,128]{1,0:T(8,128)S(1)}, f32[468,128]{1,0:T(8,128)S(1)}, u32[]{:S(2)}, u32[]{:S(2)}) collective-permute-start(f32[468,128]{1,0:T(8,128)S(1)} %get-tuple-element.37), channel_id=1, source_target_pairs={{0,15},{1,2},{2,1},{3,4},{4,3},{5,6},{6,5},{7,8},{8,7},{9,10},{10,... | collective-permute-start | bytes 718856 | tf_op jit(solution)/shard_map/ppermute | solution.py:362
  16.7 0.0 collective-permute-done.2.inner_in
  16.7 3.9 %collective-permute-done.3.outer_in = f32[468,128]{1,0:T(8,128)S(1)} collective-permute-done((f32[468,128]{1,0:T(8,128)S(1)}, f32[468,128]{1,0:T(8,128)S(1)}, u32[]{:S(2)}, u32[]{:S(2)}) %collective-permute-start.3) | collective-permute-done | bytes 239648 | tf_op jit(solution)/shard_map/ppermute | solution.py:362
  20.6 2.0 %second_solve.1 = (f32[48,2240]{1,0:T(8,128)S(1)}, f32[48,2240]{1,0:T(8,128)S(1)}, f32[48,2240]{1,0:T(8,128)S(1)}, f32[48,2240]{1,0:T(8,128)S(1)}, f32[16,2240]{1,0:T(8,128)S(1)}, /*index=5*/f32[16,2240]{1,0:T(8,128)S(1)}) custom-call(s32[1]{0:T(128)} %bitcast.parity, f32[468,128]{1,0:T(8,128)S(1)} %collective-permute-done.2.inner_in, ...), custom_call_target="tpu_custom_call" | custom-call | tf_op jit(solution)/shard_map/second_solve/pallas_call | solution.py:422
  22.6 0.3 collective-permute-start.4
  22.9 4.2 %collective-permute-start.5 = (f32[16,2240]{1,0:T(8,128)S(1)}, f32[16,2240]{1,0:T(8,128)S(1)}, u32[]{:S(2)}, u32[]{:S(2)}) collective-permute-start(f32[16,2240]{1,0:T(8,128)S(1)} %get-tuple-element.42), channel_id=1, source_target_pairs={{0,15},{1,2},{2,1},{3,4},{4,3},{5,6},{6,5},{7,8},{8,7},{9,10},{10,... | collective-permute-start | bytes 430088 | tf_op jit(solution)/shard_map/ppermute | solution.py:362
  27.1 0.0 collective-permute-done.4.inner_in
  27.1 3.1 %collective-permute-done.5.outer_in = f32[16,2240]{1,0:T(8,128)S(1)} collective-permute-done((f32[16,2240]{1,0:T(8,128)S(1)}, f32[16,2240]{1,0:T(8,128)S(1)}, u32[]{:S(2)}, u32[]{:S(2)}) %collective-permute-start.5) | collective-permute-done | bytes 143392 | tf_op jit(solution)/shard_map/ppermute | solution.py:362
  30.2 0.5 %sums.1 = (f32[48,2240]{1,0:T(8,128)S(1)}, f32[16,2240]{1,0:T(8,128)S(1)}, f32[16,8,128]{2,1,0:T(8,128)S(1)}) custom-call(s32[1]{0:T(128)} %bitcast.parity, f32[16,2240]{1,0:T(8,128)S(1)} %collective-permute-done.4.inner_in, f32[16,2240]{1,0:T(8,128)S(1)} %collective-permute-done.5.outer_in, f32[48,2240]{1,0:T(8,128)S(1)} %get-tuple-element.43.second, ...), custom_call_target="tpu_custom_call" | custom-call | tf_op jit(solution)/shard_map/sums/pallas_call | solution.py:433
  30.7 12.3 %all_to_all.5.came = f32[16,8,128]{2,1,0:T(8,128)S(1)} all-to-all(f32[16,8,128]{2,1,0:T(8,128)S(1)} %get-tuple-element.48), channel_id=1, replica_groups=mesh['members'=2,'lon'=16] {'lon'}, dimensions={0} | all-to-all | bytes 131072 | tf_op jit(solution)/shard_map/all_to_all | solution.py:442
  43.0 3.2 %finish.1 = (f32[32,2240]{1,0:T(8,128)}, f32[6,32,2240]{2,1,0:T(8,128)}, f32[6,32,2240]{2,1,0:T(8,128)}, f32[6,32,2240]{2,1,0:T(8,128)}) custom-call(f32[16,8,128]{2,1,0:T(8,128)S(1)} %all_to_all.5.came, f32[48,2240]{1,0:T(8,128)S(1)} %get-tuple-element.44.z, f32[48,2240]{1,0:T(8,128)S(1)} %get-tuple-element.49.w, f32[16,2240]{1,0:T(8,128)S(1)} %get-tuple-element.50.edges, ...), custom_call_target="tpu_custom_call" | custom-call | tf_op jit(solution)/shard_map/finish/pallas_call | solution.py:444
Async XLA Ops:
  1.7 8.0 %collective-permute-start = (f32[8,2240]{1,0:T(8,128)S(1)}, f32[8,2240]{1,0:T(8,128)S(1)}, u32[]{:S(2)}, u32[]{:S(2)}) collective-permute-start(f32[8,2240]{1,0:T(8,128)S(1)} %get-tuple-element.28.inner), channel_id=1, source_target_pairs={{0,1},{1,0},{2,3},{3,2},{4,5},{5,4},{6,7},{7,6},{8,9},{9,8},{10,11... | collective-permute-start | bytes 215048 | tf_op jit(solution)/shard_map/ppermute | solution.py:362
  2.2 7.7 %collective-permute-start.1 = (f32[8,2240]{1,0:T(8,128)S(1)}, f32[8,2240]{1,0:T(8,128)S(1)}, u32[]{:S(2)}, u32[]{:S(2)}) collective-permute-start(f32[8,2240]{1,0:T(8,128)S(1)} %get-tuple-element.29.outer), channel_id=1, source_target_pairs={{0,15},{1,2},{2,1},{3,4},{4,3},{5,6},{6,5},{7,8},{8,7},{9,10},{10,... | collective-permute-start | bytes 215048 | tf_op jit(solution)/shard_map/ppermute | solution.py:362
  12.1 4.6 %collective-permute-start.2 = (f32[468,128]{1,0:T(8,128)S(1)}, f32[468,128]{1,0:T(8,128)S(1)}, u32[]{:S(2)}, u32[]{:S(2)}) collective-permute-start(f32[468,128]{1,0:T(8,128)S(1)} %get-tuple-element.36), channel_id=1, source_target_pairs={{0,1},{1,0},{2,3},{3,2},{4,5},{5,4},{6,7},{7,6},{8,9},{9,8},{10,11... | collective-permute-start | bytes 718856 | tf_op jit(solution)/shard_map/ppermute | solution.py:362
  12.2 8.4 %collective-permute-start.3 = (f32[468,128]{1,0:T(8,128)S(1)}, f32[468,128]{1,0:T(8,128)S(1)}, u32[]{:S(2)}, u32[]{:S(2)}) collective-permute-start(f32[468,128]{1,0:T(8,128)S(1)} %get-tuple-element.37), channel_id=1, source_target_pairs={{0,15},{1,2},{2,1},{3,4},{4,3},{5,6},{6,5},{7,8},{8,7},{9,10},{10,... | collective-permute-start | bytes 718856 | tf_op jit(solution)/shard_map/ppermute | solution.py:362
  22.6 4.5 %collective-permute-start.4 = (f32[16,2240]{1,0:T(8,128)S(1)}, f32[16,2240]{1,0:T(8,128)S(1)}, u32[]{:S(2)}, u32[]{:S(2)}) collective-permute-start(f32[16,2240]{1,0:T(8,128)S(1)} %get-tuple-element.41), channel_id=1, source_target_pairs={{0,1},{1,0},{2,3},{3,2},{4,5},{5,4},{6,7},{7,6},{8,9},{9,8},{10,11... | collective-permute-start | bytes 430088 | tf_op jit(solution)/shard_map/ppermute | solution.py:362
  22.9 7.3 %collective-permute-start.5 = (f32[16,2240]{1,0:T(8,128)S(1)}, f32[16,2240]{1,0:T(8,128)S(1)}, u32[]{:S(2)}, u32[]{:S(2)}) collective-permute-start(f32[16,2240]{1,0:T(8,128)S(1)} %get-tuple-element.42), channel_id=1, source_target_pairs={{0,15},{1,2},{2,1},{3,4},{4,3},{5,6},{6,5},{7,8},{8,7},{9,10},{10,... | collective-permute-start | bytes 430088 | tf_op jit(solution)/shard_map/ppermute | solution.py:362

commit v5 on v4

--- a/solution.py
+++ b/solution.py
@@ -147,25 +147,23 @@
     return jnp.concatenate(blocks, axis=1)[:, :lat]
 
 
-def first_edges(parity, source, bottom, inner, outer, source_w, source_e, bottom_w, bottom_e, sems):
-    last = source.shape[0] - OV
-    pairs = [(source, 0, source_w), (bottom, 0, bottom_w), (source, last, source_e), (bottom, last, bottom_e)]
+def first_edges(parity, source, bottom, outer, rows, depth, sems):
+    start = pl.multiple_of(parity[0] * (source.shape[0] - OV), OV)
+    at = pl.ds(start, OV)
     copies = [
-        pltpu.make_async_copy(held.at[pl.ds(at, OV)], block, sems.at[i])
-        for i, (held, at, block) in enumerate(pairs)
+        pltpu.make_async_copy(source.at[at], rows, sems.at[0]),
+        pltpu.make_async_copy(bottom.at[at], depth, sems.at[1]),
     ]
     for copy in copies:
         copy.start()
     for copy in copies:
         copy.wait()
-    west = jnp.where(bottom_w[...] > 0, source_w[...], 0.0)
-    east = jnp.where(bottom_e[...] > 0, source_e[...], 0.0)
-    outer[...], inner[...] = pick(parity, east, west)
-
-
-def prepare(inner, outer, source_h, diagonal_h, bottom_h, *refs):
-    tables_h, (masked, coef, depth, source), held = refs[:4], refs[4:8], refs[8:12]
-    diagonal, bottom, sems = refs[12:]
+    outer[...] = jnp.where(depth[...] > 0, rows[...], 0.0)
+
+
+def prepare(parity, after, source_h, diagonal_h, bottom_h, *refs):
+    tables_h, (inner, masked, coef, depth, source), held = refs[:4], refs[4:9], refs[9:13]
+    diagonal, bottom, sems = refs[13:]
     pairs = [(source_h, source), (bottom_h, bottom), (diagonal_h, diagonal)]
     pairs += list(zip(tables_h, held))
     copies = [pltpu.make_async_copy(a, b, sems.at[i]) for i, (a, b) in enumerate(pairs)]
@@ -177,16 +175,14 @@
     masked[...] = jnp.where(wet, source[...], 0.0)
     coef[...] = jnp.where(wet, 4.0 + diagonal[...], 0.0)
     depth[...] = bottom[...].astype(F32)
+    inner[...] = pick(parity, masked[:OV], masked[source.shape[0] - OV :])[0]
     for copy in copies[3:]:
         copy.wait()
 
 
-def first_solve(parity, inner_in, outer_in, masked, coef, u_h, v_h, forward, inverse, lon, scale,
-                first, inner, outer, u, v, wide, spectral, restored, out, sems):
+def first_solve(parity, inner_in, outer_in, masked, coef, forward, inverse, lon, scale,
+                first, inner, outer, wide, spectral, restored, out):
     cells, lat = masked.shape
-    copies = [pltpu.make_async_copy(a, b, sems.at[i]) for i, (a, b) in enumerate([(u_h, u), (v_h, v)])]
-    for copy in copies:
-        copy.start()
     west, east = pick(parity, inner_in[...], outer_in[...])
     x = jnp.concatenate([west, masked[...], east], axis=0)
     tile_solve(x, forward, inverse, lon, scale, wide, spectral, restored, out)
@@ -197,8 +193,19 @@
     to_outer, to_inner = pick(parity, to_east, to_west)
     pack(inner, to_inner)
     pack(outer, to_outer)
+
+
+def absorb(after, u_h, v_h, u, v, u_before, v_before, sems):
+    copies = [pltpu.make_async_copy(a, b, sems.at[i]) for i, (a, b) in enumerate([(u_h, u), (v_h, v)])]
     for copy in copies:
-        copy.wait()
+        copy.start()
+    levels, cells, lat = u.shape
+    copies[0].wait()
+    for level in range(levels):
+        u_before[level] = jnp.concatenate([jnp.zeros((1, lat), F32), u[level, : cells - 1]], axis=0)
+    copies[1].wait()
+    for level in range(levels):
+        v_before[level] = jnp.concatenate([jnp.zeros((cells, 1), F32), v[level, :, : lat - 1]], axis=1)
 
 
 def second_solve(parity, inner_in, outer_in, first, coef_own, depth, u, forward, inverse, lon, scale,
@@ -265,35 +272,21 @@
         if whole < lat:
             blank = jnp.zeros((OV, LANE - lat + whole), F32)
             total = total + jnp.concatenate([rows[:, whole:], blank], axis=1)
-        return jnp.sum(total, axis=0, keepdims=True)
-
-    parts = [
-        partial(masked, z_own),
-        partial(z_own, y_own),
-        partial(masked, m),
-        partial(y_own, m),
-        partial(z_own, x),
-        partial(m, x),
-        partial(land, land),
-        jnp.zeros((1, LANE), F32),
-    ]
-    sent[...] = jnp.broadcast_to(jnp.concatenate(parts, axis=0)[None], sent.shape)
-
-
-def send(copies, level, at, u_rows, v_out, w_out, u_new, v_new, w_vel, sems):
-    own = slice(at - OV, at)
-    for held, rows, result in ((u_rows, slice(at, at + OV), u_new), (v_out, own, v_new), (w_out, own, w_vel)):
-        copies.append(
-            pltpu.make_async_copy(held.at[level, rows], result.at[level, own], sems.at[len(copies)])
-        )
-        copies[-1].start()
-
-
-def finish(came, z, w, edges, source, depth, u_vel, v_vel, solution, u_new, v_new, w_vel,
-           s_rows, d_rows, u_rows, v_out, w_out, s_out, sems):
+        return jnp.sum(jnp.sum(total, axis=0, keepdims=True), axis=1, keepdims=True)
+
+    pairs = [(masked, z_own), (z_own, y_own), (masked, m), (y_own, m), (z_own, x), (m, x), (land, land)]
+    lane = lax.broadcasted_iota(jnp.int32, (1, LANE), 1)
+    row = jnp.zeros((1, LANE), F32)
+    for i, (a, b) in enumerate(pairs):
+        row = jnp.where(lane == i, partial(a, b), row)
+    sent[...] = jnp.broadcast_to(row[None], sent.shape)
+
+
+def finish(came, z, w, edges, source, depth, u_vel, v_vel, u_before, v_before, solution, u_new, v_new, w_vel,
+           s_rows, d_rows, u_out, v_out, w_out, s_out, sems):
     cells, lat = source.shape
-    total = jnp.sum(jnp.sum(came[...], axis=0), axis=1, keepdims=True)
-    rz, zy, rw, yw, zx, wx, ll = [total[i : i + 1] for i in range(7)]
+    total = jnp.sum(came[...], axis=0)
+    rz, zy, rw, yw, zx, wx, ll = [total[:, i : i + 1] for i in range(7)]
     step0 = (rz + ll) / (zy + ll)
     rest = (zy - rz) / (zy + ll)
     new = rz - step0 * (zy + rw) + step0 * step0 * yw + rest * rest * ll
@@ -305,50 +298,60 @@
     of_w = jnp.broadcast_to(-step1 * step0, (OV, lat))
     of_land = jnp.broadcast_to(step0 + step1 * (rest + beta), (OV, lat))
 
-    copies = []
     d_rows[:OV] = jnp.broadcast_to(edges[1:2], (OV, lat))
     d_rows[OV : OV + cells] = depth[...]
     d_rows[OV + cells :] = jnp.broadcast_to(edges[OV + 1 : OV + 2], (OV, lat))
-    for at in range(0, cells + 2 * OV, OV):
+    first_row = lax.broadcasted_iota(jnp.int32, (OV, 3 * LANE), 0) == 0
+    copies = []
+
+    def rows_of_surface(at):
         s = of_z * z[at : at + OV] + of_w * w[at : at + OV]
         if OV <= at < OV + cells:
-            d = d_rows[at : at + OV]
-            s = jnp.where(d > 0, s, of_land * source[at - OV : at])
+            s = jnp.where(d_rows[at : at + OV] > 0, s, of_land * source[at - OV : at])
             s_out[at - OV : at] = s
         s_rows[at : at + OV] = s
-    copies.append(pltpu.make_async_copy(s_out, solution, sems.at[0]))
-    copies[-1].start()
-
-    s_west = s_rows[OV - 1 : OV]
-    s_first = s_rows[OV : OV + 1]
-    d_west = jnp.minimum(d_rows[OV - 1 : OV], d_rows[OV : OV + 1])
-    for level in range(KL):
-        left = edges[level + 2 : level + 3] - gravity_step * (s_first - s_west)
-        u_rows[level, :OV] = jnp.broadcast_to(jnp.where(d_west > level, left, 0.0), (OV, lat))
+
+    def send(held, result):
+        copies.append(pltpu.make_async_copy(held, result, sems.at[len(copies)]))
+        copies[-1].start()
+
+    rows_of_surface(0)
+    rows_of_surface(OV)
     zero = jnp.zeros((OV, 1), F32)
-    for block in range(cells // OV):
-        at = OV + block * OV
+    for at in range(OV, OV + cells, OV):
+        rows_of_surface(at + OV)
         own = slice(at - OV, at)
-        s = s_rows[at : at + OV]
-        d = d_rows[at : at + OV]
+        s, d = s_rows[at : at + OV], d_rows[at : at + OV]
         slope_e = gravity_step * (s_rows[at + 1 : at + OV + 1] - s)
         depth_e = jnp.minimum(d, d_rows[at + 1 : at + OV + 1])
+        slope_w = gravity_step * (s - s_rows[at - 1 : at + OV - 1])
+        depth_w = jnp.minimum(d, d_rows[at - 1 : at + OV - 1])
         slope_n = gravity_step * (jnp.concatenate([s[:, 1:], zero], axis=1) - s)
         depth_n = jnp.minimum(d, jnp.concatenate([d[:, 1:], zero], axis=1))
-        w_sum = jnp.zeros((OV, lat), F32)
-        for level in range(KL - 1, -1, -1):
-            u = jnp.where(depth_e > level, u_vel[level, own] - slope_e, 0.0)
-            u_rows[level, at : at + OV] = u
-            v = jnp.where(depth_n > level, v_vel[level, own] - slope_n, 0.0)
-            v_out[level, own] = v
-            south = jnp.concatenate([zero, v[:, :-1]], axis=1)
-            flow = (u - u_rows[level, at - 1 : at + OV - 1]) + (v - south)
-            w_sum = w_sum + jnp.where(d > level, flow, 0.0)
-            w_out[level, own] = w_sum
-            if block == 0:
-                send(copies, level, at, u_rows, v_out, w_out, u_new, v_new, w_vel, sems)
-        if block > 0:
-            send(copies, slice(None), at, u_rows, v_out, w_out, u_new, v_new, w_vel, sems)
+        slope_s = jnp.concatenate([zero, slope_n[:, :-1]], axis=1)
+        depth_s = jnp.concatenate([zero, depth_n[:, :-1]], axis=1)
+        for first in range(0, lat, 3 * LANE):
+            part = slice(first, min(first + 3 * LANE, lat))
+            d_p, de, dw, dn, ds = [x[:, part] for x in (d, depth_e, depth_w, depth_n, depth_s)]
+            se, sw, sn, ss = [x[:, part] for x in (slope_e, slope_w, slope_n, slope_s)]
+            w_sum = jnp.zeros(d_p.shape, F32)
+            for level in range(KL - 1, -1, -1):
+                u = jnp.where(de > level, u_vel[level, own, part] - se, 0.0)
+                v = jnp.where(dn > level, v_vel[level, own, part] - sn, 0.0)
+                before = u_before[level, own, part]
+                if at == OV:
+                    edge = jnp.broadcast_to(edges[level + 2 : level + 3, part], before.shape)
+                    before = jnp.where(first_row[:, : before.shape[1]], edge, before)
+                u_west = jnp.where(dw > level, before - sw, 0.0)
+                v_south = jnp.where(ds > level, v_before[level, own, part] - ss, 0.0)
+                w_sum = w_sum + jnp.where(d_p > level, (u - u_west) + (v - v_south), 0.0)
+                u_out[level, own, part] = u
+                v_out[level, own, part] = v
+                w_out[level, own, part] = w_sum
+        for held, result in ((u_out, u_new), (v_out, v_new), (w_out, w_vel)):
+            send(held.at[:, own], result.at[:, own])
+        if at == cells:
+            send(s_out, solution)
     for copy in copies:
         copy.wait()
 
@@ -376,24 +379,24 @@
         ("source", source), ("diagonal", diagonal), ("u", u_vel), ("v", v_vel), ("bottom", bottom))}
     consts = [pltpu.with_memory_space_constraint(x, pltpu.HBM) for x in consts]
 
-    inner, outer = pl.pallas_call(
+    outer = pl.pallas_call(
         first_edges,
         in_specs=[SM, HB, HB],
-        out_specs=[VM] * 2,
-        out_shape=[pltpu.VMEM((OV, lat), F32)] * 2,
-        scratch_shapes=[pltpu.VMEM((OV, lat), F32)] * 2
-        + [pltpu.VMEM((OV, lat), jnp.int32)] * 2
-        + [pltpu.SemaphoreType.DMA((4,))],
+        out_specs=VM,
+        out_shape=pltpu.VMEM((OV, lat), F32),
+        scratch_shapes=[pltpu.VMEM((OV, lat), F32), pltpu.VMEM((OV, lat), jnp.int32),
+                        pltpu.SemaphoreType.DMA((2,))],
         compiler_params=PARAMS,
         name="first_edges",
     )(parity, hbm["source"], hbm["bottom"])
-    near = swap_pairs(inner, False), swap_pairs(outer, True)
-
-    masked, coef_own, depth, source_v, *held = pl.pallas_call(
+    outer_in = swap_pairs(outer, True)
+
+    inner, masked, coef_own, depth, source_v, *held = pl.pallas_call(
         prepare,
-        in_specs=[HB] * 9,
-        out_specs=[VM] * 8,
-        out_shape=[pltpu.VMEM((cells, lat), F32)] * 4
+        in_specs=[SM] + [HB] * 8,
+        out_specs=[VM] * 9,
+        out_shape=[pltpu.VMEM((OV, lat), F32)]
+        + [pltpu.VMEM((cells, lat), F32)] * 4
         + [pltpu.VMEM(table.shape, table.dtype) for table in consts],
         scratch_shapes=[
             pltpu.VMEM((cells, lat), F32),
@@ -403,21 +406,32 @@
         compiler_params=PARAMS,
         cost_estimate=pl.CostEstimate(flops=10**6, bytes_accessed=7 * 10**6, transcendentals=0),
         name="prepare",
-    )(inner, outer, hbm["source"], hbm["diagonal"], hbm["bottom"], *consts)
+    )(parity, outer, hbm["source"], hbm["diagonal"], hbm["bottom"], *consts)
+    near = swap_pairs(inner, False), outer_in
 
     blocks = -(-lat // LANE)
-    first, inner, outer, u_v, v_v = pl.pallas_call(
+    first, inner, outer = pl.pallas_call(
         first_solve,
-        in_specs=[SM] + [VM] * 4 + [HB] * 2 + [VM] * 4,
-        out_specs=[VM] * 5,
+        in_specs=[SM] + [VM] * 8,
+        out_specs=[VM] * 3,
         out_shape=[pltpu.VMEM((span, lat), F32)]
-        + [pltpu.VMEM(((3 * OV + 2) * blocks, LANE), F32)] * 2
-        + [pltpu.VMEM((KL, cells, lat), F32)] * 2,
-        scratch_shapes=solve_scratch(span, lat) + [pltpu.SemaphoreType.DMA((2,))],
+        + [pltpu.VMEM(((3 * OV + 2) * blocks, LANE), F32)] * 2,
+        scratch_shapes=solve_scratch(span, lat),
         compiler_params=PARAMS,
         name="first_solve",
-    )(parity, *near, masked, coef_own, hbm["u"], hbm["v"], *held)
+    )(parity, *near, masked, coef_own, *held)
     near = swap_pairs(inner, False), swap_pairs(outer, True)
+
+    u_v, v_v, u_shift, v_shift = pl.pallas_call(
+        absorb,
+        in_specs=[HB] * 3,
+        out_specs=[VM] * 4,
+        out_shape=[pltpu.VMEM((KL, cells, lat), F32)] * 4,
+        scratch_shapes=[pltpu.SemaphoreType.DMA((2,))],
+        compiler_params=PARAMS,
+        cost_estimate=pl.CostEstimate(flops=10**6, bytes_accessed=7 * 10**6, transcendentals=0),
+        name="absorb",
+    )(first, hbm["u"], hbm["v"])
 
     z, y, coef, second, inner, outer = pl.pallas_call(
         second_solve,
@@ -435,7 +449,7 @@
         in_specs=[SM] + [VM] * 7,
         out_specs=[VM] * 3,
         out_shape=[pltpu.VMEM((span, lat), F32), pltpu.VMEM((2 * OV, lat), F32),
-                   pltpu.VMEM((devices, 8, LANE), F32)],
+                   pltpu.VMEM((devices, 1, LANE), F32)],
         compiler_params=PARAMS,
         name="sums",
     )(parity, *near, second, z, y, coef, source_v)
@@ -443,21 +457,15 @@
 
     return pl.pallas_call(
         finish,
-        in_specs=[VM] * 8,
+        in_specs=[VM] * 10,
         out_specs=[HB] * 4,
         out_shape=[shape(cells, lat)] + [shape(KL, cells, lat)] * 3,
-        scratch_shapes=[
-            pltpu.VMEM((span, lat), F32),
-            pltpu.VMEM((span, lat), F32),
-            pltpu.VMEM((KL, OV + cells, lat), F32),
-            pltpu.VMEM((KL, cells, lat), F32),
-            pltpu.VMEM((KL, cells, lat), F32),
-            pltpu.VMEM((cells, lat), F32),
-            pltpu.SemaphoreType.DMA((1 + 3 * (KL + cells // OV - 1),)),
-        ],
+        scratch_shapes=[pltpu.VMEM((span, lat), F32)] * 2
+        + [pltpu.VMEM((KL, cells, lat), F32)] * 3
+        + [pltpu.VMEM((cells, lat), F32), pltpu.SemaphoreType.DMA((1 + 3 * (cells // OV),))],
         compiler_params=PARAMS,
         name="finish",
-    )(came, z, w, edges, source_v, depth, u_v, v_v)
+    )(came, z, w, edges, source_v, depth, u_v, v_v, u_shift, v_shift)
 
 
 def solution(mesh):

time: 46.4 us -> 45.1 us (0.972)
  starting transfers between devices: 15.2 us -> 12.2 us
  Pallas kernels: 10.8 us -> 13.2 us
  blocking collectives: 12.3 us -> 10.6 us
  waiting for transfers between devices: 7.15 us -> 8.14 us
    ppermute x6, starting transfers between devices: 15.2 us -> 12.2 us  [swap_pairs(): return lax.ppermute(block, 'lon', route)]
    pallas_call x4 -> x5, Pallas kernels: 8.28 us -> 10.6 us  [the longest x1 3.6 us: body(): pl.pallas_call(finish, in_specs=[VM] * 10, out_specs=[HB] * 4, out_shape=...]
    all_to_all x1, blocking collectives: 12.3 us -> 10.6 us  [body(): came = lax.all_to_all(sent, 'lon', 0, 0)]
    ppermute x6, waiting for transfers between devices: 7.15 us -> 8.14 us  [swap_pairs(): return lax.ppermute(block, 'lon', route)]
  transfers between devices with their start and end apart: 6 -> 6, of which waited for: 3 -> 4; matrix products, arithmetic and copies ran while one was open for 0% -> 0% of each run, Pallas kernels for 4% -> 10%
where the time goes in v5:
time: 45.1 us; the launch traced here: 44.8 us
  Pallas kernels  13.2 us (29%)
  starting transfers between devices  12.2 us (27%)
  blocking collectives  10.6 us (24%)
  waiting for transfers between devices  8.14 us (18%)
  between operations  0.7 us (2%)
    ppermute x6, starting transfers between devices, swap_pairs(): return lax.ppermute(block, 'lon', route)  12.2 us
    all_to_all x1, blocking collectives, body(): came = lax.all_to_all(sent, 'lon', 0, 0)  10.6 us
    ppermute x6, waiting for transfers between devices, swap_pairs(): return lax.ppermute(block, 'lon', route)  8.14 us
    pallas_call x1, Pallas kernels, body(): pl.pallas_call(finish, in_specs=[VM] * 10, out_specs=[HB] * 4, out_shape=...  3.6 us
    pallas_call x1, Pallas kernels, body(): pl.pallas_call(absorb, in_specs=[HB] * 3, out_specs=[VM] * 4, out_shape=[...  2.55 us
    pallas_call x1, Pallas kernels, body(): pl.pallas_call(second_solve, in_specs=[SM] + [VM] * 10, out_specs=[VM] *...  1.96 us
    pallas_call x1, Pallas kernels, body(): pl.pallas_call(prepare, in_specs=[SM] + [HB] * 8, out_specs=[VM] * 9, out...  1.88 us
    pallas_call x1, Pallas kernels, body(): pl.pallas_call(first_solve, in_specs=[SM] + [VM] * 8, out_specs=[VM] * 3,...  1.65 us
  transfers between devices with their start and end apart: 6, of which 4 were waited for; matrix products, arithmetic and copies ran while one was open for 0% of the time, Pallas kernels for 10%

profile of v5, /device:TPU:0, one launch (start us, length us, event | category | flops | bytes accessed | tf_op | source)
XLA Modules:
  0.0 44.8 jit_solution(7858333173755553434)
XLA Ops:
  0.6 0.9 %first_edges.1.after = f32[8,2240]{1,0:T(8,128)S(1)} custom-call(s32[1]{0:T(128)} %bitcast.parity, f32[32,2240]{1,0:T(8,128)} %source_h.1, s32[32,2240]{1,0:T(8,128)} %bottom_h.1), custom_call_target="tpu_custom_call" | custom-call | tf_op jit(solution)/shard_map/first_edges/pallas_call | solution.py:382
  1.6 5.5 %collective-permute-start.1 = (f32[8,2240]{1,0:T(8,128)S(1)}, f32[8,2240]{1,0:T(8,128)S(1)}, u32[]{:S(2)}, u32[]{:S(2)}) collective-permute-start(f32[8,2240]{1,0:T(8,128)S(1)} %first_edges.1.after), channel_id=1, source_target_pairs={{0,15},{1,2},{2,1},{3,4},{4,3},{5,6},{6,5},{7,8},{8,7},{9,10},{10,... | collective-permute-start | bytes 215048 | tf_op jit(solution)/shard_map/ppermute | solution.py:365
  7.1 1.9 %prepare.1 = (f32[8,2240]{1,0:T(8,128)S(1)}, f32[32,2240]{1,0:T(8,128)S(1)}, f32[32,2240]{1,0:T(8,128)S(1)}, f32[32,2240]{1,0:T(8,128)S(1)}, f32[32,2240]{1,0:T(...) custom-call(s32[1]{0:T(128)} %bitcast.parity, ...), custom_call_target="tpu_custom_call" | custom-call | flops 1000000 | bytes 7000000 | tf_op jit(solution)/shard_map/prepare/pallas_call | solution.py:394
  9.0 0.1 collective-permute-start
  9.0 0.1 collective-permute-done.1.outer_in
  9.1 1.2 %collective-permute-done.inner_in = f32[8,2240]{1,0:T(8,128)S(1)} collective-permute-done((f32[8,2240]{1,0:T(8,128)S(1)}, f32[8,2240]{1,0:T(8,128)S(1)}, u32[]{:S(2)}, u32[]{:S(2)}) %collective-permute-start) | collective-permute-done | bytes 71712 | tf_op jit(solution)/shard_map/ppermute | solution.py:365
  10.3 1.6 %first_solve.1 = (f32[48,2240]{1,0:T(8,128)S(1)}, f32[468,128]{1,0:T(8,128)S(1)}, f32[468,128]{1,0:T(8,128)S(1)}) custom-call(s32[1]{0:T(128)} %bitcast.parity, f32[8,2240]{1,0:T(8,128)S(1)} %collective-permute-done.inner_in, f32[8,2240]{1,0:T(8,128)S(1)} %collective-permute-done.1.outer_in, f32[32,2240]{1,0:T(8,128)S(1)} %get-tuple-element.30.masked, ...), custom_call_target="tpu_custom_call" | custom-call | tf_op jit(solution)/shard_map/first_solve/pallas_call | solution.py:413
  12.0 0.2 collective-permute-start.2
  12.2 3.2 %collective-permute-start.3 = (f32[468,128]{1,0:T(8,128)S(1)}, f32[468,128]{1,0:T(8,128)S(1)}, u32[]{:S(2)}, u32[]{:S(2)}) collective-permute-start(f32[468,128]{1,0:T(8,128)S(1)} %get-tuple-element.37), channel_id=1, source_target_pairs={{0,15},{1,2},{2,1},{3,4},{4,3},{5,6},{6,5},{7,8},{8,7},{9,10},{10,... | collective-permute-start | bytes 718856 | tf_op jit(solution)/shard_map/ppermute | solution.py:365
  15.4 2.5 %absorb.1 = (f32[6,32,2240]{2,1,0:T(8,128)S(1)}, f32[6,32,2240]{2,1,0:T(8,128)S(1)}, f32[6,32,2240]{2,1,0:T(8,128)S(1)}, f32[6,32,2240]{2,1,0:T(8,128)S(1)}) custom-call(f32[48,2240]{1,0:T(8,128)S(1)} %get-tuple-element.38.after.first, f32[6,32,2240]{2,1,0:T(8,128)} %u_h.1, f32[6,32,2240]{2,1,0:T(8,128)} %v_h.1), custom_call_target="tpu_custom_call" | custom-call | flops 1000000 | bytes 7000000 | tf_op jit(solution)/shard_map/absorb/pallas_call | solution.py:425
  17.9 0.0 collective-permute-done.2.inner_in
  17.9 2.6 %collective-permute-done.3.outer_in = f32[468,128]{1,0:T(8,128)S(1)} collective-permute-done((f32[468,128]{1,0:T(8,128)S(1)}, f32[468,128]{1,0:T(8,128)S(1)}, u32[]{:S(2)}, u32[]{:S(2)}) %collective-permute-start.3) | collective-permute-done | bytes 239648 | tf_op jit(solution)/shard_map/ppermute | solution.py:365
  20.6 2.0 %second_solve.1 = (f32[48,2240]{1,0:T(8,128)S(1)}, f32[48,2240]{1,0:T(8,128)S(1)}, f32[48,2240]{1,0:T(8,128)S(1)}, f32[48,2240]{1,0:T(8,128)S(1)}, f32[16,2240]{1,0:T(8,128)S(1)}, /*index=5*/f32[16,2240]{1,0:T(8,128)S(1)}) custom-call(s32[1]{0:T(128)} %bitcast.parity, f32[468,128]{1,0:T(8,128)S(1)} %collective-permute-done.2.inner_in, ...), custom_call_target="tpu_custom_call" | custom-call | tf_op jit(solution)/shard_map/second_solve/pallas_call | solution.py:436
  22.5 0.2 collective-permute-start.4
  22.7 3.0 %collective-permute-start.5 = (f32[16,2240]{1,0:T(8,128)S(1)}, f32[16,2240]{1,0:T(8,128)S(1)}, u32[]{:S(2)}, u32[]{:S(2)}) collective-permute-start(f32[16,2240]{1,0:T(8,128)S(1)} %get-tuple-element.42), channel_id=1, source_target_pairs={{0,15},{1,2},{2,1},{3,4},{4,3},{5,6},{6,5},{7,8},{8,7},{9,10},{10,... | collective-permute-start | bytes 430088 | tf_op jit(solution)/shard_map/ppermute | solution.py:365
  25.7 0.0 collective-permute-done.4.inner_in
  25.7 4.2 %collective-permute-done.5.outer_in = f32[16,2240]{1,0:T(8,128)S(1)} collective-permute-done((f32[16,2240]{1,0:T(8,128)S(1)}, f32[16,2240]{1,0:T(8,128)S(1)}, u32[]{:S(2)}, u32[]{:S(2)}) %collective-permute-start.5) | collective-permute-done | bytes 143392 | tf_op jit(solution)/shard_map/ppermute | solution.py:365
  30.0 0.6 %sums.1 = (f32[48,2240]{1,0:T(8,128)S(1)}, f32[16,2240]{1,0:T(8,128)S(1)}, f32[16,1,128]{2,1,0:T(1,128)S(1)}) custom-call(s32[1]{0:T(128)} %bitcast.parity, f32[16,2240]{1,0:T(8,128)S(1)} %collective-permute-done.4.inner_in, f32[16,2240]{1,0:T(8,128)S(1)} %collective-permute-done.5.outer_in, f32[48,2240]{1,0:T(8,128)S(1)} %get-tuple-element.43.second, ...), custom_call_target="tpu_custom_call" | custom-call | tf_op jit(solution)/shard_map/sums/pallas_call | solution.py:447
  30.6 10.6 %all_to_all.5.came = f32[16,1,128]{2,1,0:T(1,128)S(1)} all-to-all(f32[16,1,128]{2,1,0:T(1,128)S(1)} %get-tuple-element.48), channel_id=1, replica_groups=mesh['members'=2,'lon'=16] {'lon'}, dimensions={0} | all-to-all | bytes 16384 | tf_op jit(solution)/shard_map/all_to_all | solution.py:456
  41.2 3.6 %finish.1 = (f32[32,2240]{1,0:T(8,128)}, f32[6,32,2240]{2,1,0:T(8,128)}, f32[6,32,2240]{2,1,0:T(8,128)}, f32[6,32,2240]{2,1,0:T(8,128)}) custom-call(f32[16,1,128]{2,1,0:T(1,128)S(1)} %all_to_all.5.came, f32[48,2240]{1,0:T(8,128)S(1)} %get-tuple-element.44.z, f32[48,2240]{1,0:T(8,128)S(1)} %get-tuple-element.49.w, f32[16,2240]{1,0:T(8,128)S(1)} %get-tuple-element.50.edges, ...), custom_call_target="tpu_custom_call" | custom-call | tf_op jit(solution)/shard_map/finish/pallas_call | solution.py:458
Async XLA Ops:
  1.6 7.5 %collective-permute-start.1 = (f32[8,2240]{1,0:T(8,128)S(1)}, f32[8,2240]{1,0:T(8,128)S(1)}, u32[]{:S(2)}, u32[]{:S(2)}) collective-permute-start(f32[8,2240]{1,0:T(8,128)S(1)} %first_edges.1.after), channel_id=1, source_target_pairs={{0,15},{1,2},{2,1},{3,4},{4,3},{5,6},{6,5},{7,8},{8,7},{9,10},{10,... | collective-permute-start | bytes 215048 | tf_op jit(solution)/shard_map/ppermute | solution.py:365
  9.0 1.3 %collective-permute-start = (f32[8,2240]{1,0:T(8,128)S(1)}, f32[8,2240]{1,0:T(8,128)S(1)}, u32[]{:S(2)}, u32[]{:S(2)}) collective-permute-start(f32[8,2240]{1,0:T(8,128)S(1)} %get-tuple-element.29), channel_id=1, source_target_pairs={{0,1},{1,0},{2,3},{3,2},{4,5},{5,4},{6,7},{7,6},{8,9},{9,8},{10,11... | collective-permute-start | bytes 215048 | tf_op jit(solution)/shard_map/ppermute | solution.py:365
  12.0 6.0 %collective-permute-start.2 = (f32[468,128]{1,0:T(8,128)S(1)}, f32[468,128]{1,0:T(8,128)S(1)}, u32[]{:S(2)}, u32[]{:S(2)}) collective-permute-start(f32[468,128]{1,0:T(8,128)S(1)} %get-tuple-element.36), channel_id=1, source_target_pairs={{0,1},{1,0},{2,3},{3,2},{4,5},{5,4},{6,7},{7,6},{8,9},{9,8},{10,11... | collective-permute-start | bytes 718856 | tf_op jit(solution)/shard_map/ppermute | solution.py:365
  12.2 8.4 %collective-permute-start.3 = (f32[468,128]{1,0:T(8,128)S(1)}, f32[468,128]{1,0:T(8,128)S(1)}, u32[]{:S(2)}, u32[]{:S(2)}) collective-permute-start(f32[468,128]{1,0:T(8,128)S(1)} %get-tuple-element.37), channel_id=1, source_target_pairs={{0,15},{1,2},{2,1},{3,4},{4,3},{5,6},{6,5},{7,8},{8,7},{9,10},{10,... | collective-permute-start | bytes 718856 | tf_op jit(solution)/shard_map/ppermute | solution.py:365
  22.5 3.2 %collective-permute-start.4 = (f32[16,2240]{1,0:T(8,128)S(1)}, f32[16,2240]{1,0:T(8,128)S(1)}, u32[]{:S(2)}, u32[]{:S(2)}) collective-permute-start(f32[16,2240]{1,0:T(8,128)S(1)} %get-tuple-element.41), channel_id=1, source_target_pairs={{0,1},{1,0},{2,3},{3,2},{4,5},{5,4},{6,7},{7,6},{8,9},{9,8},{10,11... | collective-permute-start | bytes 430088 | tf_op jit(solution)/shard_map/ppermute | solution.py:365
  22.7 7.3 %collective-permute-start.5 = (f32[16,2240]{1,0:T(8,128)S(1)}, f32[16,2240]{1,0:T(8,128)S(1)}, u32[]{:S(2)}, u32[]{:S(2)}) collective-permute-start(f32[16,2240]{1,0:T(8,128)S(1)} %get-tuple-element.42), channel_id=1, source_target_pairs={{0,15},{1,2},{2,1},{3,4},{4,3},{5,6},{6,5},{7,8},{8,7},{9,10},{10,... | collective-permute-start | bytes 430088 | tf_op jit(solution)/shard_map/ppermute | solution.py:365

commit v6 on v5

--- a/solution.py
+++ b/solution.py
@@ -39,26 +39,15 @@
     return high, low
 
 
-def window_at(tile):
-    return divmod(tile * LT - OV + LANE, LANE)
-
-
 def tables(span):
     lon_basis, lon_value = sine_basis(span)
     lat_basis, lat_value = sine_basis(LT + 2 * OV)
     high, low = halves(lat_basis)
-    forward = np.zeros((8, 2 * LANE, 2 * LANE), ml_dtypes.bfloat16)
-    inverse = np.zeros((8, 2 * LANE, 2 * LANE), ml_dtypes.bfloat16)
-    for kind in range(8):
-        lane = window_at(kind)[1]
-        forward[kind, lane : lane + LANE, :LANE] = high
-        forward[kind, lane : lane + LANE, LANE:] = low
-        inverse[kind, :LANE, lane : lane + LANE] = high.T
-        inverse[kind, LANE:, lane : lane + LANE] = low.T
+    lat = np.block([[high, low], [high, np.zeros_like(low)]])
     high, low = halves(lon_basis)
     lon = np.concatenate([high, low, high], axis=1)
     scale = 1.0 / (lon_value[:, None] + lat_value[None, :] + tile_shift)
-    return forward, inverse, lon, scale.astype(np.float32)
+    return lat, lon, scale.astype(np.float32)
 
 
 def split(x):
@@ -66,61 +55,62 @@
     return high, (x - high.astype(F32)).astype(BF16)
 
 
-def tile_solve(x, forward, inverse, lon, scale, wide, spectral, restored, out):
+def tile_solve(x, lat_basis, lon, scale, wide, rows, spectral, out):
     span, lat = x.shape
     tiles = lat // LT
     high, low = split(x)
-    wide[:, :LANE] = jnp.zeros((2 * span, LANE), BF16)
-    wide[:, LANE + lat :] = jnp.zeros((2 * span, wide.shape[1] - LANE - lat), BF16)
-    wide[:span, LANE : LANE + lat] = high
-    wide[span:, LANE : LANE + lat] = low
-    for kind in range(8):
-        group = range(kind, tiles, 8)
-        starts = [window_at(t)[0] * LANE for t in group]
-        rows = jnp.concatenate([wide[:, s : s + 2 * LANE] for s in starts], axis=0)
-        product = jnp.dot(rows, forward[kind], preferred_element_type=F32)
-        for i, t in enumerate(group):
-            part = product[2 * span * i : 2 * span * (i + 1)]
-            part = part[:, :LANE] + part[:, LANE:]
-            high, low = split(part[:span] + part[span:])
-            at = pl.ds(t * LANE, LANE)
-            spectral[:span, at] = high
-            spectral[span : 2 * span, at] = high
-            spectral[2 * span :, at] = low
+    for at, part in ((0, high), (span, low)):
+        wide[at : at + span, :LANE] = jnp.zeros((span, LANE), BF16)
+        wide[at : at + span, LANE : LANE + lat] = part
+        wide[at : at + span, LANE + lat :] = jnp.zeros((span, wide.shape[1] - LANE - lat), BF16)
+    for t in range(tiles):
+        block, lane = divmod(LANE + t * LT - OV, LANE)
+        window = wide[:, block * LANE : (block + 2) * LANE][:, lane : lane + LANE]
+        rows[t * span : (t + 1) * span, :LANE] = window[:span]
+        rows[t * span : (t + 1) * span, LANE:] = window[span:]
     chunk = 4
     for first in range(0, tiles, chunk):
         n = min(chunk, tiles - first)
-        c = jnp.dot(lon[...], spectral[:, pl.ds(first * LANE, n * LANE)], preferred_element_type=F32)
+        product = jnp.dot(
+            rows[first * span : (first + n) * span], lat_basis[...], preferred_element_type=F32
+        )
+        high, low = split(product[:, :LANE] + product[:, LANE:])
+        for i in range(n):
+            at = slice((first + i) * LANE, (first + i + 1) * LANE)
+            spectral[:span, at] = high[i * span : (i + 1) * span]
+            spectral[span : 2 * span, at] = high[i * span : (i + 1) * span]
+            spectral[2 * span :, at] = low[i * span : (i + 1) * span]
+    for first in range(0, tiles, chunk):
+        n = min(chunk, tiles - first)
+        c = jnp.dot(lon[...], spectral[:, first * LANE : (first + n) * LANE], preferred_element_type=F32)
         c = c * jnp.concatenate([scale[...]] * n, axis=1)
         high, low = split(c)
         c = jnp.concatenate([high, high, low], axis=0)
         c = jnp.dot(lon[...], c, preferred_element_type=F32)
         high, low = split(c)
         for i in range(n):
-            for side in range(2):
-                at = pl.ds((2 * (first + i) + side) * LANE, LANE)
-                restored[:span, at] = high[:, i * LANE : (i + 1) * LANE]
-                restored[span:, at] = low[:, i * LANE : (i + 1) * LANE]
+            at = slice((first + i) * span, (first + i + 1) * span)
+            rows[at, :LANE] = high[:, i * LANE : (i + 1) * LANE]
+            rows[at, LANE:] = low[:, i * LANE : (i + 1) * LANE]
     out[...] = jnp.zeros(out.shape, F32)
-    for kind in range(8):
-        group = range(kind, tiles, 8)
-        rows = jnp.concatenate(
-            [restored[:, pl.ds(2 * t * LANE, 2 * LANE)] for t in group], axis=0
+    for first in range(0, tiles, chunk):
+        n = min(chunk, tiles - first)
+        product = jnp.dot(
+            rows[first * span : (first + n) * span], lat_basis[...], preferred_element_type=F32
         )
-        product = jnp.dot(rows, inverse[kind], preferred_element_type=F32)
-        for i, t in enumerate(group):
-            part = product[2 * span * i : 2 * span * (i + 1)]
-            at = pl.ds(window_at(t)[0] * LANE, 2 * LANE)
-            out[:, at] += part[:span] + part[span:]
+        product = product[:, :LANE] + product[:, LANE:]
+        for i in range(n):
+            at = (first + i) * LT
+            out[:, at : at + LANE] += product[i * span : (i + 1) * span]
 
 
 def solve_scratch(span, lat):
     tiles = lat // LT
-    lanes = (window_at(tiles - 1)[0] + 2) * LANE
+    lanes = -(-(LANE + lat + OV) // LANE) * LANE
     return [
         pltpu.VMEM((2 * span, lanes), BF16),
+        pltpu.VMEM((tiles * span, 2 * LANE), BF16),
         pltpu.VMEM((3 * span, tiles * LANE), BF16),
-        pltpu.VMEM((2 * span, 2 * tiles * LANE), BF16),
         pltpu.VMEM((span, lanes), F32),
     ]
 
@@ -162,8 +152,8 @@
 
 
 def prepare(parity, after, source_h, diagonal_h, bottom_h, *refs):
-    tables_h, (inner, masked, coef, depth, source), held = refs[:4], refs[4:9], refs[9:13]
-    diagonal, bottom, sems = refs[13:]
+    tables_h, (inner, masked, coef, depth, source), held = refs[:3], refs[3:8], refs[8:11]
+    diagonal, bottom, sems = refs[11:]
     pairs = [(source_h, source), (bottom_h, bottom), (diagonal_h, diagonal)]
     pairs += list(zip(tables_h, held))
     copies = [pltpu.make_async_copy(a, b, sems.at[i]) for i, (a, b) in enumerate(pairs)]
@@ -180,13 +170,13 @@
         copy.wait()
 
 
-def first_solve(parity, inner_in, outer_in, masked, coef, forward, inverse, lon, scale,
-                first, inner, outer, wide, spectral, restored, out):
+def first_solve(parity, inner_in, outer_in, masked, coef, lat_basis, lon, scale,
+                first, inner, outer, wide, rows, spectral, out):
     cells, lat = masked.shape
     west, east = pick(parity, inner_in[...], outer_in[...])
     x = jnp.concatenate([west, masked[...], east], axis=0)
-    tile_solve(x, forward, inverse, lon, scale, wide, spectral, restored, out)
-    first[...] = out[:, LANE : LANE + lat]
+    tile_solve(x, lat_basis, lon, scale, wide, rows, spectral, out)
+    first[...] = out[:, OV : OV + lat]
     reach, edge = 2 * OV + 1, OV + 1
     to_west = jnp.concatenate([first[:reach], coef[:edge]], axis=0)
     to_east = jnp.concatenate([first[cells - 1 :], coef[cells - edge :]], axis=0)
@@ -195,21 +185,16 @@
     pack(outer, to_outer)
 
 
-def absorb(after, u_h, v_h, u, v, u_before, v_before, sems):
+def absorb(after, u_h, v_h, u, v, sems):
     copies = [pltpu.make_async_copy(a, b, sems.at[i]) for i, (a, b) in enumerate([(u_h, u), (v_h, v)])]
     for copy in copies:
         copy.start()
-    levels, cells, lat = u.shape
-    copies[0].wait()
-    for level in range(levels):
-        u_before[level] = jnp.concatenate([jnp.zeros((1, lat), F32), u[level, : cells - 1]], axis=0)
-    copies[1].wait()
-    for level in range(levels):
-        v_before[level] = jnp.concatenate([jnp.zeros((cells, 1), F32), v[level, :, : lat - 1]], axis=1)
-
-
-def second_solve(parity, inner_in, outer_in, first, coef_own, depth, u, forward, inverse, lon, scale,
-                 z, y, coef, second, inner, outer, wide, spectral, restored, out, m_rows, c_rows):
+    for copy in copies:
+        copy.wait()
+
+
+def second_solve(parity, inner_in, outer_in, first, coef_own, depth, u, lat_basis, lon, scale,
+                 z, y, coef, second, inner, outer, wide, rows, spectral, out, m_rows, c_rows):
     cells, lat = coef_own.shape
     span = cells + 2 * OV
     reach, edge = 2 * OV + 1, OV + 1
@@ -234,8 +219,8 @@
     beside = m_rows[OV - 1 : OV - 1 + span] + m_rows[OV + 1 : OV + 1 + span]
     image = jnp.where(c > 0, c * m - (beside + lat_beside(m)), 0.0)
     y[...] = image
-    tile_solve(image, forward, inverse, lon, scale, wide, spectral, restored, out)
-    second[...] = out[:, LANE : LANE + lat]
+    tile_solve(image, lat_basis, lon, scale, wide, rows, spectral, out)
+    second[...] = out[:, OV : OV + lat]
     to_west = jnp.concatenate([second[:edge], depth[:1], jnp.zeros((KL, lat), F32)], axis=0)
     u_rows = [u[level, cells - 1 : cells] for level in range(KL)]
     to_east = jnp.concatenate([second[span - edge :], depth[cells - 1 :]] + u_rows, axis=0)
@@ -282,8 +267,8 @@
     sent[...] = jnp.broadcast_to(row[None], sent.shape)
 
 
-def finish(came, z, w, edges, source, depth, u_vel, v_vel, u_before, v_before, solution, u_new, v_new, w_vel,
-           s_rows, d_rows, u_out, v_out, w_out, s_out, sems):
+def finish(came, z, w, edges, source, depth, u_vel, v_vel, solution, u_new, v_new, w_vel,
+           s_rows, d_rows, u_rows, v_out, w_out, s_out, sems):
     cells, lat = source.shape
     total = jnp.sum(came[...], axis=0)
     rz, zy, rw, yw, zx, wx, ll = [total[:, i : i + 1] for i in range(7)]
@@ -298,60 +283,49 @@
     of_w = jnp.broadcast_to(-step1 * step0, (OV, lat))
     of_land = jnp.broadcast_to(step0 + step1 * (rest + beta), (OV, lat))
 
+    copies = []
     d_rows[:OV] = jnp.broadcast_to(edges[1:2], (OV, lat))
     d_rows[OV : OV + cells] = depth[...]
     d_rows[OV + cells :] = jnp.broadcast_to(edges[OV + 1 : OV + 2], (OV, lat))
-    first_row = lax.broadcasted_iota(jnp.int32, (OV, 3 * LANE), 0) == 0
-    copies = []
-
-    def rows_of_surface(at):
+    for at in range(0, cells + 2 * OV, OV):
         s = of_z * z[at : at + OV] + of_w * w[at : at + OV]
         if OV <= at < OV + cells:
-            s = jnp.where(d_rows[at : at + OV] > 0, s, of_land * source[at - OV : at])
+            d = d_rows[at : at + OV]
+            s = jnp.where(d > 0, s, of_land * source[at - OV : at])
             s_out[at - OV : at] = s
         s_rows[at : at + OV] = s
-
-    def send(held, result):
-        copies.append(pltpu.make_async_copy(held, result, sems.at[len(copies)]))
-        copies[-1].start()
-
-    rows_of_surface(0)
-    rows_of_surface(OV)
+    copies.append(pltpu.make_async_copy(s_out, solution, sems.at[0]))
+    copies[-1].start()
+
+    s_west = s_rows[OV - 1 : OV]
+    s_first = s_rows[OV : OV + 1]
+    d_west = jnp.minimum(d_rows[OV - 1 : OV], d_rows[OV : OV + 1])
+    for level in range(KL):
+        left = edges[level + 2 : level + 3] - gravity_step * (s_first - s_west)
+        u_rows[level, :OV] = jnp.broadcast_to(jnp.where(d_west > level, left, 0.0), (OV, lat))
     zero = jnp.zeros((OV, 1), F32)
-    for at in range(OV, OV + cells, OV):
-        rows_of_surface(at + OV)
+    for block in range(cells // OV):
+        at = OV + block * OV
         own = slice(at - OV, at)
-        s, d = s_rows[at : at + OV], d_rows[at : at + OV]
+        s = s_rows[at : at + OV]
+        d = d_rows[at : at + OV]
         slope_e = gravity_step * (s_rows[at + 1 : at + OV + 1] - s)
         depth_e = jnp.minimum(d, d_rows[at + 1 : at + OV + 1])
-        slope_w = gravity_step * (s - s_rows[at - 1 : at + OV - 1])
-        depth_w = jnp.minimum(d, d_rows[at - 1 : at + OV - 1])
         slope_n = gravity_step * (jnp.concatenate([s[:, 1:], zero], axis=1) - s)
         depth_n = jnp.minimum(d, jnp.concatenate([d[:, 1:], zero], axis=1))
-        slope_s = jnp.concatenate([zero, slope_n[:, :-1]], axis=1)
-        depth_s = jnp.concatenate([zero, depth_n[:, :-1]], axis=1)
-        for first in range(0, lat, 3 * LANE):
-            part = slice(first, min(first + 3 * LANE, lat))
-            d_p, de, dw, dn, ds = [x[:, part] for x in (d, depth_e, depth_w, depth_n, depth_s)]
-            se, sw, sn, ss = [x[:, part] for x in (slope_e, slope_w, slope_n, slope_s)]
-            w_sum = jnp.zeros(d_p.shape, F32)
-            for level in range(KL - 1, -1, -1):
-                u = jnp.where(de > level, u_vel[level, own, part] - se, 0.0)
-                v = jnp.where(dn > level, v_vel[level, own, part] - sn, 0.0)
-                before = u_before[level, own, part]
-                if at == OV:
-                    edge = jnp.broadcast_to(edges[level + 2 : level + 3, part], before.shape)
-                    before = jnp.where(first_row[:, : before.shape[1]], edge, before)
-                u_west = jnp.where(dw > level, before - sw, 0.0)
-                v_south = jnp.where(ds > level, v_before[level, own, part] - ss, 0.0)
-                w_sum = w_sum + jnp.where(d_p > level, (u - u_west) + (v - v_south), 0.0)
-                u_out[level, own, part] = u
-                v_out[level, own, part] = v
-                w_out[level, own, part] = w_sum
-        for held, result in ((u_out, u_new), (v_out, v_new), (w_out, w_vel)):
-            send(held.at[:, own], result.at[:, own])
-        if at == cells:
-            send(s_out, solution)
+        w_sum = jnp.zeros((OV, lat), F32)
+        for level in range(KL - 1, -1, -1):
+            u = jnp.where(depth_e > level, u_vel[level, own] - slope_e, 0.0)
+            u_rows[level, at : at + OV] = u
+            v = jnp.where(depth_n > level, v_vel[level, own] - slope_n, 0.0)
+            v_out[level, own] = v
+            south = jnp.concatenate([zero, v[:, :-1]], axis=1)
+            flow = (u - u_rows[level, at - 1 : at + OV - 1]) + (v - south)
+            w_sum = w_sum + jnp.where(d > level, flow, 0.0)
+            w_out[level, own] = w_sum
+        for held, result in ((u_rows.at[:, at : at + OV], u_new), (v_out.at[:, own], v_new), (w_out.at[:, own], w_vel)):
+            copies.append(pltpu.make_async_copy(held, result.at[:, own], sems.at[len(copies)]))
+            copies[-1].start()
     for copy in copies:
         copy.wait()
 
@@ -393,15 +367,15 @@
 
     inner, masked, coef_own, depth, source_v, *held = pl.pallas_call(
         prepare,
-        in_specs=[SM] + [HB] * 8,
-        out_specs=[VM] * 9,
+        in_specs=[SM] + [HB] * 7,
+        out_specs=[VM] * 8,
         out_shape=[pltpu.VMEM((OV, lat), F32)]
         + [pltpu.VMEM((cells, lat), F32)] * 4
         + [pltpu.VMEM(table.shape, table.dtype) for table in consts],
         scratch_shapes=[
             pltpu.VMEM((cells, lat), F32),
             pltpu.VMEM((cells, lat), jnp.int32),
-            pltpu.SemaphoreType.DMA((7,)),
+            pltpu.SemaphoreType.DMA((6,)),
         ],
         compiler_params=PARAMS,
         cost_estimate=pl.CostEstimate(flops=10**6, bytes_accessed=7 * 10**6, transcendentals=0),
@@ -412,7 +386,7 @@
     blocks = -(-lat // LANE)
     first, inner, outer = pl.pallas_call(
         first_solve,
-        in_specs=[SM] + [VM] * 8,
+        in_specs=[SM] + [VM] * 7,
         out_specs=[VM] * 3,
         out_shape=[pltpu.VMEM((span, lat), F32)]
         + [pltpu.VMEM(((3 * OV + 2) * blocks, LANE), F32)] * 2,
@@ -422,11 +396,11 @@
     )(parity, *near, masked, coef_own, *held)
     near = swap_pairs(inner, False), swap_pairs(outer, True)
 
-    u_v, v_v, u_shift, v_shift = pl.pallas_call(
+    u_v, v_v = pl.pallas_call(
         absorb,
         in_specs=[HB] * 3,
-        out_specs=[VM] * 4,
-        out_shape=[pltpu.VMEM((KL, cells, lat), F32)] * 4,
+        out_specs=[VM] * 2,
+        out_shape=[pltpu.VMEM((KL, cells, lat), F32)] * 2,
         scratch_shapes=[pltpu.SemaphoreType.DMA((2,))],
         compiler_params=PARAMS,
         cost_estimate=pl.CostEstimate(flops=10**6, bytes_accessed=7 * 10**6, transcendentals=0),
@@ -435,7 +409,7 @@
 
     z, y, coef, second, inner, outer = pl.pallas_call(
         second_solve,
-        in_specs=[SM] + [VM] * 10,
+        in_specs=[SM] + [VM] * 9,
         out_specs=[VM] * 6,
         out_shape=[pltpu.VMEM((span, lat), F32)] * 4 + [pltpu.VMEM((2 * OV, lat), F32)] * 2,
         scratch_shapes=solve_scratch(span, lat) + [pltpu.VMEM((span + 2 * OV, lat), F32)] * 2,
@@ -457,15 +431,16 @@
 
     return pl.pallas_call(
         finish,
-        in_specs=[VM] * 10,
+        in_specs=[VM] * 8,
         out_specs=[HB] * 4,
         out_shape=[shape(cells, lat)] + [shape(KL, cells, lat)] * 3,
         scratch_shapes=[pltpu.VMEM((span, lat), F32)] * 2
-        + [pltpu.VMEM((KL, cells, lat), F32)] * 3
+        + [pltpu.VMEM((KL, OV + cells, lat), F32)]
+        + [pltpu.VMEM((KL, cells, lat), F32)] * 2
         + [pltpu.VMEM((cells, lat), F32), pltpu.SemaphoreType.DMA((1 + 3 * (cells // OV),))],
         compiler_params=PARAMS,
         name="finish",
-    )(came, z, w, edges, source_v, depth, u_v, v_v, u_shift, v_shift)
+    )(came, z, w, edges, source_v, depth, u_v, v_v)
 
 
 def solution(mesh):

time: 45.1 us -> 45.1 us (level)
  starting transfers between devices: 12.2 us -> 13.3 us
  Pallas kernels: 13.2 us -> 12.2 us
  waiting for transfers between devices: 8.14 us -> 7.52 us
  blocking collectives: 10.6 us -> 11.2 us
    ppermute x6, starting transfers between devices: 12.2 us -> 13.3 us  [swap_pairs(): return lax.ppermute(block, 'lon', route)]
    pallas_call x5, Pallas kernels: 11.6 us -> 10.6 us  [the longest x1 3.32 us: body(): pl.pallas_call(finish, in_specs=[VM] * 8, out_specs=[HB] * 4, out_shape=[...]
    ppermute x6, waiting for transfers between devices: 8.14 us -> 7.52 us  [swap_pairs(): return lax.ppermute(block, 'lon', route)]
    all_to_all x1, blocking collectives: 10.6 us -> 11.2 us  [body(): came = lax.all_to_all(sent, 'lon', 0, 0)]
  transfers between devices with their start and end apart: 6 -> 6, of which waited for: 4 -> 4; matrix products, arithmetic and copies ran while one was open for 0% -> 0% of each run, Pallas kernels for 10% -> 7%
where the time goes in v6:
time: 45.1 us; the launch traced here: 44.9 us
  starting transfers between devices  13.3 us (29%)
  Pallas kernels  12.2 us (27%)
  blocking collectives  11.2 us (25%)
  waiting for transfers between devices  7.52 us (17%)
  between operations  0.7 us (2%)
    ppermute x6, starting transfers between devices, swap_pairs(): return lax.ppermute(block, 'lon', route)  13.3 us
    all_to_all x1, blocking collectives, body(): came = lax.all_to_all(sent, 'lon', 0, 0)  11.2 us
    ppermute x6, waiting for transfers between devices, swap_pairs(): return lax.ppermute(block, 'lon', route)  7.52 us
    pallas_call x1, Pallas kernels, body(): pl.pallas_call(finish, in_specs=[VM] * 8, out_specs=[HB] * 4, out_shape=[...  3.32 us
    pallas_call x1, Pallas kernels, body(): pl.pallas_call(second_solve, in_specs=[SM] + [VM] * 9, out_specs=[VM] * 6...  2.2 us
    pallas_call x1, Pallas kernels, body(): pl.pallas_call(absorb, in_specs=[HB] * 3, out_specs=[VM] * 2, out_shape=[...  2.02 us
    pallas_call x1, Pallas kernels, body(): pl.pallas_call(first_solve, in_specs=[SM] + [VM] * 7, out_specs=[VM] * 3,...  1.76 us
    pallas_call x1, Pallas kernels, body(): pl.pallas_call(prepare, in_specs=[SM] + [HB] * 7, out_specs=[VM] * 8, out...  1.31 us
  transfers between devices with their start and end apart: 6, of which 4 were waited for; matrix products, arithmetic and copies ran while one was open for 0% of the time, Pallas kernels for 7%

profile of v6, /device:TPU:0, one launch (start us, length us, event | category | flops | bytes accessed | tf_op | source)
XLA Modules:
  0.0 44.9 jit_solution(15005022385924125546)
XLA Ops:
  0.6 0.9 %first_edges.1.after = f32[8,2240]{1,0:T(8,128)S(1)} custom-call(s32[1]{0:T(128)} %bitcast.parity, f32[32,2240]{1,0:T(8,128)} %source_h.1, s32[32,2240]{1,0:T(8,128)} %bottom_h.1), custom_call_target="tpu_custom_call" | custom-call | tf_op jit(solution)/shard_map/first_edges/pallas_call | solution.py:356
  1.6 5.5 %collective-permute-start.1 = (f32[8,2240]{1,0:T(8,128)S(1)}, f32[8,2240]{1,0:T(8,128)S(1)}, u32[]{:S(2)}, u32[]{:S(2)}) collective-permute-start(f32[8,2240]{1,0:T(8,128)S(1)} %first_edges.1.after), channel_id=1, source_target_pairs={{0,15},{1,2},{2,1},{3,4},{4,3},{5,6},{6,5},{7,8},{8,7},{9,10},{10,... | collective-permute-start | bytes 215048 | tf_op jit(solution)/shard_map/ppermute | solution.py:339
  7.1 1.3 %prepare.1 = (f32[8,2240]{1,0:T(8,128)S(1)}, f32[32,2240]{1,0:T(8,128)S(1)}, f32[32,2240]{1,0:T(8,128)S(1)}, f32[32,2240]{1,0:T(8,128)S(1)}, f32[32,2240]{1,0:T(...) custom-call(s32[1]{0:T(128)} %bitcast.parity, ...), custom_call_target="tpu_custom_call" | custom-call | flops 1000000 | bytes 7000000 | tf_op jit(solution)/shard_map/prepare/pallas_call | solution.py:368
  8.4 0.1 collective-permute-start
  8.5 0.6 %collective-permute-done.1.outer_in = f32[8,2240]{1,0:T(8,128)S(1)} collective-permute-done((f32[8,2240]{1,0:T(8,128)S(1)}, f32[8,2240]{1,0:T(8,128)S(1)}, u32[]{:S(2)}, u32[]{:S(2)}) %collective-permute-start.1) | collective-permute-done | bytes 71712 | tf_op jit(solution)/shard_map/ppermute | solution.py:339
  9.1 0.6 %collective-permute-done.inner_in = f32[8,2240]{1,0:T(8,128)S(1)} collective-permute-done((f32[8,2240]{1,0:T(8,128)S(1)}, f32[8,2240]{1,0:T(8,128)S(1)}, u32[]{:S(2)}, u32[]{:S(2)}) %collective-permute-start) | collective-permute-done | bytes 71712 | tf_op jit(solution)/shard_map/ppermute | solution.py:339
  9.7 1.8 %first_solve.1 = (f32[48,2240]{1,0:T(8,128)S(1)}, f32[468,128]{1,0:T(8,128)S(1)}, f32[468,128]{1,0:T(8,128)S(1)}) custom-call(s32[1]{0:T(128)} %bitcast.parity, f32[8,2240]{1,0:T(8,128)S(1)} %collective-permute-done.inner_in, f32[8,2240]{1,0:T(8,128)S(1)} %collective-permute-done.1.outer_in, f32[32,2240]{1,0:T(8,128)S(1)} %get-tuple-element.27.masked, ...), custom_call_target="tpu_custom_call" | custom-call | tf_op jit(solution)/shard_map/first_solve/pallas_call | solution.py:387
  11.5 0.2 collective-permute-start.2
  11.7 3.8 %collective-permute-start.3 = (f32[468,128]{1,0:T(8,128)S(1)}, f32[468,128]{1,0:T(8,128)S(1)}, u32[]{:S(2)}, u32[]{:S(2)}) collective-permute-start(f32[468,128]{1,0:T(8,128)S(1)} %get-tuple-element.33), channel_id=1, source_target_pairs={{0,15},{1,2},{2,1},{3,4},{4,3},{5,6},{6,5},{7,8},{8,7},{9,10},{10,... | collective-permute-start | bytes 718856 | tf_op jit(solution)/shard_map/ppermute | solution.py:339
  15.5 2.0 %absorb.1 = (f32[6,32,2240]{2,1,0:T(8,128)S(1)}, f32[6,32,2240]{2,1,0:T(8,128)S(1)}) custom-call(f32[48,2240]{1,0:T(8,128)S(1)} %get-tuple-element.34.after.first, f32[6,32,2240]{2,1,0:T(8,128)} %u_h.1, f32[6,32,2240]{2,1,0:T(8,128)} %v_h.1), custom_call_target="tpu_custom_call" | custom-call | flops 1000000 | bytes 7000000 | tf_op jit(solution)/shard_map/absorb/pallas_call | solution.py:399
  17.5 0.0 collective-permute-done.2.inner_in
  17.5 2.6 %collective-permute-done.3.outer_in = f32[468,128]{1,0:T(8,128)S(1)} collective-permute-done((f32[468,128]{1,0:T(8,128)S(1)}, f32[468,128]{1,0:T(8,128)S(1)}, u32[]{:S(2)}, u32[]{:S(2)}) %collective-permute-start.3) | collective-permute-done | bytes 239648 | tf_op jit(solution)/shard_map/ppermute | solution.py:339
  20.1 2.2 %second_solve.1 = (f32[48,2240]{1,0:T(8,128)S(1)}, f32[48,2240]{1,0:T(8,128)S(1)}, f32[48,2240]{1,0:T(8,128)S(1)}, f32[48,2240]{1,0:T(8,128)S(1)}, f32[16,2240]{1,0:T(8,128)S(1)}, /*index=5*/f32[16,2240]{1,0:T(8,128)S(1)}) custom-call(s32[1]{0:T(128)} %bitcast.parity, f32[468,128]{1,0:T(8,128)S(1)} %collective-permute-done.2.inner_in, ...), custom_call_target="tpu_custom_call" | custom-call | tf_op jit(solution)/shard_map/second_solve/pallas_call | solution.py:410
  22.3 0.2 collective-permute-start.4
  22.5 3.6 %collective-permute-start.5 = (f32[16,2240]{1,0:T(8,128)S(1)}, f32[16,2240]{1,0:T(8,128)S(1)}, u32[]{:S(2)}, u32[]{:S(2)}) collective-permute-start(f32[16,2240]{1,0:T(8,128)S(1)} %get-tuple-element.38), channel_id=1, source_target_pairs={{0,15},{1,2},{2,1},{3,4},{4,3},{5,6},{6,5},{7,8},{8,7},{9,10},{10,... | collective-permute-start | bytes 430088 | tf_op jit(solution)/shard_map/ppermute | solution.py:339
  26.1 0.0 collective-permute-done.4.inner_in
  26.1 3.7 %collective-permute-done.5.outer_in = f32[16,2240]{1,0:T(8,128)S(1)} collective-permute-done((f32[16,2240]{1,0:T(8,128)S(1)}, f32[16,2240]{1,0:T(8,128)S(1)}, u32[]{:S(2)}, u32[]{:S(2)}) %collective-permute-start.5) | collective-permute-done | bytes 143392 | tf_op jit(solution)/shard_map/ppermute | solution.py:339
  29.8 0.6 %sums.1 = (f32[48,2240]{1,0:T(8,128)S(1)}, f32[16,2240]{1,0:T(8,128)S(1)}, f32[16,1,128]{2,1,0:T(1,128)S(1)}) custom-call(s32[1]{0:T(128)} %bitcast.parity, f32[16,2240]{1,0:T(8,128)S(1)} %collective-permute-done.4.inner_in, f32[16,2240]{1,0:T(8,128)S(1)} %collective-permute-done.5.outer_in, f32[48,2240]{1,0:T(8,128)S(1)} %get-tuple-element.39.second, ...), custom_call_target="tpu_custom_call" | custom-call | tf_op jit(solution)/shard_map/sums/pallas_call | solution.py:421
  30.4 11.2 %all_to_all.5.came = f32[16,1,128]{2,1,0:T(1,128)S(1)} all-to-all(f32[16,1,128]{2,1,0:T(1,128)S(1)} %get-tuple-element.44), channel_id=1, replica_groups=mesh['members'=2,'lon'=16] {'lon'}, dimensions={0} | all-to-all | bytes 16384 | tf_op jit(solution)/shard_map/all_to_all | solution.py:430
  41.6 3.3 %finish.1 = (f32[32,2240]{1,0:T(8,128)}, f32[6,32,2240]{2,1,0:T(8,128)}, f32[6,32,2240]{2,1,0:T(8,128)}, f32[6,32,2240]{2,1,0:T(8,128)}) custom-call(f32[16,1,128]{2,1,0:T(1,128)S(1)} %all_to_all.5.came, f32[48,2240]{1,0:T(8,128)S(1)} %get-tuple-element.40.z, f32[48,2240]{1,0:T(8,128)S(1)} %get-tuple-element.45.w, f32[16,2240]{1,0:T(8,128)S(1)} %get-tuple-element.46.edges, ...), custom_call_target="tpu_custom_call" | custom-call | tf_op jit(solution)/shard_map/finish/pallas_call | solution.py:432
Async XLA Ops:
  1.6 7.5 %collective-permute-start.1 = (f32[8,2240]{1,0:T(8,128)S(1)}, f32[8,2240]{1,0:T(8,128)S(1)}, u32[]{:S(2)}, u32[]{:S(2)}) collective-permute-start(f32[8,2240]{1,0:T(8,128)S(1)} %first_edges.1.after), channel_id=1, source_target_pairs={{0,15},{1,2},{2,1},{3,4},{4,3},{5,6},{6,5},{7,8},{8,7},{9,10},{10,... | collective-permute-start | bytes 215048 | tf_op jit(solution)/shard_map/ppermute | solution.py:339
  8.4 1.3 %collective-permute-start = (f32[8,2240]{1,0:T(8,128)S(1)}, f32[8,2240]{1,0:T(8,128)S(1)}, u32[]{:S(2)}, u32[]{:S(2)}) collective-permute-start(f32[8,2240]{1,0:T(8,128)S(1)} %get-tuple-element.26), channel_id=1, source_target_pairs={{0,1},{1,0},{2,3},{3,2},{4,5},{5,4},{6,7},{7,6},{8,9},{9,8},{10,11... | collective-permute-start | bytes 215048 | tf_op jit(solution)/shard_map/ppermute | solution.py:339
  11.5 6.0 %collective-permute-start.2 = (f32[468,128]{1,0:T(8,128)S(1)}, f32[468,128]{1,0:T(8,128)S(1)}, u32[]{:S(2)}, u32[]{:S(2)}) collective-permute-start(f32[468,128]{1,0:T(8,128)S(1)} %get-tuple-element.32), channel_id=1, source_target_pairs={{0,1},{1,0},{2,3},{3,2},{4,5},{5,4},{6,7},{7,6},{8,9},{9,8},{10,11... | collective-permute-start | bytes 718856 | tf_op jit(solution)/shard_map/ppermute | solution.py:339
  11.7 8.4 %collective-permute-start.3 = (f32[468,128]{1,0:T(8,128)S(1)}, f32[468,128]{1,0:T(8,128)S(1)}, u32[]{:S(2)}, u32[]{:S(2)}) collective-permute-start(f32[468,128]{1,0:T(8,128)S(1)} %get-tuple-element.33), channel_id=1, source_target_pairs={{0,15},{1,2},{2,1},{3,4},{4,3},{5,6},{6,5},{7,8},{8,7},{9,10},{10,... | collective-permute-start | bytes 718856 | tf_op jit(solution)/shard_map/ppermute | solution.py:339
  22.3 3.8 %collective-permute-start.4 = (f32[16,2240]{1,0:T(8,128)S(1)}, f32[16,2240]{1,0:T(8,128)S(1)}, u32[]{:S(2)}, u32[]{:S(2)}) collective-permute-start(f32[16,2240]{1,0:T(8,128)S(1)} %get-tuple-element.37), channel_id=1, source_target_pairs={{0,1},{1,0},{2,3},{3,2},{4,5},{5,4},{6,7},{7,6},{8,9},{9,8},{10,11... | collective-permute-start | bytes 430088 | tf_op jit(solution)/shard_map/ppermute | solution.py:339
  22.5 7.3 %collective-permute-start.5 = (f32[16,2240]{1,0:T(8,128)S(1)}, f32[16,2240]{1,0:T(8,128)S(1)}, u32[]{:S(2)}, u32[]{:S(2)}) collective-permute-start(f32[16,2240]{1,0:T(8,128)S(1)} %get-tuple-element.38), channel_id=1, source_target_pairs={{0,15},{1,2},{2,1},{3,4},{4,3},{5,6},{6,5},{7,8},{8,7},{9,10},{10,... | collective-permute-start | bytes 430088 | tf_op jit(solution)/shard_map/ppermute | solution.py:339

commit v7 on v6

--- a/solution.py
+++ b/solution.py
@@ -55,19 +55,22 @@
     return high, (x - high.astype(F32)).astype(BF16)
 
 
-def tile_solve(x, lat_basis, lon, scale, wide, rows, spectral, out):
-    span, lat = x.shape
+def tile_solve(x, lat_basis, lon, scale, rows, spectral, out):
+    span, lat = out.shape
     tiles = lat // LT
-    high, low = split(x)
-    for at, part in ((0, high), (span, low)):
-        wide[at : at + span, :LANE] = jnp.zeros((span, LANE), BF16)
-        wide[at : at + span, LANE : LANE + lat] = part
-        wide[at : at + span, LANE + lat :] = jnp.zeros((span, wide.shape[1] - LANE - lat), BF16)
+    lane = lax.broadcasted_iota(jnp.int32, (span, LANE), 1)
+
+    def block_of(b):
+        if b < 0:
+            return jnp.zeros((span, LANE), F32)
+        return x[:, b * LANE : (b + 1) * LANE]
+
     for t in range(tiles):
-        block, lane = divmod(LANE + t * LT - OV, LANE)
-        window = wide[:, block * LANE : (block + 2) * LANE][:, lane : lane + LANE]
-        rows[t * span : (t + 1) * span, :LANE] = window[:span]
-        rows[t * span : (t + 1) * span, LANE:] = window[span:]
+        block, start = divmod(t * LT - OV, LANE)
+        left, right = [pltpu.roll(block_of(b), LANE - start, 1) for b in (block, block + 1)]
+        high, low = split(jnp.where(lane < LANE - start, left, right))
+        rows[t * span : (t + 1) * span, :LANE] = high
+        rows[t * span : (t + 1) * span, LANE:] = low
     chunk = 4
     for first in range(0, tiles, chunk):
         n = min(chunk, tiles - first)
@@ -92,7 +95,7 @@
             at = slice((first + i) * span, (first + i + 1) * span)
             rows[at, :LANE] = high[:, i * LANE : (i + 1) * LANE]
             rows[at, LANE:] = low[:, i * LANE : (i + 1) * LANE]
-    out[...] = jnp.zeros(out.shape, F32)
+    sums_of = {}
     for first in range(0, tiles, chunk):
         n = min(chunk, tiles - first)
         product = jnp.dot(
@@ -100,18 +103,28 @@
         )
         product = product[:, :LANE] + product[:, LANE:]
         for i in range(n):
-            at = (first + i) * LT
-            out[:, at : at + LANE] += product[i * span : (i + 1) * span]
+            block, start = divmod((first + i) * LT - OV, LANE)
+            part = pltpu.roll(product[i * span : (i + 1) * span], start, 1)
+            for b, inside in ((block, lane >= start), (block + 1, lane < start)):
+                if 0 <= b * LANE < lat:
+                    piece = jnp.where(inside, part, 0.0)
+                    sums_of[b] = sums_of[b] + piece if b in sums_of else piece
+        done = (first + n) * LT - OV if first + n < tiles else lat + LANE
+        for b in [b for b in sums_of if (b + 1) * LANE <= done]:
+            width = min(LANE, lat - b * LANE)
+            out[:, b * LANE : b * LANE + width] = sums_of.pop(b)[:, :width]
+
+
+def wide_lanes(lat):
+    return -(-(lat + OV) // LANE) * LANE
 
 
 def solve_scratch(span, lat):
     tiles = lat // LT
-    lanes = -(-(LANE + lat + OV) // LANE) * LANE
     return [
-        pltpu.VMEM((2 * span, lanes), BF16),
+        pltpu.VMEM((span, wide_lanes(lat)), F32),
         pltpu.VMEM((tiles * span, 2 * LANE), BF16),
         pltpu.VMEM((3 * span, tiles * LANE), BF16),
-        pltpu.VMEM((span, lanes), F32),
     ]
 
 
@@ -171,12 +184,14 @@
 
 
 def first_solve(parity, inner_in, outer_in, masked, coef, lat_basis, lon, scale,
-                first, inner, outer, wide, rows, spectral, out):
+                first, inner, outer, wide, rows, spectral):
     cells, lat = masked.shape
     west, east = pick(parity, inner_in[...], outer_in[...])
-    x = jnp.concatenate([west, masked[...], east], axis=0)
-    tile_solve(x, lat_basis, lon, scale, wide, rows, spectral, out)
-    first[...] = out[:, OV : OV + lat]
+    wide[:OV, :lat] = west
+    wide[OV : OV + cells, :lat] = masked[...]
+    wide[OV + cells :, :lat] = east
+    wide[:, lat:] = jnp.zeros((cells + 2 * OV, wide.shape[1] - lat), F32)
+    tile_solve(wide, lat_basis, lon, scale, rows, spectral, first)
     reach, edge = 2 * OV + 1, OV + 1
     to_west = jnp.concatenate([first[:reach], coef[:edge]], axis=0)
     to_east = jnp.concatenate([first[cells - 1 :], coef[cells - edge :]], axis=0)
@@ -194,7 +209,7 @@
 
 
 def second_solve(parity, inner_in, outer_in, first, coef_own, depth, u, lat_basis, lon, scale,
-                 z, y, coef, second, inner, outer, wide, rows, spectral, out, m_rows, c_rows):
+                 z, y, coef, second, inner, outer, wide, rows, spectral, m_rows, c_rows):
     cells, lat = coef_own.shape
     span = cells + 2 * OV
     reach, edge = 2 * OV + 1, OV + 1
@@ -219,8 +234,9 @@
     beside = m_rows[OV - 1 : OV - 1 + span] + m_rows[OV + 1 : OV + 1 + span]
     image = jnp.where(c > 0, c * m - (beside + lat_beside(m)), 0.0)
     y[...] = image
-    tile_solve(image, lat_basis, lon, scale, wide, rows, spectral, out)
-    second[...] = out[:, OV : OV + lat]
+    wide[:, :lat] = image
+    wide[:, lat:] = jnp.zeros((span, wide.shape[1] - lat), F32)
+    tile_solve(wide, lat_basis, lon, scale, rows, spectral, second)
     to_west = jnp.concatenate([second[:edge], depth[:1], jnp.zeros((KL, lat), F32)], axis=0)
     u_rows = [u[level, cells - 1 : cells] for level in range(KL)]
     to_east = jnp.concatenate([second[span - edge :], depth[cells - 1 :]] + u_rows, axis=0)
@@ -270,8 +286,10 @@
 def finish(came, z, w, edges, source, depth, u_vel, v_vel, solution, u_new, v_new, w_vel,
            s_rows, d_rows, u_rows, v_out, w_out, s_out, sems):
     cells, lat = source.shape
-    total = jnp.sum(came[...], axis=0)
-    rz, zy, rw, yw, zx, wx, ll = [total[:, i : i + 1] for i in range(7)]
+    total = jnp.broadcast_to(jnp.sum(came[...], axis=0), (8, LANE))
+    place = [lax.broadcasted_iota(jnp.int32, (8, LANE), axis) for axis in range(2)]
+    total = jnp.sum(jnp.where(place[0] == place[1], total, 0.0), axis=1, keepdims=True)
+    rz, zy, rw, yw, zx, wx, ll = [total[i : i + 1] for i in range(7)]
     step0 = (rz + ll) / (zy + ll)
     rest = (zy - rz) / (zy + ll)
     new = rz - step0 * (zy + rw) + step0 * step0 * yw + rest * rest * ll

time: 45.1 us -> 44.4 us (0.984)
  Pallas kernels: 12.2 us -> 11.5 us
  transfers between devices with their start and end apart: 6 -> 6, of which waited for: 4 -> 4; matrix products, arithmetic and copies ran while one was open for 0% -> 0% of each run, Pallas kernels for 7% -> 8%
where the time goes in v7:
time: 44.4 us; the launch traced here: 44.2 us
  starting transfers between devices  13.3 us (30%)
  Pallas kernels  11.5 us (26%)
  blocking collectives  11.2 us (25%)
  waiting for transfers between devices  7.52 us (17%)
  between operations  0.7 us (2%)
    ppermute x6, starting transfers between devices, swap_pairs(): return lax.ppermute(block, 'lon', route)  13.3 us
    all_to_all x1, blocking collectives, body(): came = lax.all_to_all(sent, 'lon', 0, 0)  11.2 us
    ppermute x6, waiting for transfers between devices, swap_pairs(): return lax.ppermute(block, 'lon', route)  7.52 us
    pallas_call x1, Pallas kernels, body(): pl.pallas_call(finish, in_specs=[VM] * 8, out_specs=[HB] * 4, out_shape=[...  3 us
    pallas_call x1, Pallas kernels, body(): pl.pallas_call(absorb, in_specs=[HB] * 3, out_specs=[VM] * 2, out_shape=[...  2.02 us
    pallas_call x1, Pallas kernels, body(): pl.pallas_call(second_solve, in_specs=[SM] + [VM] * 9, out_specs=[VM] * 6...  1.96 us
    pallas_call x1, Pallas kernels, body(): pl.pallas_call(first_solve, in_specs=[SM] + [VM] * 7, out_specs=[VM] * 3,...  1.59 us
    pallas_call x1, Pallas kernels, body(): pl.pallas_call(prepare, in_specs=[SM] + [HB] * 7, out_specs=[VM] * 8, out...  1.31 us
  transfers between devices with their start and end apart: 6, of which 4 were waited for; matrix products, arithmetic and copies ran while one was open for 0% of the time, Pallas kernels for 8%

profile of v7, /device:TPU:0, one launch (start us, length us, event | category | flops | bytes accessed | tf_op | source)
XLA Modules:
  0.0 44.2 jit_solution(2651007032850145772)
XLA Ops:
  0.6 0.9 %first_edges.1.after = f32[8,2240]{1,0:T(8,128)S(1)} custom-call(s32[1]{0:T(128)} %bitcast.parity, f32[32,2240]{1,0:T(8,128)} %source_h.1, s32[32,2240]{1,0:T(8,128)} %bottom_h.1), custom_call_target="tpu_custom_call" | custom-call | tf_op jit(solution)/shard_map/first_edges/pallas_call | solution.py:374
  1.6 5.5 %collective-permute-start.1 = (f32[8,2240]{1,0:T(8,128)S(1)}, f32[8,2240]{1,0:T(8,128)S(1)}, u32[]{:S(2)}, u32[]{:S(2)}) collective-permute-start(f32[8,2240]{1,0:T(8,128)S(1)} %first_edges.1.after), channel_id=1, source_target_pairs={{0,15},{1,2},{2,1},{3,4},{4,3},{5,6},{6,5},{7,8},{8,7},{9,10},{10,... | collective-permute-start | bytes 215048 | tf_op jit(solution)/shard_map/ppermute | solution.py:357
  7.1 1.3 %prepare.1 = (f32[8,2240]{1,0:T(8,128)S(1)}, f32[32,2240]{1,0:T(8,128)S(1)}, f32[32,2240]{1,0:T(8,128)S(1)}, f32[32,2240]{1,0:T(8,128)S(1)}, f32[32,2240]{1,0:T(...) custom-call(s32[1]{0:T(128)} %bitcast.parity, ...), custom_call_target="tpu_custom_call" | custom-call | flops 1000000 | bytes 7000000 | tf_op jit(solution)/shard_map/prepare/pallas_call | solution.py:386
  8.4 0.1 collective-permute-start
  8.5 0.6 %collective-permute-done.1.outer_in = f32[8,2240]{1,0:T(8,128)S(1)} collective-permute-done((f32[8,2240]{1,0:T(8,128)S(1)}, f32[8,2240]{1,0:T(8,128)S(1)}, u32[]{:S(2)}, u32[]{:S(2)}) %collective-permute-start.1) | collective-permute-done | bytes 71712 | tf_op jit(solution)/shard_map/ppermute | solution.py:357
  9.1 0.6 %collective-permute-done.inner_in = f32[8,2240]{1,0:T(8,128)S(1)} collective-permute-done((f32[8,2240]{1,0:T(8,128)S(1)}, f32[8,2240]{1,0:T(8,128)S(1)}, u32[]{:S(2)}, u32[]{:S(2)}) %collective-permute-start) | collective-permute-done | bytes 71712 | tf_op jit(solution)/shard_map/ppermute | solution.py:357
  9.7 1.6 %first_solve.1 = (f32[48,2240]{1,0:T(8,128)S(1)}, f32[468,128]{1,0:T(8,128)S(1)}, f32[468,128]{1,0:T(8,128)S(1)}) custom-call(s32[1]{0:T(128)} %bitcast.parity, f32[8,2240]{1,0:T(8,128)S(1)} %collective-permute-done.inner_in, f32[8,2240]{1,0:T(8,128)S(1)} %collective-permute-done.1.outer_in, f32[32,2240]{1,0:T(8,128)S(1)} %get-tuple-element.27.masked, ...), custom_call_target="tpu_custom_call" | custom-call | tf_op jit(solution)/shard_map/first_solve/pallas_call | solution.py:405
  11.3 0.2 collective-permute-start.2
  11.5 3.8 %collective-permute-start.3 = (f32[468,128]{1,0:T(8,128)S(1)}, f32[468,128]{1,0:T(8,128)S(1)}, u32[]{:S(2)}, u32[]{:S(2)}) collective-permute-start(f32[468,128]{1,0:T(8,128)S(1)} %get-tuple-element.33), channel_id=1, source_target_pairs={{0,15},{1,2},{2,1},{3,4},{4,3},{5,6},{6,5},{7,8},{8,7},{9,10},{10,... | collective-permute-start | bytes 718856 | tf_op jit(solution)/shard_map/ppermute | solution.py:357
  15.3 2.0 %absorb.1 = (f32[6,32,2240]{2,1,0:T(8,128)S(1)}, f32[6,32,2240]{2,1,0:T(8,128)S(1)}) custom-call(f32[48,2240]{1,0:T(8,128)S(1)} %get-tuple-element.34.after.first, f32[6,32,2240]{2,1,0:T(8,128)} %u_h.1, f32[6,32,2240]{2,1,0:T(8,128)} %v_h.1), custom_call_target="tpu_custom_call" | custom-call | flops 1000000 | bytes 7000000 | tf_op jit(solution)/shard_map/absorb/pallas_call | solution.py:417
  17.3 0.0 collective-permute-done.2.inner_in
  17.3 2.6 %collective-permute-done.3.outer_in = f32[468,128]{1,0:T(8,128)S(1)} collective-permute-done((f32[468,128]{1,0:T(8,128)S(1)}, f32[468,128]{1,0:T(8,128)S(1)}, u32[]{:S(2)}, u32[]{:S(2)}) %collective-permute-start.3) | collective-permute-done | bytes 239648 | tf_op jit(solution)/shard_map/ppermute | solution.py:357
  19.9 2.0 %second_solve.1 = (f32[48,2240]{1,0:T(8,128)S(1)}, f32[48,2240]{1,0:T(8,128)S(1)}, f32[48,2240]{1,0:T(8,128)S(1)}, f32[48,2240]{1,0:T(8,128)S(1)}, f32[16,2240]{1,0:T(8,128)S(1)}, /*index=5*/f32[16,2240]{1,0:T(8,128)S(1)}) custom-call(s32[1]{0:T(128)} %bitcast.parity, f32[468,128]{1,0:T(8,128)S(1)} %collective-permute-done.2.inner_in, ...), custom_call_target="tpu_custom_call" | custom-call | tf_op jit(solution)/shard_map/second_solve/pallas_call | solution.py:428
  21.9 0.2 collective-permute-start.4
  22.1 3.6 %collective-permute-start.5 = (f32[16,2240]{1,0:T(8,128)S(1)}, f32[16,2240]{1,0:T(8,128)S(1)}, u32[]{:S(2)}, u32[]{:S(2)}) collective-permute-start(f32[16,2240]{1,0:T(8,128)S(1)} %get-tuple-element.38), channel_id=1, source_target_pairs={{0,15},{1,2},{2,1},{3,4},{4,3},{5,6},{6,5},{7,8},{8,7},{9,10},{10,... | collective-permute-start | bytes 430088 | tf_op jit(solution)/shard_map/ppermute | solution.py:357
  25.7 0.0 collective-permute-done.4.inner_in
  25.7 3.7 %collective-permute-done.5.outer_in = f32[16,2240]{1,0:T(8,128)S(1)} collective-permute-done((f32[16,2240]{1,0:T(8,128)S(1)}, f32[16,2240]{1,0:T(8,128)S(1)}, u32[]{:S(2)}, u32[]{:S(2)}) %collective-permute-start.5) | collective-permute-done | bytes 143392 | tf_op jit(solution)/shard_map/ppermute | solution.py:357
  29.4 0.6 %sums.1 = (f32[48,2240]{1,0:T(8,128)S(1)}, f32[16,2240]{1,0:T(8,128)S(1)}, f32[16,1,128]{2,1,0:T(1,128)S(1)}) custom-call(s32[1]{0:T(128)} %bitcast.parity, f32[16,2240]{1,0:T(8,128)S(1)} %collective-permute-done.4.inner_in, f32[16,2240]{1,0:T(8,128)S(1)} %collective-permute-done.5.outer_in, f32[48,2240]{1,0:T(8,128)S(1)} %get-tuple-element.39.second, ...), custom_call_target="tpu_custom_call" | custom-call | tf_op jit(solution)/shard_map/sums/pallas_call | solution.py:439
  30.0 11.2 %all_to_all.5.came = f32[16,1,128]{2,1,0:T(1,128)S(1)} all-to-all(f32[16,1,128]{2,1,0:T(1,128)S(1)} %get-tuple-element.44), channel_id=1, replica_groups=mesh['members'=2,'lon'=16] {'lon'}, dimensions={0} | all-to-all | bytes 16384 | tf_op jit(solution)/shard_map/all_to_all | solution.py:448
  41.2 3.0 %finish.1 = (f32[32,2240]{1,0:T(8,128)}, f32[6,32,2240]{2,1,0:T(8,128)}, f32[6,32,2240]{2,1,0:T(8,128)}, f32[6,32,2240]{2,1,0:T(8,128)}) custom-call(f32[16,1,128]{2,1,0:T(1,128)S(1)} %all_to_all.5.came, f32[48,2240]{1,0:T(8,128)S(1)} %get-tuple-element.40.z, f32[48,2240]{1,0:T(8,128)S(1)} %get-tuple-element.45.w, f32[16,2240]{1,0:T(8,128)S(1)} %get-tuple-element.46.edges, ...), custom_call_target="tpu_custom_call" | custom-call | tf_op jit(solution)/shard_map/finish/pallas_call | solution.py:450
Async XLA Ops:
  1.6 7.5 %collective-permute-start.1 = (f32[8,2240]{1,0:T(8,128)S(1)}, f32[8,2240]{1,0:T(8,128)S(1)}, u32[]{:S(2)}, u32[]{:S(2)}) collective-permute-start(f32[8,2240]{1,0:T(8,128)S(1)} %first_edges.1.after), channel_id=1, source_target_pairs={{0,15},{1,2},{2,1},{3,4},{4,3},{5,6},{6,5},{7,8},{8,7},{9,10},{10,... | collective-permute-start | bytes 215048 | tf_op jit(solution)/shard_map/ppermute | solution.py:357
  8.4 1.3 %collective-permute-start = (f32[8,2240]{1,0:T(8,128)S(1)}, f32[8,2240]{1,0:T(8,128)S(1)}, u32[]{:S(2)}, u32[]{:S(2)}) collective-permute-start(f32[8,2240]{1,0:T(8,128)S(1)} %get-tuple-element.26), channel_id=1, source_target_pairs={{0,1},{1,0},{2,3},{3,2},{4,5},{5,4},{6,7},{7,6},{8,9},{9,8},{10,11... | collective-permute-start | bytes 215048 | tf_op jit(solution)/shard_map/ppermute | solution.py:357
  11.3 6.0 %collective-permute-start.2 = (f32[468,128]{1,0:T(8,128)S(1)}, f32[468,128]{1,0:T(8,128)S(1)}, u32[]{:S(2)}, u32[]{:S(2)}) collective-permute-start(f32[468,128]{1,0:T(8,128)S(1)} %get-tuple-element.32), channel_id=1, source_target_pairs={{0,1},{1,0},{2,3},{3,2},{4,5},{5,4},{6,7},{7,6},{8,9},{9,8},{10,11... | collective-permute-start | bytes 718856 | tf_op jit(solution)/shard_map/ppermute | solution.py:357
  11.5 8.4 %collective-permute-start.3 = (f32[468,128]{1,0:T(8,128)S(1)}, f32[468,128]{1,0:T(8,128)S(1)}, u32[]{:S(2)}, u32[]{:S(2)}) collective-permute-start(f32[468,128]{1,0:T(8,128)S(1)} %get-tuple-element.33), channel_id=1, source_target_pairs={{0,15},{1,2},{2,1},{3,4},{4,3},{5,6},{6,5},{7,8},{8,7},{9,10},{10,... | collective-permute-start | bytes 718856 | tf_op jit(solution)/shard_map/ppermute | solution.py:357
  21.9 3.8 %collective-permute-start.4 = (f32[16,2240]{1,0:T(8,128)S(1)}, f32[16,2240]{1,0:T(8,128)S(1)}, u32[]{:S(2)}, u32[]{:S(2)}) collective-permute-start(f32[16,2240]{1,0:T(8,128)S(1)} %get-tuple-element.37), channel_id=1, source_target_pairs={{0,1},{1,0},{2,3},{3,2},{4,5},{5,4},{6,7},{7,6},{8,9},{9,8},{10,11... | collective-permute-start | bytes 430088 | tf_op jit(solution)/shard_map/ppermute | solution.py:357
  22.1 7.3 %collective-permute-start.5 = (f32[16,2240]{1,0:T(8,128)S(1)}, f32[16,2240]{1,0:T(8,128)S(1)}, u32[]{:S(2)}, u32[]{:S(2)}) collective-permute-start(f32[16,2240]{1,0:T(8,128)S(1)} %get-tuple-element.38), channel_id=1, source_target_pairs={{0,15},{1,2},{2,1},{3,4},{4,3},{5,6},{6,5},{7,8},{8,7},{9,10},{10,... | collective-permute-start | bytes 430088 | tf_op jit(solution)/shard_map/ppermute | solution.py:357

commit v8 on v7

--- a/solution.py
+++ b/solution.py
@@ -13,6 +13,7 @@
 OV = 8
 KL = 6
 LANE = 128
+FAR = 24
 
 tile_shift = 0.1
 gravity_step = 0.5
@@ -164,26 +165,36 @@
     outer[...] = jnp.where(depth[...] > 0, rows[...], 0.0)
 
 
-def prepare(parity, after, source_h, diagonal_h, bottom_h, *refs):
-    tables_h, (inner, masked, coef, depth, source), held = refs[:3], refs[3:8], refs[8:11]
-    diagonal, bottom, sems = refs[11:]
+def prepare(parity, after, source_h, diagonal_h, bottom_h, u_h, *refs):
+    tables_h, (inner, far_inner, far_outer, masked, coef, depth, source), held = refs[:3], refs[3:10], refs[10:13]
+    diagonal, bottom, u_strip, sems = refs[13:]
+    cells, lat = source.shape
     pairs = [(source_h, source), (bottom_h, bottom), (diagonal_h, diagonal)]
+    pairs += [(u_h.at[:, pl.ds(cells - OV, OV)], u_strip)]
     pairs += list(zip(tables_h, held))
     copies = [pltpu.make_async_copy(a, b, sems.at[i]) for i, (a, b) in enumerate(pairs)]
     for copy in copies:
         copy.start()
-    for copy in copies[:3]:
+    for copy in copies[:4]:
         copy.wait()
     wet = bottom[...] > 0
     masked[...] = jnp.where(wet, source[...], 0.0)
     coef[...] = jnp.where(wet, 4.0 + diagonal[...], 0.0)
     depth[...] = bottom[...].astype(F32)
-    inner[...] = pick(parity, masked[:OV], masked[source.shape[0] - OV :])[0]
-    for copy in copies[3:]:
+    edge = OV + 1
+    blank = jnp.zeros((2 * OV - edge - 1, lat), F32)
+    to_west = jnp.concatenate([coef[:edge], blank, depth[:1]], axis=0)
+    u_rows = [u_strip[level, OV - 1 : OV] for level in range(KL)]
+    to_east = jnp.concatenate(u_rows + [depth[cells - 1 :], coef[cells - edge :]], axis=0)
+    far_outer[: 2 * OV], far_inner[: 2 * OV] = pick(parity, to_east, to_west)
+    for message in (far_outer, far_inner):
+        message[2 * OV :] = jnp.zeros((FAR - 2 * OV, lat), F32)
+    inner[...] = pick(parity, masked[:OV], masked[cells - OV :])[0]
+    for copy in copies[4:]:
         copy.wait()
 
 
-def first_solve(parity, inner_in, outer_in, masked, coef, lat_basis, lon, scale,
+def first_solve(parity, inner_in, outer_in, masked, lat_basis, lon, scale,
                 first, inner, outer, wide, rows, spectral):
     cells, lat = masked.shape
     west, east = pick(parity, inner_in[...], outer_in[...])
@@ -192,44 +203,42 @@
     wide[OV + cells :, :lat] = east
     wide[:, lat:] = jnp.zeros((cells + 2 * OV, wide.shape[1] - lat), F32)
     tile_solve(wide, lat_basis, lon, scale, rows, spectral, first)
-    reach, edge = 2 * OV + 1, OV + 1
-    to_west = jnp.concatenate([first[:reach], coef[:edge]], axis=0)
-    to_east = jnp.concatenate([first[cells - 1 :], coef[cells - edge :]], axis=0)
-    to_outer, to_inner = pick(parity, to_east, to_west)
+    to_outer, to_inner = pick(parity, first[cells - 1 :], first[: 2 * OV + 1])
     pack(inner, to_inner)
     pack(outer, to_outer)
 
 
-def absorb(after, u_h, v_h, u, v, sems):
+def absorb(parity, after, inner_in, outer_in, coef, u_h, v_h, c_rows, edges, u, v, sems):
+    cells, lat = coef.shape
     copies = [pltpu.make_async_copy(a, b, sems.at[i]) for i, (a, b) in enumerate([(u_h, u), (v_h, v)])]
     for copy in copies:
         copy.start()
+    west, east = pick(parity, inner_in[: 2 * OV], outer_in[: 2 * OV])
+    edges[:OV] = west[:OV]
+    edges[OV:] = east[OV:]
+    c_rows[: 2 * OV] = west
+    c_rows[: OV - 1] = jnp.zeros((OV - 1, lat), F32)
+    c_rows[2 * OV : 2 * OV + cells] = coef[...]
+    c_rows[2 * OV + cells :] = east
+    c_rows[3 * OV + cells + 1 :] = jnp.zeros((OV - 1, lat), F32)
     for copy in copies:
         copy.wait()
 
 
-def second_solve(parity, inner_in, outer_in, first, coef_own, depth, u, lat_basis, lon, scale,
-                 z, y, coef, second, inner, outer, wide, rows, spectral, m_rows, c_rows):
-    cells, lat = coef_own.shape
-    span = cells + 2 * OV
-    reach, edge = 2 * OV + 1, OV + 1
-    west, east = pick(
-        parity, unpack(inner_in, reach + edge, lat), unpack(outer_in, reach + edge, lat)
-    )
-    c_rows[:OV] = jnp.zeros((OV, lat), F32)
-    c_rows[OV - 1 : 2 * OV] = west[reach:]
-    c_rows[2 * OV : 2 * OV + cells] = coef_own[...]
-    c_rows[2 * OV + cells + OV :] = jnp.zeros((OV, lat), F32)
-    c_rows[2 * OV + cells : 2 * OV + cells + edge] = east[reach:]
+def second_solve(parity, inner_in, outer_in, first, c_rows, lat_basis, lon, scale,
+                 z, y, second, inner, outer, wide, rows, spectral, m_rows):
+    span, lat = first.shape
+    cells = span - 2 * OV
+    reach = 2 * OV + 1
+    west, east = pick(parity, unpack(inner_in, reach, lat), unpack(outer_in, reach, lat))
     m_rows[:OV] = jnp.zeros((OV, lat), F32)
     m_rows[OV : OV + span] = first[...]
     m_rows[OV + span :] = jnp.zeros((OV, lat), F32)
-    m_rows[OV - 1 : OV - 1 + reach] += west[:reach]
-    m_rows[OV + cells : OV + cells + reach] += east[:reach]
+    m_rows[OV - 1 : OV - 1 + reach] += west
+    m_rows[OV + cells : OV + cells + reach] += east
     m_rows[...] = jnp.where(c_rows[...] > 0, m_rows[...], 0.0)
     inside = slice(OV, OV + span)
     c, m = c_rows[inside], m_rows[inside]
-    coef[...] = c
     z[...] = m
     beside = m_rows[OV - 1 : OV - 1 + span] + m_rows[OV + 1 : OV + 1 + span]
     image = jnp.where(c > 0, c * m - (beside + lat_beside(m)), 0.0)
@@ -237,23 +246,20 @@
     wide[:, :lat] = image
     wide[:, lat:] = jnp.zeros((span, wide.shape[1] - lat), F32)
     tile_solve(wide, lat_basis, lon, scale, rows, spectral, second)
-    to_west = jnp.concatenate([second[:edge], depth[:1], jnp.zeros((KL, lat), F32)], axis=0)
-    u_rows = [u[level, cells - 1 : cells] for level in range(KL)]
-    to_east = jnp.concatenate([second[span - edge :], depth[cells - 1 :]] + u_rows, axis=0)
-    outer[...], inner[...] = pick(parity, to_east, to_west)
-
-
-def sums(parity, inner_in, outer_in, second, z, y, coef, source, w, edges, sent):
+    to_outer, to_inner = pick(parity, second[span - OV - 1 :], second[: OV + 1])
+    pack(inner, to_inner)
+    pack(outer, to_outer)
+
+
+def sums(parity, inner_in, outer_in, second, z, y, c_rows, source, w, sent):
     cells, lat = source.shape
-    west, east = pick(parity, inner_in[...], outer_in[...])
-    edges[:OV] = west[OV:]
-    edges[OV:] = east[OV:]
+    west, east = pick(parity, unpack(inner_in, OV + 1, lat), unpack(outer_in, OV + 1, lat))
     w[...] = second[...]
-    w[OV - 1 : 2 * OV] += west[: OV + 1]
-    w[cells : cells + OV + 1] += east[: OV + 1]
-    w[...] = jnp.where(coef[...] > 0, w[...], 0.0)
+    w[OV - 1 : 2 * OV] += west
+    w[cells : cells + OV + 1] += east
+    w[...] = jnp.where(c_rows[OV : 3 * OV + cells] > 0, w[...], 0.0)
     own = slice(OV, OV + cells)
-    c, m = coef[own], w[own]
+    c, m = c_rows[2 * OV : 2 * OV + cells], w[own]
     wet = c > 0
     beside = w[OV - 1 : OV - 1 + cells] + w[OV + 1 : OV + 1 + cells]
     x = jnp.where(wet, c * m - (beside + lat_beside(m)), 0.0)
@@ -302,9 +308,9 @@
     of_land = jnp.broadcast_to(step0 + step1 * (rest + beta), (OV, lat))
 
     copies = []
-    d_rows[:OV] = jnp.broadcast_to(edges[1:2], (OV, lat))
+    d_rows[:OV] = jnp.broadcast_to(edges[KL : KL + 1], (OV, lat))
     d_rows[OV : OV + cells] = depth[...]
-    d_rows[OV + cells :] = jnp.broadcast_to(edges[OV + 1 : OV + 2], (OV, lat))
+    d_rows[OV + cells :] = jnp.broadcast_to(edges[2 * OV - 1 :], (OV, lat))
     for at in range(0, cells + 2 * OV, OV):
         s = of_z * z[at : at + OV] + of_w * w[at : at + OV]
         if OV <= at < OV + cells:
@@ -319,7 +325,7 @@
     s_first = s_rows[OV : OV + 1]
     d_west = jnp.minimum(d_rows[OV - 1 : OV], d_rows[OV : OV + 1])
     for level in range(KL):
-        left = edges[level + 2 : level + 3] - gravity_step * (s_first - s_west)
+        left = edges[level : level + 1] - gravity_step * (s_first - s_west)
         u_rows[level, :OV] = jnp.broadcast_to(jnp.where(d_west > level, left, 0.0), (OV, lat))
     zero = jnp.zeros((OV, 1), F32)
     for block in range(cells // OV):
@@ -383,68 +389,70 @@
     )(parity, hbm["source"], hbm["bottom"])
     outer_in = swap_pairs(outer, True)
 
-    inner, masked, coef_own, depth, source_v, *held = pl.pallas_call(
+    inner, far_inner, far_outer, masked, coef, depth, source_v, *held = pl.pallas_call(
         prepare,
-        in_specs=[SM] + [HB] * 7,
-        out_specs=[VM] * 8,
+        in_specs=[SM] + [HB] * 8,
+        out_specs=[VM] * 10,
         out_shape=[pltpu.VMEM((OV, lat), F32)]
+        + [pltpu.VMEM((FAR, lat), F32)] * 2
         + [pltpu.VMEM((cells, lat), F32)] * 4
         + [pltpu.VMEM(table.shape, table.dtype) for table in consts],
         scratch_shapes=[
             pltpu.VMEM((cells, lat), F32),
             pltpu.VMEM((cells, lat), jnp.int32),
-            pltpu.SemaphoreType.DMA((6,)),
+            pltpu.VMEM((KL, OV, lat), F32),
+            pltpu.SemaphoreType.DMA((7,)),
         ],
         compiler_params=PARAMS,
         cost_estimate=pl.CostEstimate(flops=10**6, bytes_accessed=7 * 10**6, transcendentals=0),
         name="prepare",
-    )(parity, outer, hbm["source"], hbm["diagonal"], hbm["bottom"], *consts)
+    )(parity, outer, hbm["source"], hbm["diagonal"], hbm["bottom"], hbm["u"], *consts)
     near = swap_pairs(inner, False), outer_in
+    far = swap_pairs(far_inner, False), swap_pairs(far_outer, True)
 
     blocks = -(-lat // LANE)
     first, inner, outer = pl.pallas_call(
         first_solve,
-        in_specs=[SM] + [VM] * 7,
+        in_specs=[SM] + [VM] * 6,
         out_specs=[VM] * 3,
-        out_shape=[pltpu.VMEM((span, lat), F32)]
-        + [pltpu.VMEM(((3 * OV + 2) * blocks, LANE), F32)] * 2,
+        out_shape=[pltpu.VMEM((span, lat), F32)] + [pltpu.VMEM(((2 * OV + 1) * blocks, LANE), F32)] * 2,
         scratch_shapes=solve_scratch(span, lat),
         compiler_params=PARAMS,
         name="first_solve",
-    )(parity, *near, masked, coef_own, *held)
+    )(parity, *near, masked, *held)
     near = swap_pairs(inner, False), swap_pairs(outer, True)
 
-    u_v, v_v = pl.pallas_call(
+    c_rows, edges, u_v, v_v = pl.pallas_call(
         absorb,
-        in_specs=[HB] * 3,
-        out_specs=[VM] * 2,
-        out_shape=[pltpu.VMEM((KL, cells, lat), F32)] * 2,
+        in_specs=[SM, HB] + [VM] * 3 + [HB] * 2,
+        out_specs=[VM] * 4,
+        out_shape=[pltpu.VMEM((span + 2 * OV, lat), F32), pltpu.VMEM((2 * OV, lat), F32)]
+        + [pltpu.VMEM((KL, cells, lat), F32)] * 2,
         scratch_shapes=[pltpu.SemaphoreType.DMA((2,))],
         compiler_params=PARAMS,
         cost_estimate=pl.CostEstimate(flops=10**6, bytes_accessed=7 * 10**6, transcendentals=0),
         name="absorb",
-    )(first, hbm["u"], hbm["v"])
-
-    z, y, coef, second, inner, outer = pl.pallas_call(
+    )(parity, first, *far, coef, hbm["u"], hbm["v"])
+
+    z, y, second, inner, outer = pl.pallas_call(
         second_solve,
-        in_specs=[SM] + [VM] * 9,
-        out_specs=[VM] * 6,
-        out_shape=[pltpu.VMEM((span, lat), F32)] * 4 + [pltpu.VMEM((2 * OV, lat), F32)] * 2,
-        scratch_shapes=solve_scratch(span, lat) + [pltpu.VMEM((span + 2 * OV, lat), F32)] * 2,
+        in_specs=[SM] + [VM] * 7,
+        out_specs=[VM] * 5,
+        out_shape=[pltpu.VMEM((span, lat), F32)] * 3 + [pltpu.VMEM(((OV + 1) * blocks, LANE), F32)] * 2,
+        scratch_shapes=solve_scratch(span, lat) + [pltpu.VMEM((span + 2 * OV, lat), F32)],
         compiler_params=PARAMS,
         name="second_solve",
-    )(parity, *near, first, coef_own, depth, u_v, *held)
+    )(parity, *near, first, c_rows, *held)
     near = swap_pairs(inner, False), swap_pairs(outer, True)
 
-    w, edges, sent = pl.pallas_call(
+    w, sent = pl.pallas_call(
         sums,
         in_specs=[SM] + [VM] * 7,
-        out_specs=[VM] * 3,
-        out_shape=[pltpu.VMEM((span, lat), F32), pltpu.VMEM((2 * OV, lat), F32),
-                   pltpu.VMEM((devices, 1, LANE), F32)],
+        out_specs=[VM] * 2,
+        out_shape=[pltpu.VMEM((span, lat), F32), pltpu.VMEM((devices, 1, LANE), F32)],
         compiler_params=PARAMS,
         name="sums",
-    )(parity, *near, second, z, y, coef, source_v)
+    )(parity, *near, second, z, y, c_rows, source_v)
     came = lax.all_to_all(sent, "lon", 0, 0)
 
     return pl.pallas_call(

time: 44.4 us -> 42.9 us (0.966)
  blocking collectives: 11.2 us -> 9.97 us
  waiting for transfers between devices: 7.52 us -> 6.65 us
    all_to_all x1, blocking collectives: 11.2 us -> 9.97 us  [body(): came = lax.all_to_all(sent, 'lon', 0, 0)]
    ppermute x6 -> x8, waiting for transfers between devices: 7.52 us -> 6.65 us  [swap_pairs(): return lax.ppermute(block, 'lon', route)]
    ppermute x6 -> x8, starting transfers between devices: 13.3 us -> 13.7 us  [swap_pairs(): return lax.ppermute(block, 'lon', route)]
  transfers between devices with their start and end apart: 6 -> 8, of which waited for: 4 -> 3; matrix products, arithmetic and copies ran while one was open for 0% -> 0% of each run, Pallas kernels for 8% -> 12%
where the time goes in v8:
time: 42.9 us; the launch traced here: 42.7 us
  starting transfers between devices  13.7 us (32%)
  Pallas kernels  11.7 us (27%)
  blocking collectives  9.97 us (23%)
  waiting for transfers between devices  6.65 us (16%)
  between operations  0.71 us (2%)
    ppermute x8, starting transfers between devices, swap_pairs(): return lax.ppermute(block, 'lon', route)  13.7 us
    all_to_all x1, blocking collectives, body(): came = lax.all_to_all(sent, 'lon', 0, 0)  9.97 us
    ppermute x8, waiting for transfers between devices, swap_pairs(): return lax.ppermute(block, 'lon', route)  6.65 us
    pallas_call x1, Pallas kernels, body(): pl.pallas_call(finish, in_specs=[VM] * 8, out_specs=[HB] * 4, out_shape=[...  3 us
    pallas_call x1, Pallas kernels, body(): pl.pallas_call(absorb, in_specs=[SM, HB] + [VM] * 3 + [HB] * 2, out_specs...  2.03 us
    pallas_call x1, Pallas kernels, body(): pl.pallas_call(second_solve, in_specs=[SM] + [VM] * 7, out_specs=[VM] * 5...  1.92 us
    pallas_call x1, Pallas kernels, body(): pl.pallas_call(first_solve, in_specs=[SM] + [VM] * 6, out_specs=[VM] * 3,...  1.59 us
    pallas_call x1, Pallas kernels, body(): pl.pallas_call(prepare, in_specs=[SM] + [HB] * 8, out_specs=[VM] * 10, ou...  1.53 us
  transfers between devices with their start and end apart: 8, of which 3 were waited for; matrix products, arithmetic and copies ran while one was open for 0% of the time, Pallas kernels for 12%

profile of v8, /device:TPU:0, one launch (start us, length us, event | category | flops | bytes accessed | tf_op | source)
XLA Modules:
  0.0 42.7 jit_solution(2883351608821207082)
XLA Ops:
  0.6 0.9 %first_edges.1.after = f32[8,2240]{1,0:T(8,128)S(1)} custom-call(s32[1]{0:T(128)} %bitcast.parity, f32[32,2240]{1,0:T(8,128)} %source_h.1, s32[32,2240]{1,0:T(8,128)} %bottom_h.1), custom_call_target="tpu_custom_call" | custom-call | tf_op jit(solution)/shard_map/first_edges/pallas_call | solution.py:380
  1.6 5.5 %collective-permute-start.1 = (f32[8,2240]{1,0:T(8,128)S(1)}, f32[8,2240]{1,0:T(8,128)S(1)}, u32[]{:S(2)}, u32[]{:S(2)}) collective-permute-start(f32[8,2240]{1,0:T(8,128)S(1)} %first_edges.1.after), channel_id=1, source_target_pairs={{0,15},{1,2},{2,1},{3,4},{4,3},{5,6},{6,5},{7,8},{8,7},{9,10},{10,... | collective-permute-start | bytes 215048 | tf_op jit(solution)/shard_map/ppermute | solution.py:363
  7.1 1.5 %prepare.1 = (f32[8,2240]{1,0:T(8,128)S(1)}, f32[24,2240]{1,0:T(8,128)S(1)}, f32[24,2240]{1,0:T(8,128)S(1)}, f32[32,2240]{1,0:T(8,128)S(1)}, f32[32,2240]{1,0:T(...) custom-call(s32[1]{0:T(128)} %bitcast.parity, ...), custom_call_target="tpu_custom_call" | custom-call | flops 1000000 | bytes 7000000 | tf_op jit(solution)/shard_map/prepare/pallas_call | solution.py:392
  8.6 0.1 collective-permute-start
  8.7 0.5 %collective-permute-start.4 = (f32[24,2240]{1,0:T(8,128)S(1)}, f32[24,2240]{1,0:T(8,128)S(1)}, u32[]{:S(2)}, u32[]{:S(2)}) collective-permute-start(f32[24,2240]{1,0:T(8,128)S(1)} %get-tuple-element.36), channel_id=1, source_target_pairs={{0,1},{1,0},{2,3},{3,2},{4,5},{5,4},{6,7},{7,6},{8,9},{9,8},{10,11... | collective-permute-start | bytes 645128 | tf_op jit(solution)/shard_map/ppermute | solution.py:363
  9.2 0.3 collective-permute-start.5
  9.5 0.0 collective-permute-done.1.outer_in
  9.5 0.5 %collective-permute-done.inner_in = f32[8,2240]{1,0:T(8,128)S(1)} collective-permute-done((f32[8,2240]{1,0:T(8,128)S(1)}, f32[8,2240]{1,0:T(8,128)S(1)}, u32[]{:S(2)}, u32[]{:S(2)}) %collective-permute-start) | collective-permute-done | bytes 71712 | tf_op jit(solution)/shard_map/ppermute | solution.py:363
  10.0 1.6 %first_solve.1 = (f32[48,2240]{1,0:T(8,128)S(1)}, f32[306,128]{1,0:T(8,128)S(1)}, f32[306,128]{1,0:T(8,128)S(1)}) custom-call(s32[1]{0:T(128)} %bitcast.parity, f32[8,2240]{1,0:T(8,128)S(1)} %collective-permute-done.inner_in, f32[8,2240]{1,0:T(8,128)S(1)} %collective-permute-done.1.outer_in, f32[32,2240]{1,0:T(8,128)S(1)} %get-tuple-element.29.masked, ...), custom_call_target="tpu_custom_call" | custom-call | tf_op jit(solution)/shard_map/first_solve/pallas_call | solution.py:414
  11.5 0.2 collective-permute-start.2
  11.8 3.6 %collective-permute-start.3 = (f32[306,128]{1,0:T(8,128)S(1)}, f32[306,128]{1,0:T(8,128)S(1)}, u32[]{:S(2)}, u32[]{:S(2)}) collective-permute-start(f32[306,128]{1,0:T(8,128)S(1)} %get-tuple-element.34), channel_id=1, source_target_pairs={{0,15},{1,2},{2,1},{3,4},{4,3},{5,6},{6,5},{7,8},{8,7},{9,10},{10,... | collective-permute-start | bytes 470024 | tf_op jit(solution)/shard_map/ppermute | solution.py:363
  15.4 0.0 collective-permute-done.4.inner_in
  15.4 1.9 %collective-permute-done.5.outer_in = f32[24,2240]{1,0:T(8,128)S(1)} collective-permute-done((f32[24,2240]{1,0:T(8,128)S(1)}, f32[24,2240]{1,0:T(8,128)S(1)}, u32[]{:S(2)}, u32[]{:S(2)}) %collective-permute-start.5) | collective-permute-done | bytes 215072 | tf_op jit(solution)/shard_map/ppermute | solution.py:363
  17.4 2.0 %absorb.1 = (f32[64,2240]{1,0:T(8,128)S(1)}, f32[16,2240]{1,0:T(8,128)S(1)}, f32[6,32,2240]{2,1,0:T(8,128)S(1)}, f32[6,32,2240]{2,1,0:T(8,128)S(1)}) custom-call(s32[1]{0:T(128)} %bitcast.parity, f32[48,2240]{1,0:T(8,128)S(1)} %get-tuple-element.35.after.first, f32[24,2240]{1,0:T(8,128)S(1)} %collective-permute-done.4.inner_in, ...), custom_call_target="tpu_custom_call" | custom-call | flops 1000000 | bytes 7000000 | tf_op jit(solution)/shard_map/absorb/pallas_call | solution.py:425
  19.4 0.0 collective-permute-done.2.inner_in
  19.4 0.0 collective-permute-done.3.outer_in
  19.4 1.9 %second_solve.1 = (f32[48,2240]{1,0:T(8,128)S(1)}, f32[48,2240]{1,0:T(8,128)S(1)}, f32[48,2240]{1,0:T(8,128)S(1)}, f32[162,128]{1,0:T(8,128)S(1)}, f32[162,128]{1,0:T(8,128)S(1)}) custom-call(s32[1]{0:T(128)} %bitcast.parity, f32[306,128]{1,0:T(8,128)S(1)} %collective-permute-done.2.inner_in, f32[306,128]{1,0:T(8,128)S(1)} %collective-permute-done.3.outer_in, ...), custom_call_target="tpu_custom_call" | custom-call | tf_op jit(solution)/shard_map/second_solve/pallas_call | solution.py:437
  21.3 1.1 %collective-permute-start.6 = (f32[162,128]{1,0:T(8,128)S(1)}, f32[162,128]{1,0:T(8,128)S(1)}, u32[]{:S(2)}, u32[]{:S(2)}) collective-permute-start(f32[162,128]{1,0:T(8,128)S(1)} %get-tuple-element.40), channel_id=1, source_target_pairs={{0,1},{1,0},{2,3},{3,2},{4,5},{5,4},{6,7},{7,6},{8,9},{9,8},{10,11... | collective-permute-start | bytes 248840 | tf_op jit(solution)/shard_map/ppermute | solution.py:363
  22.5 2.4 %collective-permute-start.7 = (f32[162,128]{1,0:T(8,128)S(1)}, f32[162,128]{1,0:T(8,128)S(1)}, u32[]{:S(2)}, u32[]{:S(2)}) collective-permute-start(f32[162,128]{1,0:T(8,128)S(1)} %get-tuple-element.41), channel_id=1, source_target_pairs={{0,15},{1,2},{2,1},{3,4},{4,3},{5,6},{6,5},{7,8},{8,7},{9,10},{10,... | collective-permute-start | bytes 248840 | tf_op jit(solution)/shard_map/ppermute | solution.py:363
  24.9 0.0 collective-permute-done.6.inner_in
  24.9 4.2 %collective-permute-done.7.outer_in = f32[162,128]{1,0:T(8,128)S(1)} collective-permute-done((f32[162,128]{1,0:T(8,128)S(1)}, f32[162,128]{1,0:T(8,128)S(1)}, u32[]{:S(2)}, u32[]{:S(2)}) %collective-permute-start.7) | collective-permute-done | bytes 82976 | tf_op jit(solution)/shard_map/ppermute | solution.py:363
  29.1 0.6 %sums.1 = (f32[48,2240]{1,0:T(8,128)S(1)}, f32[16,1,128]{2,1,0:T(1,128)S(1)}) custom-call(s32[1]{0:T(128)} %bitcast.parity, f32[162,128]{1,0:T(8,128)S(1)} %collective-permute-done.6.inner_in, f32[162,128]{1,0:T(8,128)S(1)} %collective-permute-done.7.outer_in, f32[48,2240]{1,0:T(8,128)S(1)} %get-tuple-element.42.second, f32[48,2240]{1,0:T(8,128)S(1)} %get-tuple-element.43.z, ...), custom_call_target="tpu_custom_call" | custom-call | tf_op jit(solution)/shard_map/sums/pallas_call | solution.py:448
  29.7 10.0 %all_to_all.5.came = f32[16,1,128]{2,1,0:T(1,128)S(1)} all-to-all(f32[16,1,128]{2,1,0:T(1,128)S(1)} %get-tuple-element.46), channel_id=1, replica_groups=mesh['members'=2,'lon'=16] {'lon'}, dimensions={0} | all-to-all | bytes 16384 | tf_op jit(solution)/shard_map/all_to_all | solution.py:456
  39.7 3.0 %finish.1 = (f32[32,2240]{1,0:T(8,128)}, f32[6,32,2240]{2,1,0:T(8,128)}, f32[6,32,2240]{2,1,0:T(8,128)}, f32[6,32,2240]{2,1,0:T(8,128)}) custom-call(f32[16,1,128]{2,1,0:T(1,128)S(1)} %all_to_all.5.came, f32[48,2240]{1,0:T(8,128)S(1)} %get-tuple-element.43.z, f32[48,2240]{1,0:T(8,128)S(1)} %get-tuple-element.47.w, f32[16,2240]{1,0:T(8,128)S(1)} %get-tuple-element.48.edges, ...), custom_call_target="tpu_custom_call" | custom-call | tf_op jit(solution)/shard_map/finish/pallas_call | solution.py:458
Async XLA Ops:
  1.6 7.9 %collective-permute-start.1 = (f32[8,2240]{1,0:T(8,128)S(1)}, f32[8,2240]{1,0:T(8,128)S(1)}, u32[]{:S(2)}, u32[]{:S(2)}) collective-permute-start(f32[8,2240]{1,0:T(8,128)S(1)} %first_edges.1.after), channel_id=1, source_target_pairs={{0,15},{1,2},{2,1},{3,4},{4,3},{5,6},{6,5},{7,8},{8,7},{9,10},{10,... | collective-permute-start | bytes 215048 | tf_op jit(solution)/shard_map/ppermute | solution.py:363
  8.6 1.3 %collective-permute-start = (f32[8,2240]{1,0:T(8,128)S(1)}, f32[8,2240]{1,0:T(8,128)S(1)}, u32[]{:S(2)}, u32[]{:S(2)}) collective-permute-start(f32[8,2240]{1,0:T(8,128)S(1)} %get-tuple-element.28), channel_id=1, source_target_pairs={{0,1},{1,0},{2,3},{3,2},{4,5},{5,4},{6,7},{7,6},{8,9},{9,8},{10,11... | collective-permute-start | bytes 215048 | tf_op jit(solution)/shard_map/ppermute | solution.py:363
  8.7 6.7 %collective-permute-start.4 = (f32[24,2240]{1,0:T(8,128)S(1)}, f32[24,2240]{1,0:T(8,128)S(1)}, u32[]{:S(2)}, u32[]{:S(2)}) collective-permute-start(f32[24,2240]{1,0:T(8,128)S(1)} %get-tuple-element.36), channel_id=1, source_target_pairs={{0,1},{1,0},{2,3},{3,2},{4,5},{5,4},{6,7},{7,6},{8,9},{9,8},{10,11... | collective-permute-start | bytes 645128 | tf_op jit(solution)/shard_map/ppermute | solution.py:363
  9.2 8.2 %collective-permute-start.5 = (f32[24,2240]{1,0:T(8,128)S(1)}, f32[24,2240]{1,0:T(8,128)S(1)}, u32[]{:S(2)}, u32[]{:S(2)}) collective-permute-start(f32[24,2240]{1,0:T(8,128)S(1)} %get-tuple-element.37), channel_id=1, source_target_pairs={{0,15},{1,2},{2,1},{3,4},{4,3},{5,6},{6,5},{7,8},{8,7},{9,10},{10,... | collective-permute-start | bytes 645128 | tf_op jit(solution)/shard_map/ppermute | solution.py:363
  11.5 7.8 %collective-permute-start.2 = (f32[306,128]{1,0:T(8,128)S(1)}, f32[306,128]{1,0:T(8,128)S(1)}, u32[]{:S(2)}, u32[]{:S(2)}) collective-permute-start(f32[306,128]{1,0:T(8,128)S(1)} %get-tuple-element.33), channel_id=1, source_target_pairs={{0,1},{1,0},{2,3},{3,2},{4,5},{5,4},{6,7},{7,6},{8,9},{9,8},{10,11... | collective-permute-start | bytes 470024 | tf_op jit(solution)/shard_map/ppermute | solution.py:363
  11.8 7.6 %collective-permute-start.3 = (f32[306,128]{1,0:T(8,128)S(1)}, f32[306,128]{1,0:T(8,128)S(1)}, u32[]{:S(2)}, u32[]{:S(2)}) collective-permute-start(f32[306,128]{1,0:T(8,128)S(1)} %get-tuple-element.34), channel_id=1, source_target_pairs={{0,15},{1,2},{2,1},{3,4},{4,3},{5,6},{6,5},{7,8},{8,7},{9,10},{10,... | collective-permute-start | bytes 470024 | tf_op jit(solution)/shard_map/ppermute | solution.py:363
  21.3 3.5 %collective-permute-start.6 = (f32[162,128]{1,0:T(8,128)S(1)}, f32[162,128]{1,0:T(8,128)S(1)}, u32[]{:S(2)}, u32[]{:S(2)}) collective-permute-start(f32[162,128]{1,0:T(8,128)S(1)} %get-tuple-element.40), channel_id=1, source_target_pairs={{0,1},{1,0},{2,3},{3,2},{4,5},{5,4},{6,7},{7,6},{8,9},{9,8},{10,11... | collective-permute-start | bytes 248840 | tf_op jit(solution)/shard_map/ppermute | solution.py:363
  22.5 6.6 %collective-permute-start.7 = (f32[162,128]{1,0:T(8,128)S(1)}, f32[162,128]{1,0:T(8,128)S(1)}, u32[]{:S(2)}, u32[]{:S(2)}) collective-permute-start(f32[162,128]{1,0:T(8,128)S(1)} %get-tuple-element.41), channel_id=1, source_target_pairs={{0,15},{1,2},{2,1},{3,4},{4,3},{5,6},{6,5},{7,8},{8,7},{9,10},{10,... | collective-permute-start | bytes 248840 | tf_op jit(solution)/shard_map/ppermute | solution.py:363

commit v9 on v8

--- a/solution.py
+++ b/solution.py
@@ -251,7 +251,7 @@
     pack(outer, to_outer)
 
 
-def sums(parity, inner_in, outer_in, second, z, y, c_rows, source, w, sent):
+def sums(parity, inner_in, outer_in, second, z, y, c_rows, source, w, sent, held, sem):
     cells, lat = source.shape
     west, east = pick(parity, unpack(inner_in, OV + 1, lat), unpack(outer_in, OV + 1, lat))
     w[...] = second[...]
@@ -286,12 +286,18 @@
     row = jnp.zeros((1, LANE), F32)
     for i, (a, b) in enumerate(pairs):
         row = jnp.where(lane == i, partial(a, b), row)
-    sent[...] = jnp.broadcast_to(row[None], sent.shape)
-
-
-def finish(came, z, w, edges, source, depth, u_vel, v_vel, solution, u_new, v_new, w_vel,
-           s_rows, d_rows, u_rows, v_out, w_out, s_out, sems):
+    held[...] = row
+    copy = pltpu.make_async_copy(held, sent, sem)
+    copy.start()
+    copy.wait()
+
+
+def finish(came_h, z, w, edges, source, depth, u_vel, v_vel, solution, u_new, v_new, w_vel,
+           s_rows, d_rows, u_rows, v_out, w_out, s_out, came, sems):
     cells, lat = source.shape
+    fetch = pltpu.make_async_copy(came_h, came, sems.at[0])
+    fetch.start()
+    fetch.wait()
     total = jnp.broadcast_to(jnp.sum(came[...], axis=0), (8, LANE))
     place = [lax.broadcasted_iota(jnp.int32, (8, LANE), axis) for axis in range(2)]
     total = jnp.sum(jnp.where(place[0] == place[1], total, 0.0), axis=1, keepdims=True)
@@ -448,22 +454,24 @@
     w, sent = pl.pallas_call(
         sums,
         in_specs=[SM] + [VM] * 7,
-        out_specs=[VM] * 2,
-        out_shape=[pltpu.VMEM((span, lat), F32), pltpu.VMEM((devices, 1, LANE), F32)],
+        out_specs=[VM, HB],
+        out_shape=[pltpu.VMEM((span, lat), F32), pltpu.HBM((1, LANE), F32)],
+        scratch_shapes=[pltpu.VMEM((1, LANE), F32), pltpu.SemaphoreType.DMA],
         compiler_params=PARAMS,
         name="sums",
     )(parity, *near, second, z, y, c_rows, source_v)
-    came = lax.all_to_all(sent, "lon", 0, 0)
+    came = pltpu.with_memory_space_constraint(lax.all_gather(sent, "lon"), pltpu.HBM)
 
     return pl.pallas_call(
         finish,
-        in_specs=[VM] * 8,
+        in_specs=[HB] + [VM] * 7,
         out_specs=[HB] * 4,
         out_shape=[shape(cells, lat)] + [shape(KL, cells, lat)] * 3,
         scratch_shapes=[pltpu.VMEM((span, lat), F32)] * 2
         + [pltpu.VMEM((KL, OV + cells, lat), F32)]
         + [pltpu.VMEM((KL, cells, lat), F32)] * 2
-        + [pltpu.VMEM((cells, lat), F32), pltpu.SemaphoreType.DMA((1 + 3 * (cells // OV),))],
+        + [pltpu.VMEM((cells, lat), F32), pltpu.VMEM((devices, 1, LANE), F32)]
+        + [pltpu.SemaphoreType.DMA((1 + 3 * (cells // OV),))],
         compiler_params=PARAMS,
         name="finish",
     )(came, z, w, edges, source_v, depth, u_v, v_v)

time: 42.9 us -> 51.9 us (1.21)
  blocking collectives: 9.97 us -> 17.8 us
  Pallas kernels: 11.7 us -> 12.9 us
    all_gather x0 -> x1, blocking collectives: none -> 17.8 us  [body(): lax.all_gather(sent, 'lon')]
    all_to_all x1 -> x0, blocking collectives: 9.97 us -> none  [body(): came = lax.all_to_all(sent, 'lon', 0, 0)]
    pallas_call x2, Pallas kernels: 3.63 us -> 4.84 us  [the longest x1 3.68 us: body(): pl.pallas_call(finish, in_specs=[HB] + [VM] * 7, out_specs=[HB] * 4, out_...]
  transfers between devices with their start and end apart: 8 -> 8, of which waited for: 3 -> 3; matrix products, arithmetic and copies ran while one was open for 0% -> 0% of each run, Pallas kernels for 12% -> 10%
where the time goes in v9:
time: 51.9 us; the launch traced here: 51.7 us
  blocking collectives  17.8 us (34%)
  starting transfers between devices  13.7 us (26%)
  Pallas kernels  12.9 us (25%)
  waiting for transfers between devices  6.66 us (13%)
  between operations  0.71 us (1%)
    all_gather x1, blocking collectives, body(): lax.all_gather(sent, 'lon')  17.8 us
    ppermute x8, starting transfers between devices, swap_pairs(): return lax.ppermute(block, 'lon', route)  13.7 us
    ppermute x8, waiting for transfers between devices, swap_pairs(): return lax.ppermute(block, 'lon', route)  6.66 us
    pallas_call x1, Pallas kernels, body(): pl.pallas_call(finish, in_specs=[HB] + [VM] * 7, out_specs=[HB] * 4, out_...  3.68 us
    pallas_call x1, Pallas kernels, body(): pl.pallas_call(absorb, in_specs=[SM, HB] + [VM] * 3 + [HB] * 2, out_specs...  2.03 us
    pallas_call x1, Pallas kernels, body(): pl.pallas_call(second_solve, in_specs=[SM] + [VM] * 7, out_specs=[VM] * 5...  1.92 us
    pallas_call x1, Pallas kernels, body(): pl.pallas_call(first_solve, in_specs=[SM] + [VM] * 6, out_specs=[VM] * 3,...  1.59 us
    pallas_call x1, Pallas kernels, body(): pl.pallas_call(prepare, in_specs=[SM] + [HB] * 8, out_specs=[VM] * 10, ou...  1.53 us
  transfers between devices with their start and end apart: 8, of which 3 were waited for; matrix products, arithmetic and copies ran while one was open for 0% of the time, Pallas kernels for 10%

profile of v9, /device:TPU:0, one launch (start us, length us, event | category | flops | bytes accessed | tf_op | source)
XLA Modules:
  0.0 51.7 jit_solution(8074818721057547547)
XLA Ops:
  0.6 1.0 %first_edges.1.after = f32[8,2240]{1,0:T(8,128)S(1)} custom-call(s32[1]{0:T(128)} %bitcast.parity, f32[32,2240]{1,0:T(8,128)} %source_h.1, s32[32,2240]{1,0:T(8,128)} %bottom_h.1), custom_call_target="tpu_custom_call" | custom-call | tf_op jit(solution)/shard_map/first_edges/pallas_call | solution.py:386
  1.6 5.5 %collective-permute-start.1 = (f32[8,2240]{1,0:T(8,128)S(1)}, f32[8,2240]{1,0:T(8,128)S(1)}, u32[]{:S(2)}, u32[]{:S(2)}) collective-permute-start(f32[8,2240]{1,0:T(8,128)S(1)} %first_edges.1.after), channel_id=1, source_target_pairs={{0,15},{1,2},{2,1},{3,4},{4,3},{5,6},{6,5},{7,8},{8,7},{9,10},{10,... | collective-permute-start | bytes 215048 | tf_op jit(solution)/shard_map/ppermute | solution.py:369
  7.1 1.5 %prepare.1 = (f32[8,2240]{1,0:T(8,128)S(1)}, f32[24,2240]{1,0:T(8,128)S(1)}, f32[24,2240]{1,0:T(8,128)S(1)}, f32[32,2240]{1,0:T(8,128)S(1)}, f32[32,2240]{1,0:T(...) custom-call(s32[1]{0:T(128)} %bitcast.parity, ...), custom_call_target="tpu_custom_call" | custom-call | flops 1000000 | bytes 7000000 | tf_op jit(solution)/shard_map/prepare/pallas_call | solution.py:398
  8.6 0.1 collective-permute-start
  8.7 0.5 collective-permute-start.4
  9.2 0.3 collective-permute-start.5
  9.5 0.0 collective-permute-done.1.outer_in
  9.5 0.5 collective-permute-done.inner_in
  10.0 1.6 %first_solve.1 = (f32[48,2240]{1,0:T(8,128)S(1)}, f32[306,128]{1,0:T(8,128)S(1)}, f32[306,128]{1,0:T(8,128)S(1)}) custom-call(s32[1]{0:T(128)} %bitcast.parity, f32[8,2240]{1,0:T(8,128)S(1)} %collective-permute-done.inner_in, f32[8,2240]{1,0:T(8,128)S(1)} %collective-permute-done.1.outer_in, f32[32,2240]{1,0:T(8,128)S(1)} %get-tuple-element.29.masked, ...), custom_call_target="tpu_custom_call" | custom-call | tf_op jit(solution)/shard_map/first_solve/pallas_call | solution.py:420
  11.5 0.2 collective-permute-start.2
  11.8 3.6 %collective-permute-start.3 = (f32[306,128]{1,0:T(8,128)S(1)}, f32[306,128]{1,0:T(8,128)S(1)}, u32[]{:S(2)}, u32[]{:S(2)}) collective-permute-start(f32[306,128]{1,0:T(8,128)S(1)} %get-tuple-element.34), channel_id=1, source_target_pairs={{0,15},{1,2},{2,1},{3,4},{4,3},{5,6},{6,5},{7,8},{8,7},{9,10},{10,... | collective-permute-start | bytes 470024 | tf_op jit(solution)/shard_map/ppermute | solution.py:369
  15.4 0.0 collective-permute-done.4.inner_in
  15.4 1.9 %collective-permute-done.5.outer_in = f32[24,2240]{1,0:T(8,128)S(1)} collective-permute-done((f32[24,2240]{1,0:T(8,128)S(1)}, f32[24,2240]{1,0:T(8,128)S(1)}, u32[]{:S(2)}, u32[]{:S(2)}) %collective-permute-start.5) | collective-permute-done | bytes 215072 | tf_op jit(solution)/shard_map/ppermute | solution.py:369
  17.4 2.0 %absorb.1 = (f32[64,2240]{1,0:T(8,128)S(1)}, f32[16,2240]{1,0:T(8,128)S(1)}, f32[6,32,2240]{2,1,0:T(8,128)S(1)}, f32[6,32,2240]{2,1,0:T(8,128)S(1)}) custom-call(s32[1]{0:T(128)} %bitcast.parity, f32[48,2240]{1,0:T(8,128)S(1)} %get-tuple-element.35.after.first, f32[24,2240]{1,0:T(8,128)S(1)} %collective-permute-done.4.inner_in, ...), custom_call_target="tpu_custom_call" | custom-call | flops 1000000 | bytes 7000000 | tf_op jit(solution)/shard_map/absorb/pallas_call | solution.py:431
  19.4 0.0 collective-permute-done.2.inner_in
  19.4 0.0 collective-permute-done.3.outer_in
  19.4 1.9 %second_solve.1 = (f32[48,2240]{1,0:T(8,128)S(1)}, f32[48,2240]{1,0:T(8,128)S(1)}, f32[48,2240]{1,0:T(8,128)S(1)}, f32[162,128]{1,0:T(8,128)S(1)}, f32[162,128]{1,0:T(8,128)S(1)}) custom-call(s32[1]{0:T(128)} %bitcast.parity, f32[306,128]{1,0:T(8,128)S(1)} %collective-permute-done.2.inner_in, f32[306,128]{1,0:T(8,128)S(1)} %collective-permute-done.3.outer_in, ...), custom_call_target="tpu_custom_call" | custom-call | tf_op jit(solution)/shard_map/second_solve/pallas_call | solution.py:443
  21.3 1.1 %collective-permute-start.6 = (f32[162,128]{1,0:T(8,128)S(1)}, f32[162,128]{1,0:T(8,128)S(1)}, u32[]{:S(2)}, u32[]{:S(2)}) collective-permute-start(f32[162,128]{1,0:T(8,128)S(1)} %get-tuple-element.40), channel_id=1, source_target_pairs={{0,1},{1,0},{2,3},{3,2},{4,5},{5,4},{6,7},{7,6},{8,9},{9,8},{10,11... | collective-permute-start | bytes 248840 | tf_op jit(solution)/shard_map/ppermute | solution.py:369
  22.5 2.4 %collective-permute-start.7 = (f32[162,128]{1,0:T(8,128)S(1)}, f32[162,128]{1,0:T(8,128)S(1)}, u32[]{:S(2)}, u32[]{:S(2)}) collective-permute-start(f32[162,128]{1,0:T(8,128)S(1)} %get-tuple-element.41), channel_id=1, source_target_pairs={{0,15},{1,2},{2,1},{3,4},{4,3},{5,6},{6,5},{7,8},{8,7},{9,10},{10,... | collective-permute-start | bytes 248840 | tf_op jit(solution)/shard_map/ppermute | solution.py:369
  24.9 0.0 collective-permute-done.6.inner_in
  24.9 4.2 %collective-permute-done.7.outer_in = f32[162,128]{1,0:T(8,128)S(1)} collective-permute-done((f32[162,128]{1,0:T(8,128)S(1)}, f32[162,128]{1,0:T(8,128)S(1)}, u32[]{:S(2)}, u32[]{:S(2)}) %collective-permute-start.7) | collective-permute-done | bytes 82976 | tf_op jit(solution)/shard_map/ppermute | solution.py:369
  29.1 1.2 %sums.1 = (f32[48,2240]{1,0:T(8,128)S(1)}, f32[1,128]{1,0:T(1,128)}) custom-call(s32[1]{0:T(128)} %bitcast.parity, f32[162,128]{1,0:T(8,128)S(1)} %collective-permute-done.6.inner_in, f32[162,128]{1,0:T(8,128)S(1)} %collective-permute-done.7.outer_in, f32[48,2240]{1,0:T(8,128)S(1)} %get-tuple-element.42.second, f32[48,2240]{1,0:T(8,128)S(1)} %get-tuple-element.43.z, ...), custom_call_target="tpu_custom_call" | custom-call | tf_op jit(solution)/shard_map/sums/pallas_call | solution.py:454
  30.3 17.8 %all-gather.1.came_h = f32[16,1,128]{2,1,0:T(1,128)} all-gather(f32[1,1,128]{2,1,0:T(1,128)} %bitcast.2), channel_id=2, replica_groups=mesh['members'=2,'lon'=16] {'lon'}, dimensions={0}, use_global_device_ids=true | all-gather | bytes 8704 | tf_op jit(solution)/shard_map/all_gather | solution.py:463
  48.0 3.7 %finish.1 = (f32[32,2240]{1,0:T(8,128)}, f32[6,32,2240]{2,1,0:T(8,128)}, f32[6,32,2240]{2,1,0:T(8,128)}, f32[6,32,2240]{2,1,0:T(8,128)}) custom-call(f32[16,1,128]{2,1,0:T(1,128)} %all-gather.1.came_h, f32[48,2240]{1,0:T(8,128)S(1)} %get-tuple-element.43.z, f32[48,2240]{1,0:T(8,128)S(1)} %get-tuple-element.47.w, f32[16,2240]{1,0:T(8,128)S(1)} %get-tuple-element.48.edges, ...), custom_call_target="tpu_custom_call" | custom-call | tf_op jit(solution)/shard_map/finish/pallas_call | solution.py:465
Async XLA Ops:
  1.6 7.9 %collective-permute-start.1 = (f32[8,2240]{1,0:T(8,128)S(1)}, f32[8,2240]{1,0:T(8,128)S(1)}, u32[]{:S(2)}, u32[]{:S(2)}) collective-permute-start(f32[8,2240]{1,0:T(8,128)S(1)} %first_edges.1.after), channel_id=1, source_target_pairs={{0,15},{1,2},{2,1},{3,4},{4,3},{5,6},{6,5},{7,8},{8,7},{9,10},{10,... | collective-permute-start | bytes 215048 | tf_op jit(solution)/shard_map/ppermute | solution.py:369
  8.6 1.3 %collective-permute-start = (f32[8,2240]{1,0:T(8,128)S(1)}, f32[8,2240]{1,0:T(8,128)S(1)}, u32[]{:S(2)}, u32[]{:S(2)}) collective-permute-start(f32[8,2240]{1,0:T(8,128)S(1)} %get-tuple-element.28), channel_id=1, source_target_pairs={{0,1},{1,0},{2,3},{3,2},{4,5},{5,4},{6,7},{7,6},{8,9},{9,8},{10,11... | collective-permute-start | bytes 215048 | tf_op jit(solution)/shard_map/ppermute | solution.py:369
  8.7 6.7 %collective-permute-start.4 = (f32[24,2240]{1,0:T(8,128)S(1)}, f32[24,2240]{1,0:T(8,128)S(1)}, u32[]{:S(2)}, u32[]{:S(2)}) collective-permute-start(f32[24,2240]{1,0:T(8,128)S(1)} %get-tuple-element.36), channel_id=1, source_target_pairs={{0,1},{1,0},{2,3},{3,2},{4,5},{5,4},{6,7},{7,6},{8,9},{9,8},{10,11... | collective-permute-start | bytes 645128 | tf_op jit(solution)/shard_map/ppermute | solution.py:369
  9.2 8.2 %collective-permute-start.5 = (f32[24,2240]{1,0:T(8,128)S(1)}, f32[24,2240]{1,0:T(8,128)S(1)}, u32[]{:S(2)}, u32[]{:S(2)}) collective-permute-start(f32[24,2240]{1,0:T(8,128)S(1)} %get-tuple-element.37), channel_id=1, source_target_pairs={{0,15},{1,2},{2,1},{3,4},{4,3},{5,6},{6,5},{7,8},{8,7},{9,10},{10,... | collective-permute-start | bytes 645128 | tf_op jit(solution)/shard_map/ppermute | solution.py:369
  11.5 7.8 %collective-permute-start.2 = (f32[306,128]{1,0:T(8,128)S(1)}, f32[306,128]{1,0:T(8,128)S(1)}, u32[]{:S(2)}, u32[]{:S(2)}) collective-permute-start(f32[306,128]{1,0:T(8,128)S(1)} %get-tuple-element.33), channel_id=1, source_target_pairs={{0,1},{1,0},{2,3},{3,2},{4,5},{5,4},{6,7},{7,6},{8,9},{9,8},{10,11... | collective-permute-start | bytes 470024 | tf_op jit(solution)/shard_map/ppermute | solution.py:369
  11.8 7.6 %collective-permute-start.3 = (f32[306,128]{1,0:T(8,128)S(1)}, f32[306,128]{1,0:T(8,128)S(1)}, u32[]{:S(2)}, u32[]{:S(2)}) collective-permute-start(f32[306,128]{1,0:T(8,128)S(1)} %get-tuple-element.34), channel_id=1, source_target_pairs={{0,15},{1,2},{2,1},{3,4},{4,3},{5,6},{6,5},{7,8},{8,7},{9,10},{10,... | collective-permute-start | bytes 470024 | tf_op jit(solution)/shard_map/ppermute | solution.py:369
  21.3 3.5 %collective-permute-start.6 = (f32[162,128]{1,0:T(8,128)S(1)}, f32[162,128]{1,0:T(8,128)S(1)}, u32[]{:S(2)}, u32[]{:S(2)}) collective-permute-start(f32[162,128]{1,0:T(8,128)S(1)} %get-tuple-element.40), channel_id=1, source_target_pairs={{0,1},{1,0},{2,3},{3,2},{4,5},{5,4},{6,7},{7,6},{8,9},{9,8},{10,11... | collective-permute-start | bytes 248840 | tf_op jit(solution)/shard_map/ppermute | solution.py:369
  22.5 6.6 %collective-permute-start.7 = (f32[162,128]{1,0:T(8,128)S(1)}, f32[162,128]{1,0:T(8,128)S(1)}, u32[]{:S(2)}, u32[]{:S(2)}) collective-permute-start(f32[162,128]{1,0:T(8,128)S(1)} %get-tuple-element.41), channel_id=1, source_target_pairs={{0,15},{1,2},{2,1},{3,4},{4,3},{5,6},{6,5},{7,8},{8,7},{9,10},{10,... | collective-permute-start | bytes 248840 | tf_op jit(solution)/shard_map/ppermute | solution.py:369

commit v10 on v8

--- a/solution.py
+++ b/solution.py
@@ -66,54 +66,67 @@
             return jnp.zeros((span, LANE), F32)
         return x[:, b * LANE : (b + 1) * LANE]
 
-    for t in range(tiles):
-        block, start = divmod(t * LT - OV, LANE)
-        left, right = [pltpu.roll(block_of(b), LANE - start, 1) for b in (block, block + 1)]
-        high, low = split(jnp.where(lane < LANE - start, left, right))
-        rows[t * span : (t + 1) * span, :LANE] = high
-        rows[t * span : (t + 1) * span, LANE:] = low
     chunk = 4
-    for first in range(0, tiles, chunk):
-        n = min(chunk, tiles - first)
+    groups = [range(first, min(first + chunk, tiles)) for first in range(0, tiles, chunk)]
+    held = {}
+
+    def lanes_of(group):
+        return slice(group[0] * LANE, (group[-1] + 1) * LANE)
+
+    def cut(group):
+        for t in group:
+            block, start = divmod(t * LT - OV, LANE)
+            left, right = [pltpu.roll(block_of(b), LANE - start, 1) for b in (block, block + 1)]
+            high, low = split(jnp.where(lane < LANE - start, left, right))
+            rows[t * span : (t + 1) * span, :LANE] = high
+            rows[t * span : (t + 1) * span, LANE:] = low
+
+    def along_lat(group):
         product = jnp.dot(
-            rows[first * span : (first + n) * span], lat_basis[...], preferred_element_type=F32
+            rows[group[0] * span : (group[-1] + 1) * span], lat_basis[...], preferred_element_type=F32
         )
-        high, low = split(product[:, :LANE] + product[:, LANE:])
-        for i in range(n):
-            at = slice((first + i) * LANE, (first + i + 1) * LANE)
+        return product[:, :LANE] + product[:, LANE:]
+
+    def lat_there(group):
+        high, low = split(along_lat(group))
+        for i, t in enumerate(group):
+            at = slice(t * LANE, (t + 1) * LANE)
             spectral[:span, at] = high[i * span : (i + 1) * span]
             spectral[span : 2 * span, at] = high[i * span : (i + 1) * span]
             spectral[2 * span :, at] = low[i * span : (i + 1) * span]
-    for first in range(0, tiles, chunk):
-        n = min(chunk, tiles - first)
-        c = jnp.dot(lon[...], spectral[:, first * LANE : (first + n) * LANE], preferred_element_type=F32)
-        c = c * jnp.concatenate([scale[...]] * n, axis=1)
+
+    def lon_there(group):
+        c = jnp.dot(lon[...], spectral[:, lanes_of(group)], preferred_element_type=F32)
+        high, low = split(c * jnp.concatenate([scale[...]] * len(group), axis=1))
+        spectral[:, lanes_of(group)] = jnp.concatenate([high, high, low], axis=0)
+
+    def lon_back(group):
+        c = jnp.dot(lon[...], spectral[:, lanes_of(group)], preferred_element_type=F32)
         high, low = split(c)
-        c = jnp.concatenate([high, high, low], axis=0)
-        c = jnp.dot(lon[...], c, preferred_element_type=F32)
-        high, low = split(c)
-        for i in range(n):
-            at = slice((first + i) * span, (first + i + 1) * span)
+        for i, t in enumerate(group):
+            at = slice(t * span, (t + 1) * span)
             rows[at, :LANE] = high[:, i * LANE : (i + 1) * LANE]
             rows[at, LANE:] = low[:, i * LANE : (i + 1) * LANE]
-    sums_of = {}
-    for first in range(0, tiles, chunk):
-        n = min(chunk, tiles - first)
-        product = jnp.dot(
-            rows[first * span : (first + n) * span], lat_basis[...], preferred_element_type=F32
-        )
-        product = product[:, :LANE] + product[:, LANE:]
-        for i in range(n):
-            block, start = divmod((first + i) * LT - OV, LANE)
+
+    def lat_back(group):
+        product = along_lat(group)
+        for i, t in enumerate(group):
+            block, start = divmod(t * LT - OV, LANE)
             part = pltpu.roll(product[i * span : (i + 1) * span], start, 1)
             for b, inside in ((block, lane >= start), (block + 1, lane < start)):
                 if 0 <= b * LANE < lat:
                     piece = jnp.where(inside, part, 0.0)
-                    sums_of[b] = sums_of[b] + piece if b in sums_of else piece
-        done = (first + n) * LT - OV if first + n < tiles else lat + LANE
-        for b in [b for b in sums_of if (b + 1) * LANE <= done]:
+                    held[b] = held[b] + piece if b in held else piece
+        done = (group[-1] + 1) * LT - OV if group[-1] + 1 < tiles else lat + LANE
+        for b in [b for b in held if (b + 1) * LANE <= done]:
             width = min(LANE, lat - b * LANE)
-            out[:, b * LANE : b * LANE + width] = sums_of.pop(b)[:, :width]
+            out[:, b * LANE : b * LANE + width] = held.pop(b)[:, :width]
+
+    stages = [cut, lat_there, lon_there, lon_back, lat_back]
+    for step in range(len(groups) + len(stages) - 1):
+        for i in reversed(range(len(stages))):
+            if 0 <= step - i < len(groups):
+                stages[i](groups[step - i])
 
 
 def wide_lanes(lat):
@@ -208,14 +221,16 @@
     pack(outer, to_outer)
 
 
-def absorb(parity, after, inner_in, outer_in, coef, u_h, v_h, c_rows, edges, u, v, sems):
+def absorb(parity, after, inner_in, outer_in, coef, depth, u_h, v_h, c_rows, d_rows, edge, u, v, sems):
     cells, lat = coef.shape
     copies = [pltpu.make_async_copy(a, b, sems.at[i]) for i, (a, b) in enumerate([(u_h, u), (v_h, v)])]
     for copy in copies:
         copy.start()
     west, east = pick(parity, inner_in[: 2 * OV], outer_in[: 2 * OV])
-    edges[:OV] = west[:OV]
-    edges[OV:] = east[OV:]
+    edge[...] = west[:OV]
+    d_rows[:OV] = jnp.broadcast_to(west[KL : KL + 1], (OV, lat))
+    d_rows[OV : OV + cells] = depth[...]
+    d_rows[OV + cells :] = jnp.broadcast_to(east[2 * OV - 1 :], (OV, lat))
     c_rows[: 2 * OV] = west
     c_rows[: OV - 1] = jnp.zeros((OV - 1, lat), F32)
     c_rows[2 * OV : 2 * OV + cells] = coef[...]
@@ -289,8 +304,8 @@
     sent[...] = jnp.broadcast_to(row[None], sent.shape)
 
 
-def finish(came, z, w, edges, source, depth, u_vel, v_vel, solution, u_new, v_new, w_vel,
-           s_rows, d_rows, u_rows, v_out, w_out, s_out, sems):
+def finish(came, z, w, d_rows, edge, source, u_vel, v_vel, solution, u_new, v_new, w_vel,
+           s_rows, u_rows, v_out, w_out, s_out, sems):
     cells, lat = source.shape
     total = jnp.broadcast_to(jnp.sum(came[...], axis=0), (8, LANE))
     place = [lax.broadcasted_iota(jnp.int32, (8, LANE), axis) for axis in range(2)]
@@ -308,48 +323,51 @@
     of_land = jnp.broadcast_to(step0 + step1 * (rest + beta), (OV, lat))
 
     copies = []
-    d_rows[:OV] = jnp.broadcast_to(edges[KL : KL + 1], (OV, lat))
-    d_rows[OV : OV + cells] = depth[...]
-    d_rows[OV + cells :] = jnp.broadcast_to(edges[2 * OV - 1 :], (OV, lat))
-    for at in range(0, cells + 2 * OV, OV):
+
+    def send(held, result):
+        copies.append(pltpu.make_async_copy(held, result, sems.at[len(copies)]))
+        copies[-1].start()
+
+    def surface_rows(at):
         s = of_z * z[at : at + OV] + of_w * w[at : at + OV]
         if OV <= at < OV + cells:
-            d = d_rows[at : at + OV]
-            s = jnp.where(d > 0, s, of_land * source[at - OV : at])
+            s = jnp.where(d_rows[at : at + OV] > 0, s, of_land * source[at - OV : at])
             s_out[at - OV : at] = s
         s_rows[at : at + OV] = s
-    copies.append(pltpu.make_async_copy(s_out, solution, sems.at[0]))
-    copies[-1].start()
-
-    s_west = s_rows[OV - 1 : OV]
-    s_first = s_rows[OV : OV + 1]
+
+    surface_rows(0)
+    surface_rows(OV)
+    slope = gravity_step * (s_rows[OV : OV + 1] - s_rows[OV - 1 : OV])
     d_west = jnp.minimum(d_rows[OV - 1 : OV], d_rows[OV : OV + 1])
     for level in range(KL):
-        left = edges[level : level + 1] - gravity_step * (s_first - s_west)
-        u_rows[level, :OV] = jnp.broadcast_to(jnp.where(d_west > level, left, 0.0), (OV, lat))
+        u = jnp.where(d_west > level, edge[level : level + 1] - slope, 0.0)
+        u_rows[level, :OV] = jnp.broadcast_to(u, (OV, lat))
     zero = jnp.zeros((OV, 1), F32)
-    for block in range(cells // OV):
-        at = OV + block * OV
+    for at in range(OV, OV + cells, OV):
         own = slice(at - OV, at)
+        surface_rows(at + OV)
         s = s_rows[at : at + OV]
         d = d_rows[at : at + OV]
-        slope_e = gravity_step * (s_rows[at + 1 : at + OV + 1] - s)
-        depth_e = jnp.minimum(d, d_rows[at + 1 : at + OV + 1])
-        slope_n = gravity_step * (jnp.concatenate([s[:, 1:], zero], axis=1) - s)
-        depth_n = jnp.minimum(d, jnp.concatenate([d[:, 1:], zero], axis=1))
+        slope = gravity_step * (s_rows[at + 1 : at + OV + 1] - s)
+        face = jnp.minimum(d, d_rows[at + 1 : at + OV + 1])
+        for level in range(KL):
+            u_rows[level, at : at + OV] = jnp.where(face > level, u_vel[level, own] - slope, 0.0)
+        send(u_rows.at[:, at : at + OV], u_new.at[:, own])
+        slope = gravity_step * (jnp.concatenate([s[:, 1:], zero], axis=1) - s)
+        face = jnp.minimum(d, jnp.concatenate([d[:, 1:], zero], axis=1))
+        for level in range(KL):
+            v_out[level, own] = jnp.where(face > level, v_vel[level, own] - slope, 0.0)
+        send(v_out.at[:, own], v_new.at[:, own])
         w_sum = jnp.zeros((OV, lat), F32)
         for level in range(KL - 1, -1, -1):
-            u = jnp.where(depth_e > level, u_vel[level, own] - slope_e, 0.0)
-            u_rows[level, at : at + OV] = u
-            v = jnp.where(depth_n > level, v_vel[level, own] - slope_n, 0.0)
-            v_out[level, own] = v
-            south = jnp.concatenate([zero, v[:, :-1]], axis=1)
-            flow = (u - u_rows[level, at - 1 : at + OV - 1]) + (v - south)
+            v = v_out[level, own]
+            flow = u_rows[level, at : at + OV] - u_rows[level, at - 1 : at + OV - 1]
+            flow = flow + (v - jnp.concatenate([zero, v[:, :-1]], axis=1))
             w_sum = w_sum + jnp.where(d > level, flow, 0.0)
             w_out[level, own] = w_sum
-        for held, result in ((u_rows.at[:, at : at + OV], u_new), (v_out.at[:, own], v_new), (w_out.at[:, own], w_vel)):
-            copies.append(pltpu.make_async_copy(held, result.at[:, own], sems.at[len(copies)]))
-            copies[-1].start()
+        send(w_out.at[:, own], w_vel.at[:, own])
+        if at == cells:
+            send(s_out, solution)
     for copy in copies:
         copy.wait()
 
@@ -422,17 +440,17 @@
     )(parity, *near, masked, *held)
     near = swap_pairs(inner, False), swap_pairs(outer, True)
 
-    c_rows, edges, u_v, v_v = pl.pallas_call(
+    c_rows, d_rows, edge, u_v, v_v = pl.pallas_call(
         absorb,
-        in_specs=[SM, HB] + [VM] * 3 + [HB] * 2,
-        out_specs=[VM] * 4,
-        out_shape=[pltpu.VMEM((span + 2 * OV, lat), F32), pltpu.VMEM((2 * OV, lat), F32)]
+        in_specs=[SM, HB] + [VM] * 4 + [HB] * 2,
+        out_specs=[VM] * 5,
+        out_shape=[pltpu.VMEM((span + 2 * OV, lat), F32), pltpu.VMEM((span, lat), F32), pltpu.VMEM((OV, lat), F32)]
         + [pltpu.VMEM((KL, cells, lat), F32)] * 2,
         scratch_shapes=[pltpu.SemaphoreType.DMA((2,))],
         compiler_params=PARAMS,
         cost_estimate=pl.CostEstimate(flops=10**6, bytes_accessed=7 * 10**6, transcendentals=0),
         name="absorb",
-    )(parity, first, *far, coef, hbm["u"], hbm["v"])
+    )(parity, first, *far, coef, depth, hbm["u"], hbm["v"])
 
     z, y, second, inner, outer = pl.pallas_call(
         second_solve,
@@ -460,13 +478,13 @@
         in_specs=[VM] * 8,
         out_specs=[HB] * 4,
         out_shape=[shape(cells, lat)] + [shape(KL, cells, lat)] * 3,
-        scratch_shapes=[pltpu.VMEM((span, lat), F32)] * 2
+        scratch_shapes=[pltpu.VMEM((span, lat), F32)]
         + [pltpu.VMEM((KL, OV + cells, lat), F32)]
         + [pltpu.VMEM((KL, cells, lat), F32)] * 2
         + [pltpu.VMEM((cells, lat), F32), pltpu.SemaphoreType.DMA((1 + 3 * (cells // OV),))],
         compiler_params=PARAMS,
         name="finish",
-    )(came, z, w, edges, source_v, depth, u_v, v_v)
+    )(came, z, w, d_rows, edge, source_v, u_v, v_v)
 
 
 def solution(mesh):

time: 42.9 us -> 43 us (level)
  no operation moved by 1% of the time
where the time goes in v10:
time: 43 us; the launch traced here: 42.8 us
  starting transfers between devices  13.8 us (32%)
  Pallas kernels  11.7 us (27%)
  blocking collectives  10.1 us (23%)
  waiting for transfers between devices  6.48 us (15%)
  between operations  0.71 us (2%)
    ppermute x8, starting transfers between devices, swap_pairs(): return lax.ppermute(block, 'lon', route)  13.8 us
    all_to_all x1, blocking collectives, body(): came = lax.all_to_all(sent, 'lon', 0, 0)  10.1 us
    ppermute x8, waiting for transfers between devices, swap_pairs(): return lax.ppermute(block, 'lon', route)  6.48 us
    pallas_call x1, Pallas kernels, body(): pl.pallas_call(finish, in_specs=[VM] * 8, out_specs=[HB] * 4, out_shape=[...  3.02 us
    pallas_call x1, Pallas kernels, body(): pl.pallas_call(absorb, in_specs=[SM, HB] + [VM] * 4 + [HB] * 2, out_specs...  2.03 us
    pallas_call x1, Pallas kernels, body(): pl.pallas_call(second_solve, in_specs=[SM] + [VM] * 7, out_specs=[VM] * 5...  1.86 us
    pallas_call x1, Pallas kernels, body(): pl.pallas_call(first_solve, in_specs=[SM] + [VM] * 6, out_specs=[VM] * 3,...  1.68 us
    pallas_call x1, Pallas kernels, body(): pl.pallas_call(prepare, in_specs=[SM] + [HB] * 8, out_specs=[VM] * 10, ou...  1.53 us
  transfers between devices with their start and end apart: 8, of which 3 were waited for; matrix products, arithmetic and copies ran while one was open for 0% of the time, Pallas kernels for 12%

profile of v10, /device:TPU:0, one launch (start us, length us, event | category | flops | bytes accessed | tf_op | source)
XLA Modules:
  0.0 42.8 jit_solution(14113090399938680377)
XLA Ops:
  0.6 0.9 %first_edges.1.after = f32[8,2240]{1,0:T(8,128)S(1)} custom-call(s32[1]{0:T(128)} %bitcast.parity, f32[32,2240]{1,0:T(8,128)} %source_h.1, s32[32,2240]{1,0:T(8,128)} %bottom_h.1), custom_call_target="tpu_custom_call" | custom-call | tf_op jit(solution)/shard_map/first_edges/pallas_call | solution.py:398
  1.6 5.5 %collective-permute-start.1 = (f32[8,2240]{1,0:T(8,128)S(1)}, f32[8,2240]{1,0:T(8,128)S(1)}, u32[]{:S(2)}, u32[]{:S(2)}) collective-permute-start(f32[8,2240]{1,0:T(8,128)S(1)} %first_edges.1.after), channel_id=1, source_target_pairs={{0,15},{1,2},{2,1},{3,4},{4,3},{5,6},{6,5},{7,8},{8,7},{9,10},{10,... | collective-permute-start | bytes 215048 | tf_op jit(solution)/shard_map/ppermute | solution.py:381
  7.1 1.5 %prepare.1 = (f32[8,2240]{1,0:T(8,128)S(1)}, f32[24,2240]{1,0:T(8,128)S(1)}, f32[24,2240]{1,0:T(8,128)S(1)}, f32[32,2240]{1,0:T(8,128)S(1)}, f32[32,2240]{1,0:T(...) custom-call(s32[1]{0:T(128)} %bitcast.parity, ...), custom_call_target="tpu_custom_call" | custom-call | flops 1000000 | bytes 7000000 | tf_op jit(solution)/shard_map/prepare/pallas_call | solution.py:410
  8.6 0.1 collective-permute-start
  8.7 0.5 %collective-permute-start.4 = (f32[24,2240]{1,0:T(8,128)S(1)}, f32[24,2240]{1,0:T(8,128)S(1)}, u32[]{:S(2)}, u32[]{:S(2)}) collective-permute-start(f32[24,2240]{1,0:T(8,128)S(1)} %get-tuple-element.37), channel_id=1, source_target_pairs={{0,1},{1,0},{2,3},{3,2},{4,5},{5,4},{6,7},{7,6},{8,9},{9,8},{10,11... | collective-permute-start | bytes 645128 | tf_op jit(solution)/shard_map/ppermute | solution.py:381
  9.2 0.3 collective-permute-start.5
  9.5 0.0 collective-permute-done.1.outer_in
  9.5 0.5 %collective-permute-done.inner_in = f32[8,2240]{1,0:T(8,128)S(1)} collective-permute-done((f32[8,2240]{1,0:T(8,128)S(1)}, f32[8,2240]{1,0:T(8,128)S(1)}, u32[]{:S(2)}, u32[]{:S(2)}) %collective-permute-start) | collective-permute-done | bytes 71712 | tf_op jit(solution)/shard_map/ppermute | solution.py:381
  10.0 1.7 %first_solve.1 = (f32[48,2240]{1,0:T(8,128)S(1)}, f32[306,128]{1,0:T(8,128)S(1)}, f32[306,128]{1,0:T(8,128)S(1)}) custom-call(s32[1]{0:T(128)} %bitcast.parity, f32[8,2240]{1,0:T(8,128)S(1)} %collective-permute-done.inner_in, f32[8,2240]{1,0:T(8,128)S(1)} %collective-permute-done.1.outer_in, f32[32,2240]{1,0:T(8,128)S(1)} %get-tuple-element.30.masked, ...), custom_call_target="tpu_custom_call" | custom-call | tf_op jit(solution)/shard_map/first_solve/pallas_call | solution.py:432
  11.6 0.2 collective-permute-start.2
  11.9 3.6 %collective-permute-start.3 = (f32[306,128]{1,0:T(8,128)S(1)}, f32[306,128]{1,0:T(8,128)S(1)}, u32[]{:S(2)}, u32[]{:S(2)}) collective-permute-start(f32[306,128]{1,0:T(8,128)S(1)} %get-tuple-element.35), channel_id=1, source_target_pairs={{0,15},{1,2},{2,1},{3,4},{4,3},{5,6},{6,5},{7,8},{8,7},{9,10},{10,... | collective-permute-start | bytes 470024 | tf_op jit(solution)/shard_map/ppermute | solution.py:381
  15.5 0.0 collective-permute-done.4.inner_in
  15.5 1.9 %collective-permute-done.5.outer_in = f32[24,2240]{1,0:T(8,128)S(1)} collective-permute-done((f32[24,2240]{1,0:T(8,128)S(1)}, f32[24,2240]{1,0:T(8,128)S(1)}, u32[]{:S(2)}, u32[]{:S(2)}) %collective-permute-start.5) | collective-permute-done | bytes 215072 | tf_op jit(solution)/shard_map/ppermute | solution.py:381
  17.4 2.0 %absorb.1 = (f32[64,2240]{1,0:T(8,128)S(1)}, f32[48,2240]{1,0:T(8,128)S(1)}, f32[8,2240]{1,0:T(8,128)S(1)}, f32[6,32,2240]{2,1,0:T(8,128)S(1)}, f32[6,32,2240]{2,1,0:T(8,128)S(1)}) custom-call(s32[1]{0:T(128)} %bitcast.parity, f32[48,2240]{1,0:T(8,128)S(1)} %get-tuple-element.36.after.first, f32[24,2240]{1,0:T(8,128)S(1)} %collective-permute-done.4.inner_in, ...), custom_call_target="tpu_custom_call" | custom-call | flops 1000000 | bytes 7000000 | tf_op jit(solution)/shard_map/absorb/pallas_call | solution.py:443
  19.4 0.0 collective-permute-done.2.inner_in
  19.4 0.0 collective-permute-done.3.outer_in
  19.4 1.9 %second_solve.1 = (f32[48,2240]{1,0:T(8,128)S(1)}, f32[48,2240]{1,0:T(8,128)S(1)}, f32[48,2240]{1,0:T(8,128)S(1)}, f32[162,128]{1,0:T(8,128)S(1)}, f32[162,128]{1,0:T(8,128)S(1)}) custom-call(s32[1]{0:T(128)} %bitcast.parity, f32[306,128]{1,0:T(8,128)S(1)} %collective-permute-done.2.inner_in, f32[306,128]{1,0:T(8,128)S(1)} %collective-permute-done.3.outer_in, ...), custom_call_target="tpu_custom_call" | custom-call | tf_op jit(solution)/shard_map/second_solve/pallas_call | solution.py:455
  21.3 1.1 %collective-permute-start.6 = (f32[162,128]{1,0:T(8,128)S(1)}, f32[162,128]{1,0:T(8,128)S(1)}, u32[]{:S(2)}, u32[]{:S(2)}) collective-permute-start(f32[162,128]{1,0:T(8,128)S(1)} %get-tuple-element.42), channel_id=1, source_target_pairs={{0,1},{1,0},{2,3},{3,2},{4,5},{5,4},{6,7},{7,6},{8,9},{9,8},{10,11... | collective-permute-start | bytes 248840 | tf_op jit(solution)/shard_map/ppermute | solution.py:381
  22.4 2.5 %collective-permute-start.7 = (f32[162,128]{1,0:T(8,128)S(1)}, f32[162,128]{1,0:T(8,128)S(1)}, u32[]{:S(2)}, u32[]{:S(2)}) collective-permute-start(f32[162,128]{1,0:T(8,128)S(1)} %get-tuple-element.43), channel_id=1, source_target_pairs={{0,15},{1,2},{2,1},{3,4},{4,3},{5,6},{6,5},{7,8},{8,7},{9,10},{10,... | collective-permute-start | bytes 248840 | tf_op jit(solution)/shard_map/ppermute | solution.py:381
  24.9 0.0 collective-permute-done.6.inner_in
  24.9 4.1 %collective-permute-done.7.outer_in = f32[162,128]{1,0:T(8,128)S(1)} collective-permute-done((f32[162,128]{1,0:T(8,128)S(1)}, f32[162,128]{1,0:T(8,128)S(1)}, u32[]{:S(2)}, u32[]{:S(2)}) %collective-permute-start.7) | collective-permute-done | bytes 82976 | tf_op jit(solution)/shard_map/ppermute | solution.py:381
  29.0 0.6 %sums.1 = (f32[48,2240]{1,0:T(8,128)S(1)}, f32[16,1,128]{2,1,0:T(1,128)S(1)}) custom-call(s32[1]{0:T(128)} %bitcast.parity, f32[162,128]{1,0:T(8,128)S(1)} %collective-permute-done.6.inner_in, f32[162,128]{1,0:T(8,128)S(1)} %collective-permute-done.7.outer_in, f32[48,2240]{1,0:T(8,128)S(1)} %get-tuple-element.44.second, f32[48,2240]{1,0:T(8,128)S(1)} %get-tuple-element.45.z, ...), custom_call_target="tpu_custom_call" | custom-call | tf_op jit(solution)/shard_map/sums/pallas_call | solution.py:466
  29.7 10.1 %all_to_all.5.came = f32[16,1,128]{2,1,0:T(1,128)S(1)} all-to-all(f32[16,1,128]{2,1,0:T(1,128)S(1)} %get-tuple-element.48), channel_id=1, replica_groups=mesh['members'=2,'lon'=16] {'lon'}, dimensions={0} | all-to-all | bytes 16384 | tf_op jit(solution)/shard_map/all_to_all | solution.py:474
  39.7 3.0 %finish.1 = (f32[32,2240]{1,0:T(8,128)}, f32[6,32,2240]{2,1,0:T(8,128)}, f32[6,32,2240]{2,1,0:T(8,128)}, f32[6,32,2240]{2,1,0:T(8,128)}) custom-call(f32[16,1,128]{2,1,0:T(1,128)S(1)} %all_to_all.5.came, f32[48,2240]{1,0:T(8,128)S(1)} %get-tuple-element.45.z, f32[48,2240]{1,0:T(8,128)S(1)} %get-tuple-element.49.w, f32[48,2240]{1,0:T(8,128)S(1)} %get-tuple-element.50.d_rows, ...), custom_call_target="tpu_custom_call" | custom-call | tf_op jit(solution)/shard_map/finish/pallas_call | solution.py:476
Async XLA Ops:
  1.6 7.9 %collective-permute-start.1 = (f32[8,2240]{1,0:T(8,128)S(1)}, f32[8,2240]{1,0:T(8,128)S(1)}, u32[]{:S(2)}, u32[]{:S(2)}) collective-permute-start(f32[8,2240]{1,0:T(8,128)S(1)} %first_edges.1.after), channel_id=1, source_target_pairs={{0,15},{1,2},{2,1},{3,4},{4,3},{5,6},{6,5},{7,8},{8,7},{9,10},{10,... | collective-permute-start | bytes 215048 | tf_op jit(solution)/shard_map/ppermute | solution.py:381
  8.6 1.3 %collective-permute-start = (f32[8,2240]{1,0:T(8,128)S(1)}, f32[8,2240]{1,0:T(8,128)S(1)}, u32[]{:S(2)}, u32[]{:S(2)}) collective-permute-start(f32[8,2240]{1,0:T(8,128)S(1)} %get-tuple-element.29), channel_id=1, source_target_pairs={{0,1},{1,0},{2,3},{3,2},{4,5},{5,4},{6,7},{7,6},{8,9},{9,8},{10,11... | collective-permute-start | bytes 215048 | tf_op jit(solution)/shard_map/ppermute | solution.py:381
  8.7 6.8 %collective-permute-start.4 = (f32[24,2240]{1,0:T(8,128)S(1)}, f32[24,2240]{1,0:T(8,128)S(1)}, u32[]{:S(2)}, u32[]{:S(2)}) collective-permute-start(f32[24,2240]{1,0:T(8,128)S(1)} %get-tuple-element.37), channel_id=1, source_target_pairs={{0,1},{1,0},{2,3},{3,2},{4,5},{5,4},{6,7},{7,6},{8,9},{9,8},{10,11... | collective-permute-start | bytes 645128 | tf_op jit(solution)/shard_map/ppermute | solution.py:381
  9.2 8.2 %collective-permute-start.5 = (f32[24,2240]{1,0:T(8,128)S(1)}, f32[24,2240]{1,0:T(8,128)S(1)}, u32[]{:S(2)}, u32[]{:S(2)}) collective-permute-start(f32[24,2240]{1,0:T(8,128)S(1)} %get-tuple-element.38), channel_id=1, source_target_pairs={{0,15},{1,2},{2,1},{3,4},{4,3},{5,6},{6,5},{7,8},{8,7},{9,10},{10,... | collective-permute-start | bytes 645128 | tf_op jit(solution)/shard_map/ppermute | solution.py:381
  11.6 7.8 %collective-permute-start.2 = (f32[306,128]{1,0:T(8,128)S(1)}, f32[306,128]{1,0:T(8,128)S(1)}, u32[]{:S(2)}, u32[]{:S(2)}) collective-permute-start(f32[306,128]{1,0:T(8,128)S(1)} %get-tuple-element.34), channel_id=1, source_target_pairs={{0,1},{1,0},{2,3},{3,2},{4,5},{5,4},{6,7},{7,6},{8,9},{9,8},{10,11... | collective-permute-start | bytes 470024 | tf_op jit(solution)/shard_map/ppermute | solution.py:381
  11.9 7.5 %collective-permute-start.3 = (f32[306,128]{1,0:T(8,128)S(1)}, f32[306,128]{1,0:T(8,128)S(1)}, u32[]{:S(2)}, u32[]{:S(2)}) collective-permute-start(f32[306,128]{1,0:T(8,128)S(1)} %get-tuple-element.35), channel_id=1, source_target_pairs={{0,15},{1,2},{2,1},{3,4},{4,3},{5,6},{6,5},{7,8},{8,7},{9,10},{10,... | collective-permute-start | bytes 470024 | tf_op jit(solution)/shard_map/ppermute | solution.py:381
  21.3 3.6 %collective-permute-start.6 = (f32[162,128]{1,0:T(8,128)S(1)}, f32[162,128]{1,0:T(8,128)S(1)}, u32[]{:S(2)}, u32[]{:S(2)}) collective-permute-start(f32[162,128]{1,0:T(8,128)S(1)} %get-tuple-element.42), channel_id=1, source_target_pairs={{0,1},{1,0},{2,3},{3,2},{4,5},{5,4},{6,7},{7,6},{8,9},{9,8},{10,11... | collective-permute-start | bytes 248840 | tf_op jit(solution)/shard_map/ppermute | solution.py:381
  22.4 6.6 %collective-permute-start.7 = (f32[162,128]{1,0:T(8,128)S(1)}, f32[162,128]{1,0:T(8,128)S(1)}, u32[]{:S(2)}, u32[]{:S(2)}) collective-permute-start(f32[162,128]{1,0:T(8,128)S(1)} %get-tuple-element.43), channel_id=1, source_target_pairs={{0,15},{1,2},{2,1},{3,4},{4,3},{5,6},{6,5},{7,8},{8,7},{9,10},{10,... | collective-permute-start | bytes 248840 | tf_op jit(solution)/shard_map/ppermute | solution.py:381

commit v11 on v10

--- a/solution.py
+++ b/solution.py
@@ -322,54 +322,71 @@
     of_w = jnp.broadcast_to(-step1 * step0, (OV, lat))
     of_land = jnp.broadcast_to(step0 + step1 * (rest + beta), (OV, lat))
 
-    copies = []
-
-    def send(held, result):
-        copies.append(pltpu.make_async_copy(held, result, sems.at[len(copies)]))
-        copies[-1].start()
-
-    def surface_rows(at):
-        s = of_z * z[at : at + OV] + of_w * w[at : at + OV]
-        if OV <= at < OV + cells:
-            s = jnp.where(d_rows[at : at + OV] > 0, s, of_land * source[at - OV : at])
-            s_out[at - OV : at] = s
-        s_rows[at : at + OV] = s
-
-    surface_rows(0)
-    surface_rows(OV)
+    for at in (0, OV + cells):
+        s_rows[at : at + OV] = of_z * z[at : at + OV] + of_w * w[at : at + OV]
+
+    def rows_at(start):
+        return pl.ds(pl.multiple_of(start, OV), OV)
+
+    def surface_rows(block, _):
+        own, at = rows_at(block * OV), rows_at(block * OV + OV)
+        s = of_z * z[at] + of_w * w[at]
+        s = jnp.where(d_rows[at] > 0, s, of_land * source[own])
+        s_out[own] = s
+        s_rows[at] = s
+        return 0
+
+    lax.fori_loop(0, cells // OV, surface_rows, 0)
+    send_s = pltpu.make_async_copy(s_out, solution, sems.at[0])
+    send_s.start()
     slope = gravity_step * (s_rows[OV : OV + 1] - s_rows[OV - 1 : OV])
     d_west = jnp.minimum(d_rows[OV - 1 : OV], d_rows[OV : OV + 1])
     for level in range(KL):
         u = jnp.where(d_west > level, edge[level : level + 1] - slope, 0.0)
         u_rows[level, :OV] = jnp.broadcast_to(u, (OV, lat))
     zero = jnp.zeros((OV, 1), F32)
-    for at in range(OV, OV + cells, OV):
-        own = slice(at - OV, at)
-        surface_rows(at + OV)
-        s = s_rows[at : at + OV]
-        d = d_rows[at : at + OV]
-        slope = gravity_step * (s_rows[at + 1 : at + OV + 1] - s)
-        face = jnp.minimum(d, d_rows[at + 1 : at + OV + 1])
-        for level in range(KL):
-            u_rows[level, at : at + OV] = jnp.where(face > level, u_vel[level, own] - slope, 0.0)
-        send(u_rows.at[:, at : at + OV], u_new.at[:, own])
-        slope = gravity_step * (jnp.concatenate([s[:, 1:], zero], axis=1) - s)
-        face = jnp.minimum(d, jnp.concatenate([d[:, 1:], zero], axis=1))
-        for level in range(KL):
-            v_out[level, own] = jnp.where(face > level, v_vel[level, own] - slope, 0.0)
-        send(v_out.at[:, own], v_new.at[:, own])
+    last = lax.broadcasted_iota(jnp.int32, (OV, lat), 0) == OV - 1
+    first = lax.broadcasted_iota(jnp.int32, (OV, lat), 0) == 0
+
+    def sends(block):
+        own, at = rows_at(block * OV), rows_at(block * OV + OV)
+        pairs = [(u_rows.at[:, at], u_new), (v_out.at[:, own], v_new), (w_out.at[:, own], w_vel)]
+        return [
+            pltpu.make_async_copy(held, result.at[:, own], sems.at[1 + 3 * block + i])
+            for i, (held, result) in enumerate(pairs)
+        ]
+
+    def next_row(rows, after):
+        return jnp.where(last, after[:1], pltpu.roll(rows, OV - 1, 0))
+
+    def faces(block, _):
+        own, at = rows_at(block * OV), rows_at(block * OV + OV)
+        before, after = rows_at(block * OV), rows_at(block * OV + 2 * OV)
+        to_u, to_v, to_w = sends(block)
+        s, d = s_rows[at], d_rows[at]
+        slope_e = gravity_step * (next_row(s, s_rows[after]) - s)
+        face_e = jnp.minimum(d, next_row(d, d_rows[after]))
+        slope_n = gravity_step * (jnp.concatenate([s[:, 1:], zero], axis=1) - s)
+        face_n = jnp.minimum(d, jnp.concatenate([d[:, 1:], zero], axis=1))
         w_sum = jnp.zeros((OV, lat), F32)
         for level in range(KL - 1, -1, -1):
-            v = v_out[level, own]
-            flow = u_rows[level, at : at + OV] - u_rows[level, at - 1 : at + OV - 1]
-            flow = flow + (v - jnp.concatenate([zero, v[:, :-1]], axis=1))
-            w_sum = w_sum + jnp.where(d > level, flow, 0.0)
+            u = jnp.where(face_e > level, u_vel[level, own] - slope_e, 0.0)
+            u_rows[level, at] = u
+            v = jnp.where(face_n > level, v_vel[level, own] - slope_n, 0.0)
+            v_out[level, own] = v
+            west = jnp.where(first, u_rows[level, before][OV - 1 :], pltpu.roll(u, 1, 0))
+            south = jnp.concatenate([zero, v[:, :-1]], axis=1)
+            w_sum = w_sum + jnp.where(d > level, (u - west) + (v - south), 0.0)
             w_out[level, own] = w_sum
-        send(w_out.at[:, own], w_vel.at[:, own])
-        if at == cells:
-            send(s_out, solution)
-    for copy in copies:
-        copy.wait()
+        for copy in (to_u, to_v, to_w):
+            copy.start()
+        return 0
+
+    lax.fori_loop(0, cells // OV, faces, 0)
+    send_s.wait()
+    for block in range(cells // OV):
+        for copy in sends(block):
+            copy.wait()
 
 
 def swap_pairs(block, outward):

time: 43 us -> 43.1 us (level)
  no operation moved by 1% of the time
where the time goes in v11:
time: 43.1 us; the launch traced here: 42.9 us
  starting transfers between devices  13.8 us (32%)
  Pallas kernels  11.8 us (27%)
  blocking collectives  10.1 us (23%)
  waiting for transfers between devices  6.48 us (15%)
  between operations  0.71 us (2%)
    ppermute x8, starting transfers between devices, swap_pairs(): return lax.ppermute(block, 'lon', route)  13.8 us
    all_to_all x1, blocking collectives, body(): came = lax.all_to_all(sent, 'lon', 0, 0)  10.1 us
    ppermute x8, waiting for transfers between devices, swap_pairs(): return lax.ppermute(block, 'lon', route)  6.48 us
    pallas_call x1, Pallas kernels, body(): pl.pallas_call(finish, in_specs=[VM] * 8, out_specs=[HB] * 4, out_shape=[...  3.16 us
    pallas_call x1, Pallas kernels, body(): pl.pallas_call(absorb, in_specs=[SM, HB] + [VM] * 4 + [HB] * 2, out_specs...  2.03 us
    pallas_call x1, Pallas kernels, body(): pl.pallas_call(second_solve, in_specs=[SM] + [VM] * 7, out_specs=[VM] * 5...  1.86 us
    pallas_call x1, Pallas kernels, body(): pl.pallas_call(first_solve, in_specs=[SM] + [VM] * 6, out_specs=[VM] * 3,...  1.68 us
    pallas_call x1, Pallas kernels, body(): pl.pallas_call(prepare, in_specs=[SM] + [HB] * 8, out_specs=[VM] * 10, ou...  1.53 us
  transfers between devices with their start and end apart: 8, of which 3 were waited for; matrix products, arithmetic and copies ran while one was open for 0% of the time, Pallas kernels for 12%

profile of v11, /device:TPU:0, one launch (start us, length us, event | category | flops | bytes accessed | tf_op | source)
XLA Modules:
  0.0 42.9 jit_solution(566902772539374138)
XLA Ops:
  0.6 0.9 %first_edges.1.after = f32[8,2240]{1,0:T(8,128)S(1)} custom-call(s32[1]{0:T(128)} %bitcast.parity, f32[32,2240]{1,0:T(8,128)} %source_h.1, s32[32,2240]{1,0:T(8,128)} %bottom_h.1), custom_call_target="tpu_custom_call" | custom-call | tf_op jit(solution)/shard_map/first_edges/pallas_call | solution.py:415
  1.6 5.5 %collective-permute-start.1 = (f32[8,2240]{1,0:T(8,128)S(1)}, f32[8,2240]{1,0:T(8,128)S(1)}, u32[]{:S(2)}, u32[]{:S(2)}) collective-permute-start(f32[8,2240]{1,0:T(8,128)S(1)} %first_edges.1.after), channel_id=1, source_target_pairs={{0,15},{1,2},{2,1},{3,4},{4,3},{5,6},{6,5},{7,8},{8,7},{9,10},{10,... | collective-permute-start | bytes 215048 | tf_op jit(solution)/shard_map/ppermute | solution.py:398
  7.1 1.5 %prepare.1 = (f32[8,2240]{1,0:T(8,128)S(1)}, f32[24,2240]{1,0:T(8,128)S(1)}, f32[24,2240]{1,0:T(8,128)S(1)}, f32[32,2240]{1,0:T(8,128)S(1)}, f32[32,2240]{1,0:T(...) custom-call(s32[1]{0:T(128)} %bitcast.parity, ...), custom_call_target="tpu_custom_call" | custom-call | flops 1000000 | bytes 7000000 | tf_op jit(solution)/shard_map/prepare/pallas_call | solution.py:427
  8.6 0.1 collective-permute-start
  8.7 0.5 %collective-permute-start.4 = (f32[24,2240]{1,0:T(8,128)S(1)}, f32[24,2240]{1,0:T(8,128)S(1)}, u32[]{:S(2)}, u32[]{:S(2)}) collective-permute-start(f32[24,2240]{1,0:T(8,128)S(1)} %get-tuple-element.37), channel_id=1, source_target_pairs={{0,1},{1,0},{2,3},{3,2},{4,5},{5,4},{6,7},{7,6},{8,9},{9,8},{10,11... | collective-permute-start | bytes 645128 | tf_op jit(solution)/shard_map/ppermute | solution.py:398
  9.2 0.3 collective-permute-start.5
  9.5 0.0 collective-permute-done.1.outer_in
  9.5 0.5 %collective-permute-done.inner_in = f32[8,2240]{1,0:T(8,128)S(1)} collective-permute-done((f32[8,2240]{1,0:T(8,128)S(1)}, f32[8,2240]{1,0:T(8,128)S(1)}, u32[]{:S(2)}, u32[]{:S(2)}) %collective-permute-start) | collective-permute-done | bytes 71712 | tf_op jit(solution)/shard_map/ppermute | solution.py:398
  10.0 1.7 %first_solve.1 = (f32[48,2240]{1,0:T(8,128)S(1)}, f32[306,128]{1,0:T(8,128)S(1)}, f32[306,128]{1,0:T(8,128)S(1)}) custom-call(s32[1]{0:T(128)} %bitcast.parity, f32[8,2240]{1,0:T(8,128)S(1)} %collective-permute-done.inner_in, f32[8,2240]{1,0:T(8,128)S(1)} %collective-permute-done.1.outer_in, f32[32,2240]{1,0:T(8,128)S(1)} %get-tuple-element.30.masked, ...), custom_call_target="tpu_custom_call" | custom-call | tf_op jit(solution)/shard_map/first_solve/pallas_call | solution.py:449
  11.6 0.2 collective-permute-start.2
  11.9 3.6 %collective-permute-start.3 = (f32[306,128]{1,0:T(8,128)S(1)}, f32[306,128]{1,0:T(8,128)S(1)}, u32[]{:S(2)}, u32[]{:S(2)}) collective-permute-start(f32[306,128]{1,0:T(8,128)S(1)} %get-tuple-element.35), channel_id=1, source_target_pairs={{0,15},{1,2},{2,1},{3,4},{4,3},{5,6},{6,5},{7,8},{8,7},{9,10},{10,... | collective-permute-start | bytes 470024 | tf_op jit(solution)/shard_map/ppermute | solution.py:398
  15.5 0.0 collective-permute-done.4.inner_in
  15.5 1.9 %collective-permute-done.5.outer_in = f32[24,2240]{1,0:T(8,128)S(1)} collective-permute-done((f32[24,2240]{1,0:T(8,128)S(1)}, f32[24,2240]{1,0:T(8,128)S(1)}, u32[]{:S(2)}, u32[]{:S(2)}) %collective-permute-start.5) | collective-permute-done | bytes 215072 | tf_op jit(solution)/shard_map/ppermute | solution.py:398
  17.4 2.0 %absorb.1 = (f32[64,2240]{1,0:T(8,128)S(1)}, f32[48,2240]{1,0:T(8,128)S(1)}, f32[8,2240]{1,0:T(8,128)S(1)}, f32[6,32,2240]{2,1,0:T(8,128)S(1)}, f32[6,32,2240]{2,1,0:T(8,128)S(1)}) custom-call(s32[1]{0:T(128)} %bitcast.parity, f32[48,2240]{1,0:T(8,128)S(1)} %get-tuple-element.36.after.first, f32[24,2240]{1,0:T(8,128)S(1)} %collective-permute-done.4.inner_in, ...), custom_call_target="tpu_custom_call" | custom-call | flops 1000000 | bytes 7000000 | tf_op jit(solution)/shard_map/absorb/pallas_call | solution.py:460
  19.4 0.0 collective-permute-done.2.inner_in
  19.4 0.0 collective-permute-done.3.outer_in
  19.4 1.9 %second_solve.1 = (f32[48,2240]{1,0:T(8,128)S(1)}, f32[48,2240]{1,0:T(8,128)S(1)}, f32[48,2240]{1,0:T(8,128)S(1)}, f32[162,128]{1,0:T(8,128)S(1)}, f32[162,128]{1,0:T(8,128)S(1)}) custom-call(s32[1]{0:T(128)} %bitcast.parity, f32[306,128]{1,0:T(8,128)S(1)} %collective-permute-done.2.inner_in, f32[306,128]{1,0:T(8,128)S(1)} %collective-permute-done.3.outer_in, ...), custom_call_target="tpu_custom_call" | custom-call | tf_op jit(solution)/shard_map/second_solve/pallas_call | solution.py:472
  21.3 1.1 %collective-permute-start.6 = (f32[162,128]{1,0:T(8,128)S(1)}, f32[162,128]{1,0:T(8,128)S(1)}, u32[]{:S(2)}, u32[]{:S(2)}) collective-permute-start(f32[162,128]{1,0:T(8,128)S(1)} %get-tuple-element.42), channel_id=1, source_target_pairs={{0,1},{1,0},{2,3},{3,2},{4,5},{5,4},{6,7},{7,6},{8,9},{9,8},{10,11... | collective-permute-start | bytes 248840 | tf_op jit(solution)/shard_map/ppermute | solution.py:398
  22.4 2.5 %collective-permute-start.7 = (f32[162,128]{1,0:T(8,128)S(1)}, f32[162,128]{1,0:T(8,128)S(1)}, u32[]{:S(2)}, u32[]{:S(2)}) collective-permute-start(f32[162,128]{1,0:T(8,128)S(1)} %get-tuple-element.43), channel_id=1, source_target_pairs={{0,15},{1,2},{2,1},{3,4},{4,3},{5,6},{6,5},{7,8},{8,7},{9,10},{10,... | collective-permute-start | bytes 248840 | tf_op jit(solution)/shard_map/ppermute | solution.py:398
  24.9 0.0 collective-permute-done.6.inner_in
  24.9 4.1 %collective-permute-done.7.outer_in = f32[162,128]{1,0:T(8,128)S(1)} collective-permute-done((f32[162,128]{1,0:T(8,128)S(1)}, f32[162,128]{1,0:T(8,128)S(1)}, u32[]{:S(2)}, u32[]{:S(2)}) %collective-permute-start.7) | collective-permute-done | bytes 82976 | tf_op jit(solution)/shard_map/ppermute | solution.py:398
  29.0 0.6 %sums.1 = (f32[48,2240]{1,0:T(8,128)S(1)}, f32[16,1,128]{2,1,0:T(1,128)S(1)}) custom-call(s32[1]{0:T(128)} %bitcast.parity, f32[162,128]{1,0:T(8,128)S(1)} %collective-permute-done.6.inner_in, f32[162,128]{1,0:T(8,128)S(1)} %collective-permute-done.7.outer_in, f32[48,2240]{1,0:T(8,128)S(1)} %get-tuple-element.44.second, f32[48,2240]{1,0:T(8,128)S(1)} %get-tuple-element.45.z, ...), custom_call_target="tpu_custom_call" | custom-call | tf_op jit(solution)/shard_map/sums/pallas_call | solution.py:483
  29.7 10.1 %all_to_all.5.came = f32[16,1,128]{2,1,0:T(1,128)S(1)} all-to-all(f32[16,1,128]{2,1,0:T(1,128)S(1)} %get-tuple-element.48), channel_id=1, replica_groups=mesh['members'=2,'lon'=16] {'lon'}, dimensions={0} | all-to-all | bytes 16384 | tf_op jit(solution)/shard_map/all_to_all | solution.py:491
  39.7 3.2 %finish.1 = (f32[32,2240]{1,0:T(8,128)}, f32[6,32,2240]{2,1,0:T(8,128)}, f32[6,32,2240]{2,1,0:T(8,128)}, f32[6,32,2240]{2,1,0:T(8,128)}) custom-call(f32[16,1,128]{2,1,0:T(1,128)S(1)} %all_to_all.5.came, f32[48,2240]{1,0:T(8,128)S(1)} %get-tuple-element.45.z, f32[48,2240]{1,0:T(8,128)S(1)} %get-tuple-element.49.w, f32[48,2240]{1,0:T(8,128)S(1)} %get-tuple-element.50.d_rows, ...), custom_call_target="tpu_custom_call" | custom-call | tf_op jit(solution)/shard_map/finish/pallas_call | solution.py:493
Async XLA Ops:
  1.6 7.9 %collective-permute-start.1 = (f32[8,2240]{1,0:T(8,128)S(1)}, f32[8,2240]{1,0:T(8,128)S(1)}, u32[]{:S(2)}, u32[]{:S(2)}) collective-permute-start(f32[8,2240]{1,0:T(8,128)S(1)} %first_edges.1.after), channel_id=1, source_target_pairs={{0,15},{1,2},{2,1},{3,4},{4,3},{5,6},{6,5},{7,8},{8,7},{9,10},{10,... | collective-permute-start | bytes 215048 | tf_op jit(solution)/shard_map/ppermute | solution.py:398
  8.6 1.3 %collective-permute-start = (f32[8,2240]{1,0:T(8,128)S(1)}, f32[8,2240]{1,0:T(8,128)S(1)}, u32[]{:S(2)}, u32[]{:S(2)}) collective-permute-start(f32[8,2240]{1,0:T(8,128)S(1)} %get-tuple-element.29), channel_id=1, source_target_pairs={{0,1},{1,0},{2,3},{3,2},{4,5},{5,4},{6,7},{7,6},{8,9},{9,8},{10,11... | collective-permute-start | bytes 215048 | tf_op jit(solution)/shard_map/ppermute | solution.py:398
  8.7 6.8 %collective-permute-start.4 = (f32[24,2240]{1,0:T(8,128)S(1)}, f32[24,2240]{1,0:T(8,128)S(1)}, u32[]{:S(2)}, u32[]{:S(2)}) collective-permute-start(f32[24,2240]{1,0:T(8,128)S(1)} %get-tuple-element.37), channel_id=1, source_target_pairs={{0,1},{1,0},{2,3},{3,2},{4,5},{5,4},{6,7},{7,6},{8,9},{9,8},{10,11... | collective-permute-start | bytes 645128 | tf_op jit(solution)/shard_map/ppermute | solution.py:398
  9.2 8.2 %collective-permute-start.5 = (f32[24,2240]{1,0:T(8,128)S(1)}, f32[24,2240]{1,0:T(8,128)S(1)}, u32[]{:S(2)}, u32[]{:S(2)}) collective-permute-start(f32[24,2240]{1,0:T(8,128)S(1)} %get-tuple-element.38), channel_id=1, source_target_pairs={{0,15},{1,2},{2,1},{3,4},{4,3},{5,6},{6,5},{7,8},{8,7},{9,10},{10,... | collective-permute-start | bytes 645128 | tf_op jit(solution)/shard_map/ppermute | solution.py:398
  11.6 7.8 %collective-permute-start.2 = (f32[306,128]{1,0:T(8,128)S(1)}, f32[306,128]{1,0:T(8,128)S(1)}, u32[]{:S(2)}, u32[]{:S(2)}) collective-permute-start(f32[306,128]{1,0:T(8,128)S(1)} %get-tuple-element.34), channel_id=1, source_target_pairs={{0,1},{1,0},{2,3},{3,2},{4,5},{5,4},{6,7},{7,6},{8,9},{9,8},{10,11... | collective-permute-start | bytes 470024 | tf_op jit(solution)/shard_map/ppermute | solution.py:398
  11.9 7.5 %collective-permute-start.3 = (f32[306,128]{1,0:T(8,128)S(1)}, f32[306,128]{1,0:T(8,128)S(1)}, u32[]{:S(2)}, u32[]{:S(2)}) collective-permute-start(f32[306,128]{1,0:T(8,128)S(1)} %get-tuple-element.35), channel_id=1, source_target_pairs={{0,15},{1,2},{2,1},{3,4},{4,3},{5,6},{6,5},{7,8},{8,7},{9,10},{10,... | collective-permute-start | bytes 470024 | tf_op jit(solution)/shard_map/ppermute | solution.py:398
  21.3 3.6 %collective-permute-start.6 = (f32[162,128]{1,0:T(8,128)S(1)}, f32[162,128]{1,0:T(8,128)S(1)}, u32[]{:S(2)}, u32[]{:S(2)}) collective-permute-start(f32[162,128]{1,0:T(8,128)S(1)} %get-tuple-element.42), channel_id=1, source_target_pairs={{0,1},{1,0},{2,3},{3,2},{4,5},{5,4},{6,7},{7,6},{8,9},{9,8},{10,11... | collective-permute-start | bytes 248840 | tf_op jit(solution)/shard_map/ppermute | solution.py:398
  22.4 6.6 %collective-permute-start.7 = (f32[162,128]{1,0:T(8,128)S(1)}, f32[162,128]{1,0:T(8,128)S(1)}, u32[]{:S(2)}, u32[]{:S(2)}) collective-permute-start(f32[162,128]{1,0:T(8,128)S(1)} %get-tuple-element.43), channel_id=1, source_target_pairs={{0,15},{1,2},{2,1},{3,4},{4,3},{5,6},{6,5},{7,8},{8,7},{9,10},{10,... | collective-permute-start | bytes 248840 | tf_op jit(solution)/shard_map/ppermute | solution.py:398

commit v12 on v10

--- a/solution.py
+++ b/solution.py
@@ -471,7 +471,8 @@
         compiler_params=PARAMS,
         name="sums",
     )(parity, *near, second, z, y, c_rows, source_v)
-    came = lax.all_to_all(sent, "lon", 0, 0)
+    ring = [list(reversed(range(devices)))]
+    came = lax.all_to_all(sent, "lon", 0, 0, axis_index_groups=ring)
 
     return pl.pallas_call(
         finish,

time: 43 us -> 40.8 us (0.949)
  blocking collectives: 10.1 us -> 7.9 us
    all_to_all x1, blocking collectives: 10.1 us -> 7.9 us  [body(): came = lax.all_to_all(sent, 'lon', 0, 0, axis_index_groups=ring)]
  transfers between devices with their start and end apart: 8 -> 8, of which waited for: 3 -> 3; matrix products, arithmetic and copies ran while one was open for 0% -> 0% of each run, Pallas kernels for 12% -> 13%
where the time goes in v12:
time: 40.8 us; the launch traced here: 40.6 us
  starting transfers between devices  13.8 us (34%)
  Pallas kernels  11.7 us (29%)
  blocking collectives  7.9 us (19%)
  waiting for transfers between devices  6.48 us (16%)
  between operations  0.71 us (2%)
    ppermute x8, starting transfers between devices, swap_pairs(): return lax.ppermute(block, 'lon', route)  13.8 us
    all_to_all x1, blocking collectives, body(): came = lax.all_to_all(sent, 'lon', 0, 0, axis_index_groups=ring)  7.9 us
    ppermute x8, waiting for transfers between devices, swap_pairs(): return lax.ppermute(block, 'lon', route)  6.48 us
    pallas_call x1, Pallas kernels, body(): pl.pallas_call(finish, in_specs=[VM] * 8, out_specs=[HB] * 4, out_shape=[...  3.02 us
    pallas_call x1, Pallas kernels, body(): pl.pallas_call(absorb, in_specs=[SM, HB] + [VM] * 4 + [HB] * 2, out_specs...  2.03 us
    pallas_call x1, Pallas kernels, body(): pl.pallas_call(second_solve, in_specs=[SM] + [VM] * 7, out_specs=[VM] * 5...  1.86 us
    pallas_call x1, Pallas kernels, body(): pl.pallas_call(first_solve, in_specs=[SM] + [VM] * 6, out_specs=[VM] * 3,...  1.68 us
    pallas_call x1, Pallas kernels, body(): pl.pallas_call(prepare, in_specs=[SM] + [HB] * 8, out_specs=[VM] * 10, ou...  1.53 us
  transfers between devices with their start and end apart: 8, of which 3 were waited for; matrix products, arithmetic and copies ran while one was open for 0% of the time, Pallas kernels for 13%

profile of v12, /device:TPU:0, one launch (start us, length us, event | category | flops | bytes accessed | tf_op | source)
XLA Modules:
  0.0 40.6 jit_solution(5118806315421534662)
XLA Ops:
  0.6 0.9 %first_edges.1.after = f32[8,2240]{1,0:T(8,128)S(1)} custom-call(s32[1]{0:T(128)} %bitcast.parity, f32[32,2240]{1,0:T(8,128)} %source_h.1, s32[32,2240]{1,0:T(8,128)} %bottom_h.1), custom_call_target="tpu_custom_call" | custom-call | tf_op jit(solution)/shard_map/first_edges/pallas_call | solution.py:398
  1.6 5.5 %collective-permute-start.1 = (f32[8,2240]{1,0:T(8,128)S(1)}, f32[8,2240]{1,0:T(8,128)S(1)}, u32[]{:S(2)}, u32[]{:S(2)}) collective-permute-start(f32[8,2240]{1,0:T(8,128)S(1)} %first_edges.1.after), channel_id=1, source_target_pairs={{0,15},{1,2},{2,1},{3,4},{4,3},{5,6},{6,5},{7,8},{8,7},{9,10},{10,... | collective-permute-start | bytes 215048 | tf_op jit(solution)/shard_map/ppermute | solution.py:381
  7.1 1.5 %prepare.1 = (f32[8,2240]{1,0:T(8,128)S(1)}, f32[24,2240]{1,0:T(8,128)S(1)}, f32[24,2240]{1,0:T(8,128)S(1)}, f32[32,2240]{1,0:T(8,128)S(1)}, f32[32,2240]{1,0:T(...) custom-call(s32[1]{0:T(128)} %bitcast.parity, ...), custom_call_target="tpu_custom_call" | custom-call | flops 1000000 | bytes 7000000 | tf_op jit(solution)/shard_map/prepare/pallas_call | solution.py:410
  8.6 0.1 collective-permute-start
  8.7 0.5 %collective-permute-start.4 = (f32[24,2240]{1,0:T(8,128)S(1)}, f32[24,2240]{1,0:T(8,128)S(1)}, u32[]{:S(2)}, u32[]{:S(2)}) collective-permute-start(f32[24,2240]{1,0:T(8,128)S(1)} %get-tuple-element.37), channel_id=1, source_target_pairs={{0,1},{1,0},{2,3},{3,2},{4,5},{5,4},{6,7},{7,6},{8,9},{9,8},{10,11... | collective-permute-start | bytes 645128 | tf_op jit(solution)/shard_map/ppermute | solution.py:381
  9.2 0.3 collective-permute-start.5
  9.5 0.0 collective-permute-done.1.outer_in
  9.5 0.5 %collective-permute-done.inner_in = f32[8,2240]{1,0:T(8,128)S(1)} collective-permute-done((f32[8,2240]{1,0:T(8,128)S(1)}, f32[8,2240]{1,0:T(8,128)S(1)}, u32[]{:S(2)}, u32[]{:S(2)}) %collective-permute-start) | collective-permute-done | bytes 71712 | tf_op jit(solution)/shard_map/ppermute | solution.py:381
  10.0 1.7 %first_solve.1 = (f32[48,2240]{1,0:T(8,128)S(1)}, f32[306,128]{1,0:T(8,128)S(1)}, f32[306,128]{1,0:T(8,128)S(1)}) custom-call(s32[1]{0:T(128)} %bitcast.parity, f32[8,2240]{1,0:T(8,128)S(1)} %collective-permute-done.inner_in, f32[8,2240]{1,0:T(8,128)S(1)} %collective-permute-done.1.outer_in, f32[32,2240]{1,0:T(8,128)S(1)} %get-tuple-element.30.masked, ...), custom_call_target="tpu_custom_call" | custom-call | tf_op jit(solution)/shard_map/first_solve/pallas_call | solution.py:432
  11.6 0.2 collective-permute-start.2
  11.9 3.6 %collective-permute-start.3 = (f32[306,128]{1,0:T(8,128)S(1)}, f32[306,128]{1,0:T(8,128)S(1)}, u32[]{:S(2)}, u32[]{:S(2)}) collective-permute-start(f32[306,128]{1,0:T(8,128)S(1)} %get-tuple-element.35), channel_id=1, source_target_pairs={{0,15},{1,2},{2,1},{3,4},{4,3},{5,6},{6,5},{7,8},{8,7},{9,10},{10,... | collective-permute-start | bytes 470024 | tf_op jit(solution)/shard_map/ppermute | solution.py:381
  15.5 0.0 collective-permute-done.4.inner_in
  15.5 1.9 %collective-permute-done.5.outer_in = f32[24,2240]{1,0:T(8,128)S(1)} collective-permute-done((f32[24,2240]{1,0:T(8,128)S(1)}, f32[24,2240]{1,0:T(8,128)S(1)}, u32[]{:S(2)}, u32[]{:S(2)}) %collective-permute-start.5) | collective-permute-done | bytes 215072 | tf_op jit(solution)/shard_map/ppermute | solution.py:381
  17.4 2.0 %absorb.1 = (f32[64,2240]{1,0:T(8,128)S(1)}, f32[48,2240]{1,0:T(8,128)S(1)}, f32[8,2240]{1,0:T(8,128)S(1)}, f32[6,32,2240]{2,1,0:T(8,128)S(1)}, f32[6,32,2240]{2,1,0:T(8,128)S(1)}) custom-call(s32[1]{0:T(128)} %bitcast.parity, f32[48,2240]{1,0:T(8,128)S(1)} %get-tuple-element.36.after.first, f32[24,2240]{1,0:T(8,128)S(1)} %collective-permute-done.4.inner_in, ...), custom_call_target="tpu_custom_call" | custom-call | flops 1000000 | bytes 7000000 | tf_op jit(solution)/shard_map/absorb/pallas_call | solution.py:443
  19.4 0.0 collective-permute-done.2.inner_in
  19.4 0.0 collective-permute-done.3.outer_in
  19.4 1.9 %second_solve.1 = (f32[48,2240]{1,0:T(8,128)S(1)}, f32[48,2240]{1,0:T(8,128)S(1)}, f32[48,2240]{1,0:T(8,128)S(1)}, f32[162,128]{1,0:T(8,128)S(1)}, f32[162,128]{1,0:T(8,128)S(1)}) custom-call(s32[1]{0:T(128)} %bitcast.parity, f32[306,128]{1,0:T(8,128)S(1)} %collective-permute-done.2.inner_in, f32[306,128]{1,0:T(8,128)S(1)} %collective-permute-done.3.outer_in, ...), custom_call_target="tpu_custom_call" | custom-call | tf_op jit(solution)/shard_map/second_solve/pallas_call | solution.py:455
  21.3 1.1 %collective-permute-start.6 = (f32[162,128]{1,0:T(8,128)S(1)}, f32[162,128]{1,0:T(8,128)S(1)}, u32[]{:S(2)}, u32[]{:S(2)}) collective-permute-start(f32[162,128]{1,0:T(8,128)S(1)} %get-tuple-element.42), channel_id=1, source_target_pairs={{0,1},{1,0},{2,3},{3,2},{4,5},{5,4},{6,7},{7,6},{8,9},{9,8},{10,11... | collective-permute-start | bytes 248840 | tf_op jit(solution)/shard_map/ppermute | solution.py:381
  22.4 2.5 %collective-permute-start.7 = (f32[162,128]{1,0:T(8,128)S(1)}, f32[162,128]{1,0:T(8,128)S(1)}, u32[]{:S(2)}, u32[]{:S(2)}) collective-permute-start(f32[162,128]{1,0:T(8,128)S(1)} %get-tuple-element.43), channel_id=1, source_target_pairs={{0,15},{1,2},{2,1},{3,4},{4,3},{5,6},{6,5},{7,8},{8,7},{9,10},{10,... | collective-permute-start | bytes 248840 | tf_op jit(solution)/shard_map/ppermute | solution.py:381
  24.9 0.0 collective-permute-done.6.inner_in
  24.9 4.1 %collective-permute-done.7.outer_in = f32[162,128]{1,0:T(8,128)S(1)} collective-permute-done((f32[162,128]{1,0:T(8,128)S(1)}, f32[162,128]{1,0:T(8,128)S(1)}, u32[]{:S(2)}, u32[]{:S(2)}) %collective-permute-start.7) | collective-permute-done | bytes 82976 | tf_op jit(solution)/shard_map/ppermute | solution.py:381
  29.0 0.6 %sums.1 = (f32[48,2240]{1,0:T(8,128)S(1)}, f32[16,1,128]{2,1,0:T(1,128)S(1)}) custom-call(s32[1]{0:T(128)} %bitcast.parity, f32[162,128]{1,0:T(8,128)S(1)} %collective-permute-done.6.inner_in, f32[162,128]{1,0:T(8,128)S(1)} %collective-permute-done.7.outer_in, f32[48,2240]{1,0:T(8,128)S(1)} %get-tuple-element.44.second, f32[48,2240]{1,0:T(8,128)S(1)} %get-tuple-element.45.z, ...), custom_call_target="tpu_custom_call" | custom-call | tf_op jit(solution)/shard_map/sums/pallas_call | solution.py:466
  29.7 7.9 %all_to_all.5.came = f32[16,1,128]{2,1,0:T(1,128)S(1)} all-to-all(f32[16,1,128]{2,1,0:T(1,128)S(1)} %get-tuple-element.48), channel_id=1, replica_groups={{15,14,13,12,11,10,9,8,7,6,5,4,3,2,1,0},{31,30,29,28,27,26,25,24,23,22,..., dimensions={0} | all-to-all | bytes 16384 | tf_op jit(solution)/shard_map/all_to_all | solution.py:475
  37.6 3.0 %finish.1 = (f32[32,2240]{1,0:T(8,128)}, f32[6,32,2240]{2,1,0:T(8,128)}, f32[6,32,2240]{2,1,0:T(8,128)}, f32[6,32,2240]{2,1,0:T(8,128)}) custom-call(f32[16,1,128]{2,1,0:T(1,128)S(1)} %all_to_all.5.came, f32[48,2240]{1,0:T(8,128)S(1)} %get-tuple-element.45.z, f32[48,2240]{1,0:T(8,128)S(1)} %get-tuple-element.49.w, f32[48,2240]{1,0:T(8,128)S(1)} %get-tuple-element.50.d_rows, ...), custom_call_target="tpu_custom_call" | custom-call | tf_op jit(solution)/shard_map/finish/pallas_call | solution.py:477
Async XLA Ops:
  1.6 7.9 %collective-permute-start.1 = (f32[8,2240]{1,0:T(8,128)S(1)}, f32[8,2240]{1,0:T(8,128)S(1)}, u32[]{:S(2)}, u32[]{:S(2)}) collective-permute-start(f32[8,2240]{1,0:T(8,128)S(1)} %first_edges.1.after), channel_id=1, source_target_pairs={{0,15},{1,2},{2,1},{3,4},{4,3},{5,6},{6,5},{7,8},{8,7},{9,10},{10,... | collective-permute-start | bytes 215048 | tf_op jit(solution)/shard_map/ppermute | solution.py:381
  8.6 1.3 %collective-permute-start = (f32[8,2240]{1,0:T(8,128)S(1)}, f32[8,2240]{1,0:T(8,128)S(1)}, u32[]{:S(2)}, u32[]{:S(2)}) collective-permute-start(f32[8,2240]{1,0:T(8,128)S(1)} %get-tuple-element.29), channel_id=1, source_target_pairs={{0,1},{1,0},{2,3},{3,2},{4,5},{5,4},{6,7},{7,6},{8,9},{9,8},{10,11... | collective-permute-start | bytes 215048 | tf_op jit(solution)/shard_map/ppermute | solution.py:381
  8.7 6.8 %collective-permute-start.4 = (f32[24,2240]{1,0:T(8,128)S(1)}, f32[24,2240]{1,0:T(8,128)S(1)}, u32[]{:S(2)}, u32[]{:S(2)}) collective-permute-start(f32[24,2240]{1,0:T(8,128)S(1)} %get-tuple-element.37), channel_id=1, source_target_pairs={{0,1},{1,0},{2,3},{3,2},{4,5},{5,4},{6,7},{7,6},{8,9},{9,8},{10,11... | collective-permute-start | bytes 645128 | tf_op jit(solution)/shard_map/ppermute | solution.py:381
  9.2 8.2 %collective-permute-start.5 = (f32[24,2240]{1,0:T(8,128)S(1)}, f32[24,2240]{1,0:T(8,128)S(1)}, u32[]{:S(2)}, u32[]{:S(2)}) collective-permute-start(f32[24,2240]{1,0:T(8,128)S(1)} %get-tuple-element.38), channel_id=1, source_target_pairs={{0,15},{1,2},{2,1},{3,4},{4,3},{5,6},{6,5},{7,8},{8,7},{9,10},{10,... | collective-permute-start | bytes 645128 | tf_op jit(solution)/shard_map/ppermute | solution.py:381
  11.6 7.8 %collective-permute-start.2 = (f32[306,128]{1,0:T(8,128)S(1)}, f32[306,128]{1,0:T(8,128)S(1)}, u32[]{:S(2)}, u32[]{:S(2)}) collective-permute-start(f32[306,128]{1,0:T(8,128)S(1)} %get-tuple-element.34), channel_id=1, source_target_pairs={{0,1},{1,0},{2,3},{3,2},{4,5},{5,4},{6,7},{7,6},{8,9},{9,8},{10,11... | collective-permute-start | bytes 470024 | tf_op jit(solution)/shard_map/ppermute | solution.py:381
  11.9 7.5 %collective-permute-start.3 = (f32[306,128]{1,0:T(8,128)S(1)}, f32[306,128]{1,0:T(8,128)S(1)}, u32[]{:S(2)}, u32[]{:S(2)}) collective-permute-start(f32[306,128]{1,0:T(8,128)S(1)} %get-tuple-element.35), channel_id=1, source_target_pairs={{0,15},{1,2},{2,1},{3,4},{4,3},{5,6},{6,5},{7,8},{8,7},{9,10},{10,... | collective-permute-start | bytes 470024 | tf_op jit(solution)/shard_map/ppermute | solution.py:381
  21.3 3.6 %collective-permute-start.6 = (f32[162,128]{1,0:T(8,128)S(1)}, f32[162,128]{1,0:T(8,128)S(1)}, u32[]{:S(2)}, u32[]{:S(2)}) collective-permute-start(f32[162,128]{1,0:T(8,128)S(1)} %get-tuple-element.42), channel_id=1, source_target_pairs={{0,1},{1,0},{2,3},{3,2},{4,5},{5,4},{6,7},{7,6},{8,9},{9,8},{10,11... | collective-permute-start | bytes 248840 | tf_op jit(solution)/shard_map/ppermute | solution.py:381
  22.4 6.6 %collective-permute-start.7 = (f32[162,128]{1,0:T(8,128)S(1)}, f32[162,128]{1,0:T(8,128)S(1)}, u32[]{:S(2)}, u32[]{:S(2)}) collective-permute-start(f32[162,128]{1,0:T(8,128)S(1)} %get-tuple-element.43), channel_id=1, source_target_pairs={{0,15},{1,2},{2,1},{3,4},{4,3},{5,6},{6,5},{7,8},{8,7},{9,10},{10,... | collective-permute-start | bytes 248840 | tf_op jit(solution)/shard_map/ppermute | solution.py:381

commit v13 on v12

--- a/solution.py
+++ b/solution.py
@@ -221,7 +221,7 @@
     pack(outer, to_outer)
 
 
-def absorb(parity, after, inner_in, outer_in, coef, depth, u_h, v_h, c_rows, d_rows, edge, u, v, sems):
+def absorb(parity, first, inner_in, outer_in, coef, depth, u_h, v_h, c_rows, z_rows, d_rows, edge, u, v, sems):
     cells, lat = coef.shape
     copies = [pltpu.make_async_copy(a, b, sems.at[i]) for i, (a, b) in enumerate([(u_h, u), (v_h, v)])]
     for copy in copies:
@@ -236,26 +236,27 @@
     c_rows[2 * OV : 2 * OV + cells] = coef[...]
     c_rows[2 * OV + cells :] = east
     c_rows[3 * OV + cells + 1 :] = jnp.zeros((OV - 1, lat), F32)
+    z_rows[:OV] = jnp.zeros((OV, lat), F32)
+    z_rows[3 * OV + cells :] = jnp.zeros((OV, lat), F32)
+    inside = slice(OV, 3 * OV + cells)
+    z_rows[inside] = jnp.where(c_rows[inside] > 0, first[...], 0.0)
     for copy in copies:
         copy.wait()
 
 
-def second_solve(parity, inner_in, outer_in, first, c_rows, lat_basis, lon, scale,
-                 z, y, second, inner, outer, wide, rows, spectral, m_rows):
-    span, lat = first.shape
+def second_solve(parity, outer_in, inner_in, z_rows, c_rows, lat_basis, lon, scale,
+                 z, y, second, inner, outer, wide, rows, spectral):
+    span, lat = y.shape
     cells = span - 2 * OV
     reach = 2 * OV + 1
     west, east = pick(parity, unpack(inner_in, reach, lat), unpack(outer_in, reach, lat))
-    m_rows[:OV] = jnp.zeros((OV, lat), F32)
-    m_rows[OV : OV + span] = first[...]
-    m_rows[OV + span :] = jnp.zeros((OV, lat), F32)
-    m_rows[OV - 1 : OV - 1 + reach] += west
-    m_rows[OV + cells : OV + cells + reach] += east
-    m_rows[...] = jnp.where(c_rows[...] > 0, m_rows[...], 0.0)
+    z[...] = z_rows[...]
+    for came, start in ((west, OV - 1), (east, OV + cells)):
+        at = slice(start, start + reach)
+        z[at] += jnp.where(c_rows[at] > 0, came, 0.0)
     inside = slice(OV, OV + span)
-    c, m = c_rows[inside], m_rows[inside]
-    z[...] = m
-    beside = m_rows[OV - 1 : OV - 1 + span] + m_rows[OV + 1 : OV + 1 + span]
+    c, m = c_rows[inside], z[inside]
+    beside = z[OV - 1 : OV - 1 + span] + z[OV + 1 : OV + 1 + span]
     image = jnp.where(c > 0, c * m - (beside + lat_beside(m)), 0.0)
     y[...] = image
     wide[:, :lat] = image
@@ -266,42 +267,55 @@
     pack(outer, to_outer)
 
 
-def sums(parity, inner_in, outer_in, second, z, y, c_rows, source, w, sent):
+def dot(a, b):
+    cells, lat = a.shape
+    product = a * b
+    rows = product[:OV]
+    for at in range(OV, cells, OV):
+        rows = rows + product[at : at + OV]
+    whole = lat // LANE * LANE
+    total = rows[:, :LANE]
+    for at in range(LANE, whole, LANE):
+        total = total + rows[:, at : at + LANE]
+    if whole < lat:
+        blank = jnp.zeros((OV, LANE - lat + whole), F32)
+        total = total + jnp.concatenate([rows[:, whole:], blank], axis=1)
+    return jnp.sum(jnp.sum(total, axis=0, keepdims=True), axis=1, keepdims=True)
+
+
+def in_lanes(row, sums):
+    lane = lax.broadcasted_iota(jnp.int32, row.shape, 1)
+    for i, value in sums.items():
+        row = jnp.where(lane == i, value, row)
+    return row
+
+
+def early_sums(z, y, c_rows, second, source, w_rows, masked, row):
     cells, lat = source.shape
+    inside = slice(OV, 3 * OV + cells)
+    w_rows[...] = jnp.where(c_rows[inside] > 0, second[...], 0.0)
+    own = slice(2 * OV, 2 * OV + cells)
+    wet = c_rows[own] > 0
+    masked[...] = jnp.where(wet, source[...], 0.0)
+    land = jnp.where(wet, 0.0, source[...])
+    z_own = z[own]
+    sums_of = {0: dot(masked[...], z_own), 1: dot(z_own, y[OV : OV + cells]), 6: dot(land, land)}
+    row[...] = in_lanes(jnp.zeros((1, LANE), F32), sums_of)
+
+
+def sums(parity, outer_in, inner_in, w_rows, z, y, c_rows, masked, row, w, sent):
+    cells, lat = masked.shape
     west, east = pick(parity, unpack(inner_in, OV + 1, lat), unpack(outer_in, OV + 1, lat))
-    w[...] = second[...]
-    w[OV - 1 : 2 * OV] += west
-    w[cells : cells + OV + 1] += east
-    w[...] = jnp.where(c_rows[OV : 3 * OV + cells] > 0, w[...], 0.0)
+    w[...] = w_rows[...]
+    for came, start in ((west, OV - 1), (east, cells)):
+        wet = c_rows[OV + start : 2 * OV + start + 1] > 0
+        w[start : start + OV + 1] += jnp.where(wet, came, 0.0)
     own = slice(OV, OV + cells)
     c, m = c_rows[2 * OV : 2 * OV + cells], w[own]
-    wet = c > 0
     beside = w[OV - 1 : OV - 1 + cells] + w[OV + 1 : OV + 1 + cells]
-    x = jnp.where(wet, c * m - (beside + lat_beside(m)), 0.0)
-    masked = jnp.where(wet, source[...], 0.0)
-    land = jnp.where(wet, 0.0, source[...])
-    z_own, y_own = z[own], y[own]
-
-    def partial(a, b):
-        product = a * b
-        rows = product[:OV]
-        for at in range(OV, cells, OV):
-            rows = rows + product[at : at + OV]
-        whole = lat // LANE * LANE
-        total = rows[:, :LANE]
-        for at in range(LANE, whole, LANE):
-            total = total + rows[:, at : at + LANE]
-        if whole < lat:
-            blank = jnp.zeros((OV, LANE - lat + whole), F32)
-            total = total + jnp.concatenate([rows[:, whole:], blank], axis=1)
-        return jnp.sum(jnp.sum(total, axis=0, keepdims=True), axis=1, keepdims=True)
-
-    pairs = [(masked, z_own), (z_own, y_own), (masked, m), (y_own, m), (z_own, x), (m, x), (land, land)]
-    lane = lax.broadcasted_iota(jnp.int32, (1, LANE), 1)
-    row = jnp.zeros((1, LANE), F32)
-    for i, (a, b) in enumerate(pairs):
-        row = jnp.where(lane == i, partial(a, b), row)
-    sent[...] = jnp.broadcast_to(row[None], sent.shape)
+    x = jnp.where(c > 0, c * m - (beside + lat_beside(m)), 0.0)
+    sums_of = {2: dot(masked[...], m), 3: dot(y[own], m), 4: dot(z[2 * OV : 2 * OV + cells], x), 5: dot(m, x)}
+    sent[...] = jnp.broadcast_to(in_lanes(row[...], sums_of)[None], sent.shape)
 
 
 def finish(came, z, w, d_rows, edge, source, u_vel, v_vel, solution, u_new, v_new, w_vel,
@@ -329,7 +343,7 @@
         copies[-1].start()
 
     def surface_rows(at):
-        s = of_z * z[at : at + OV] + of_w * w[at : at + OV]
+        s = of_z * z[at + OV : at + 2 * OV] + of_w * w[at : at + OV]
         if OV <= at < OV + cells:
             s = jnp.where(d_rows[at : at + OV] > 0, s, of_land * source[at - OV : at])
             s_out[at - OV : at] = s
@@ -381,6 +395,11 @@
     return lax.ppermute(block, "lon", route)
 
 
+def swap(inner, outer):
+    outer = swap_pairs(outer, True)
+    return outer, swap_pairs(inner, False)
+
+
 def shape(*dims):
     return jax.ShapeDtypeStruct(dims, F32)
 
@@ -426,7 +445,7 @@
         name="prepare",
     )(parity, outer, hbm["source"], hbm["diagonal"], hbm["bottom"], hbm["u"], *consts)
     near = swap_pairs(inner, False), outer_in
-    far = swap_pairs(far_inner, False), swap_pairs(far_outer, True)
+    far = swap(far_inner, far_outer)[::-1]
 
     blocks = -(-lat // LANE)
     first, inner, outer = pl.pallas_call(
@@ -438,13 +457,14 @@
         compiler_params=PARAMS,
         name="first_solve",
     )(parity, *near, masked, *held)
-    near = swap_pairs(inner, False), swap_pairs(outer, True)
-
-    c_rows, d_rows, edge, u_v, v_v = pl.pallas_call(
+    near = swap(inner, outer)
+
+    c_rows, z_rows, d_rows, edge, u_v, v_v = pl.pallas_call(
         absorb,
-        in_specs=[SM, HB] + [VM] * 4 + [HB] * 2,
-        out_specs=[VM] * 5,
-        out_shape=[pltpu.VMEM((span + 2 * OV, lat), F32), pltpu.VMEM((span, lat), F32), pltpu.VMEM((OV, lat), F32)]
+        in_specs=[SM] + [VM] * 5 + [HB] * 2,
+        out_specs=[VM] * 6,
+        out_shape=[pltpu.VMEM((span + 2 * OV, lat), F32)] * 2
+        + [pltpu.VMEM((span, lat), F32), pltpu.VMEM((OV, lat), F32)]
         + [pltpu.VMEM((KL, cells, lat), F32)] * 2,
         scratch_shapes=[pltpu.SemaphoreType.DMA((2,))],
         compiler_params=PARAMS,
@@ -456,22 +476,34 @@
         second_solve,
         in_specs=[SM] + [VM] * 7,
         out_specs=[VM] * 5,
-        out_shape=[pltpu.VMEM((span, lat), F32)] * 3 + [pltpu.VMEM(((OV + 1) * blocks, LANE), F32)] * 2,
-        scratch_shapes=solve_scratch(span, lat) + [pltpu.VMEM((span + 2 * OV, lat), F32)],
+        out_shape=[pltpu.VMEM((span + 2 * OV, lat), F32)]
+        + [pltpu.VMEM((span, lat), F32)] * 2
+        + [pltpu.VMEM(((OV + 1) * blocks, LANE), F32)] * 2,
+        scratch_shapes=solve_scratch(span, lat),
         compiler_params=PARAMS,
         name="second_solve",
-    )(parity, *near, first, c_rows, *held)
-    near = swap_pairs(inner, False), swap_pairs(outer, True)
+    )(parity, *near, z_rows, c_rows, *held)
+    near = swap(inner, outer)
+
+    w_rows, masked, row = pl.pallas_call(
+        early_sums,
+        in_specs=[VM] * 5,
+        out_specs=[VM] * 3,
+        out_shape=[pltpu.VMEM((span, lat), F32), pltpu.VMEM((cells, lat), F32), pltpu.VMEM((1, LANE), F32)],
+        compiler_params=PARAMS,
+        cost_estimate=pl.CostEstimate(flops=10**6, bytes_accessed=7 * 10**6, transcendentals=0),
+        name="early_sums",
+    )(z, y, c_rows, second, source_v)
 
     w, sent = pl.pallas_call(
         sums,
-        in_specs=[SM] + [VM] * 7,
+        in_specs=[SM] + [VM] * 8,
         out_specs=[VM] * 2,
         out_shape=[pltpu.VMEM((span, lat), F32), pltpu.VMEM((devices, 1, LANE), F32)],
         compiler_params=PARAMS,
         name="sums",
-    )(parity, *near, second, z, y, c_rows, source_v)
-    ring = [list(reversed(range(devices)))]
+    )(parity, *near, w_rows, z, y, c_rows, masked, row)
+    ring = [[(i + devices // 2) % devices for i in range(devices)]]
     came = lax.all_to_all(sent, "lon", 0, 0, axis_index_groups=ring)
 
     return pl.pallas_call(

time: 40.8 us -> 40.9 us (level)
  blocking collectives: 7.9 us -> 9.19 us
  waiting for transfers between devices: 6.48 us -> 5.4 us
    all_to_all x1, blocking collectives: 7.9 us -> 9.19 us  [body(): came = lax.all_to_all(sent, 'lon', 0, 0, axis_index_groups=ring)]
    ppermute x8, waiting for transfers between devices: 6.48 us -> 5.4 us  [swap_pairs(): return lax.ppermute(block, 'lon', route)]
    pallas_call x2 -> x3, Pallas kernels: 2.66 us -> 2.73 us  [the longest x1 2.03 us: body(): pl.pallas_call(absorb, in_specs=[SM] + [VM] * 5 + [HB] * 2, out_specs=[VM...]
where the time goes in v13:
time: 40.9 us; the launch traced here: 40.7 us
  starting transfers between devices  13.6 us (33%)
  Pallas kernels  11.8 us (29%)
  blocking collectives  9.19 us (22%)
  waiting for transfers between devices  5.4 us (13%)
  between operations  0.71 us (2%)
    ppermute x8, starting transfers between devices, swap_pairs(): return lax.ppermute(block, 'lon', route)  13.6 us
    all_to_all x1, blocking collectives, body(): came = lax.all_to_all(sent, 'lon', 0, 0, axis_index_groups=ring)  9.19 us
    ppermute x8, waiting for transfers between devices, swap_pairs(): return lax.ppermute(block, 'lon', route)  5.4 us
    pallas_call x1, Pallas kernels, body(): pl.pallas_call(finish, in_specs=[VM] * 8, out_specs=[HB] * 4, out_shape=[...  3.02 us
    pallas_call x1, Pallas kernels, body(): pl.pallas_call(absorb, in_specs=[SM] + [VM] * 5 + [HB] * 2, out_specs=[VM...  2.03 us
    pallas_call x1, Pallas kernels, body(): pl.pallas_call(second_solve, in_specs=[SM] + [VM] * 7, out_specs=[VM] * 5...  1.87 us
    pallas_call x1, Pallas kernels, body(): pl.pallas_call(first_solve, in_specs=[SM] + [VM] * 6, out_specs=[VM] * 3,...  1.68 us
    pallas_call x1, Pallas kernels, body(): pl.pallas_call(prepare, in_specs=[SM] + [HB] * 8, out_specs=[VM] * 10, ou...  1.53 us
  transfers between devices with their start and end apart: 8, of which 3 were waited for; matrix products, arithmetic and copies ran while one was open for 0% of the time, Pallas kernels for 13%

profile of v13, /device:TPU:0, one launch (start us, length us, event | category | flops | bytes accessed | tf_op | source)
XLA Modules:
  0.0 40.7 jit_solution(6743730555669688529)
XLA Ops:
  0.6 0.9 %first_edges.1.after = f32[8,2240]{1,0:T(8,128)S(1)} custom-call(s32[1]{0:T(128)} %bitcast.parity, f32[32,2240]{1,0:T(8,128)} %source_h.1, s32[32,2240]{1,0:T(8,128)} %bottom_h.1), custom_call_target="tpu_custom_call" | custom-call | tf_op jit(solution)/shard_map/first_edges/pallas_call | solution.py:417
  1.6 5.5 %collective-permute-start.1 = (f32[8,2240]{1,0:T(8,128)S(1)}, f32[8,2240]{1,0:T(8,128)S(1)}, u32[]{:S(2)}, u32[]{:S(2)}) collective-permute-start(f32[8,2240]{1,0:T(8,128)S(1)} %first_edges.1.after), channel_id=1, source_target_pairs={{0,15},{1,2},{2,1},{3,4},{4,3},{5,6},{6,5},{7,8},{8,7},{9,10},{10,... | collective-permute-start | bytes 215048 | tf_op jit(solution)/shard_map/ppermute | solution.py:395
  7.1 1.5 %prepare.1 = (f32[8,2240]{1,0:T(8,128)S(1)}, f32[24,2240]{1,0:T(8,128)S(1)}, f32[24,2240]{1,0:T(8,128)S(1)}, f32[32,2240]{1,0:T(8,128)S(1)}, f32[32,2240]{1,0:T(...) custom-call(s32[1]{0:T(128)} %bitcast.parity, ...), custom_call_target="tpu_custom_call" | custom-call | flops 1000000 | bytes 7000000 | tf_op jit(solution)/shard_map/prepare/pallas_call | solution.py:429
  8.6 0.1 collective-permute-start
  8.7 0.5 %collective-permute-start.4 = (f32[24,2240]{1,0:T(8,128)S(1)}, f32[24,2240]{1,0:T(8,128)S(1)}, u32[]{:S(2)}, u32[]{:S(2)}) collective-permute-start(f32[24,2240]{1,0:T(8,128)S(1)} %get-tuple-element.41), channel_id=1, source_target_pairs={{0,1},{1,0},{2,3},{3,2},{4,5},{5,4},{6,7},{7,6},{8,9},{9,8},{10,11... | collective-permute-start | bytes 645128 | tf_op jit(solution)/shard_map/ppermute | solution.py:395
  9.2 0.3 collective-permute-start.5
  9.5 0.0 collective-permute-done.1.outer_in
  9.5 0.5 %collective-permute-done.inner_in = f32[8,2240]{1,0:T(8,128)S(1)} collective-permute-done((f32[8,2240]{1,0:T(8,128)S(1)}, f32[8,2240]{1,0:T(8,128)S(1)}, u32[]{:S(2)}, u32[]{:S(2)}) %collective-permute-start) | collective-permute-done | bytes 71712 | tf_op jit(solution)/shard_map/ppermute | solution.py:395
  10.0 1.7 %first_solve.1 = (f32[48,2240]{1,0:T(8,128)S(1)}, f32[306,128]{1,0:T(8,128)S(1)}, f32[306,128]{1,0:T(8,128)S(1)}) custom-call(s32[1]{0:T(128)} %bitcast.parity, f32[8,2240]{1,0:T(8,128)S(1)} %collective-permute-done.inner_in, f32[8,2240]{1,0:T(8,128)S(1)} %collective-permute-done.1.outer_in, f32[32,2240]{1,0:T(8,128)S(1)} %get-tuple-element.34.masked, ...), custom_call_target="tpu_custom_call" | custom-call | tf_op jit(solution)/shard_map/first_solve/pallas_call | solution.py:451
  11.6 3.8 %collective-permute-start.2 = (f32[306,128]{1,0:T(8,128)S(1)}, f32[306,128]{1,0:T(8,128)S(1)}, u32[]{:S(2)}, u32[]{:S(2)}) collective-permute-start(f32[306,128]{1,0:T(8,128)S(1)} %get-tuple-element.38), channel_id=1, source_target_pairs={{0,15},{1,2},{2,1},{3,4},{4,3},{5,6},{6,5},{7,8},{8,7},{9,10},{10,... | collective-permute-start | bytes 470024 | tf_op jit(solution)/shard_map/ppermute | solution.py:395
  15.4 0.0 collective-permute-start.3
  15.4 0.0 collective-permute-done.4.inner_in
  15.4 1.9 %collective-permute-done.5.outer_in = f32[24,2240]{1,0:T(8,128)S(1)} collective-permute-done((f32[24,2240]{1,0:T(8,128)S(1)}, f32[24,2240]{1,0:T(8,128)S(1)}, u32[]{:S(2)}, u32[]{:S(2)}) %collective-permute-start.5) | collective-permute-done | bytes 215072 | tf_op jit(solution)/shard_map/ppermute | solution.py:395
  17.4 2.0 %absorb.1 = (f32[64,2240]{1,0:T(8,128)S(1)}, f32[64,2240]{1,0:T(8,128)S(1)}, f32[48,2240]{1,0:T(8,128)S(1)}, f32[8,2240]{1,0:T(8,128)S(1)}, f32[6,32,2240]{2,1,0:T(8,128)S(1)}, /*index=5*/f32[6,32,2240]{2,1,0:T(8,128)S(1)}) custom-call(s32[1]{0:T(128)} %bitcast.parity, f32[48,2240]{1,0:T(8,128)S(1)} %get-tuple-element.40.first, ...), custom_call_target="tpu_custom_call" | custom-call | flops 1000000 | bytes 7000000 | tf_op jit(solution)/shard_map/absorb/pallas_call | solution.py:462
  19.4 0.0 collective-permute-done.2.outer_in
  19.4 0.0 collective-permute-done.3.inner_in
  19.4 1.9 %second_solve.1 = (f32[64,2240]{1,0:T(8,128)S(1)}, f32[48,2240]{1,0:T(8,128)S(1)}, f32[48,2240]{1,0:T(8,128)S(1)}, f32[162,128]{1,0:T(8,128)S(1)}, f32[162,128]{1,0:T(8,128)S(1)}) custom-call(s32[1]{0:T(128)} %bitcast.parity, f32[306,128]{1,0:T(8,128)S(1)} %collective-permute-done.2.outer_in, f32[306,128]{1,0:T(8,128)S(1)} %collective-permute-done.3.inner_in, ...), custom_call_target="tpu_custom_call" | custom-call | tf_op jit(solution)/shard_map/second_solve/pallas_call | solution.py:475
  21.3 3.5 %collective-permute-start.6 = (f32[162,128]{1,0:T(8,128)S(1)}, f32[162,128]{1,0:T(8,128)S(1)}, u32[]{:S(2)}, u32[]{:S(2)}) collective-permute-start(f32[162,128]{1,0:T(8,128)S(1)} %get-tuple-element.47), channel_id=1, source_target_pairs={{0,15},{1,2},{2,1},{3,4},{4,3},{5,6},{6,5},{7,8},{8,7},{9,10},{10,... | collective-permute-start | bytes 248840 | tf_op jit(solution)/shard_map/ppermute | solution.py:395
  24.8 0.0 collective-permute-start.7
  24.8 0.2 early_sums.1
  25.0 3.0 %collective-permute-done.6.outer_in = f32[162,128]{1,0:T(8,128)S(1)} collective-permute-done((f32[162,128]{1,0:T(8,128)S(1)}, f32[162,128]{1,0:T(8,128)S(1)}, u32[]{:S(2)}, u32[]{:S(2)}) %collective-permute-start.6) | collective-permute-done | bytes 82976 | tf_op jit(solution)/shard_map/ppermute | solution.py:395
  28.0 0.0 collective-permute-done.7.inner_in
  28.0 0.5 %sums.1 = (f32[48,2240]{1,0:T(8,128)S(1)}, f32[16,1,128]{2,1,0:T(1,128)S(1)}) custom-call(s32[1]{0:T(128)} %bitcast.parity, f32[162,128]{1,0:T(8,128)S(1)} %collective-permute-done.6.outer_in, f32[162,128]{1,0:T(8,128)S(1)} %collective-permute-done.7.inner_in, f32[48,2240]{1,0:T(8,128)S(1)} %get-tuple-element.53.w_rows, f32[64,2240]{1,0:T(8,128)S(1)} %get-tuple-element.49.z, ...), custom_call_target="tpu_custom_call" | custom-call | tf_op jit(solution)/shard_map/sums/pallas_call | solution.py:498
  28.4 9.2 %all_to_all.5.came = f32[16,1,128]{2,1,0:T(1,128)S(1)} all-to-all(f32[16,1,128]{2,1,0:T(1,128)S(1)} %get-tuple-element.56), channel_id=1, replica_groups={{8,9,10,11,12,13,14,15,0,1,2,3,4,5,6,7},{24,25,26,27,28,29,30,31,16,17,..., dimensions={0} | all-to-all | bytes 16384 | tf_op jit(solution)/shard_map/all_to_all | solution.py:507
  37.6 3.0 %finish.1 = (f32[32,2240]{1,0:T(8,128)}, f32[6,32,2240]{2,1,0:T(8,128)}, f32[6,32,2240]{2,1,0:T(8,128)}, f32[6,32,2240]{2,1,0:T(8,128)}) custom-call(f32[16,1,128]{2,1,0:T(1,128)S(1)} %all_to_all.5.came, f32[64,2240]{1,0:T(8,128)S(1)} %get-tuple-element.49.z, f32[48,2240]{1,0:T(8,128)S(1)} %get-tuple-element.57.w, f32[48,2240]{1,0:T(8,128)S(1)} %get-tuple-element.58.d_rows, ...), custom_call_target="tpu_custom_call" | custom-call | tf_op jit(solution)/shard_map/finish/pallas_call | solution.py:509
Async XLA Ops:
  1.6 7.9 %collective-permute-start.1 = (f32[8,2240]{1,0:T(8,128)S(1)}, f32[8,2240]{1,0:T(8,128)S(1)}, u32[]{:S(2)}, u32[]{:S(2)}) collective-permute-start(f32[8,2240]{1,0:T(8,128)S(1)} %first_edges.1.after), channel_id=1, source_target_pairs={{0,15},{1,2},{2,1},{3,4},{4,3},{5,6},{6,5},{7,8},{8,7},{9,10},{10,... | collective-permute-start | bytes 215048 | tf_op jit(solution)/shard_map/ppermute | solution.py:395
  8.6 1.3 %collective-permute-start = (f32[8,2240]{1,0:T(8,128)S(1)}, f32[8,2240]{1,0:T(8,128)S(1)}, u32[]{:S(2)}, u32[]{:S(2)}) collective-permute-start(f32[8,2240]{1,0:T(8,128)S(1)} %get-tuple-element.33), channel_id=1, source_target_pairs={{0,1},{1,0},{2,3},{3,2},{4,5},{5,4},{6,7},{7,6},{8,9},{9,8},{10,11... | collective-permute-start | bytes 215048 | tf_op jit(solution)/shard_map/ppermute | solution.py:395
  8.7 6.7 %collective-permute-start.4 = (f32[24,2240]{1,0:T(8,128)S(1)}, f32[24,2240]{1,0:T(8,128)S(1)}, u32[]{:S(2)}, u32[]{:S(2)}) collective-permute-start(f32[24,2240]{1,0:T(8,128)S(1)} %get-tuple-element.41), channel_id=1, source_target_pairs={{0,1},{1,0},{2,3},{3,2},{4,5},{5,4},{6,7},{7,6},{8,9},{9,8},{10,11... | collective-permute-start | bytes 645128 | tf_op jit(solution)/shard_map/ppermute | solution.py:395
  9.2 8.2 %collective-permute-start.5 = (f32[24,2240]{1,0:T(8,128)S(1)}, f32[24,2240]{1,0:T(8,128)S(1)}, u32[]{:S(2)}, u32[]{:S(2)}) collective-permute-start(f32[24,2240]{1,0:T(8,128)S(1)} %get-tuple-element.42), channel_id=1, source_target_pairs={{0,15},{1,2},{2,1},{3,4},{4,3},{5,6},{6,5},{7,8},{8,7},{9,10},{10,... | collective-permute-start | bytes 645128 | tf_op jit(solution)/shard_map/ppermute | solution.py:395
  11.6 7.8 %collective-permute-start.2 = (f32[306,128]{1,0:T(8,128)S(1)}, f32[306,128]{1,0:T(8,128)S(1)}, u32[]{:S(2)}, u32[]{:S(2)}) collective-permute-start(f32[306,128]{1,0:T(8,128)S(1)} %get-tuple-element.38), channel_id=1, source_target_pairs={{0,15},{1,2},{2,1},{3,4},{4,3},{5,6},{6,5},{7,8},{8,7},{9,10},{10,... | collective-permute-start | bytes 470024 | tf_op jit(solution)/shard_map/ppermute | solution.py:395
  15.4 4.0 %collective-permute-start.3 = (f32[306,128]{1,0:T(8,128)S(1)}, f32[306,128]{1,0:T(8,128)S(1)}, u32[]{:S(2)}, u32[]{:S(2)}) collective-permute-start(f32[306,128]{1,0:T(8,128)S(1)} %get-tuple-element.39), channel_id=1, source_target_pairs={{0,1},{1,0},{2,3},{3,2},{4,5},{5,4},{6,7},{7,6},{8,9},{9,8},{10,11... | collective-permute-start | bytes 470024 | tf_op jit(solution)/shard_map/ppermute | solution.py:395
  21.3 6.7 %collective-permute-start.6 = (f32[162,128]{1,0:T(8,128)S(1)}, f32[162,128]{1,0:T(8,128)S(1)}, u32[]{:S(2)}, u32[]{:S(2)}) collective-permute-start(f32[162,128]{1,0:T(8,128)S(1)} %get-tuple-element.47), channel_id=1, source_target_pairs={{0,15},{1,2},{2,1},{3,4},{4,3},{5,6},{6,5},{7,8},{8,7},{9,10},{10,... | collective-permute-start | bytes 248840 | tf_op jit(solution)/shard_map/ppermute | solution.py:395
  24.8 3.2 %collective-permute-start.7 = (f32[162,128]{1,0:T(8,128)S(1)}, f32[162,128]{1,0:T(8,128)S(1)}, u32[]{:S(2)}, u32[]{:S(2)}) collective-permute-start(f32[162,128]{1,0:T(8,128)S(1)} %get-tuple-element.48), channel_id=1, source_target_pairs={{0,1},{1,0},{2,3},{3,2},{4,5},{5,4},{6,7},{7,6},{8,9},{9,8},{10,11... | collective-permute-start | bytes 248840 | tf_op jit(solution)/shard_map/ppermute | solution.py:395

commit v14 on v13

--- a/solution.py
+++ b/solution.py
@@ -503,7 +503,7 @@
         compiler_params=PARAMS,
         name="sums",
     )(parity, *near, w_rows, z, y, c_rows, masked, row)
-    ring = [[(i + devices // 2) % devices for i in range(devices)]]
+    ring = [list(reversed(range(devices)))]
     came = lax.all_to_all(sent, "lon", 0, 0, axis_index_groups=ring)
 
     return pl.pallas_call(

time: 40.9 us -> 39.9 us (0.976)
  blocking collectives: 9.19 us -> 8.19 us
    all_to_all x1, blocking collectives: 9.19 us -> 8.19 us  [body(): came = lax.all_to_all(sent, 'lon', 0, 0, axis_index_groups=ring)]
  transfers between devices with their start and end apart: 8 -> 8, of which waited for: 3 -> 3; matrix products, arithmetic and copies ran while one was open for 0% -> 0% of each run, Pallas kernels for 13% -> 14%
where the time goes in v14:
time: 39.9 us; the launch traced here: 39.7 us
  starting transfers between devices  13.6 us (34%)
  Pallas kernels  11.8 us (30%)
  blocking collectives  8.19 us (21%)
  waiting for transfers between devices  5.4 us (14%)
  between operations  0.71 us (2%)
    ppermute x8, starting transfers between devices, swap_pairs(): return lax.ppermute(block, 'lon', route)  13.6 us
    all_to_all x1, blocking collectives, body(): came = lax.all_to_all(sent, 'lon', 0, 0, axis_index_groups=ring)  8.19 us
    ppermute x8, waiting for transfers between devices, swap_pairs(): return lax.ppermute(block, 'lon', route)  5.4 us
    pallas_call x1, Pallas kernels, body(): pl.pallas_call(finish, in_specs=[VM] * 8, out_specs=[HB] * 4, out_shape=[...  3.02 us
    pallas_call x1, Pallas kernels, body(): pl.pallas_call(absorb, in_specs=[SM] + [VM] * 5 + [HB] * 2, out_specs=[VM...  2.03 us
    pallas_call x1, Pallas kernels, body(): pl.pallas_call(second_solve, in_specs=[SM] + [VM] * 7, out_specs=[VM] * 5...  1.87 us
    pallas_call x1, Pallas kernels, body(): pl.pallas_call(first_solve, in_specs=[SM] + [VM] * 6, out_specs=[VM] * 3,...  1.68 us
    pallas_call x1, Pallas kernels, body(): pl.pallas_call(prepare, in_specs=[SM] + [HB] * 8, out_specs=[VM] * 10, ou...  1.53 us
  transfers between devices with their start and end apart: 8, of which 3 were waited for; matrix products, arithmetic and copies ran while one was open for 0% of the time, Pallas kernels for 14%

profile of v14, /device:TPU:0, one launch (start us, length us, event | category | flops | bytes accessed | tf_op | source)
XLA Modules:
  0.0 39.7 jit_solution(3210200460904663268)
XLA Ops:
  0.6 0.9 %first_edges.1.after = f32[8,2240]{1,0:T(8,128)S(1)} custom-call(s32[1]{0:T(128)} %bitcast.parity, f32[32,2240]{1,0:T(8,128)} %source_h.1, s32[32,2240]{1,0:T(8,128)} %bottom_h.1), custom_call_target="tpu_custom_call" | custom-call | tf_op jit(solution)/shard_map/first_edges/pallas_call | solution.py:417
  1.6 5.5 %collective-permute-start.1 = (f32[8,2240]{1,0:T(8,128)S(1)}, f32[8,2240]{1,0:T(8,128)S(1)}, u32[]{:S(2)}, u32[]{:S(2)}) collective-permute-start(f32[8,2240]{1,0:T(8,128)S(1)} %first_edges.1.after), channel_id=1, source_target_pairs={{0,15},{1,2},{2,1},{3,4},{4,3},{5,6},{6,5},{7,8},{8,7},{9,10},{10,... | collective-permute-start | bytes 215048 | tf_op jit(solution)/shard_map/ppermute | solution.py:395
  7.1 1.5 %prepare.1 = (f32[8,2240]{1,0:T(8,128)S(1)}, f32[24,2240]{1,0:T(8,128)S(1)}, f32[24,2240]{1,0:T(8,128)S(1)}, f32[32,2240]{1,0:T(8,128)S(1)}, f32[32,2240]{1,0:T(...) custom-call(s32[1]{0:T(128)} %bitcast.parity, ...), custom_call_target="tpu_custom_call" | custom-call | flops 1000000 | bytes 7000000 | tf_op jit(solution)/shard_map/prepare/pallas_call | solution.py:429
  8.6 0.1 collective-permute-start
  8.7 0.5 %collective-permute-start.4 = (f32[24,2240]{1,0:T(8,128)S(1)}, f32[24,2240]{1,0:T(8,128)S(1)}, u32[]{:S(2)}, u32[]{:S(2)}) collective-permute-start(f32[24,2240]{1,0:T(8,128)S(1)} %get-tuple-element.41), channel_id=1, source_target_pairs={{0,1},{1,0},{2,3},{3,2},{4,5},{5,4},{6,7},{7,6},{8,9},{9,8},{10,11... | collective-permute-start | bytes 645128 | tf_op jit(solution)/shard_map/ppermute | solution.py:395
  9.2 0.3 collective-permute-start.5
  9.5 0.0 collective-permute-done.1.outer_in
  9.5 0.5 %collective-permute-done.inner_in = f32[8,2240]{1,0:T(8,128)S(1)} collective-permute-done((f32[8,2240]{1,0:T(8,128)S(1)}, f32[8,2240]{1,0:T(8,128)S(1)}, u32[]{:S(2)}, u32[]{:S(2)}) %collective-permute-start) | collective-permute-done | bytes 71712 | tf_op jit(solution)/shard_map/ppermute | solution.py:395
  10.0 1.7 %first_solve.1 = (f32[48,2240]{1,0:T(8,128)S(1)}, f32[306,128]{1,0:T(8,128)S(1)}, f32[306,128]{1,0:T(8,128)S(1)}) custom-call(s32[1]{0:T(128)} %bitcast.parity, f32[8,2240]{1,0:T(8,128)S(1)} %collective-permute-done.inner_in, f32[8,2240]{1,0:T(8,128)S(1)} %collective-permute-done.1.outer_in, f32[32,2240]{1,0:T(8,128)S(1)} %get-tuple-element.34.masked, ...), custom_call_target="tpu_custom_call" | custom-call | tf_op jit(solution)/shard_map/first_solve/pallas_call | solution.py:451
  11.6 3.8 %collective-permute-start.2 = (f32[306,128]{1,0:T(8,128)S(1)}, f32[306,128]{1,0:T(8,128)S(1)}, u32[]{:S(2)}, u32[]{:S(2)}) collective-permute-start(f32[306,128]{1,0:T(8,128)S(1)} %get-tuple-element.38), channel_id=1, source_target_pairs={{0,15},{1,2},{2,1},{3,4},{4,3},{5,6},{6,5},{7,8},{8,7},{9,10},{10,... | collective-permute-start | bytes 470024 | tf_op jit(solution)/shard_map/ppermute | solution.py:395
  15.4 0.0 collective-permute-start.3
  15.4 0.0 collective-permute-done.4.inner_in
  15.4 1.9 %collective-permute-done.5.outer_in = f32[24,2240]{1,0:T(8,128)S(1)} collective-permute-done((f32[24,2240]{1,0:T(8,128)S(1)}, f32[24,2240]{1,0:T(8,128)S(1)}, u32[]{:S(2)}, u32[]{:S(2)}) %collective-permute-start.5) | collective-permute-done | bytes 215072 | tf_op jit(solution)/shard_map/ppermute | solution.py:395
  17.4 2.0 %absorb.1 = (f32[64,2240]{1,0:T(8,128)S(1)}, f32[64,2240]{1,0:T(8,128)S(1)}, f32[48,2240]{1,0:T(8,128)S(1)}, f32[8,2240]{1,0:T(8,128)S(1)}, f32[6,32,2240]{2,1,0:T(8,128)S(1)}, /*index=5*/f32[6,32,2240]{2,1,0:T(8,128)S(1)}) custom-call(s32[1]{0:T(128)} %bitcast.parity, f32[48,2240]{1,0:T(8,128)S(1)} %get-tuple-element.40.first, ...), custom_call_target="tpu_custom_call" | custom-call | flops 1000000 | bytes 7000000 | tf_op jit(solution)/shard_map/absorb/pallas_call | solution.py:462
  19.4 0.0 collective-permute-done.2.outer_in
  19.4 0.0 collective-permute-done.3.inner_in
  19.4 1.9 %second_solve.1 = (f32[64,2240]{1,0:T(8,128)S(1)}, f32[48,2240]{1,0:T(8,128)S(1)}, f32[48,2240]{1,0:T(8,128)S(1)}, f32[162,128]{1,0:T(8,128)S(1)}, f32[162,128]{1,0:T(8,128)S(1)}) custom-call(s32[1]{0:T(128)} %bitcast.parity, f32[306,128]{1,0:T(8,128)S(1)} %collective-permute-done.2.outer_in, f32[306,128]{1,0:T(8,128)S(1)} %collective-permute-done.3.inner_in, ...), custom_call_target="tpu_custom_call" | custom-call | tf_op jit(solution)/shard_map/second_solve/pallas_call | solution.py:475
  21.3 3.5 %collective-permute-start.6 = (f32[162,128]{1,0:T(8,128)S(1)}, f32[162,128]{1,0:T(8,128)S(1)}, u32[]{:S(2)}, u32[]{:S(2)}) collective-permute-start(f32[162,128]{1,0:T(8,128)S(1)} %get-tuple-element.47), channel_id=1, source_target_pairs={{0,15},{1,2},{2,1},{3,4},{4,3},{5,6},{6,5},{7,8},{8,7},{9,10},{10,... | collective-permute-start | bytes 248840 | tf_op jit(solution)/shard_map/ppermute | solution.py:395
  24.8 0.0 collective-permute-start.7
  24.8 0.2 early_sums.1
  25.0 3.0 %collective-permute-done.6.outer_in = f32[162,128]{1,0:T(8,128)S(1)} collective-permute-done((f32[162,128]{1,0:T(8,128)S(1)}, f32[162,128]{1,0:T(8,128)S(1)}, u32[]{:S(2)}, u32[]{:S(2)}) %collective-permute-start.6) | collective-permute-done | bytes 82976 | tf_op jit(solution)/shard_map/ppermute | solution.py:395
  28.0 0.0 collective-permute-done.7.inner_in
  28.0 0.5 %sums.1 = (f32[48,2240]{1,0:T(8,128)S(1)}, f32[16,1,128]{2,1,0:T(1,128)S(1)}) custom-call(s32[1]{0:T(128)} %bitcast.parity, f32[162,128]{1,0:T(8,128)S(1)} %collective-permute-done.6.outer_in, f32[162,128]{1,0:T(8,128)S(1)} %collective-permute-done.7.inner_in, f32[48,2240]{1,0:T(8,128)S(1)} %get-tuple-element.53.w_rows, f32[64,2240]{1,0:T(8,128)S(1)} %get-tuple-element.49.z, ...), custom_call_target="tpu_custom_call" | custom-call | tf_op jit(solution)/shard_map/sums/pallas_call | solution.py:498
  28.4 8.2 %all_to_all.5.came = f32[16,1,128]{2,1,0:T(1,128)S(1)} all-to-all(f32[16,1,128]{2,1,0:T(1,128)S(1)} %get-tuple-element.56), channel_id=1, replica_groups={{15,14,13,12,11,10,9,8,7,6,5,4,3,2,1,0},{31,30,29,28,27,26,25,24,23,22,..., dimensions={0} | all-to-all | bytes 16384 | tf_op jit(solution)/shard_map/all_to_all | solution.py:507
  36.6 3.0 %finish.1 = (f32[32,2240]{1,0:T(8,128)}, f32[6,32,2240]{2,1,0:T(8,128)}, f32[6,32,2240]{2,1,0:T(8,128)}, f32[6,32,2240]{2,1,0:T(8,128)}) custom-call(f32[16,1,128]{2,1,0:T(1,128)S(1)} %all_to_all.5.came, f32[64,2240]{1,0:T(8,128)S(1)} %get-tuple-element.49.z, f32[48,2240]{1,0:T(8,128)S(1)} %get-tuple-element.57.w, f32[48,2240]{1,0:T(8,128)S(1)} %get-tuple-element.58.d_rows, ...), custom_call_target="tpu_custom_call" | custom-call | tf_op jit(solution)/shard_map/finish/pallas_call | solution.py:509
Async XLA Ops:
  1.6 7.9 %collective-permute-start.1 = (f32[8,2240]{1,0:T(8,128)S(1)}, f32[8,2240]{1,0:T(8,128)S(1)}, u32[]{:S(2)}, u32[]{:S(2)}) collective-permute-start(f32[8,2240]{1,0:T(8,128)S(1)} %first_edges.1.after), channel_id=1, source_target_pairs={{0,15},{1,2},{2,1},{3,4},{4,3},{5,6},{6,5},{7,8},{8,7},{9,10},{10,... | collective-permute-start | bytes 215048 | tf_op jit(solution)/shard_map/ppermute | solution.py:395
  8.6 1.3 %collective-permute-start = (f32[8,2240]{1,0:T(8,128)S(1)}, f32[8,2240]{1,0:T(8,128)S(1)}, u32[]{:S(2)}, u32[]{:S(2)}) collective-permute-start(f32[8,2240]{1,0:T(8,128)S(1)} %get-tuple-element.33), channel_id=1, source_target_pairs={{0,1},{1,0},{2,3},{3,2},{4,5},{5,4},{6,7},{7,6},{8,9},{9,8},{10,11... | collective-permute-start | bytes 215048 | tf_op jit(solution)/shard_map/ppermute | solution.py:395
  8.7 6.7 %collective-permute-start.4 = (f32[24,2240]{1,0:T(8,128)S(1)}, f32[24,2240]{1,0:T(8,128)S(1)}, u32[]{:S(2)}, u32[]{:S(2)}) collective-permute-start(f32[24,2240]{1,0:T(8,128)S(1)} %get-tuple-element.41), channel_id=1, source_target_pairs={{0,1},{1,0},{2,3},{3,2},{4,5},{5,4},{6,7},{7,6},{8,9},{9,8},{10,11... | collective-permute-start | bytes 645128 | tf_op jit(solution)/shard_map/ppermute | solution.py:395
  9.2 8.2 %collective-permute-start.5 = (f32[24,2240]{1,0:T(8,128)S(1)}, f32[24,2240]{1,0:T(8,128)S(1)}, u32[]{:S(2)}, u32[]{:S(2)}) collective-permute-start(f32[24,2240]{1,0:T(8,128)S(1)} %get-tuple-element.42), channel_id=1, source_target_pairs={{0,15},{1,2},{2,1},{3,4},{4,3},{5,6},{6,5},{7,8},{8,7},{9,10},{10,... | collective-permute-start | bytes 645128 | tf_op jit(solution)/shard_map/ppermute | solution.py:395
  11.6 7.8 %collective-permute-start.2 = (f32[306,128]{1,0:T(8,128)S(1)}, f32[306,128]{1,0:T(8,128)S(1)}, u32[]{:S(2)}, u32[]{:S(2)}) collective-permute-start(f32[306,128]{1,0:T(8,128)S(1)} %get-tuple-element.38), channel_id=1, source_target_pairs={{0,15},{1,2},{2,1},{3,4},{4,3},{5,6},{6,5},{7,8},{8,7},{9,10},{10,... | collective-permute-start | bytes 470024 | tf_op jit(solution)/shard_map/ppermute | solution.py:395
  15.4 4.0 %collective-permute-start.3 = (f32[306,128]{1,0:T(8,128)S(1)}, f32[306,128]{1,0:T(8,128)S(1)}, u32[]{:S(2)}, u32[]{:S(2)}) collective-permute-start(f32[306,128]{1,0:T(8,128)S(1)} %get-tuple-element.39), channel_id=1, source_target_pairs={{0,1},{1,0},{2,3},{3,2},{4,5},{5,4},{6,7},{7,6},{8,9},{9,8},{10,11... | collective-permute-start | bytes 470024 | tf_op jit(solution)/shard_map/ppermute | solution.py:395
  21.3 6.7 %collective-permute-start.6 = (f32[162,128]{1,0:T(8,128)S(1)}, f32[162,128]{1,0:T(8,128)S(1)}, u32[]{:S(2)}, u32[]{:S(2)}) collective-permute-start(f32[162,128]{1,0:T(8,128)S(1)} %get-tuple-element.47), channel_id=1, source_target_pairs={{0,15},{1,2},{2,1},{3,4},{4,3},{5,6},{6,5},{7,8},{8,7},{9,10},{10,... | collective-permute-start | bytes 248840 | tf_op jit(solution)/shard_map/ppermute | solution.py:395
  24.8 3.2 %collective-permute-start.7 = (f32[162,128]{1,0:T(8,128)S(1)}, f32[162,128]{1,0:T(8,128)S(1)}, u32[]{:S(2)}, u32[]{:S(2)}) collective-permute-start(f32[162,128]{1,0:T(8,128)S(1)} %get-tuple-element.48), channel_id=1, source_target_pairs={{0,1},{1,0},{2,3},{3,2},{4,5},{5,4},{6,7},{7,6},{8,9},{9,8},{10,11... | collective-permute-start | bytes 248840 | tf_op jit(solution)/shard_map/ppermute | solution.py:395

commit v15 on v14

--- a/solution.py
+++ b/solution.py
@@ -221,11 +221,8 @@
     pack(outer, to_outer)
 
 
-def absorb(parity, first, inner_in, outer_in, coef, depth, u_h, v_h, c_rows, z_rows, d_rows, edge, u, v, sems):
+def absorb(parity, first, inner_in, outer_in, coef, depth, c_rows, z_rows, d_rows, edge):
     cells, lat = coef.shape
-    copies = [pltpu.make_async_copy(a, b, sems.at[i]) for i, (a, b) in enumerate([(u_h, u), (v_h, v)])]
-    for copy in copies:
-        copy.start()
     west, east = pick(parity, inner_in[: 2 * OV], outer_in[: 2 * OV])
     edge[...] = west[:OV]
     d_rows[:OV] = jnp.broadcast_to(west[KL : KL + 1], (OV, lat))
@@ -240,8 +237,6 @@
     z_rows[3 * OV + cells :] = jnp.zeros((OV, lat), F32)
     inside = slice(OV, 3 * OV + cells)
     z_rows[inside] = jnp.where(c_rows[inside] > 0, first[...], 0.0)
-    for copy in copies:
-        copy.wait()
 
 
 def second_solve(parity, outer_in, inner_in, z_rows, c_rows, lat_basis, lon, scale,
@@ -290,7 +285,10 @@
     return row
 
 
-def early_sums(z, y, c_rows, second, source, w_rows, masked, row):
+def early_sums(z, y, c_rows, second, source, u_h, v_h, w_rows, masked, row, u, v, sems):
+    copies = [pltpu.make_async_copy(a, b, sems.at[i]) for i, (a, b) in enumerate([(u_h, u), (v_h, v)])]
+    for copy in copies:
+        copy.start()
     cells, lat = source.shape
     inside = slice(OV, 3 * OV + cells)
     w_rows[...] = jnp.where(c_rows[inside] > 0, second[...], 0.0)
@@ -301,6 +299,8 @@
     z_own = z[own]
     sums_of = {0: dot(masked[...], z_own), 1: dot(z_own, y[OV : OV + cells]), 6: dot(land, land)}
     row[...] = in_lanes(jnp.zeros((1, LANE), F32), sums_of)
+    for copy in copies:
+        copy.wait()
 
 
 def sums(parity, outer_in, inner_in, w_rows, z, y, c_rows, masked, row, w, sent):
@@ -459,18 +459,16 @@
     )(parity, *near, masked, *held)
     near = swap(inner, outer)
 
-    c_rows, z_rows, d_rows, edge, u_v, v_v = pl.pallas_call(
+    c_rows, z_rows, d_rows, edge = pl.pallas_call(
         absorb,
-        in_specs=[SM] + [VM] * 5 + [HB] * 2,
-        out_specs=[VM] * 6,
+        in_specs=[SM] + [VM] * 5,
+        out_specs=[VM] * 4,
         out_shape=[pltpu.VMEM((span + 2 * OV, lat), F32)] * 2
-        + [pltpu.VMEM((span, lat), F32), pltpu.VMEM((OV, lat), F32)]
-        + [pltpu.VMEM((KL, cells, lat), F32)] * 2,
-        scratch_shapes=[pltpu.SemaphoreType.DMA((2,))],
+        + [pltpu.VMEM((span, lat), F32), pltpu.VMEM((OV, lat), F32)],
         compiler_params=PARAMS,
         cost_estimate=pl.CostEstimate(flops=10**6, bytes_accessed=7 * 10**6, transcendentals=0),
         name="absorb",
-    )(parity, first, *far, coef, depth, hbm["u"], hbm["v"])
+    )(parity, first, *far, coef, depth)
 
     z, y, second, inner, outer = pl.pallas_call(
         second_solve,
@@ -485,15 +483,17 @@
     )(parity, *near, z_rows, c_rows, *held)
     near = swap(inner, outer)
 
-    w_rows, masked, row = pl.pallas_call(
+    w_rows, masked, row, u_v, v_v = pl.pallas_call(
         early_sums,
-        in_specs=[VM] * 5,
-        out_specs=[VM] * 3,
-        out_shape=[pltpu.VMEM((span, lat), F32), pltpu.VMEM((cells, lat), F32), pltpu.VMEM((1, LANE), F32)],
+        in_specs=[VM] * 5 + [HB] * 2,
+        out_specs=[VM] * 5,
+        out_shape=[pltpu.VMEM((span, lat), F32), pltpu.VMEM((cells, lat), F32), pltpu.VMEM((1, LANE), F32)]
+        + [pltpu.VMEM((KL, cells, lat), F32)] * 2,
+        scratch_shapes=[pltpu.SemaphoreType.DMA((2,))],
         compiler_params=PARAMS,
         cost_estimate=pl.CostEstimate(flops=10**6, bytes_accessed=7 * 10**6, transcendentals=0),
         name="early_sums",
-    )(z, y, c_rows, second, source_v)
+    )(z, y, c_rows, second, source_v, hbm["u"], hbm["v"])
 
     w, sent = pl.pallas_call(
         sums,

time: 39.9 us -> 39.9 us (level)
  waiting for transfers between devices: 5.4 us -> 4.96 us
    ppermute x8, waiting for transfers between devices: 5.4 us -> 4.96 us  [swap_pairs(): return lax.ppermute(block, 'lon', route)]
  transfers between devices with their start and end apart: 8 -> 8, of which waited for: 3 -> 4; matrix products, arithmetic and copies ran while one was open for 0% -> 0% of each run, Pallas kernels for 14% -> 14%
where the time goes in v15:
time: 39.9 us; the launch traced here: 39.7 us
  starting transfers between devices  13.8 us (35%)
  Pallas kernels  11.7 us (29%)
  blocking collectives  8.45 us (21%)
  waiting for transfers between devices  4.96 us (12%)
  between operations  0.7 us (2%)
    ppermute x8, starting transfers between devices, swap_pairs(): return lax.ppermute(block, 'lon', route)  13.8 us
    all_to_all x1, blocking collectives, body(): came = lax.all_to_all(sent, 'lon', 0, 0, axis_index_groups=ring)  8.45 us
    ppermute x8, waiting for transfers between devices, swap_pairs(): return lax.ppermute(block, 'lon', route)  4.96 us
    pallas_call x1, Pallas kernels, body(): pl.pallas_call(finish, in_specs=[VM] * 8, out_specs=[HB] * 4, out_shape=[...  3.02 us
    pallas_call x1, Pallas kernels, body(): pl.pallas_call(early_sums, in_specs=[VM] * 5 + [HB] * 2, out_specs=[VM] *...  2.03 us
    pallas_call x1, Pallas kernels, body(): pl.pallas_call(second_solve, in_specs=[SM] + [VM] * 7, out_specs=[VM] * 5...  1.87 us
    pallas_call x1, Pallas kernels, body(): pl.pallas_call(first_solve, in_specs=[SM] + [VM] * 6, out_specs=[VM] * 3,...  1.68 us
    pallas_call x1, Pallas kernels, body(): pl.pallas_call(prepare, in_specs=[SM] + [HB] * 8, out_specs=[VM] * 10, ou...  1.53 us
  transfers between devices with their start and end apart: 8, of which 4 were waited for; matrix products, arithmetic and copies ran while one was open for 0% of the time, Pallas kernels for 14%

profile of v15, /device:TPU:0, one launch (start us, length us, event | category | flops | bytes accessed | tf_op | source)
XLA Modules:
  0.0 39.7 jit_solution(7749029506285625791)
XLA Ops:
  0.6 0.9 %first_edges.1.after = f32[8,2240]{1,0:T(8,128)S(1)} custom-call(s32[1]{0:T(128)} %bitcast.parity, f32[32,2240]{1,0:T(8,128)} %source_h.1, s32[32,2240]{1,0:T(8,128)} %bottom_h.1), custom_call_target="tpu_custom_call" | custom-call | tf_op jit(solution)/shard_map/first_edges/pallas_call | solution.py:417
  1.6 5.5 %collective-permute-start.1 = (f32[8,2240]{1,0:T(8,128)S(1)}, f32[8,2240]{1,0:T(8,128)S(1)}, u32[]{:S(2)}, u32[]{:S(2)}) collective-permute-start(f32[8,2240]{1,0:T(8,128)S(1)} %first_edges.1.after), channel_id=1, source_target_pairs={{0,15},{1,2},{2,1},{3,4},{4,3},{5,6},{6,5},{7,8},{8,7},{9,10},{10,... | collective-permute-start | bytes 215048 | tf_op jit(solution)/shard_map/ppermute | solution.py:395
  7.1 1.5 %prepare.1 = (f32[8,2240]{1,0:T(8,128)S(1)}, f32[24,2240]{1,0:T(8,128)S(1)}, f32[24,2240]{1,0:T(8,128)S(1)}, f32[32,2240]{1,0:T(8,128)S(1)}, f32[32,2240]{1,0:T(...) custom-call(s32[1]{0:T(128)} %bitcast.parity, ...), custom_call_target="tpu_custom_call" | custom-call | flops 1000000 | bytes 7000000 | tf_op jit(solution)/shard_map/prepare/pallas_call | solution.py:429
  8.6 0.1 collective-permute-start
  8.7 0.5 %collective-permute-start.4 = (f32[24,2240]{1,0:T(8,128)S(1)}, f32[24,2240]{1,0:T(8,128)S(1)}, u32[]{:S(2)}, u32[]{:S(2)}) collective-permute-start(f32[24,2240]{1,0:T(8,128)S(1)} %get-tuple-element.41), channel_id=1, source_target_pairs={{0,1},{1,0},{2,3},{3,2},{4,5},{5,4},{6,7},{7,6},{8,9},{9,8},{10,11... | collective-permute-start | bytes 645128 | tf_op jit(solution)/shard_map/ppermute | solution.py:395
  9.2 0.3 collective-permute-start.5
  9.5 0.0 collective-permute-done.1.outer_in
  9.5 0.5 %collective-permute-done.inner_in = f32[8,2240]{1,0:T(8,128)S(1)} collective-permute-done((f32[8,2240]{1,0:T(8,128)S(1)}, f32[8,2240]{1,0:T(8,128)S(1)}, u32[]{:S(2)}, u32[]{:S(2)}) %collective-permute-start) | collective-permute-done | bytes 71712 | tf_op jit(solution)/shard_map/ppermute | solution.py:395
  10.0 1.7 %first_solve.1 = (f32[48,2240]{1,0:T(8,128)S(1)}, f32[306,128]{1,0:T(8,128)S(1)}, f32[306,128]{1,0:T(8,128)S(1)}) custom-call(s32[1]{0:T(128)} %bitcast.parity, f32[8,2240]{1,0:T(8,128)S(1)} %collective-permute-done.inner_in, f32[8,2240]{1,0:T(8,128)S(1)} %collective-permute-done.1.outer_in, f32[32,2240]{1,0:T(8,128)S(1)} %get-tuple-element.34.masked, ...), custom_call_target="tpu_custom_call" | custom-call | tf_op jit(solution)/shard_map/first_solve/pallas_call | solution.py:451
  11.6 3.8 %collective-permute-start.2 = (f32[306,128]{1,0:T(8,128)S(1)}, f32[306,128]{1,0:T(8,128)S(1)}, u32[]{:S(2)}, u32[]{:S(2)}) collective-permute-start(f32[306,128]{1,0:T(8,128)S(1)} %get-tuple-element.38), channel_id=1, source_target_pairs={{0,15},{1,2},{2,1},{3,4},{4,3},{5,6},{6,5},{7,8},{8,7},{9,10},{10,... | collective-permute-start | bytes 470024 | tf_op jit(solution)/shard_map/ppermute | solution.py:395
  15.4 0.0 collective-permute-start.3
  15.4 0.0 collective-permute-done.4.inner_in
  15.4 1.9 %collective-permute-done.5.outer_in = f32[24,2240]{1,0:T(8,128)S(1)} collective-permute-done((f32[24,2240]{1,0:T(8,128)S(1)}, f32[24,2240]{1,0:T(8,128)S(1)}, u32[]{:S(2)}, u32[]{:S(2)}) %collective-permute-start.5) | collective-permute-done | bytes 215072 | tf_op jit(solution)/shard_map/ppermute | solution.py:395
  17.4 0.2 absorb.1
  17.5 1.6 %collective-permute-done.2.outer_in = f32[306,128]{1,0:T(8,128)S(1)} collective-permute-done((f32[306,128]{1,0:T(8,128)S(1)}, f32[306,128]{1,0:T(8,128)S(1)}, u32[]{:S(2)}, u32[]{:S(2)}) %collective-permute-start.2) | collective-permute-done | bytes 156704 | tf_op jit(solution)/shard_map/ppermute | solution.py:395
  19.2 0.0 collective-permute-done.3.inner_in
  19.2 1.9 %second_solve.1 = (f32[64,2240]{1,0:T(8,128)S(1)}, f32[48,2240]{1,0:T(8,128)S(1)}, f32[48,2240]{1,0:T(8,128)S(1)}, f32[162,128]{1,0:T(8,128)S(1)}, f32[162,128]{1,0:T(8,128)S(1)}) custom-call(s32[1]{0:T(128)} %bitcast.parity, f32[306,128]{1,0:T(8,128)S(1)} %collective-permute-done.2.outer_in, f32[306,128]{1,0:T(8,128)S(1)} %collective-permute-done.3.inner_in, ...), custom_call_target="tpu_custom_call" | custom-call | tf_op jit(solution)/shard_map/second_solve/pallas_call | solution.py:473
  21.0 3.7 %collective-permute-start.6 = (f32[162,128]{1,0:T(8,128)S(1)}, f32[162,128]{1,0:T(8,128)S(1)}, u32[]{:S(2)}, u32[]{:S(2)}) collective-permute-start(f32[162,128]{1,0:T(8,128)S(1)} %get-tuple-element.47), channel_id=1, source_target_pairs={{0,15},{1,2},{2,1},{3,4},{4,3},{5,6},{6,5},{7,8},{8,7},{9,10},{10,... | collective-permute-start | bytes 248840 | tf_op jit(solution)/shard_map/ppermute | solution.py:395
  24.8 0.0 collective-permute-start.7
  24.8 2.0 %early_sums.1 = (f32[48,2240]{1,0:T(8,128)S(1)}, f32[32,2240]{1,0:T(8,128)S(1)}, f32[1,128]{1,0:T(1,128)S(1)}, f32[6,32,2240]{2,1,0:T(8,128)S(1)}, f32[6,32,2240]{2,1,0:T(8,128)S(1)}) custom-call(f32[64,2240]{1,0:T(8,128)S(1)} %get-tuple-element.49.z, f32[48,2240]{1,0:T(8,128)S(1)} %get-tuple-element.50.y, f32[64,2240]{1,0:T(8,128)S(1)} %get-tuple-element.46.c_rows, ...), custom_call_target="tpu_custom_call" | custom-call | flops 1000000 | bytes 7000000 | tf_op jit(solution)/shard_map/early_sums/pallas_call | solution.py:486
  26.8 0.9 %collective-permute-done.6.outer_in = f32[162,128]{1,0:T(8,128)S(1)} collective-permute-done((f32[162,128]{1,0:T(8,128)S(1)}, f32[162,128]{1,0:T(8,128)S(1)}, u32[]{:S(2)}, u32[]{:S(2)}) %collective-permute-start.6) | collective-permute-done | bytes 82976 | tf_op jit(solution)/shard_map/ppermute | solution.py:395
  27.7 0.0 collective-permute-done.7.inner_in
  27.7 0.5 %sums.1 = (f32[48,2240]{1,0:T(8,128)S(1)}, f32[16,1,128]{2,1,0:T(1,128)S(1)}) custom-call(s32[1]{0:T(128)} %bitcast.parity, f32[162,128]{1,0:T(8,128)S(1)} %collective-permute-done.6.outer_in, f32[162,128]{1,0:T(8,128)S(1)} %collective-permute-done.7.inner_in, f32[48,2240]{1,0:T(8,128)S(1)} %get-tuple-element.53.w_rows, f32[64,2240]{1,0:T(8,128)S(1)} %get-tuple-element.49.z, ...), custom_call_target="tpu_custom_call" | custom-call | tf_op jit(solution)/shard_map/sums/pallas_call | solution.py:498
  28.2 8.4 %all_to_all.5.came = f32[16,1,128]{2,1,0:T(1,128)S(1)} all-to-all(f32[16,1,128]{2,1,0:T(1,128)S(1)} %get-tuple-element.56), channel_id=1, replica_groups={{15,14,13,12,11,10,9,8,7,6,5,4,3,2,1,0},{31,30,29,28,27,26,25,24,23,22,..., dimensions={0} | all-to-all | bytes 16384 | tf_op jit(solution)/shard_map/all_to_all | solution.py:507
  36.7 3.0 %finish.1 = (f32[32,2240]{1,0:T(8,128)}, f32[6,32,2240]{2,1,0:T(8,128)}, f32[6,32,2240]{2,1,0:T(8,128)}, f32[6,32,2240]{2,1,0:T(8,128)}) custom-call(f32[16,1,128]{2,1,0:T(1,128)S(1)} %all_to_all.5.came, f32[64,2240]{1,0:T(8,128)S(1)} %get-tuple-element.49.z, f32[48,2240]{1,0:T(8,128)S(1)} %get-tuple-element.57.w, f32[48,2240]{1,0:T(8,128)S(1)} %get-tuple-element.58.d_rows, ...), custom_call_target="tpu_custom_call" | custom-call | tf_op jit(solution)/shard_map/finish/pallas_call | solution.py:509
Async XLA Ops:
  1.6 7.9 %collective-permute-start.1 = (f32[8,2240]{1,0:T(8,128)S(1)}, f32[8,2240]{1,0:T(8,128)S(1)}, u32[]{:S(2)}, u32[]{:S(2)}) collective-permute-start(f32[8,2240]{1,0:T(8,128)S(1)} %first_edges.1.after), channel_id=1, source_target_pairs={{0,15},{1,2},{2,1},{3,4},{4,3},{5,6},{6,5},{7,8},{8,7},{9,10},{10,... | collective-permute-start | bytes 215048 | tf_op jit(solution)/shard_map/ppermute | solution.py:395
  8.6 1.3 %collective-permute-start = (f32[8,2240]{1,0:T(8,128)S(1)}, f32[8,2240]{1,0:T(8,128)S(1)}, u32[]{:S(2)}, u32[]{:S(2)}) collective-permute-start(f32[8,2240]{1,0:T(8,128)S(1)} %get-tuple-element.33), channel_id=1, source_target_pairs={{0,1},{1,0},{2,3},{3,2},{4,5},{5,4},{6,7},{7,6},{8,9},{9,8},{10,11... | collective-permute-start | bytes 215048 | tf_op jit(solution)/shard_map/ppermute | solution.py:395
  8.7 6.7 %collective-permute-start.4 = (f32[24,2240]{1,0:T(8,128)S(1)}, f32[24,2240]{1,0:T(8,128)S(1)}, u32[]{:S(2)}, u32[]{:S(2)}) collective-permute-start(f32[24,2240]{1,0:T(8,128)S(1)} %get-tuple-element.41), channel_id=1, source_target_pairs={{0,1},{1,0},{2,3},{3,2},{4,5},{5,4},{6,7},{7,6},{8,9},{9,8},{10,11... | collective-permute-start | bytes 645128 | tf_op jit(solution)/shard_map/ppermute | solution.py:395
  9.2 8.2 %collective-permute-start.5 = (f32[24,2240]{1,0:T(8,128)S(1)}, f32[24,2240]{1,0:T(8,128)S(1)}, u32[]{:S(2)}, u32[]{:S(2)}) collective-permute-start(f32[24,2240]{1,0:T(8,128)S(1)} %get-tuple-element.42), channel_id=1, source_target_pairs={{0,15},{1,2},{2,1},{3,4},{4,3},{5,6},{6,5},{7,8},{8,7},{9,10},{10,... | collective-permute-start | bytes 645128 | tf_op jit(solution)/shard_map/ppermute | solution.py:395
  11.6 7.5 %collective-permute-start.2 = (f32[306,128]{1,0:T(8,128)S(1)}, f32[306,128]{1,0:T(8,128)S(1)}, u32[]{:S(2)}, u32[]{:S(2)}) collective-permute-start(f32[306,128]{1,0:T(8,128)S(1)} %get-tuple-element.38), channel_id=1, source_target_pairs={{0,15},{1,2},{2,1},{3,4},{4,3},{5,6},{6,5},{7,8},{8,7},{9,10},{10,... | collective-permute-start | bytes 470024 | tf_op jit(solution)/shard_map/ppermute | solution.py:395
  15.4 3.7 %collective-permute-start.3 = (f32[306,128]{1,0:T(8,128)S(1)}, f32[306,128]{1,0:T(8,128)S(1)}, u32[]{:S(2)}, u32[]{:S(2)}) collective-permute-start(f32[306,128]{1,0:T(8,128)S(1)} %get-tuple-element.39), channel_id=1, source_target_pairs={{0,1},{1,0},{2,3},{3,2},{4,5},{5,4},{6,7},{7,6},{8,9},{9,8},{10,11... | collective-permute-start | bytes 470024 | tf_op jit(solution)/shard_map/ppermute | solution.py:395
  21.0 6.7 %collective-permute-start.6 = (f32[162,128]{1,0:T(8,128)S(1)}, f32[162,128]{1,0:T(8,128)S(1)}, u32[]{:S(2)}, u32[]{:S(2)}) collective-permute-start(f32[162,128]{1,0:T(8,128)S(1)} %get-tuple-element.47), channel_id=1, source_target_pairs={{0,15},{1,2},{2,1},{3,4},{4,3},{5,6},{6,5},{7,8},{8,7},{9,10},{10,... | collective-permute-start | bytes 248840 | tf_op jit(solution)/shard_map/ppermute | solution.py:395
  24.8 2.9 %collective-permute-start.7 = (f32[162,128]{1,0:T(8,128)S(1)}, f32[162,128]{1,0:T(8,128)S(1)}, u32[]{:S(2)}, u32[]{:S(2)}) collective-permute-start(f32[162,128]{1,0:T(8,128)S(1)} %get-tuple-element.48), channel_id=1, source_target_pairs={{0,1},{1,0},{2,3},{3,2},{4,5},{5,4},{6,7},{7,6},{8,9},{9,8},{10,11... | collective-permute-start | bytes 248840 | tf_op jit(solution)/shard_map/ppermute | solution.py:395

commit v16 on v15

--- a/solution.py
+++ b/solution.py
@@ -164,23 +164,24 @@
     return jnp.concatenate(blocks, axis=1)[:, :lat]
 
 
-def first_edges(parity, source, bottom, outer, rows, depth, sems):
-    start = pl.multiple_of(parity[0] * (source.shape[0] - OV), OV)
-    at = pl.ds(start, OV)
-    copies = [
-        pltpu.make_async_copy(source.at[at], rows, sems.at[0]),
-        pltpu.make_async_copy(bottom.at[at], depth, sems.at[1]),
-    ]
+def first_edges(parity, source, bottom, outer, inner, rows, depth, sems):
+    last = source.shape[0] - OV
+    copies = []
+    for i, start in enumerate((parity[0] * last, (1 - parity[0]) * last)):
+        at = pl.ds(pl.multiple_of(start, OV), OV)
+        copies.append(pltpu.make_async_copy(source.at[at], rows.at[i], sems.at[2 * i]))
+        copies.append(pltpu.make_async_copy(bottom.at[at], depth.at[i], sems.at[2 * i + 1]))
     for copy in copies:
         copy.start()
     for copy in copies:
         copy.wait()
-    outer[...] = jnp.where(depth[...] > 0, rows[...], 0.0)
+    outer[...] = jnp.where(depth[0] > 0, rows[0], 0.0)
+    inner[...] = jnp.where(depth[1] > 0, rows[1], 0.0)
 
 
 def prepare(parity, after, source_h, diagonal_h, bottom_h, u_h, *refs):
-    tables_h, (inner, far_inner, far_outer, masked, coef, depth, source), held = refs[:3], refs[3:10], refs[10:13]
-    diagonal, bottom, u_strip, sems = refs[13:]
+    tables_h, (far_inner, far_outer, masked, coef, depth, source), held = refs[:3], refs[3:9], refs[9:12]
+    diagonal, bottom, u_strip, sems = refs[12:]
     cells, lat = source.shape
     pairs = [(source_h, source), (bottom_h, bottom), (diagonal_h, diagonal)]
     pairs += [(u_h.at[:, pl.ds(cells - OV, OV)], u_strip)]
@@ -202,12 +203,11 @@
     far_outer[: 2 * OV], far_inner[: 2 * OV] = pick(parity, to_east, to_west)
     for message in (far_outer, far_inner):
         message[2 * OV :] = jnp.zeros((FAR - 2 * OV, lat), F32)
-    inner[...] = pick(parity, masked[:OV], masked[cells - OV :])[0]
     for copy in copies[4:]:
         copy.wait()
 
 
-def first_solve(parity, inner_in, outer_in, masked, lat_basis, lon, scale,
+def first_solve(parity, outer_in, inner_in, masked, lat_basis, lon, scale,
                 first, inner, outer, wide, rows, spectral):
     cells, lat = masked.shape
     west, east = pick(parity, inner_in[...], outer_in[...])
@@ -414,24 +414,23 @@
         ("source", source), ("diagonal", diagonal), ("u", u_vel), ("v", v_vel), ("bottom", bottom))}
     consts = [pltpu.with_memory_space_constraint(x, pltpu.HBM) for x in consts]
 
-    outer = pl.pallas_call(
+    outer, inner = pl.pallas_call(
         first_edges,
         in_specs=[SM, HB, HB],
-        out_specs=VM,
-        out_shape=pltpu.VMEM((OV, lat), F32),
-        scratch_shapes=[pltpu.VMEM((OV, lat), F32), pltpu.VMEM((OV, lat), jnp.int32),
-                        pltpu.SemaphoreType.DMA((2,))],
+        out_specs=[VM] * 2,
+        out_shape=[pltpu.VMEM((OV, lat), F32)] * 2,
+        scratch_shapes=[pltpu.VMEM((2, OV, lat), F32), pltpu.VMEM((2, OV, lat), jnp.int32),
+                        pltpu.SemaphoreType.DMA((4,))],
         compiler_params=PARAMS,
         name="first_edges",
     )(parity, hbm["source"], hbm["bottom"])
-    outer_in = swap_pairs(outer, True)
-
-    inner, far_inner, far_outer, masked, coef, depth, source_v, *held = pl.pallas_call(
+    near = swap(inner, outer)
+
+    far_inner, far_outer, masked, coef, depth, source_v, *held = pl.pallas_call(
         prepare,
         in_specs=[SM] + [HB] * 8,
-        out_specs=[VM] * 10,
-        out_shape=[pltpu.VMEM((OV, lat), F32)]
-        + [pltpu.VMEM((FAR, lat), F32)] * 2
+        out_specs=[VM] * 9,
+        out_shape=[pltpu.VMEM((FAR, lat), F32)] * 2
         + [pltpu.VMEM((cells, lat), F32)] * 4
         + [pltpu.VMEM(table.shape, table.dtype) for table in consts],
         scratch_shapes=[
@@ -443,8 +442,7 @@
         compiler_params=PARAMS,
         cost_estimate=pl.CostEstimate(flops=10**6, bytes_accessed=7 * 10**6, transcendentals=0),
         name="prepare",
-    )(parity, outer, hbm["source"], hbm["diagonal"], hbm["bottom"], hbm["u"], *consts)
-    near = swap_pairs(inner, False), outer_in
+    )(parity, inner, hbm["source"], hbm["diagonal"], hbm["bottom"], hbm["u"], *consts)
     far = swap(far_inner, far_outer)[::-1]
 
     blocks = -(-lat // LANE)

time: 39.9 us -> 40 us (level)
  waiting for transfers between devices: 4.96 us -> 4.3 us
  starting transfers between devices: 13.8 us -> 14.4 us
    ppermute x8, waiting for transfers between devices: 4.96 us -> 4.3 us  [swap_pairs(): return lax.ppermute(block, 'lon', route)]
    ppermute x8, starting transfers between devices: 13.8 us -> 14.4 us  [swap_pairs(): return lax.ppermute(block, 'lon', route)]
  transfers between devices with their start and end apart: 8 -> 8, of which waited for: 4 -> 3; matrix products, arithmetic and copies ran while one was open for 0% -> 0% of each run, Pallas kernels for 14% -> 14%
where the time goes in v16:
time: 40 us; the launch traced here: 39.8 us
  starting transfers between devices  14.4 us (36%)
  Pallas kernels  11.8 us (30%)
  blocking collectives  8.54 us (21%)
  waiting for transfers between devices  4.3 us (11%)
  between operations  0.69 us (2%)
    ppermute x8, starting transfers between devices, swap_pairs(): return lax.ppermute(block, 'lon', route)  14.4 us
    all_to_all x1, blocking collectives, body(): came = lax.all_to_all(sent, 'lon', 0, 0, axis_index_groups=ring)  8.54 us
    ppermute x8, waiting for transfers between devices, swap_pairs(): return lax.ppermute(block, 'lon', route)  4.3 us
    pallas_call x1, Pallas kernels, body(): pl.pallas_call(finish, in_specs=[VM] * 8, out_specs=[HB] * 4, out_shape=[...  3.02 us
    pallas_call x1, Pallas kernels, body(): pl.pallas_call(early_sums, in_specs=[VM] * 5 + [HB] * 2, out_specs=[VM] *...  2.03 us
    pallas_call x1, Pallas kernels, body(): pl.pallas_call(second_solve, in_specs=[SM] + [VM] * 7, out_specs=[VM] * 5...  1.87 us
    pallas_call x1, Pallas kernels, body(): pl.pallas_call(first_solve, in_specs=[SM] + [VM] * 6, out_specs=[VM] * 3,...  1.68 us
    pallas_call x1, Pallas kernels, body(): pl.pallas_call(prepare, in_specs=[SM] + [HB] * 8, out_specs=[VM] * 9, out...  1.53 us
  transfers between devices with their start and end apart: 8, of which 3 were waited for; matrix products, arithmetic and copies ran while one was open for 0% of the time, Pallas kernels for 14%

profile of v16, /device:TPU:0, one launch (start us, length us, event | category | flops | bytes accessed | tf_op | source)
XLA Modules:
  0.0 39.8 jit_solution(837554635581742300)
XLA Ops:
  0.6 1.0 %first_edges.1 = (f32[8,2240]{1,0:T(8,128)S(1)}, f32[8,2240]{1,0:T(8,128)S(1)}) custom-call(s32[1]{0:T(128)} %bitcast.parity, f32[32,2240]{1,0:T(8,128)} %source_h.1, s32[32,2240]{1,0:T(8,128)} %bottom_h.1), custom_call_target="tpu_custom_call" | custom-call | tf_op jit(solution)/shard_map/first_edges/pallas_call | solution.py:417
  1.7 5.5 %collective-permute-start = (f32[8,2240]{1,0:T(8,128)S(1)}, f32[8,2240]{1,0:T(8,128)S(1)}, u32[]{:S(2)}, u32[]{:S(2)}) collective-permute-start(f32[8,2240]{1,0:T(8,128)S(1)} %get-tuple-element.34), channel_id=1, source_target_pairs={{0,15},{1,2},{2,1},{3,4},{4,3},{5,6},{6,5},{7,8},{8,7},{9,10},{10,... | collective-permute-start | bytes 215048 | tf_op jit(solution)/shard_map/ppermute | solution.py:395
  7.2 0.0 collective-permute-start.1
  7.2 1.5 %prepare.1 = (f32[24,2240]{1,0:T(8,128)S(1)}, f32[24,2240]{1,0:T(8,128)S(1)}, f32[32,2240]{1,0:T(8,128)S(1)}, f32[32,2240]{1,0:T(8,128)S(1)}, f32[32,2240]{1,0:T...) custom-call(s32[1]{0:T(128)} %bitcast.parity, ...), custom_call_target="tpu_custom_call" | custom-call | flops 1000000 | bytes 7000000 | tf_op jit(solution)/shard_map/prepare/pallas_call | solution.py:429
  8.7 0.6 %collective-permute-start.4 = (f32[24,2240]{1,0:T(8,128)S(1)}, f32[24,2240]{1,0:T(8,128)S(1)}, u32[]{:S(2)}, u32[]{:S(2)}) collective-permute-start(f32[24,2240]{1,0:T(8,128)S(1)} %get-tuple-element.43), channel_id=1, source_target_pairs={{0,1},{1,0},{2,3},{3,2},{4,5},{5,4},{6,7},{7,6},{8,9},{9,8},{10,11... | collective-permute-start | bytes 645128 | tf_op jit(solution)/shard_map/ppermute | solution.py:395
  9.3 0.3 collective-permute-start.5
  9.6 0.0 collective-permute-done.outer_in
  9.6 0.0 collective-permute-done.1.inner_in
  9.6 1.7 %first_solve.1 = (f32[48,2240]{1,0:T(8,128)S(1)}, f32[306,128]{1,0:T(8,128)S(1)}, f32[306,128]{1,0:T(8,128)S(1)}) custom-call(s32[1]{0:T(128)} %bitcast.parity, f32[8,2240]{1,0:T(8,128)S(1)} %collective-permute-done.outer_in, f32[8,2240]{1,0:T(8,128)S(1)} %collective-permute-done.1.inner_in, f32[32,2240]{1,0:T(8,128)S(1)} %get-tuple-element.36.masked, ...), custom_call_target="tpu_custom_call" | custom-call | tf_op jit(solution)/shard_map/first_solve/pallas_call | solution.py:449
  11.3 4.2 %collective-permute-start.2 = (f32[306,128]{1,0:T(8,128)S(1)}, f32[306,128]{1,0:T(8,128)S(1)}, u32[]{:S(2)}, u32[]{:S(2)}) collective-permute-start(f32[306,128]{1,0:T(8,128)S(1)} %get-tuple-element.40), channel_id=1, source_target_pairs={{0,15},{1,2},{2,1},{3,4},{4,3},{5,6},{6,5},{7,8},{8,7},{9,10},{10,... | collective-permute-start | bytes 470024 | tf_op jit(solution)/shard_map/ppermute | solution.py:395
  15.5 0.0 collective-permute-start.3
  15.5 0.0 collective-permute-done.4.inner_in
  15.5 1.9 %collective-permute-done.5.outer_in = f32[24,2240]{1,0:T(8,128)S(1)} collective-permute-done((f32[24,2240]{1,0:T(8,128)S(1)}, f32[24,2240]{1,0:T(8,128)S(1)}, u32[]{:S(2)}, u32[]{:S(2)}) %collective-permute-start.5) | collective-permute-done | bytes 215072 | tf_op jit(solution)/shard_map/ppermute | solution.py:395
  17.4 0.2 absorb.1
  17.6 1.6 %collective-permute-done.2.outer_in = f32[306,128]{1,0:T(8,128)S(1)} collective-permute-done((f32[306,128]{1,0:T(8,128)S(1)}, f32[306,128]{1,0:T(8,128)S(1)}, u32[]{:S(2)}, u32[]{:S(2)}) %collective-permute-start.2) | collective-permute-done | bytes 156704 | tf_op jit(solution)/shard_map/ppermute | solution.py:395
  19.2 0.0 collective-permute-done.3.inner_in
  19.2 1.9 %second_solve.1 = (f32[64,2240]{1,0:T(8,128)S(1)}, f32[48,2240]{1,0:T(8,128)S(1)}, f32[48,2240]{1,0:T(8,128)S(1)}, f32[162,128]{1,0:T(8,128)S(1)}, f32[162,128]{1,0:T(8,128)S(1)}) custom-call(s32[1]{0:T(128)} %bitcast.parity, f32[306,128]{1,0:T(8,128)S(1)} %collective-permute-done.2.outer_in, f32[306,128]{1,0:T(8,128)S(1)} %collective-permute-done.3.inner_in, ...), custom_call_target="tpu_custom_call" | custom-call | tf_op jit(solution)/shard_map/second_solve/pallas_call | solution.py:471
  21.0 3.8 %collective-permute-start.6 = (f32[162,128]{1,0:T(8,128)S(1)}, f32[162,128]{1,0:T(8,128)S(1)}, u32[]{:S(2)}, u32[]{:S(2)}) collective-permute-start(f32[162,128]{1,0:T(8,128)S(1)} %get-tuple-element.49), channel_id=1, source_target_pairs={{0,15},{1,2},{2,1},{3,4},{4,3},{5,6},{6,5},{7,8},{8,7},{9,10},{10,... | collective-permute-start | bytes 248840 | tf_op jit(solution)/shard_map/ppermute | solution.py:395
  24.9 0.0 collective-permute-start.7
  24.9 2.0 %early_sums.1 = (f32[48,2240]{1,0:T(8,128)S(1)}, f32[32,2240]{1,0:T(8,128)S(1)}, f32[1,128]{1,0:T(1,128)S(1)}, f32[6,32,2240]{2,1,0:T(8,128)S(1)}, f32[6,32,2240]{2,1,0:T(8,128)S(1)}) custom-call(f32[64,2240]{1,0:T(8,128)S(1)} %get-tuple-element.51.z, f32[48,2240]{1,0:T(8,128)S(1)} %get-tuple-element.52.y, f32[64,2240]{1,0:T(8,128)S(1)} %get-tuple-element.48.c_rows, ...), custom_call_target="tpu_custom_call" | custom-call | flops 1000000 | bytes 7000000 | tf_op jit(solution)/shard_map/early_sums/pallas_call | solution.py:484
  26.9 0.8 %collective-permute-done.6.outer_in = f32[162,128]{1,0:T(8,128)S(1)} collective-permute-done((f32[162,128]{1,0:T(8,128)S(1)}, f32[162,128]{1,0:T(8,128)S(1)}, u32[]{:S(2)}, u32[]{:S(2)}) %collective-permute-start.6) | collective-permute-done | bytes 82976 | tf_op jit(solution)/shard_map/ppermute | solution.py:395
  27.7 0.0 collective-permute-done.7.inner_in
  27.7 0.5 %sums.1 = (f32[48,2240]{1,0:T(8,128)S(1)}, f32[16,1,128]{2,1,0:T(1,128)S(1)}) custom-call(s32[1]{0:T(128)} %bitcast.parity, f32[162,128]{1,0:T(8,128)S(1)} %collective-permute-done.6.outer_in, f32[162,128]{1,0:T(8,128)S(1)} %collective-permute-done.7.inner_in, f32[48,2240]{1,0:T(8,128)S(1)} %get-tuple-element.55.w_rows, f32[64,2240]{1,0:T(8,128)S(1)} %get-tuple-element.51.z, ...), custom_call_target="tpu_custom_call" | custom-call | tf_op jit(solution)/shard_map/sums/pallas_call | solution.py:496
  28.2 8.5 %all_to_all.5.came = f32[16,1,128]{2,1,0:T(1,128)S(1)} all-to-all(f32[16,1,128]{2,1,0:T(1,128)S(1)} %get-tuple-element.58), channel_id=1, replica_groups={{15,14,13,12,11,10,9,8,7,6,5,4,3,2,1,0},{31,30,29,28,27,26,25,24,23,22,..., dimensions={0} | all-to-all | bytes 16384 | tf_op jit(solution)/shard_map/all_to_all | solution.py:505
  36.8 3.0 %finish.1 = (f32[32,2240]{1,0:T(8,128)}, f32[6,32,2240]{2,1,0:T(8,128)}, f32[6,32,2240]{2,1,0:T(8,128)}, f32[6,32,2240]{2,1,0:T(8,128)}) custom-call(f32[16,1,128]{2,1,0:T(1,128)S(1)} %all_to_all.5.came, f32[64,2240]{1,0:T(8,128)S(1)} %get-tuple-element.51.z, f32[48,2240]{1,0:T(8,128)S(1)} %get-tuple-element.59.w, f32[48,2240]{1,0:T(8,128)S(1)} %get-tuple-element.60.d_rows, ...), custom_call_target="tpu_custom_call" | custom-call | tf_op jit(solution)/shard_map/finish/pallas_call | solution.py:507
Async XLA Ops:
  1.7 7.9 %collective-permute-start = (f32[8,2240]{1,0:T(8,128)S(1)}, f32[8,2240]{1,0:T(8,128)S(1)}, u32[]{:S(2)}, u32[]{:S(2)}) collective-permute-start(f32[8,2240]{1,0:T(8,128)S(1)} %get-tuple-element.34), channel_id=1, source_target_pairs={{0,15},{1,2},{2,1},{3,4},{4,3},{5,6},{6,5},{7,8},{8,7},{9,10},{10,... | collective-permute-start | bytes 215048 | tf_op jit(solution)/shard_map/ppermute | solution.py:395
  7.2 2.4 %collective-permute-start.1 = (f32[8,2240]{1,0:T(8,128)S(1)}, f32[8,2240]{1,0:T(8,128)S(1)}, u32[]{:S(2)}, u32[]{:S(2)}) collective-permute-start(f32[8,2240]{1,0:T(8,128)S(1)} %get-tuple-element.35.after), channel_id=1, source_target_pairs={{0,1},{1,0},{2,3},{3,2},{4,5},{5,4},{6,7},{7,6},{8,9},{9,8},{10,11... | collective-permute-start | bytes 215048 | tf_op jit(solution)/shard_map/ppermute | solution.py:395
  8.7 6.8 %collective-permute-start.4 = (f32[24,2240]{1,0:T(8,128)S(1)}, f32[24,2240]{1,0:T(8,128)S(1)}, u32[]{:S(2)}, u32[]{:S(2)}) collective-permute-start(f32[24,2240]{1,0:T(8,128)S(1)} %get-tuple-element.43), channel_id=1, source_target_pairs={{0,1},{1,0},{2,3},{3,2},{4,5},{5,4},{6,7},{7,6},{8,9},{9,8},{10,11... | collective-permute-start | bytes 645128 | tf_op jit(solution)/shard_map/ppermute | solution.py:395
  9.3 8.2 %collective-permute-start.5 = (f32[24,2240]{1,0:T(8,128)S(1)}, f32[24,2240]{1,0:T(8,128)S(1)}, u32[]{:S(2)}, u32[]{:S(2)}) collective-permute-start(f32[24,2240]{1,0:T(8,128)S(1)} %get-tuple-element.44), channel_id=1, source_target_pairs={{0,15},{1,2},{2,1},{3,4},{4,3},{5,6},{6,5},{7,8},{8,7},{9,10},{10,... | collective-permute-start | bytes 645128 | tf_op jit(solution)/shard_map/ppermute | solution.py:395
  11.3 7.9 %collective-permute-start.2 = (f32[306,128]{1,0:T(8,128)S(1)}, f32[306,128]{1,0:T(8,128)S(1)}, u32[]{:S(2)}, u32[]{:S(2)}) collective-permute-start(f32[306,128]{1,0:T(8,128)S(1)} %get-tuple-element.40), channel_id=1, source_target_pairs={{0,15},{1,2},{2,1},{3,4},{4,3},{5,6},{6,5},{7,8},{8,7},{9,10},{10,... | collective-permute-start | bytes 470024 | tf_op jit(solution)/shard_map/ppermute | solution.py:395
  15.5 3.6 %collective-permute-start.3 = (f32[306,128]{1,0:T(8,128)S(1)}, f32[306,128]{1,0:T(8,128)S(1)}, u32[]{:S(2)}, u32[]{:S(2)}) collective-permute-start(f32[306,128]{1,0:T(8,128)S(1)} %get-tuple-element.41), channel_id=1, source_target_pairs={{0,1},{1,0},{2,3},{3,2},{4,5},{5,4},{6,7},{7,6},{8,9},{9,8},{10,11... | collective-permute-start | bytes 470024 | tf_op jit(solution)/shard_map/ppermute | solution.py:395
  21.0 6.7 %collective-permute-start.6 = (f32[162,128]{1,0:T(8,128)S(1)}, f32[162,128]{1,0:T(8,128)S(1)}, u32[]{:S(2)}, u32[]{:S(2)}) collective-permute-start(f32[162,128]{1,0:T(8,128)S(1)} %get-tuple-element.49), channel_id=1, source_target_pairs={{0,15},{1,2},{2,1},{3,4},{4,3},{5,6},{6,5},{7,8},{8,7},{9,10},{10,... | collective-permute-start | bytes 248840 | tf_op jit(solution)/shard_map/ppermute | solution.py:395
  24.9 2.9 %collective-permute-start.7 = (f32[162,128]{1,0:T(8,128)S(1)}, f32[162,128]{1,0:T(8,128)S(1)}, u32[]{:S(2)}, u32[]{:S(2)}) collective-permute-start(f32[162,128]{1,0:T(8,128)S(1)} %get-tuple-element.50), channel_id=1, source_target_pairs={{0,1},{1,0},{2,3},{3,2},{4,5},{5,4},{6,7},{7,6},{8,9},{9,8},{10,11... | collective-permute-start | bytes 248840 | tf_op jit(solution)/shard_map/ppermute | solution.py:395

commit v17 on v16

--- a/solution.py
+++ b/solution.py
@@ -221,7 +221,7 @@
     pack(outer, to_outer)
 
 
-def absorb(parity, first, inner_in, outer_in, coef, depth, c_rows, z_rows, d_rows, edge):
+def absorb(parity, first, outer_in, inner_in, coef, depth, c_rows, z_rows, d_rows, edge):
     cells, lat = coef.shape
     west, east = pick(parity, inner_in[: 2 * OV], outer_in[: 2 * OV])
     edge[...] = west[:OV]
@@ -443,7 +443,7 @@
         cost_estimate=pl.CostEstimate(flops=10**6, bytes_accessed=7 * 10**6, transcendentals=0),
         name="prepare",
     )(parity, inner, hbm["source"], hbm["diagonal"], hbm["bottom"], hbm["u"], *consts)
-    far = swap(far_inner, far_outer)[::-1]
+    far = swap(far_inner, far_outer)
 
     blocks = -(-lat // LANE)
     first, inner, outer = pl.pallas_call(

time: 40 us -> 40 us (level)
  waiting for transfers between devices: 4.3 us -> 3.58 us
  starting transfers between devices: 14.4 us -> 14.8 us
    ppermute x8, waiting for transfers between devices: 4.3 us -> 3.58 us  [swap_pairs(): return lax.ppermute(block, 'lon', route)]
where the time goes in v17:
time: 40 us; the launch traced here: 39.8 us
  starting transfers between devices  14.8 us (37%)
  Pallas kernels  11.8 us (30%)
  blocking collectives  8.86 us (22%)
  waiting for transfers between devices  3.58 us (9%)
  between operations  0.7 us (2%)
    ppermute x8, starting transfers between devices, swap_pairs(): return lax.ppermute(block, 'lon', route)  14.8 us
    all_to_all x1, blocking collectives, body(): came = lax.all_to_all(sent, 'lon', 0, 0, axis_index_groups=ring)  8.86 us
    ppermute x8, waiting for transfers between devices, swap_pairs(): return lax.ppermute(block, 'lon', route)  3.58 us
    pallas_call x1, Pallas kernels, body(): pl.pallas_call(finish, in_specs=[VM] * 8, out_specs=[HB] * 4, out_shape=[...  3.02 us
    pallas_call x1, Pallas kernels, body(): pl.pallas_call(early_sums, in_specs=[VM] * 5 + [HB] * 2, out_specs=[VM] *...  2.03 us
    pallas_call x1, Pallas kernels, body(): pl.pallas_call(second_solve, in_specs=[SM] + [VM] * 7, out_specs=[VM] * 5...  1.87 us
    pallas_call x1, Pallas kernels, body(): pl.pallas_call(first_solve, in_specs=[SM] + [VM] * 6, out_specs=[VM] * 3,...  1.68 us
    pallas_call x1, Pallas kernels, body(): pl.pallas_call(prepare, in_specs=[SM] + [HB] * 8, out_specs=[VM] * 9, out...  1.53 us
  transfers between devices with their start and end apart: 8, of which 3 were waited for; matrix products, arithmetic and copies ran while one was open for 0% of the time, Pallas kernels for 14%

profile of v17, /device:TPU:0, one launch (start us, length us, event | category | flops | bytes accessed | tf_op | source)
XLA Modules:
  0.0 39.8 jit_solution(9892484388831797338)
XLA Ops:
  0.6 1.0 %first_edges.1 = (f32[8,2240]{1,0:T(8,128)S(1)}, f32[8,2240]{1,0:T(8,128)S(1)}) custom-call(s32[1]{0:T(128)} %bitcast.parity, f32[32,2240]{1,0:T(8,128)} %source_h.1, s32[32,2240]{1,0:T(8,128)} %bottom_h.1), custom_call_target="tpu_custom_call" | custom-call | tf_op jit(solution)/shard_map/first_edges/pallas_call | solution.py:417
  1.7 5.5 %collective-permute-start = (f32[8,2240]{1,0:T(8,128)S(1)}, f32[8,2240]{1,0:T(8,128)S(1)}, u32[]{:S(2)}, u32[]{:S(2)}) collective-permute-start(f32[8,2240]{1,0:T(8,128)S(1)} %get-tuple-element.34), channel_id=1, source_target_pairs={{0,15},{1,2},{2,1},{3,4},{4,3},{5,6},{6,5},{7,8},{8,7},{9,10},{10,... | collective-permute-start | bytes 215048 | tf_op jit(solution)/shard_map/ppermute | solution.py:395
  7.2 0.0 collective-permute-start.1
  7.2 1.5 %prepare.1 = (f32[24,2240]{1,0:T(8,128)S(1)}, f32[24,2240]{1,0:T(8,128)S(1)}, f32[32,2240]{1,0:T(8,128)S(1)}, f32[32,2240]{1,0:T(8,128)S(1)}, f32[32,2240]{1,0:T...) custom-call(s32[1]{0:T(128)} %bitcast.parity, ...), custom_call_target="tpu_custom_call" | custom-call | flops 1000000 | bytes 7000000 | tf_op jit(solution)/shard_map/prepare/pallas_call | solution.py:429
  8.7 0.8 %collective-permute-start.4 = (f32[24,2240]{1,0:T(8,128)S(1)}, f32[24,2240]{1,0:T(8,128)S(1)}, u32[]{:S(2)}, u32[]{:S(2)}) collective-permute-start(f32[24,2240]{1,0:T(8,128)S(1)} %get-tuple-element.43), channel_id=1, source_target_pairs={{0,15},{1,2},{2,1},{3,4},{4,3},{5,6},{6,5},{7,8},{8,7},{9,10},{10,... | collective-permute-start | bytes 645128 | tf_op jit(solution)/shard_map/ppermute | solution.py:395
  9.5 0.0 collective-permute-start.5
  9.5 0.0 collective-permute-done.outer_in
  9.5 0.0 collective-permute-done.1.inner_in
  9.5 1.7 %first_solve.1 = (f32[48,2240]{1,0:T(8,128)S(1)}, f32[306,128]{1,0:T(8,128)S(1)}, f32[306,128]{1,0:T(8,128)S(1)}) custom-call(s32[1]{0:T(128)} %bitcast.parity, f32[8,2240]{1,0:T(8,128)S(1)} %collective-permute-done.outer_in, f32[8,2240]{1,0:T(8,128)S(1)} %collective-permute-done.1.inner_in, f32[32,2240]{1,0:T(8,128)S(1)} %get-tuple-element.36.masked, ...), custom_call_target="tpu_custom_call" | custom-call | tf_op jit(solution)/shard_map/first_solve/pallas_call | solution.py:449
  11.2 4.3 %collective-permute-start.2 = (f32[306,128]{1,0:T(8,128)S(1)}, f32[306,128]{1,0:T(8,128)S(1)}, u32[]{:S(2)}, u32[]{:S(2)}) collective-permute-start(f32[306,128]{1,0:T(8,128)S(1)} %get-tuple-element.40), channel_id=1, source_target_pairs={{0,15},{1,2},{2,1},{3,4},{4,3},{5,6},{6,5},{7,8},{8,7},{9,10},{10,... | collective-permute-start | bytes 470024 | tf_op jit(solution)/shard_map/ppermute | solution.py:395
  15.5 0.0 collective-permute-start.3
  15.5 1.4 %collective-permute-done.4.outer_in = f32[24,2240]{1,0:T(8,128)S(1)} collective-permute-done((f32[24,2240]{1,0:T(8,128)S(1)}, f32[24,2240]{1,0:T(8,128)S(1)}, u32[]{:S(2)}, u32[]{:S(2)}) %collective-permute-start.4) | collective-permute-done | bytes 215072 | tf_op jit(solution)/shard_map/ppermute | solution.py:395
  16.9 0.0 collective-permute-done.5.inner_in
  16.9 0.2 absorb.1
  17.1 1.6 %collective-permute-done.2.outer_in = f32[306,128]{1,0:T(8,128)S(1)} collective-permute-done((f32[306,128]{1,0:T(8,128)S(1)}, f32[306,128]{1,0:T(8,128)S(1)}, u32[]{:S(2)}, u32[]{:S(2)}) %collective-permute-start.2) | collective-permute-done | bytes 156704 | tf_op jit(solution)/shard_map/ppermute | solution.py:395
  18.8 0.0 collective-permute-done.3.inner_in
  18.8 1.9 %second_solve.1 = (f32[64,2240]{1,0:T(8,128)S(1)}, f32[48,2240]{1,0:T(8,128)S(1)}, f32[48,2240]{1,0:T(8,128)S(1)}, f32[162,128]{1,0:T(8,128)S(1)}, f32[162,128]{1,0:T(8,128)S(1)}) custom-call(s32[1]{0:T(128)} %bitcast.parity, f32[306,128]{1,0:T(8,128)S(1)} %collective-permute-done.2.outer_in, f32[306,128]{1,0:T(8,128)S(1)} %collective-permute-done.3.inner_in, ...), custom_call_target="tpu_custom_call" | custom-call | tf_op jit(solution)/shard_map/second_solve/pallas_call | solution.py:471
  20.6 4.2 %collective-permute-start.6 = (f32[162,128]{1,0:T(8,128)S(1)}, f32[162,128]{1,0:T(8,128)S(1)}, u32[]{:S(2)}, u32[]{:S(2)}) collective-permute-start(f32[162,128]{1,0:T(8,128)S(1)} %get-tuple-element.49), channel_id=1, source_target_pairs={{0,15},{1,2},{2,1},{3,4},{4,3},{5,6},{6,5},{7,8},{8,7},{9,10},{10,... | collective-permute-start | bytes 248840 | tf_op jit(solution)/shard_map/ppermute | solution.py:395
  24.9 0.0 collective-permute-start.7
  24.9 2.0 %early_sums.1 = (f32[48,2240]{1,0:T(8,128)S(1)}, f32[32,2240]{1,0:T(8,128)S(1)}, f32[1,128]{1,0:T(1,128)S(1)}, f32[6,32,2240]{2,1,0:T(8,128)S(1)}, f32[6,32,2240]{2,1,0:T(8,128)S(1)}) custom-call(f32[64,2240]{1,0:T(8,128)S(1)} %get-tuple-element.51.z, f32[48,2240]{1,0:T(8,128)S(1)} %get-tuple-element.52.y, f32[64,2240]{1,0:T(8,128)S(1)} %get-tuple-element.48.c_rows, ...), custom_call_target="tpu_custom_call" | custom-call | flops 1000000 | bytes 7000000 | tf_op jit(solution)/shard_map/early_sums/pallas_call | solution.py:484
  26.9 0.5 %collective-permute-done.6.outer_in = f32[162,128]{1,0:T(8,128)S(1)} collective-permute-done((f32[162,128]{1,0:T(8,128)S(1)}, f32[162,128]{1,0:T(8,128)S(1)}, u32[]{:S(2)}, u32[]{:S(2)}) %collective-permute-start.6) | collective-permute-done | bytes 82976 | tf_op jit(solution)/shard_map/ppermute | solution.py:395
  27.4 0.0 collective-permute-done.7.inner_in
  27.4 0.5 %sums.1 = (f32[48,2240]{1,0:T(8,128)S(1)}, f32[16,1,128]{2,1,0:T(1,128)S(1)}) custom-call(s32[1]{0:T(128)} %bitcast.parity, f32[162,128]{1,0:T(8,128)S(1)} %collective-permute-done.6.outer_in, f32[162,128]{1,0:T(8,128)S(1)} %collective-permute-done.7.inner_in, f32[48,2240]{1,0:T(8,128)S(1)} %get-tuple-element.55.w_rows, f32[64,2240]{1,0:T(8,128)S(1)} %get-tuple-element.51.z, ...), custom_call_target="tpu_custom_call" | custom-call | tf_op jit(solution)/shard_map/sums/pallas_call | solution.py:496
  27.9 8.9 %all_to_all.5.came = f32[16,1,128]{2,1,0:T(1,128)S(1)} all-to-all(f32[16,1,128]{2,1,0:T(1,128)S(1)} %get-tuple-element.58), channel_id=1, replica_groups={{15,14,13,12,11,10,9,8,7,6,5,4,3,2,1,0},{31,30,29,28,27,26,25,24,23,22,..., dimensions={0} | all-to-all | bytes 16384 | tf_op jit(solution)/shard_map/all_to_all | solution.py:505
  36.7 3.0 %finish.1 = (f32[32,2240]{1,0:T(8,128)}, f32[6,32,2240]{2,1,0:T(8,128)}, f32[6,32,2240]{2,1,0:T(8,128)}, f32[6,32,2240]{2,1,0:T(8,128)}) custom-call(f32[16,1,128]{2,1,0:T(1,128)S(1)} %all_to_all.5.came, f32[64,2240]{1,0:T(8,128)S(1)} %get-tuple-element.51.z, f32[48,2240]{1,0:T(8,128)S(1)} %get-tuple-element.59.w, f32[48,2240]{1,0:T(8,128)S(1)} %get-tuple-element.60.d_rows, ...), custom_call_target="tpu_custom_call" | custom-call | tf_op jit(solution)/shard_map/finish/pallas_call | solution.py:507
Async XLA Ops:
  1.7 7.8 %collective-permute-start = (f32[8,2240]{1,0:T(8,128)S(1)}, f32[8,2240]{1,0:T(8,128)S(1)}, u32[]{:S(2)}, u32[]{:S(2)}) collective-permute-start(f32[8,2240]{1,0:T(8,128)S(1)} %get-tuple-element.34), channel_id=1, source_target_pairs={{0,15},{1,2},{2,1},{3,4},{4,3},{5,6},{6,5},{7,8},{8,7},{9,10},{10,... | collective-permute-start | bytes 215048 | tf_op jit(solution)/shard_map/ppermute | solution.py:395
  7.2 2.4 %collective-permute-start.1 = (f32[8,2240]{1,0:T(8,128)S(1)}, f32[8,2240]{1,0:T(8,128)S(1)}, u32[]{:S(2)}, u32[]{:S(2)}) collective-permute-start(f32[8,2240]{1,0:T(8,128)S(1)} %get-tuple-element.35.after), channel_id=1, source_target_pairs={{0,1},{1,0},{2,3},{3,2},{4,5},{5,4},{6,7},{7,6},{8,9},{9,8},{10,11... | collective-permute-start | bytes 215048 | tf_op jit(solution)/shard_map/ppermute | solution.py:395
  8.7 8.2 %collective-permute-start.4 = (f32[24,2240]{1,0:T(8,128)S(1)}, f32[24,2240]{1,0:T(8,128)S(1)}, u32[]{:S(2)}, u32[]{:S(2)}) collective-permute-start(f32[24,2240]{1,0:T(8,128)S(1)} %get-tuple-element.43), channel_id=1, source_target_pairs={{0,15},{1,2},{2,1},{3,4},{4,3},{5,6},{6,5},{7,8},{8,7},{9,10},{10,... | collective-permute-start | bytes 645128 | tf_op jit(solution)/shard_map/ppermute | solution.py:395
  9.5 7.4 %collective-permute-start.5 = (f32[24,2240]{1,0:T(8,128)S(1)}, f32[24,2240]{1,0:T(8,128)S(1)}, u32[]{:S(2)}, u32[]{:S(2)}) collective-permute-start(f32[24,2240]{1,0:T(8,128)S(1)} %get-tuple-element.44), channel_id=1, source_target_pairs={{0,1},{1,0},{2,3},{3,2},{4,5},{5,4},{6,7},{7,6},{8,9},{9,8},{10,11... | collective-permute-start | bytes 645128 | tf_op jit(solution)/shard_map/ppermute | solution.py:395
  11.2 7.5 %collective-permute-start.2 = (f32[306,128]{1,0:T(8,128)S(1)}, f32[306,128]{1,0:T(8,128)S(1)}, u32[]{:S(2)}, u32[]{:S(2)}) collective-permute-start(f32[306,128]{1,0:T(8,128)S(1)} %get-tuple-element.40), channel_id=1, source_target_pairs={{0,15},{1,2},{2,1},{3,4},{4,3},{5,6},{6,5},{7,8},{8,7},{9,10},{10,... | collective-permute-start | bytes 470024 | tf_op jit(solution)/shard_map/ppermute | solution.py:395
  15.5 3.2 %collective-permute-start.3 = (f32[306,128]{1,0:T(8,128)S(1)}, f32[306,128]{1,0:T(8,128)S(1)}, u32[]{:S(2)}, u32[]{:S(2)}) collective-permute-start(f32[306,128]{1,0:T(8,128)S(1)} %get-tuple-element.41), channel_id=1, source_target_pairs={{0,1},{1,0},{2,3},{3,2},{4,5},{5,4},{6,7},{7,6},{8,9},{9,8},{10,11... | collective-permute-start | bytes 470024 | tf_op jit(solution)/shard_map/ppermute | solution.py:395
  20.6 6.8 %collective-permute-start.6 = (f32[162,128]{1,0:T(8,128)S(1)}, f32[162,128]{1,0:T(8,128)S(1)}, u32[]{:S(2)}, u32[]{:S(2)}) collective-permute-start(f32[162,128]{1,0:T(8,128)S(1)} %get-tuple-element.49), channel_id=1, source_target_pairs={{0,15},{1,2},{2,1},{3,4},{4,3},{5,6},{6,5},{7,8},{8,7},{9,10},{10,... | collective-permute-start | bytes 248840 | tf_op jit(solution)/shard_map/ppermute | solution.py:395
  24.9 2.5 %collective-permute-start.7 = (f32[162,128]{1,0:T(8,128)S(1)}, f32[162,128]{1,0:T(8,128)S(1)}, u32[]{:S(2)}, u32[]{:S(2)}) collective-permute-start(f32[162,128]{1,0:T(8,128)S(1)} %get-tuple-element.50), channel_id=1, source_target_pairs={{0,1},{1,0},{2,3},{3,2},{4,5},{5,4},{6,7},{7,6},{8,9},{9,8},{10,11... | collective-permute-start | bytes 248840 | tf_op jit(solution)/shard_map/ppermute | solution.py:395

commit v18 on v16

--- a/solution.py
+++ b/solution.py
@@ -221,8 +221,10 @@
     pack(outer, to_outer)
 
 
-def absorb(parity, first, inner_in, outer_in, coef, depth, c_rows, z_rows, d_rows, edge):
+def absorb(parity, first, inner_in, outer_in, coef, depth, u_h, c_rows, z_rows, d_rows, face_e, face_n, edge, u, sem):
     cells, lat = coef.shape
+    copy = pltpu.make_async_copy(u_h, u, sem)
+    copy.start()
     west, east = pick(parity, inner_in[: 2 * OV], outer_in[: 2 * OV])
     edge[...] = west[:OV]
     d_rows[:OV] = jnp.broadcast_to(west[KL : KL + 1], (OV, lat))
@@ -237,6 +239,11 @@
     z_rows[3 * OV + cells :] = jnp.zeros((OV, lat), F32)
     inside = slice(OV, 3 * OV + cells)
     z_rows[inside] = jnp.where(c_rows[inside] > 0, first[...], 0.0)
+    own = slice(OV, OV + cells)
+    face_e[...] = jnp.minimum(d_rows[own], d_rows[OV + 1 : OV + cells + 1])
+    zero = jnp.zeros((cells, 1), F32)
+    face_n[...] = jnp.minimum(d_rows[own], jnp.concatenate([d_rows[own][:, 1:], zero], axis=1))
+    copy.wait()
 
 
 def second_solve(parity, outer_in, inner_in, z_rows, c_rows, lat_basis, lon, scale,
@@ -285,10 +292,9 @@
     return row
 
 
-def early_sums(z, y, c_rows, second, source, u_h, v_h, w_rows, masked, row, u, v, sems):
-    copies = [pltpu.make_async_copy(a, b, sems.at[i]) for i, (a, b) in enumerate([(u_h, u), (v_h, v)])]
-    for copy in copies:
-        copy.start()
+def early_sums(z, y, c_rows, second, source, v_h, w_rows, masked, row, v, sem):
+    copy = pltpu.make_async_copy(v_h, v, sem)
+    copy.start()
     cells, lat = source.shape
     inside = slice(OV, 3 * OV + cells)
     w_rows[...] = jnp.where(c_rows[inside] > 0, second[...], 0.0)
@@ -299,8 +305,7 @@
     z_own = z[own]
     sums_of = {0: dot(masked[...], z_own), 1: dot(z_own, y[OV : OV + cells]), 6: dot(land, land)}
     row[...] = in_lanes(jnp.zeros((1, LANE), F32), sums_of)
-    for copy in copies:
-        copy.wait()
+    copy.wait()
 
 
 def sums(parity, outer_in, inner_in, w_rows, z, y, c_rows, masked, row, w, sent):
@@ -318,7 +323,7 @@
     sent[...] = jnp.broadcast_to(in_lanes(row[...], sums_of)[None], sent.shape)
 
 
-def finish(came, z, w, d_rows, edge, source, u_vel, v_vel, solution, u_new, v_new, w_vel,
+def finish(came, z, w, d_rows, face_e, face_n, edge, source, u_vel, v_vel, solution, u_new, v_new, w_vel,
            s_rows, u_rows, v_out, w_out, s_out, sems):
     cells, lat = source.shape
     total = jnp.broadcast_to(jnp.sum(came[...], axis=0), (8, LANE))
@@ -351,11 +356,12 @@
 
     surface_rows(0)
     surface_rows(OV)
-    slope = gravity_step * (s_rows[OV : OV + 1] - s_rows[OV - 1 : OV])
-    d_west = jnp.minimum(d_rows[OV - 1 : OV], d_rows[OV : OV + 1])
+    slope = jnp.broadcast_to(gravity_step * (s_rows[OV : OV + 1] - s_rows[OV - 1 : OV]), (OV, lat))
+    d_west = jnp.broadcast_to(jnp.minimum(d_rows[OV - 1 : OV], d_rows[OV : OV + 1]), (OV, lat))
+    levels = lax.broadcasted_iota(jnp.int32, (OV, lat), 0).astype(F32)
+    left = jnp.where(d_west > levels, edge[...] - slope, 0.0)
     for level in range(KL):
-        u = jnp.where(d_west > level, edge[level : level + 1] - slope, 0.0)
-        u_rows[level, :OV] = jnp.broadcast_to(u, (OV, lat))
+        u_rows[level, OV - 1 : OV] = left[level : level + 1]
     zero = jnp.zeros((OV, 1), F32)
     for at in range(OV, OV + cells, OV):
         own = slice(at - OV, at)
@@ -363,12 +369,12 @@
         s = s_rows[at : at + OV]
         d = d_rows[at : at + OV]
         slope = gravity_step * (s_rows[at + 1 : at + OV + 1] - s)
-        face = jnp.minimum(d, d_rows[at + 1 : at + OV + 1])
+        face = face_e[own]
         for level in range(KL):
             u_rows[level, at : at + OV] = jnp.where(face > level, u_vel[level, own] - slope, 0.0)
         send(u_rows.at[:, at : at + OV], u_new.at[:, own])
         slope = gravity_step * (jnp.concatenate([s[:, 1:], zero], axis=1) - s)
-        face = jnp.minimum(d, jnp.concatenate([d[:, 1:], zero], axis=1))
+        face = face_n[own]
         for level in range(KL):
             v_out[level, own] = jnp.where(face > level, v_vel[level, own] - slope, 0.0)
         send(v_out.at[:, own], v_new.at[:, own])
@@ -457,16 +463,19 @@
     )(parity, *near, masked, *held)
     near = swap(inner, outer)
 
-    c_rows, z_rows, d_rows, edge = pl.pallas_call(
+    c_rows, z_rows, d_rows, face_e, face_n, edge, u_v = pl.pallas_call(
         absorb,
-        in_specs=[SM] + [VM] * 5,
-        out_specs=[VM] * 4,
+        in_specs=[SM] + [VM] * 5 + [HB],
+        out_specs=[VM] * 7,
         out_shape=[pltpu.VMEM((span + 2 * OV, lat), F32)] * 2
-        + [pltpu.VMEM((span, lat), F32), pltpu.VMEM((OV, lat), F32)],
+        + [pltpu.VMEM((span, lat), F32)]
+        + [pltpu.VMEM((cells, lat), F32)] * 2
+        + [pltpu.VMEM((OV, lat), F32), pltpu.VMEM((KL, cells, lat), F32)],
+        scratch_shapes=[pltpu.SemaphoreType.DMA],
         compiler_params=PARAMS,
         cost_estimate=pl.CostEstimate(flops=10**6, bytes_accessed=7 * 10**6, transcendentals=0),
         name="absorb",
-    )(parity, first, *far, coef, depth)
+    )(parity, first, *far, coef, depth, hbm["u"])
 
     z, y, second, inner, outer = pl.pallas_call(
         second_solve,
@@ -481,17 +490,17 @@
     )(parity, *near, z_rows, c_rows, *held)
     near = swap(inner, outer)
 
-    w_rows, masked, row, u_v, v_v = pl.pallas_call(
+    w_rows, masked, row, v_v = pl.pallas_call(
         early_sums,
-        in_specs=[VM] * 5 + [HB] * 2,
-        out_specs=[VM] * 5,
+        in_specs=[VM] * 5 + [HB],
+        out_specs=[VM] * 4,
         out_shape=[pltpu.VMEM((span, lat), F32), pltpu.VMEM((cells, lat), F32), pltpu.VMEM((1, LANE), F32)]
-        + [pltpu.VMEM((KL, cells, lat), F32)] * 2,
-        scratch_shapes=[pltpu.SemaphoreType.DMA((2,))],
+        + [pltpu.VMEM((KL, cells, lat), F32)],
+        scratch_shapes=[pltpu.SemaphoreType.DMA],
         compiler_params=PARAMS,
         cost_estimate=pl.CostEstimate(flops=10**6, bytes_accessed=7 * 10**6, transcendentals=0),
         name="early_sums",
-    )(z, y, c_rows, second, source_v, hbm["u"], hbm["v"])
+    )(z, y, c_rows, second, source_v, hbm["v"])
 
     w, sent = pl.pallas_call(
         sums,
@@ -506,7 +515,7 @@
 
     return pl.pallas_call(
         finish,
-        in_specs=[VM] * 8,
+        in_specs=[VM] * 10,
         out_specs=[HB] * 4,
         out_shape=[shape(cells, lat)] + [shape(KL, cells, lat)] * 3,
         scratch_shapes=[pltpu.VMEM((span, lat), F32)]
@@ -515,7 +524,7 @@
         + [pltpu.VMEM((cells, lat), F32), pltpu.SemaphoreType.DMA((1 + 3 * (cells // OV),))],
         compiler_params=PARAMS,
         name="finish",
-    )(came, z, w, d_rows, edge, source_v, u_v, v_v)
+    )(came, z, w, d_rows, face_e, face_n, edge, source_v, u_v, v_v)
 
 
 def solution(mesh):

time: 40 us -> 40 us (level)
  waiting for transfers between devices: 4.3 us -> 3.52 us
  Pallas kernels: 11.8 us -> 12.5 us
    ppermute x8, waiting for transfers between devices: 4.3 us -> 3.52 us  [swap_pairs(): return lax.ppermute(block, 'lon', route)]
    pallas_call x3, Pallas kernels: 5.21 us -> 5.91 us  [the longest x1 2.94 us: body(): pl.pallas_call(finish, in_specs=[VM] * 10, out_specs=[HB] * 4, out_shape=...]
  transfers between devices with their start and end apart: 8 -> 8, of which waited for: 3 -> 3; matrix products, arithmetic and copies ran while one was open for 0% -> 0% of each run, Pallas kernels for 14% -> 16%
where the time goes in v18:
time: 40 us; the launch traced here: 39.7 us
  starting transfers between devices  14.4 us (36%)
  Pallas kernels  12.5 us (31%)
  blocking collectives  8.53 us (21%)
  waiting for transfers between devices  3.52 us (9%)
  between operations  0.7 us (2%)
    ppermute x8, starting transfers between devices, swap_pairs(): return lax.ppermute(block, 'lon', route)  14.4 us
    all_to_all x1, blocking collectives, body(): came = lax.all_to_all(sent, 'lon', 0, 0, axis_index_groups=ring)  8.53 us
    ppermute x8, waiting for transfers between devices, swap_pairs(): return lax.ppermute(block, 'lon', route)  3.52 us
    pallas_call x1, Pallas kernels, body(): pl.pallas_call(finish, in_specs=[VM] * 10, out_specs=[HB] * 4, out_shape=...  2.94 us
    pallas_call x1, Pallas kernels, body(): pl.pallas_call(second_solve, in_specs=[SM] + [VM] * 7, out_specs=[VM] * 5...  1.85 us
    pallas_call x1, Pallas kernels, body(): pl.pallas_call(first_solve, in_specs=[SM] + [VM] * 6, out_specs=[VM] * 3,...  1.68 us
    pallas_call x1, Pallas kernels, body(): pl.pallas_call(prepare, in_specs=[SM] + [HB] * 8, out_specs=[VM] * 9, out...  1.53 us
    pallas_call x1, Pallas kernels, body(): pl.pallas_call(early_sums, in_specs=[VM] * 5 + [HB], out_specs=[VM] * 4,...  1.49 us
  transfers between devices with their start and end apart: 8, of which 3 were waited for; matrix products, arithmetic and copies ran while one was open for 0% of the time, Pallas kernels for 16%

profile of v18, /device:TPU:0, one launch (start us, length us, event | category | flops | bytes accessed | tf_op | source)
XLA Modules:
  0.0 39.7 jit_solution(12566969041269365185)
XLA Ops:
  0.6 1.0 %first_edges.1 = (f32[8,2240]{1,0:T(8,128)S(1)}, f32[8,2240]{1,0:T(8,128)S(1)}) custom-call(s32[1]{0:T(128)} %bitcast.parity, f32[32,2240]{1,0:T(8,128)} %source_h.1, s32[32,2240]{1,0:T(8,128)} %bottom_h.1), custom_call_target="tpu_custom_call" | custom-call | tf_op jit(solution)/shard_map/first_edges/pallas_call | solution.py:423
  1.7 5.5 %collective-permute-start = (f32[8,2240]{1,0:T(8,128)S(1)}, f32[8,2240]{1,0:T(8,128)S(1)}, u32[]{:S(2)}, u32[]{:S(2)}) collective-permute-start(f32[8,2240]{1,0:T(8,128)S(1)} %get-tuple-element.36), channel_id=1, source_target_pairs={{0,15},{1,2},{2,1},{3,4},{4,3},{5,6},{6,5},{7,8},{8,7},{9,10},{10,... | collective-permute-start | bytes 215048 | tf_op jit(solution)/shard_map/ppermute | solution.py:401
  7.2 0.0 collective-permute-start.1
  7.2 1.5 %prepare.1 = (f32[24,2240]{1,0:T(8,128)S(1)}, f32[24,2240]{1,0:T(8,128)S(1)}, f32[32,2240]{1,0:T(8,128)S(1)}, f32[32,2240]{1,0:T(8,128)S(1)}, f32[32,2240]{1,0:T...) custom-call(s32[1]{0:T(128)} %bitcast.parity, ...), custom_call_target="tpu_custom_call" | custom-call | flops 1000000 | bytes 7000000 | tf_op jit(solution)/shard_map/prepare/pallas_call | solution.py:435
  8.7 0.6 %collective-permute-start.4 = (f32[24,2240]{1,0:T(8,128)S(1)}, f32[24,2240]{1,0:T(8,128)S(1)}, u32[]{:S(2)}, u32[]{:S(2)}) collective-permute-start(f32[24,2240]{1,0:T(8,128)S(1)} %get-tuple-element.45), channel_id=1, source_target_pairs={{0,1},{1,0},{2,3},{3,2},{4,5},{5,4},{6,7},{7,6},{8,9},{9,8},{10,11... | collective-permute-start | bytes 645128 | tf_op jit(solution)/shard_map/ppermute | solution.py:401
  9.3 0.3 collective-permute-start.5
  9.6 0.0 collective-permute-done.outer_in
  9.6 0.0 collective-permute-done.1.inner_in
  9.6 1.7 %first_solve.1 = (f32[48,2240]{1,0:T(8,128)S(1)}, f32[306,128]{1,0:T(8,128)S(1)}, f32[306,128]{1,0:T(8,128)S(1)}) custom-call(s32[1]{0:T(128)} %bitcast.parity, f32[8,2240]{1,0:T(8,128)S(1)} %collective-permute-done.outer_in, f32[8,2240]{1,0:T(8,128)S(1)} %collective-permute-done.1.inner_in, f32[32,2240]{1,0:T(8,128)S(1)} %get-tuple-element.38.masked, ...), custom_call_target="tpu_custom_call" | custom-call | tf_op jit(solution)/shard_map/first_solve/pallas_call | solution.py:455
  11.3 4.2 %collective-permute-start.2 = (f32[306,128]{1,0:T(8,128)S(1)}, f32[306,128]{1,0:T(8,128)S(1)}, u32[]{:S(2)}, u32[]{:S(2)}) collective-permute-start(f32[306,128]{1,0:T(8,128)S(1)} %get-tuple-element.42), channel_id=1, source_target_pairs={{0,15},{1,2},{2,1},{3,4},{4,3},{5,6},{6,5},{7,8},{8,7},{9,10},{10,... | collective-permute-start | bytes 470024 | tf_op jit(solution)/shard_map/ppermute | solution.py:401
  15.5 0.0 collective-permute-start.3
  15.5 0.0 collective-permute-done.4.inner_in
  15.5 1.9 %collective-permute-done.5.outer_in = f32[24,2240]{1,0:T(8,128)S(1)} collective-permute-done((f32[24,2240]{1,0:T(8,128)S(1)}, f32[24,2240]{1,0:T(8,128)S(1)}, u32[]{:S(2)}, u32[]{:S(2)}) %collective-permute-start.5) | collective-permute-done | bytes 215072 | tf_op jit(solution)/shard_map/ppermute | solution.py:401
  17.4 1.5 %absorb.1 = (f32[64,2240]{1,0:T(8,128)S(1)}, f32[64,2240]{1,0:T(8,128)S(1)}, f32[48,2240]{1,0:T(8,128)S(1)}, f32[32,2240]{1,0:T(8,128)S(1)}, f32[32,2240]{1,0:T(...) custom-call(s32[1]{0:T(128)} %bitcast.parity, f32[48,2240]{1,0:T(8,128)S(1)} %get-tuple-element.44.first, ...), custom_call_target="tpu_custom_call" | custom-call | flops 1000000 | bytes 7000000 | tf_op jit(solution)/shard_map/absorb/pallas_call | solution.py:466
  18.9 0.2 collective-permute-done.2.outer_in
  19.2 0.0 collective-permute-done.3.inner_in
  19.2 1.9 %second_solve.1 = (f32[64,2240]{1,0:T(8,128)S(1)}, f32[48,2240]{1,0:T(8,128)S(1)}, f32[48,2240]{1,0:T(8,128)S(1)}, f32[162,128]{1,0:T(8,128)S(1)}, f32[162,128]{1,0:T(8,128)S(1)}) custom-call(s32[1]{0:T(128)} %bitcast.parity, f32[306,128]{1,0:T(8,128)S(1)} %collective-permute-done.2.outer_in, f32[306,128]{1,0:T(8,128)S(1)} %collective-permute-done.3.inner_in, ...), custom_call_target="tpu_custom_call" | custom-call | tf_op jit(solution)/shard_map/second_solve/pallas_call | solution.py:480
  21.0 3.8 %collective-permute-start.6 = (f32[162,128]{1,0:T(8,128)S(1)}, f32[162,128]{1,0:T(8,128)S(1)}, u32[]{:S(2)}, u32[]{:S(2)}) collective-permute-start(f32[162,128]{1,0:T(8,128)S(1)} %get-tuple-element.51), channel_id=1, source_target_pairs={{0,15},{1,2},{2,1},{3,4},{4,3},{5,6},{6,5},{7,8},{8,7},{9,10},{10,... | collective-permute-start | bytes 248840 | tf_op jit(solution)/shard_map/ppermute | solution.py:401
  24.8 0.0 collective-permute-start.7
  24.8 1.5 %early_sums.1 = (f32[48,2240]{1,0:T(8,128)S(1)}, f32[32,2240]{1,0:T(8,128)S(1)}, f32[1,128]{1,0:T(1,128)S(1)}, f32[6,32,2240]{2,1,0:T(8,128)S(1)}) custom-call(f32[64,2240]{1,0:T(8,128)S(1)} %get-tuple-element.53.z, f32[48,2240]{1,0:T(8,128)S(1)} %get-tuple-element.54.y, f32[64,2240]{1,0:T(8,128)S(1)} %get-tuple-element.50.c_rows, ...), custom_call_target="tpu_custom_call" | custom-call | flops 1000000 | bytes 7000000 | tf_op jit(solution)/shard_map/early_sums/pallas_call | solution.py:493
  26.3 1.4 %collective-permute-done.6.outer_in = f32[162,128]{1,0:T(8,128)S(1)} collective-permute-done((f32[162,128]{1,0:T(8,128)S(1)}, f32[162,128]{1,0:T(8,128)S(1)}, u32[]{:S(2)}, u32[]{:S(2)}) %collective-permute-start.6) | collective-permute-done | bytes 82976 | tf_op jit(solution)/shard_map/ppermute | solution.py:401
  27.7 0.0 collective-permute-done.7.inner_in
  27.7 0.5 %sums.1 = (f32[48,2240]{1,0:T(8,128)S(1)}, f32[16,1,128]{2,1,0:T(1,128)S(1)}) custom-call(s32[1]{0:T(128)} %bitcast.parity, f32[162,128]{1,0:T(8,128)S(1)} %collective-permute-done.6.outer_in, f32[162,128]{1,0:T(8,128)S(1)} %collective-permute-done.7.inner_in, f32[48,2240]{1,0:T(8,128)S(1)} %get-tuple-element.57.w_rows, f32[64,2240]{1,0:T(8,128)S(1)} %get-tuple-element.53.z, ...), custom_call_target="tpu_custom_call" | custom-call | tf_op jit(solution)/shard_map/sums/pallas_call | solution.py:505
  28.2 8.5 %all_to_all.5.came = f32[16,1,128]{2,1,0:T(1,128)S(1)} all-to-all(f32[16,1,128]{2,1,0:T(1,128)S(1)} %get-tuple-element.60), channel_id=1, replica_groups={{15,14,13,12,11,10,9,8,7,6,5,4,3,2,1,0},{31,30,29,28,27,26,25,24,23,22,..., dimensions={0} | all-to-all | bytes 16384 | tf_op jit(solution)/shard_map/all_to_all | solution.py:514
  36.7 2.9 %finish.1 = (f32[32,2240]{1,0:T(8,128)}, f32[6,32,2240]{2,1,0:T(8,128)}, f32[6,32,2240]{2,1,0:T(8,128)}, f32[6,32,2240]{2,1,0:T(8,128)}) custom-call(f32[16,1,128]{2,1,0:T(1,128)S(1)} %all_to_all.5.came, f32[64,2240]{1,0:T(8,128)S(1)} %get-tuple-element.53.z, f32[48,2240]{1,0:T(8,128)S(1)} %get-tuple-element.61.w, f32[48,2240]{1,0:T(8,128)S(1)} %get-tuple-element.62.d_rows, ...), custom_call_target="tpu_custom_call" | custom-call | tf_op jit(solution)/shard_map/finish/pallas_call | solution.py:516
Async XLA Ops:
  1.7 7.9 %collective-permute-start = (f32[8,2240]{1,0:T(8,128)S(1)}, f32[8,2240]{1,0:T(8,128)S(1)}, u32[]{:S(2)}, u32[]{:S(2)}) collective-permute-start(f32[8,2240]{1,0:T(8,128)S(1)} %get-tuple-element.36), channel_id=1, source_target_pairs={{0,15},{1,2},{2,1},{3,4},{4,3},{5,6},{6,5},{7,8},{8,7},{9,10},{10,... | collective-permute-start | bytes 215048 | tf_op jit(solution)/shard_map/ppermute | solution.py:401
  7.2 2.4 %collective-permute-start.1 = (f32[8,2240]{1,0:T(8,128)S(1)}, f32[8,2240]{1,0:T(8,128)S(1)}, u32[]{:S(2)}, u32[]{:S(2)}) collective-permute-start(f32[8,2240]{1,0:T(8,128)S(1)} %get-tuple-element.37.after), channel_id=1, source_target_pairs={{0,1},{1,0},{2,3},{3,2},{4,5},{5,4},{6,7},{7,6},{8,9},{9,8},{10,11... | collective-permute-start | bytes 215048 | tf_op jit(solution)/shard_map/ppermute | solution.py:401
  8.7 6.8 %collective-permute-start.4 = (f32[24,2240]{1,0:T(8,128)S(1)}, f32[24,2240]{1,0:T(8,128)S(1)}, u32[]{:S(2)}, u32[]{:S(2)}) collective-permute-start(f32[24,2240]{1,0:T(8,128)S(1)} %get-tuple-element.45), channel_id=1, source_target_pairs={{0,1},{1,0},{2,3},{3,2},{4,5},{5,4},{6,7},{7,6},{8,9},{9,8},{10,11... | collective-permute-start | bytes 645128 | tf_op jit(solution)/shard_map/ppermute | solution.py:401
  9.3 8.2 %collective-permute-start.5 = (f32[24,2240]{1,0:T(8,128)S(1)}, f32[24,2240]{1,0:T(8,128)S(1)}, u32[]{:S(2)}, u32[]{:S(2)}) collective-permute-start(f32[24,2240]{1,0:T(8,128)S(1)} %get-tuple-element.46), channel_id=1, source_target_pairs={{0,15},{1,2},{2,1},{3,4},{4,3},{5,6},{6,5},{7,8},{8,7},{9,10},{10,... | collective-permute-start | bytes 645128 | tf_op jit(solution)/shard_map/ppermute | solution.py:401
  11.3 7.9 %collective-permute-start.2 = (f32[306,128]{1,0:T(8,128)S(1)}, f32[306,128]{1,0:T(8,128)S(1)}, u32[]{:S(2)}, u32[]{:S(2)}) collective-permute-start(f32[306,128]{1,0:T(8,128)S(1)} %get-tuple-element.42), channel_id=1, source_target_pairs={{0,15},{1,2},{2,1},{3,4},{4,3},{5,6},{6,5},{7,8},{8,7},{9,10},{10,... | collective-permute-start | bytes 470024 | tf_op jit(solution)/shard_map/ppermute | solution.py:401
  15.5 3.6 %collective-permute-start.3 = (f32[306,128]{1,0:T(8,128)S(1)}, f32[306,128]{1,0:T(8,128)S(1)}, u32[]{:S(2)}, u32[]{:S(2)}) collective-permute-start(f32[306,128]{1,0:T(8,128)S(1)} %get-tuple-element.43), channel_id=1, source_target_pairs={{0,1},{1,0},{2,3},{3,2},{4,5},{5,4},{6,7},{7,6},{8,9},{9,8},{10,11... | collective-permute-start | bytes 470024 | tf_op jit(solution)/shard_map/ppermute | solution.py:401
  21.0 6.7 %collective-permute-start.6 = (f32[162,128]{1,0:T(8,128)S(1)}, f32[162,128]{1,0:T(8,128)S(1)}, u32[]{:S(2)}, u32[]{:S(2)}) collective-permute-start(f32[162,128]{1,0:T(8,128)S(1)} %get-tuple-element.51), channel_id=1, source_target_pairs={{0,15},{1,2},{2,1},{3,4},{4,3},{5,6},{6,5},{7,8},{8,7},{9,10},{10,... | collective-permute-start | bytes 248840 | tf_op jit(solution)/shard_map/ppermute | solution.py:401
  24.8 2.9 %collective-permute-start.7 = (f32[162,128]{1,0:T(8,128)S(1)}, f32[162,128]{1,0:T(8,128)S(1)}, u32[]{:S(2)}, u32[]{:S(2)}) collective-permute-start(f32[162,128]{1,0:T(8,128)S(1)} %get-tuple-element.52), channel_id=1, source_target_pairs={{0,1},{1,0},{2,3},{3,2},{4,5},{5,4},{6,7},{7,6},{8,9},{9,8},{10,11... | collective-permute-start | bytes 248840 | tf_op jit(solution)/shard_map/ppermute | solution.py:401

commit v19 on v18

--- a/solution.py
+++ b/solution.py
@@ -66,7 +66,7 @@
             return jnp.zeros((span, LANE), F32)
         return x[:, b * LANE : (b + 1) * LANE]
 
-    chunk = 4
+    chunk = 10
     groups = [range(first, min(first + chunk, tiles)) for first in range(0, tiles, chunk)]
     held = {}
 

time: 40 us -> 39.3 us (0.982)
  waiting for transfers between devices: 3.52 us -> 4.23 us
  Pallas kernels: 12.5 us -> 11.8 us
    ppermute x8, waiting for transfers between devices: 3.52 us -> 4.23 us  [swap_pairs(): return lax.ppermute(block, 'lon', route)]
  transfers between devices with their start and end apart: 8 -> 8, of which waited for: 3 -> 3; matrix products, arithmetic and copies ran while one was open for 0% -> 0% of each run, Pallas kernels for 16% -> 15%
where the time goes in v19:
time: 39.3 us; the launch traced here: 39 us
  starting transfers between devices  14.1 us (36%)
  Pallas kernels  11.8 us (30%)
  blocking collectives  8.18 us (21%)
  waiting for transfers between devices  4.23 us (11%)
  between operations  0.69 us (2%)
    ppermute x8, starting transfers between devices, swap_pairs(): return lax.ppermute(block, 'lon', route)  14.1 us
    all_to_all x1, blocking collectives, body(): came = lax.all_to_all(sent, 'lon', 0, 0, axis_index_groups=ring)  8.18 us
    ppermute x8, waiting for transfers between devices, swap_pairs(): return lax.ppermute(block, 'lon', route)  4.23 us
    pallas_call x1, Pallas kernels, body(): pl.pallas_call(finish, in_specs=[VM] * 10, out_specs=[HB] * 4, out_shape=...  2.94 us
    pallas_call x1, Pallas kernels, body(): pl.pallas_call(second_solve, in_specs=[SM] + [VM] * 7, out_specs=[VM] * 5...  1.54 us
    pallas_call x1, Pallas kernels, body(): pl.pallas_call(prepare, in_specs=[SM] + [HB] * 8, out_specs=[VM] * 9, out...  1.53 us
    pallas_call x1, Pallas kernels, body(): pl.pallas_call(early_sums, in_specs=[VM] * 5 + [HB], out_specs=[VM] * 4,...  1.49 us
    pallas_call x1, Pallas kernels, body(): pl.pallas_call(absorb, in_specs=[SM] + [VM] * 5 + [HB], out_specs=[VM] *...  1.49 us
  transfers between devices with their start and end apart: 8, of which 3 were waited for; matrix products, arithmetic and copies ran while one was open for 0% of the time, Pallas kernels for 15%

profile of v19, /device:TPU:0, one launch (start us, length us, event | category | flops | bytes accessed | tf_op | source)
XLA Modules:
  0.0 39.0 jit_solution(2879154801337448260)
XLA Ops:
  0.6 1.0 %first_edges.1 = (f32[8,2240]{1,0:T(8,128)S(1)}, f32[8,2240]{1,0:T(8,128)S(1)}) custom-call(s32[1]{0:T(128)} %bitcast.parity, f32[32,2240]{1,0:T(8,128)} %source_h.1, s32[32,2240]{1,0:T(8,128)} %bottom_h.1), custom_call_target="tpu_custom_call" | custom-call | tf_op jit(solution)/shard_map/first_edges/pallas_call | solution.py:423
  1.7 5.5 %collective-permute-start = (f32[8,2240]{1,0:T(8,128)S(1)}, f32[8,2240]{1,0:T(8,128)S(1)}, u32[]{:S(2)}, u32[]{:S(2)}) collective-permute-start(f32[8,2240]{1,0:T(8,128)S(1)} %get-tuple-element.36), channel_id=1, source_target_pairs={{0,15},{1,2},{2,1},{3,4},{4,3},{5,6},{6,5},{7,8},{8,7},{9,10},{10,... | collective-permute-start | bytes 215048 | tf_op jit(solution)/shard_map/ppermute | solution.py:401
  7.2 0.0 collective-permute-start.1
  7.2 1.5 %prepare.1 = (f32[24,2240]{1,0:T(8,128)S(1)}, f32[24,2240]{1,0:T(8,128)S(1)}, f32[32,2240]{1,0:T(8,128)S(1)}, f32[32,2240]{1,0:T(8,128)S(1)}, f32[32,2240]{1,0:T...) custom-call(s32[1]{0:T(128)} %bitcast.parity, ...), custom_call_target="tpu_custom_call" | custom-call | flops 1000000 | bytes 7000000 | tf_op jit(solution)/shard_map/prepare/pallas_call | solution.py:435
  8.7 0.6 %collective-permute-start.4 = (f32[24,2240]{1,0:T(8,128)S(1)}, f32[24,2240]{1,0:T(8,128)S(1)}, u32[]{:S(2)}, u32[]{:S(2)}) collective-permute-start(f32[24,2240]{1,0:T(8,128)S(1)} %get-tuple-element.45), channel_id=1, source_target_pairs={{0,1},{1,0},{2,3},{3,2},{4,5},{5,4},{6,7},{7,6},{8,9},{9,8},{10,11... | collective-permute-start | bytes 645128 | tf_op jit(solution)/shard_map/ppermute | solution.py:401
  9.3 0.3 collective-permute-start.5
  9.6 0.0 collective-permute-done.outer_in
  9.6 0.0 collective-permute-done.1.inner_in
  9.6 1.3 %first_solve.1 = (f32[48,2240]{1,0:T(8,128)S(1)}, f32[306,128]{1,0:T(8,128)S(1)}, f32[306,128]{1,0:T(8,128)S(1)}) custom-call(s32[1]{0:T(128)} %bitcast.parity, f32[8,2240]{1,0:T(8,128)S(1)} %collective-permute-done.outer_in, f32[8,2240]{1,0:T(8,128)S(1)} %collective-permute-done.1.inner_in, f32[32,2240]{1,0:T(8,128)S(1)} %get-tuple-element.38.masked, ...), custom_call_target="tpu_custom_call" | custom-call | tf_op jit(solution)/shard_map/first_solve/pallas_call | solution.py:455
  10.9 4.2 %collective-permute-start.2 = (f32[306,128]{1,0:T(8,128)S(1)}, f32[306,128]{1,0:T(8,128)S(1)}, u32[]{:S(2)}, u32[]{:S(2)}) collective-permute-start(f32[306,128]{1,0:T(8,128)S(1)} %get-tuple-element.42), channel_id=1, source_target_pairs={{0,15},{1,2},{2,1},{3,4},{4,3},{5,6},{6,5},{7,8},{8,7},{9,10},{10,... | collective-permute-start | bytes 470024 | tf_op jit(solution)/shard_map/ppermute | solution.py:401
  15.2 0.0 collective-permute-start.3
  15.2 0.0 collective-permute-done.4.inner_in
  15.2 2.3 %collective-permute-done.5.outer_in = f32[24,2240]{1,0:T(8,128)S(1)} collective-permute-done((f32[24,2240]{1,0:T(8,128)S(1)}, f32[24,2240]{1,0:T(8,128)S(1)}, u32[]{:S(2)}, u32[]{:S(2)}) %collective-permute-start.5) | collective-permute-done | bytes 215072 | tf_op jit(solution)/shard_map/ppermute | solution.py:401
  17.4 1.5 %absorb.1 = (f32[64,2240]{1,0:T(8,128)S(1)}, f32[64,2240]{1,0:T(8,128)S(1)}, f32[48,2240]{1,0:T(8,128)S(1)}, f32[32,2240]{1,0:T(8,128)S(1)}, f32[32,2240]{1,0:T(...) custom-call(s32[1]{0:T(128)} %bitcast.parity, f32[48,2240]{1,0:T(8,128)S(1)} %get-tuple-element.44.first, ...), custom_call_target="tpu_custom_call" | custom-call | flops 1000000 | bytes 7000000 | tf_op jit(solution)/shard_map/absorb/pallas_call | solution.py:466
  18.9 0.2 collective-permute-done.2.outer_in
  19.2 0.0 collective-permute-done.3.inner_in
  19.2 1.5 %second_solve.1 = (f32[64,2240]{1,0:T(8,128)S(1)}, f32[48,2240]{1,0:T(8,128)S(1)}, f32[48,2240]{1,0:T(8,128)S(1)}, f32[162,128]{1,0:T(8,128)S(1)}, f32[162,128]{1,0:T(8,128)S(1)}) custom-call(s32[1]{0:T(128)} %bitcast.parity, f32[306,128]{1,0:T(8,128)S(1)} %collective-permute-done.2.outer_in, f32[306,128]{1,0:T(8,128)S(1)} %collective-permute-done.3.inner_in, ...), custom_call_target="tpu_custom_call" | custom-call | tf_op jit(solution)/shard_map/second_solve/pallas_call | solution.py:480
  20.7 3.5 %collective-permute-start.6 = (f32[162,128]{1,0:T(8,128)S(1)}, f32[162,128]{1,0:T(8,128)S(1)}, u32[]{:S(2)}, u32[]{:S(2)}) collective-permute-start(f32[162,128]{1,0:T(8,128)S(1)} %get-tuple-element.51), channel_id=1, source_target_pairs={{0,15},{1,2},{2,1},{3,4},{4,3},{5,6},{6,5},{7,8},{8,7},{9,10},{10,... | collective-permute-start | bytes 248840 | tf_op jit(solution)/shard_map/ppermute | solution.py:401
  24.2 0.0 collective-permute-start.7
  24.2 1.5 %early_sums.1 = (f32[48,2240]{1,0:T(8,128)S(1)}, f32[32,2240]{1,0:T(8,128)S(1)}, f32[1,128]{1,0:T(1,128)S(1)}, f32[6,32,2240]{2,1,0:T(8,128)S(1)}) custom-call(f32[64,2240]{1,0:T(8,128)S(1)} %get-tuple-element.53.z, f32[48,2240]{1,0:T(8,128)S(1)} %get-tuple-element.54.y, f32[64,2240]{1,0:T(8,128)S(1)} %get-tuple-element.50.c_rows, ...), custom_call_target="tpu_custom_call" | custom-call | flops 1000000 | bytes 7000000 | tf_op jit(solution)/shard_map/early_sums/pallas_call | solution.py:493
  25.7 1.7 %collective-permute-done.6.outer_in = f32[162,128]{1,0:T(8,128)S(1)} collective-permute-done((f32[162,128]{1,0:T(8,128)S(1)}, f32[162,128]{1,0:T(8,128)S(1)}, u32[]{:S(2)}, u32[]{:S(2)}) %collective-permute-start.6) | collective-permute-done | bytes 82976 | tf_op jit(solution)/shard_map/ppermute | solution.py:401
  27.4 0.0 collective-permute-done.7.inner_in
  27.4 0.5 %sums.1 = (f32[48,2240]{1,0:T(8,128)S(1)}, f32[16,1,128]{2,1,0:T(1,128)S(1)}) custom-call(s32[1]{0:T(128)} %bitcast.parity, f32[162,128]{1,0:T(8,128)S(1)} %collective-permute-done.6.outer_in, f32[162,128]{1,0:T(8,128)S(1)} %collective-permute-done.7.inner_in, f32[48,2240]{1,0:T(8,128)S(1)} %get-tuple-element.57.w_rows, f32[64,2240]{1,0:T(8,128)S(1)} %get-tuple-element.53.z, ...), custom_call_target="tpu_custom_call" | custom-call | tf_op jit(solution)/shard_map/sums/pallas_call | solution.py:505
  27.9 8.2 %all_to_all.5.came = f32[16,1,128]{2,1,0:T(1,128)S(1)} all-to-all(f32[16,1,128]{2,1,0:T(1,128)S(1)} %get-tuple-element.60), channel_id=1, replica_groups={{15,14,13,12,11,10,9,8,7,6,5,4,3,2,1,0},{31,30,29,28,27,26,25,24,23,22,..., dimensions={0} | all-to-all | bytes 16384 | tf_op jit(solution)/shard_map/all_to_all | solution.py:514
  36.1 2.9 %finish.1 = (f32[32,2240]{1,0:T(8,128)}, f32[6,32,2240]{2,1,0:T(8,128)}, f32[6,32,2240]{2,1,0:T(8,128)}, f32[6,32,2240]{2,1,0:T(8,128)}) custom-call(f32[16,1,128]{2,1,0:T(1,128)S(1)} %all_to_all.5.came, f32[64,2240]{1,0:T(8,128)S(1)} %get-tuple-element.53.z, f32[48,2240]{1,0:T(8,128)S(1)} %get-tuple-element.61.w, f32[48,2240]{1,0:T(8,128)S(1)} %get-tuple-element.62.d_rows, ...), custom_call_target="tpu_custom_call" | custom-call | tf_op jit(solution)/shard_map/finish/pallas_call | solution.py:516
Async XLA Ops:
  1.7 7.9 %collective-permute-start = (f32[8,2240]{1,0:T(8,128)S(1)}, f32[8,2240]{1,0:T(8,128)S(1)}, u32[]{:S(2)}, u32[]{:S(2)}) collective-permute-start(f32[8,2240]{1,0:T(8,128)S(1)} %get-tuple-element.36), channel_id=1, source_target_pairs={{0,15},{1,2},{2,1},{3,4},{4,3},{5,6},{6,5},{7,8},{8,7},{9,10},{10,... | collective-permute-start | bytes 215048 | tf_op jit(solution)/shard_map/ppermute | solution.py:401
  7.2 2.4 %collective-permute-start.1 = (f32[8,2240]{1,0:T(8,128)S(1)}, f32[8,2240]{1,0:T(8,128)S(1)}, u32[]{:S(2)}, u32[]{:S(2)}) collective-permute-start(f32[8,2240]{1,0:T(8,128)S(1)} %get-tuple-element.37.after), channel_id=1, source_target_pairs={{0,1},{1,0},{2,3},{3,2},{4,5},{5,4},{6,7},{7,6},{8,9},{9,8},{10,11... | collective-permute-start | bytes 215048 | tf_op jit(solution)/shard_map/ppermute | solution.py:401
  8.7 6.4 %collective-permute-start.4 = (f32[24,2240]{1,0:T(8,128)S(1)}, f32[24,2240]{1,0:T(8,128)S(1)}, u32[]{:S(2)}, u32[]{:S(2)}) collective-permute-start(f32[24,2240]{1,0:T(8,128)S(1)} %get-tuple-element.45), channel_id=1, source_target_pairs={{0,1},{1,0},{2,3},{3,2},{4,5},{5,4},{6,7},{7,6},{8,9},{9,8},{10,11... | collective-permute-start | bytes 645128 | tf_op jit(solution)/shard_map/ppermute | solution.py:401
  9.3 8.2 %collective-permute-start.5 = (f32[24,2240]{1,0:T(8,128)S(1)}, f32[24,2240]{1,0:T(8,128)S(1)}, u32[]{:S(2)}, u32[]{:S(2)}) collective-permute-start(f32[24,2240]{1,0:T(8,128)S(1)} %get-tuple-element.46), channel_id=1, source_target_pairs={{0,15},{1,2},{2,1},{3,4},{4,3},{5,6},{6,5},{7,8},{8,7},{9,10},{10,... | collective-permute-start | bytes 645128 | tf_op jit(solution)/shard_map/ppermute | solution.py:401
  10.9 8.2 %collective-permute-start.2 = (f32[306,128]{1,0:T(8,128)S(1)}, f32[306,128]{1,0:T(8,128)S(1)}, u32[]{:S(2)}, u32[]{:S(2)}) collective-permute-start(f32[306,128]{1,0:T(8,128)S(1)} %get-tuple-element.42), channel_id=1, source_target_pairs={{0,15},{1,2},{2,1},{3,4},{4,3},{5,6},{6,5},{7,8},{8,7},{9,10},{10,... | collective-permute-start | bytes 470024 | tf_op jit(solution)/shard_map/ppermute | solution.py:401
  15.2 4.0 %collective-permute-start.3 = (f32[306,128]{1,0:T(8,128)S(1)}, f32[306,128]{1,0:T(8,128)S(1)}, u32[]{:S(2)}, u32[]{:S(2)}) collective-permute-start(f32[306,128]{1,0:T(8,128)S(1)} %get-tuple-element.43), channel_id=1, source_target_pairs={{0,1},{1,0},{2,3},{3,2},{4,5},{5,4},{6,7},{7,6},{8,9},{9,8},{10,11... | collective-permute-start | bytes 470024 | tf_op jit(solution)/shard_map/ppermute | solution.py:401
  20.7 6.7 %collective-permute-start.6 = (f32[162,128]{1,0:T(8,128)S(1)}, f32[162,128]{1,0:T(8,128)S(1)}, u32[]{:S(2)}, u32[]{:S(2)}) collective-permute-start(f32[162,128]{1,0:T(8,128)S(1)} %get-tuple-element.51), channel_id=1, source_target_pairs={{0,15},{1,2},{2,1},{3,4},{4,3},{5,6},{6,5},{7,8},{8,7},{9,10},{10,... | collective-permute-start | bytes 248840 | tf_op jit(solution)/shard_map/ppermute | solution.py:401
  24.2 3.2 %collective-permute-start.7 = (f32[162,128]{1,0:T(8,128)S(1)}, f32[162,128]{1,0:T(8,128)S(1)}, u32[]{:S(2)}, u32[]{:S(2)}) collective-permute-start(f32[162,128]{1,0:T(8,128)S(1)} %get-tuple-element.52), channel_id=1, source_target_pairs={{0,1},{1,0},{2,3},{3,2},{4,5},{5,4},{6,7},{7,6},{8,9},{9,8},{10,11... | collective-permute-start | bytes 248840 | tf_op jit(solution)/shard_map/ppermute | solution.py:401

commit v20 on v19

--- a/solution.py
+++ b/solution.py
@@ -66,7 +66,7 @@
             return jnp.zeros((span, LANE), F32)
         return x[:, b * LANE : (b + 1) * LANE]
 
-    chunk = 10
+    chunk = 20
     groups = [range(first, min(first + chunk, tiles)) for first in range(0, tiles, chunk)]
     held = {}
 

time: 39.3 us -> 39.1 us (level)
  no operation moved by 1% of the time
where the time goes in v20:
time: 39.1 us; the launch traced here: 38.8 us
  starting transfers between devices  13.9 us (36%)
  Pallas kernels  11.7 us (30%)
  blocking collectives  8.02 us (21%)
  waiting for transfers between devices  4.55 us (12%)
  between operations  0.69 us (2%)
    ppermute x8, starting transfers between devices, swap_pairs(): return lax.ppermute(block, 'lon', route)  13.9 us
    all_to_all x1, blocking collectives, body(): came = lax.all_to_all(sent, 'lon', 0, 0, axis_index_groups=ring)  8.02 us
    ppermute x8, waiting for transfers between devices, swap_pairs(): return lax.ppermute(block, 'lon', route)  4.55 us
    pallas_call x1, Pallas kernels, body(): pl.pallas_call(finish, in_specs=[VM] * 10, out_specs=[HB] * 4, out_shape=...  2.94 us
    pallas_call x1, Pallas kernels, body(): pl.pallas_call(prepare, in_specs=[SM] + [HB] * 8, out_specs=[VM] * 9, out...  1.53 us
    pallas_call x1, Pallas kernels, body(): pl.pallas_call(second_solve, in_specs=[SM] + [VM] * 7, out_specs=[VM] * 5...  1.51 us
    pallas_call x1, Pallas kernels, body(): pl.pallas_call(early_sums, in_specs=[VM] * 5 + [HB], out_specs=[VM] * 4,...  1.49 us
    pallas_call x1, Pallas kernels, body(): pl.pallas_call(absorb, in_specs=[SM] + [VM] * 5 + [HB], out_specs=[VM] *...  1.49 us
  transfers between devices with their start and end apart: 8, of which 3 were waited for; matrix products, arithmetic and copies ran while one was open for 0% of the time, Pallas kernels for 15%

profile of v20, /device:TPU:0, one launch (start us, length us, event | category | flops | bytes accessed | tf_op | source)
XLA Modules:
  0.0 38.8 jit_solution(9174300057501184676)
XLA Ops:
  0.6 1.0 %first_edges.1 = (f32[8,2240]{1,0:T(8,128)S(1)}, f32[8,2240]{1,0:T(8,128)S(1)}) custom-call(s32[1]{0:T(128)} %bitcast.parity, f32[32,2240]{1,0:T(8,128)} %source_h.1, s32[32,2240]{1,0:T(8,128)} %bottom_h.1), custom_call_target="tpu_custom_call" | custom-call | tf_op jit(solution)/shard_map/first_edges/pallas_call | solution.py:423
  1.7 5.5 %collective-permute-start = (f32[8,2240]{1,0:T(8,128)S(1)}, f32[8,2240]{1,0:T(8,128)S(1)}, u32[]{:S(2)}, u32[]{:S(2)}) collective-permute-start(f32[8,2240]{1,0:T(8,128)S(1)} %get-tuple-element.36), channel_id=1, source_target_pairs={{0,15},{1,2},{2,1},{3,4},{4,3},{5,6},{6,5},{7,8},{8,7},{9,10},{10,... | collective-permute-start | bytes 215048 | tf_op jit(solution)/shard_map/ppermute | solution.py:401
  7.2 0.0 collective-permute-start.1
  7.2 1.5 %prepare.1 = (f32[24,2240]{1,0:T(8,128)S(1)}, f32[24,2240]{1,0:T(8,128)S(1)}, f32[32,2240]{1,0:T(8,128)S(1)}, f32[32,2240]{1,0:T(8,128)S(1)}, f32[32,2240]{1,0:T...) custom-call(s32[1]{0:T(128)} %bitcast.parity, ...), custom_call_target="tpu_custom_call" | custom-call | flops 1000000 | bytes 7000000 | tf_op jit(solution)/shard_map/prepare/pallas_call | solution.py:435
  8.7 0.6 %collective-permute-start.4 = (f32[24,2240]{1,0:T(8,128)S(1)}, f32[24,2240]{1,0:T(8,128)S(1)}, u32[]{:S(2)}, u32[]{:S(2)}) collective-permute-start(f32[24,2240]{1,0:T(8,128)S(1)} %get-tuple-element.45), channel_id=1, source_target_pairs={{0,1},{1,0},{2,3},{3,2},{4,5},{5,4},{6,7},{7,6},{8,9},{9,8},{10,11... | collective-permute-start | bytes 645128 | tf_op jit(solution)/shard_map/ppermute | solution.py:401
  9.3 0.3 collective-permute-start.5
  9.6 0.0 collective-permute-done.outer_in
  9.6 0.0 collective-permute-done.1.inner_in
  9.6 1.2 %first_solve.1 = (f32[48,2240]{1,0:T(8,128)S(1)}, f32[306,128]{1,0:T(8,128)S(1)}, f32[306,128]{1,0:T(8,128)S(1)}) custom-call(s32[1]{0:T(128)} %bitcast.parity, f32[8,2240]{1,0:T(8,128)S(1)} %collective-permute-done.outer_in, f32[8,2240]{1,0:T(8,128)S(1)} %collective-permute-done.1.inner_in, f32[32,2240]{1,0:T(8,128)S(1)} %get-tuple-element.38.masked, ...), custom_call_target="tpu_custom_call" | custom-call | tf_op jit(solution)/shard_map/first_solve/pallas_call | solution.py:455
  10.8 4.2 %collective-permute-start.2 = (f32[306,128]{1,0:T(8,128)S(1)}, f32[306,128]{1,0:T(8,128)S(1)}, u32[]{:S(2)}, u32[]{:S(2)}) collective-permute-start(f32[306,128]{1,0:T(8,128)S(1)} %get-tuple-element.42), channel_id=1, source_target_pairs={{0,15},{1,2},{2,1},{3,4},{4,3},{5,6},{6,5},{7,8},{8,7},{9,10},{10,... | collective-permute-start | bytes 470024 | tf_op jit(solution)/shard_map/ppermute | solution.py:401
  15.0 0.0 collective-permute-start.3
  15.0 0.0 collective-permute-done.4.inner_in
  15.0 2.4 %collective-permute-done.5.outer_in = f32[24,2240]{1,0:T(8,128)S(1)} collective-permute-done((f32[24,2240]{1,0:T(8,128)S(1)}, f32[24,2240]{1,0:T(8,128)S(1)}, u32[]{:S(2)}, u32[]{:S(2)}) %collective-permute-start.5) | collective-permute-done | bytes 215072 | tf_op jit(solution)/shard_map/ppermute | solution.py:401
  17.4 1.5 %absorb.1 = (f32[64,2240]{1,0:T(8,128)S(1)}, f32[64,2240]{1,0:T(8,128)S(1)}, f32[48,2240]{1,0:T(8,128)S(1)}, f32[32,2240]{1,0:T(8,128)S(1)}, f32[32,2240]{1,0:T(...) custom-call(s32[1]{0:T(128)} %bitcast.parity, f32[48,2240]{1,0:T(8,128)S(1)} %get-tuple-element.44.first, ...), custom_call_target="tpu_custom_call" | custom-call | flops 1000000 | bytes 7000000 | tf_op jit(solution)/shard_map/absorb/pallas_call | solution.py:466
  18.9 0.2 collective-permute-done.2.outer_in
  19.2 0.0 collective-permute-done.3.inner_in
  19.2 1.5 %second_solve.1 = (f32[64,2240]{1,0:T(8,128)S(1)}, f32[48,2240]{1,0:T(8,128)S(1)}, f32[48,2240]{1,0:T(8,128)S(1)}, f32[162,128]{1,0:T(8,128)S(1)}, f32[162,128]{1,0:T(8,128)S(1)}) custom-call(s32[1]{0:T(128)} %bitcast.parity, f32[306,128]{1,0:T(8,128)S(1)} %collective-permute-done.2.outer_in, f32[306,128]{1,0:T(8,128)S(1)} %collective-permute-done.3.inner_in, ...), custom_call_target="tpu_custom_call" | custom-call | tf_op jit(solution)/shard_map/second_solve/pallas_call | solution.py:480
  20.7 3.3 %collective-permute-start.6 = (f32[162,128]{1,0:T(8,128)S(1)}, f32[162,128]{1,0:T(8,128)S(1)}, u32[]{:S(2)}, u32[]{:S(2)}) collective-permute-start(f32[162,128]{1,0:T(8,128)S(1)} %get-tuple-element.51), channel_id=1, source_target_pairs={{0,15},{1,2},{2,1},{3,4},{4,3},{5,6},{6,5},{7,8},{8,7},{9,10},{10,... | collective-permute-start | bytes 248840 | tf_op jit(solution)/shard_map/ppermute | solution.py:401
  24.0 0.0 collective-permute-start.7
  24.0 1.5 %early_sums.1 = (f32[48,2240]{1,0:T(8,128)S(1)}, f32[32,2240]{1,0:T(8,128)S(1)}, f32[1,128]{1,0:T(1,128)S(1)}, f32[6,32,2240]{2,1,0:T(8,128)S(1)}) custom-call(f32[64,2240]{1,0:T(8,128)S(1)} %get-tuple-element.53.z, f32[48,2240]{1,0:T(8,128)S(1)} %get-tuple-element.54.y, f32[64,2240]{1,0:T(8,128)S(1)} %get-tuple-element.50.c_rows, ...), custom_call_target="tpu_custom_call" | custom-call | flops 1000000 | bytes 7000000 | tf_op jit(solution)/shard_map/early_sums/pallas_call | solution.py:493
  25.5 1.9 %collective-permute-done.6.outer_in = f32[162,128]{1,0:T(8,128)S(1)} collective-permute-done((f32[162,128]{1,0:T(8,128)S(1)}, f32[162,128]{1,0:T(8,128)S(1)}, u32[]{:S(2)}, u32[]{:S(2)}) %collective-permute-start.6) | collective-permute-done | bytes 82976 | tf_op jit(solution)/shard_map/ppermute | solution.py:401
  27.4 0.0 collective-permute-done.7.inner_in
  27.4 0.5 %sums.1 = (f32[48,2240]{1,0:T(8,128)S(1)}, f32[16,1,128]{2,1,0:T(1,128)S(1)}) custom-call(s32[1]{0:T(128)} %bitcast.parity, f32[162,128]{1,0:T(8,128)S(1)} %collective-permute-done.6.outer_in, f32[162,128]{1,0:T(8,128)S(1)} %collective-permute-done.7.inner_in, f32[48,2240]{1,0:T(8,128)S(1)} %get-tuple-element.57.w_rows, f32[64,2240]{1,0:T(8,128)S(1)} %get-tuple-element.53.z, ...), custom_call_target="tpu_custom_call" | custom-call | tf_op jit(solution)/shard_map/sums/pallas_call | solution.py:505
  27.8 8.0 %all_to_all.5.came = f32[16,1,128]{2,1,0:T(1,128)S(1)} all-to-all(f32[16,1,128]{2,1,0:T(1,128)S(1)} %get-tuple-element.60), channel_id=1, replica_groups={{15,14,13,12,11,10,9,8,7,6,5,4,3,2,1,0},{31,30,29,28,27,26,25,24,23,22,..., dimensions={0} | all-to-all | bytes 16384 | tf_op jit(solution)/shard_map/all_to_all | solution.py:514
  35.9 2.9 %finish.1 = (f32[32,2240]{1,0:T(8,128)}, f32[6,32,2240]{2,1,0:T(8,128)}, f32[6,32,2240]{2,1,0:T(8,128)}, f32[6,32,2240]{2,1,0:T(8,128)}) custom-call(f32[16,1,128]{2,1,0:T(1,128)S(1)} %all_to_all.5.came, f32[64,2240]{1,0:T(8,128)S(1)} %get-tuple-element.53.z, f32[48,2240]{1,0:T(8,128)S(1)} %get-tuple-element.61.w, f32[48,2240]{1,0:T(8,128)S(1)} %get-tuple-element.62.d_rows, ...), custom_call_target="tpu_custom_call" | custom-call | tf_op jit(solution)/shard_map/finish/pallas_call | solution.py:516
Async XLA Ops:
  1.7 7.9 %collective-permute-start = (f32[8,2240]{1,0:T(8,128)S(1)}, f32[8,2240]{1,0:T(8,128)S(1)}, u32[]{:S(2)}, u32[]{:S(2)}) collective-permute-start(f32[8,2240]{1,0:T(8,128)S(1)} %get-tuple-element.36), channel_id=1, source_target_pairs={{0,15},{1,2},{2,1},{3,4},{4,3},{5,6},{6,5},{7,8},{8,7},{9,10},{10,... | collective-permute-start | bytes 215048 | tf_op jit(solution)/shard_map/ppermute | solution.py:401
  7.2 2.4 %collective-permute-start.1 = (f32[8,2240]{1,0:T(8,128)S(1)}, f32[8,2240]{1,0:T(8,128)S(1)}, u32[]{:S(2)}, u32[]{:S(2)}) collective-permute-start(f32[8,2240]{1,0:T(8,128)S(1)} %get-tuple-element.37.after), channel_id=1, source_target_pairs={{0,1},{1,0},{2,3},{3,2},{4,5},{5,4},{6,7},{7,6},{8,9},{9,8},{10,11... | collective-permute-start | bytes 215048 | tf_op jit(solution)/shard_map/ppermute | solution.py:401
  8.7 6.3 %collective-permute-start.4 = (f32[24,2240]{1,0:T(8,128)S(1)}, f32[24,2240]{1,0:T(8,128)S(1)}, u32[]{:S(2)}, u32[]{:S(2)}) collective-permute-start(f32[24,2240]{1,0:T(8,128)S(1)} %get-tuple-element.45), channel_id=1, source_target_pairs={{0,1},{1,0},{2,3},{3,2},{4,5},{5,4},{6,7},{7,6},{8,9},{9,8},{10,11... | collective-permute-start | bytes 645128 | tf_op jit(solution)/shard_map/ppermute | solution.py:401
  9.3 8.2 %collective-permute-start.5 = (f32[24,2240]{1,0:T(8,128)S(1)}, f32[24,2240]{1,0:T(8,128)S(1)}, u32[]{:S(2)}, u32[]{:S(2)}) collective-permute-start(f32[24,2240]{1,0:T(8,128)S(1)} %get-tuple-element.46), channel_id=1, source_target_pairs={{0,15},{1,2},{2,1},{3,4},{4,3},{5,6},{6,5},{7,8},{8,7},{9,10},{10,... | collective-permute-start | bytes 645128 | tf_op jit(solution)/shard_map/ppermute | solution.py:401
  10.8 8.4 %collective-permute-start.2 = (f32[306,128]{1,0:T(8,128)S(1)}, f32[306,128]{1,0:T(8,128)S(1)}, u32[]{:S(2)}, u32[]{:S(2)}) collective-permute-start(f32[306,128]{1,0:T(8,128)S(1)} %get-tuple-element.42), channel_id=1, source_target_pairs={{0,15},{1,2},{2,1},{3,4},{4,3},{5,6},{6,5},{7,8},{8,7},{9,10},{10,... | collective-permute-start | bytes 470024 | tf_op jit(solution)/shard_map/ppermute | solution.py:401
  15.0 4.2 %collective-permute-start.3 = (f32[306,128]{1,0:T(8,128)S(1)}, f32[306,128]{1,0:T(8,128)S(1)}, u32[]{:S(2)}, u32[]{:S(2)}) collective-permute-start(f32[306,128]{1,0:T(8,128)S(1)} %get-tuple-element.43), channel_id=1, source_target_pairs={{0,1},{1,0},{2,3},{3,2},{4,5},{5,4},{6,7},{7,6},{8,9},{9,8},{10,11... | collective-permute-start | bytes 470024 | tf_op jit(solution)/shard_map/ppermute | solution.py:401
  20.7 6.7 %collective-permute-start.6 = (f32[162,128]{1,0:T(8,128)S(1)}, f32[162,128]{1,0:T(8,128)S(1)}, u32[]{:S(2)}, u32[]{:S(2)}) collective-permute-start(f32[162,128]{1,0:T(8,128)S(1)} %get-tuple-element.51), channel_id=1, source_target_pairs={{0,15},{1,2},{2,1},{3,4},{4,3},{5,6},{6,5},{7,8},{8,7},{9,10},{10,... | collective-permute-start | bytes 248840 | tf_op jit(solution)/shard_map/ppermute | solution.py:401
  24.0 3.4 %collective-permute-start.7 = (f32[162,128]{1,0:T(8,128)S(1)}, f32[162,128]{1,0:T(8,128)S(1)}, u32[]{:S(2)}, u32[]{:S(2)}) collective-permute-start(f32[162,128]{1,0:T(8,128)S(1)} %get-tuple-element.52), channel_id=1, source_target_pairs={{0,1},{1,0},{2,3},{3,2},{4,5},{5,4},{6,7},{7,6},{8,9},{9,8},{10,11... | collective-permute-start | bytes 248840 | tf_op jit(solution)/shard_map/ppermute | solution.py:401

commit v21 on v20

--- a/solution.py
+++ b/solution.py
@@ -46,7 +46,7 @@
     high, low = halves(lat_basis)
     lat = np.block([[high, low], [high, np.zeros_like(low)]])
     high, low = halves(lon_basis)
-    lon = np.concatenate([high, low, high], axis=1)
+    lon = np.block([[high, high], [low, np.zeros_like(low)]])
     scale = 1.0 / (lon_value[:, None] + lat_value[None, :] + tile_shift)
     return lat, lon, scale.astype(np.float32)
 
@@ -87,22 +87,24 @@
         )
         return product[:, :LANE] + product[:, LANE:]
 
+    def along_lon(group):
+        product = jnp.dot(lon[...], spectral[:, lanes_of(group)], preferred_element_type=F32)
+        return product[:span] + product[span:]
+
     def lat_there(group):
         high, low = split(along_lat(group))
         for i, t in enumerate(group):
             at = slice(t * LANE, (t + 1) * LANE)
             spectral[:span, at] = high[i * span : (i + 1) * span]
-            spectral[span : 2 * span, at] = high[i * span : (i + 1) * span]
-            spectral[2 * span :, at] = low[i * span : (i + 1) * span]
+            spectral[span:, at] = low[i * span : (i + 1) * span]
 
     def lon_there(group):
-        c = jnp.dot(lon[...], spectral[:, lanes_of(group)], preferred_element_type=F32)
+        c = along_lon(group)
         high, low = split(c * jnp.concatenate([scale[...]] * len(group), axis=1))
-        spectral[:, lanes_of(group)] = jnp.concatenate([high, high, low], axis=0)
+        spectral[:, lanes_of(group)] = jnp.concatenate([high, low], axis=0)
 
     def lon_back(group):
-        c = jnp.dot(lon[...], spectral[:, lanes_of(group)], preferred_element_type=F32)
-        high, low = split(c)
+        high, low = split(along_lon(group))
         for i, t in enumerate(group):
             at = slice(t * span, (t + 1) * span)
             rows[at, :LANE] = high[:, i * LANE : (i + 1) * LANE]
@@ -138,7 +140,7 @@
     return [
         pltpu.VMEM((span, wide_lanes(lat)), F32),
         pltpu.VMEM((tiles * span, 2 * LANE), BF16),
-        pltpu.VMEM((3 * span, tiles * LANE), BF16),
+        pltpu.VMEM((2 * span, tiles * LANE), BF16),
     ]
 
 

time: 39.1 us -> 39.1 us (level)
  no operation moved by 1% of the time
where the time goes in v21:
time: 39.1 us; the launch traced here: 38.8 us
  starting transfers between devices  13.9 us (36%)
  Pallas kernels  11.7 us (30%)
  blocking collectives  8.02 us (21%)
  waiting for transfers between devices  4.55 us (12%)
  between operations  0.69 us (2%)
    ppermute x8, starting transfers between devices, swap_pairs(): return lax.ppermute(block, 'lon', route)  13.9 us
    all_to_all x1, blocking collectives, body(): came = lax.all_to_all(sent, 'lon', 0, 0, axis_index_groups=ring)  8.02 us
    ppermute x8, waiting for transfers between devices, swap_pairs(): return lax.ppermute(block, 'lon', route)  4.55 us
    pallas_call x1, Pallas kernels, body(): pl.pallas_call(finish, in_specs=[VM] * 10, out_specs=[HB] * 4, out_shape=...  2.94 us
    pallas_call x1, Pallas kernels, body(): pl.pallas_call(second_solve, in_specs=[SM] + [VM] * 7, out_specs=[VM] * 5...  1.54 us
    pallas_call x1, Pallas kernels, body(): pl.pallas_call(prepare, in_specs=[SM] + [HB] * 8, out_specs=[VM] * 9, out...  1.53 us
    pallas_call x1, Pallas kernels, body(): pl.pallas_call(early_sums, in_specs=[VM] * 5 + [HB], out_specs=[VM] * 4,...  1.49 us
    pallas_call x1, Pallas kernels, body(): pl.pallas_call(absorb, in_specs=[SM] + [VM] * 5 + [HB], out_specs=[VM] *...  1.49 us
  transfers between devices with their start and end apart: 8, of which 3 were waited for; matrix products, arithmetic and copies ran while one was open for 0% of the time, Pallas kernels for 15%

profile of v21, /device:TPU:0, one launch (start us, length us, event | category | flops | bytes accessed | tf_op | source)
XLA Modules:
  0.0 38.8 jit_solution(372376468720313646)
XLA Ops:
  0.6 1.0 %first_edges.1 = (f32[8,2240]{1,0:T(8,128)S(1)}, f32[8,2240]{1,0:T(8,128)S(1)}) custom-call(s32[1]{0:T(128)} %bitcast.parity, f32[32,2240]{1,0:T(8,128)} %source_h.1, s32[32,2240]{1,0:T(8,128)} %bottom_h.1), custom_call_target="tpu_custom_call" | custom-call | tf_op jit(solution)/shard_map/first_edges/pallas_call | solution.py:425
  1.7 5.5 %collective-permute-start = (f32[8,2240]{1,0:T(8,128)S(1)}, f32[8,2240]{1,0:T(8,128)S(1)}, u32[]{:S(2)}, u32[]{:S(2)}) collective-permute-start(f32[8,2240]{1,0:T(8,128)S(1)} %get-tuple-element.36), channel_id=1, source_target_pairs={{0,15},{1,2},{2,1},{3,4},{4,3},{5,6},{6,5},{7,8},{8,7},{9,10},{10,... | collective-permute-start | bytes 215048 | tf_op jit(solution)/shard_map/ppermute | solution.py:403
  7.2 0.0 collective-permute-start.1
  7.2 1.5 %prepare.1 = (f32[24,2240]{1,0:T(8,128)S(1)}, f32[24,2240]{1,0:T(8,128)S(1)}, f32[32,2240]{1,0:T(8,128)S(1)}, f32[32,2240]{1,0:T(8,128)S(1)}, f32[32,2240]{1,0:T...) custom-call(s32[1]{0:T(128)} %bitcast.parity, ...), custom_call_target="tpu_custom_call" | custom-call | flops 1000000 | bytes 7000000 | tf_op jit(solution)/shard_map/prepare/pallas_call | solution.py:437
  8.7 0.6 %collective-permute-start.4 = (f32[24,2240]{1,0:T(8,128)S(1)}, f32[24,2240]{1,0:T(8,128)S(1)}, u32[]{:S(2)}, u32[]{:S(2)}) collective-permute-start(f32[24,2240]{1,0:T(8,128)S(1)} %get-tuple-element.45), channel_id=1, source_target_pairs={{0,1},{1,0},{2,3},{3,2},{4,5},{5,4},{6,7},{7,6},{8,9},{9,8},{10,11... | collective-permute-start | bytes 645128 | tf_op jit(solution)/shard_map/ppermute | solution.py:403
  9.3 0.3 collective-permute-start.5
  9.6 0.0 collective-permute-done.outer_in
  9.6 0.0 collective-permute-done.1.inner_in
  9.6 1.2 %first_solve.1 = (f32[48,2240]{1,0:T(8,128)S(1)}, f32[306,128]{1,0:T(8,128)S(1)}, f32[306,128]{1,0:T(8,128)S(1)}) custom-call(s32[1]{0:T(128)} %bitcast.parity, f32[8,2240]{1,0:T(8,128)S(1)} %collective-permute-done.outer_in, f32[8,2240]{1,0:T(8,128)S(1)} %collective-permute-done.1.inner_in, f32[32,2240]{1,0:T(8,128)S(1)} %get-tuple-element.38.masked, ...), custom_call_target="tpu_custom_call" | custom-call | tf_op jit(solution)/shard_map/first_solve/pallas_call | solution.py:457
  10.8 4.2 %collective-permute-start.2 = (f32[306,128]{1,0:T(8,128)S(1)}, f32[306,128]{1,0:T(8,128)S(1)}, u32[]{:S(2)}, u32[]{:S(2)}) collective-permute-start(f32[306,128]{1,0:T(8,128)S(1)} %get-tuple-element.42), channel_id=1, source_target_pairs={{0,15},{1,2},{2,1},{3,4},{4,3},{5,6},{6,5},{7,8},{8,7},{9,10},{10,... | collective-permute-start | bytes 470024 | tf_op jit(solution)/shard_map/ppermute | solution.py:403
  15.0 0.0 collective-permute-start.3
  15.0 0.0 collective-permute-done.4.inner_in
  15.0 2.4 %collective-permute-done.5.outer_in = f32[24,2240]{1,0:T(8,128)S(1)} collective-permute-done((f32[24,2240]{1,0:T(8,128)S(1)}, f32[24,2240]{1,0:T(8,128)S(1)}, u32[]{:S(2)}, u32[]{:S(2)}) %collective-permute-start.5) | collective-permute-done | bytes 215072 | tf_op jit(solution)/shard_map/ppermute | solution.py:403
  17.4 1.5 %absorb.1 = (f32[64,2240]{1,0:T(8,128)S(1)}, f32[64,2240]{1,0:T(8,128)S(1)}, f32[48,2240]{1,0:T(8,128)S(1)}, f32[32,2240]{1,0:T(8,128)S(1)}, f32[32,2240]{1,0:T(...) custom-call(s32[1]{0:T(128)} %bitcast.parity, f32[48,2240]{1,0:T(8,128)S(1)} %get-tuple-element.44.first, ...), custom_call_target="tpu_custom_call" | custom-call | flops 1000000 | bytes 7000000 | tf_op jit(solution)/shard_map/absorb/pallas_call | solution.py:468
  18.9 0.2 collective-permute-done.2.outer_in
  19.2 0.0 collective-permute-done.3.inner_in
  19.2 1.5 %second_solve.1 = (f32[64,2240]{1,0:T(8,128)S(1)}, f32[48,2240]{1,0:T(8,128)S(1)}, f32[48,2240]{1,0:T(8,128)S(1)}, f32[162,128]{1,0:T(8,128)S(1)}, f32[162,128]{1,0:T(8,128)S(1)}) custom-call(s32[1]{0:T(128)} %bitcast.parity, f32[306,128]{1,0:T(8,128)S(1)} %collective-permute-done.2.outer_in, f32[306,128]{1,0:T(8,128)S(1)} %collective-permute-done.3.inner_in, ...), custom_call_target="tpu_custom_call" | custom-call | tf_op jit(solution)/shard_map/second_solve/pallas_call | solution.py:482
  20.7 3.3 %collective-permute-start.6 = (f32[162,128]{1,0:T(8,128)S(1)}, f32[162,128]{1,0:T(8,128)S(1)}, u32[]{:S(2)}, u32[]{:S(2)}) collective-permute-start(f32[162,128]{1,0:T(8,128)S(1)} %get-tuple-element.51), channel_id=1, source_target_pairs={{0,15},{1,2},{2,1},{3,4},{4,3},{5,6},{6,5},{7,8},{8,7},{9,10},{10,... | collective-permute-start | bytes 248840 | tf_op jit(solution)/shard_map/ppermute | solution.py:403
  24.0 0.0 collective-permute-start.7
  24.0 1.5 %early_sums.1 = (f32[48,2240]{1,0:T(8,128)S(1)}, f32[32,2240]{1,0:T(8,128)S(1)}, f32[1,128]{1,0:T(1,128)S(1)}, f32[6,32,2240]{2,1,0:T(8,128)S(1)}) custom-call(f32[64,2240]{1,0:T(8,128)S(1)} %get-tuple-element.53.z, f32[48,2240]{1,0:T(8,128)S(1)} %get-tuple-element.54.y, f32[64,2240]{1,0:T(8,128)S(1)} %get-tuple-element.50.c_rows, ...), custom_call_target="tpu_custom_call" | custom-call | flops 1000000 | bytes 7000000 | tf_op jit(solution)/shard_map/early_sums/pallas_call | solution.py:495
  25.5 1.9 %collective-permute-done.6.outer_in = f32[162,128]{1,0:T(8,128)S(1)} collective-permute-done((f32[162,128]{1,0:T(8,128)S(1)}, f32[162,128]{1,0:T(8,128)S(1)}, u32[]{:S(2)}, u32[]{:S(2)}) %collective-permute-start.6) | collective-permute-done | bytes 82976 | tf_op jit(solution)/shard_map/ppermute | solution.py:403
  27.4 0.0 collective-permute-done.7.inner_in
  27.4 0.5 %sums.1 = (f32[48,2240]{1,0:T(8,128)S(1)}, f32[16,1,128]{2,1,0:T(1,128)S(1)}) custom-call(s32[1]{0:T(128)} %bitcast.parity, f32[162,128]{1,0:T(8,128)S(1)} %collective-permute-done.6.outer_in, f32[162,128]{1,0:T(8,128)S(1)} %collective-permute-done.7.inner_in, f32[48,2240]{1,0:T(8,128)S(1)} %get-tuple-element.57.w_rows, f32[64,2240]{1,0:T(8,128)S(1)} %get-tuple-element.53.z, ...), custom_call_target="tpu_custom_call" | custom-call | tf_op jit(solution)/shard_map/sums/pallas_call | solution.py:507
  27.9 8.0 %all_to_all.5.came = f32[16,1,128]{2,1,0:T(1,128)S(1)} all-to-all(f32[16,1,128]{2,1,0:T(1,128)S(1)} %get-tuple-element.60), channel_id=1, replica_groups={{15,14,13,12,11,10,9,8,7,6,5,4,3,2,1,0},{31,30,29,28,27,26,25,24,23,22,..., dimensions={0} | all-to-all | bytes 16384 | tf_op jit(solution)/shard_map/all_to_all | solution.py:516
  35.9 2.9 %finish.1 = (f32[32,2240]{1,0:T(8,128)}, f32[6,32,2240]{2,1,0:T(8,128)}, f32[6,32,2240]{2,1,0:T(8,128)}, f32[6,32,2240]{2,1,0:T(8,128)}) custom-call(f32[16,1,128]{2,1,0:T(1,128)S(1)} %all_to_all.5.came, f32[64,2240]{1,0:T(8,128)S(1)} %get-tuple-element.53.z, f32[48,2240]{1,0:T(8,128)S(1)} %get-tuple-element.61.w, f32[48,2240]{1,0:T(8,128)S(1)} %get-tuple-element.62.d_rows, ...), custom_call_target="tpu_custom_call" | custom-call | tf_op jit(solution)/shard_map/finish/pallas_call | solution.py:518
Async XLA Ops:
  1.7 7.9 %collective-permute-start = (f32[8,2240]{1,0:T(8,128)S(1)}, f32[8,2240]{1,0:T(8,128)S(1)}, u32[]{:S(2)}, u32[]{:S(2)}) collective-permute-start(f32[8,2240]{1,0:T(8,128)S(1)} %get-tuple-element.36), channel_id=1, source_target_pairs={{0,15},{1,2},{2,1},{3,4},{4,3},{5,6},{6,5},{7,8},{8,7},{9,10},{10,... | collective-permute-start | bytes 215048 | tf_op jit(solution)/shard_map/ppermute | solution.py:403
  7.2 2.4 %collective-permute-start.1 = (f32[8,2240]{1,0:T(8,128)S(1)}, f32[8,2240]{1,0:T(8,128)S(1)}, u32[]{:S(2)}, u32[]{:S(2)}) collective-permute-start(f32[8,2240]{1,0:T(8,128)S(1)} %get-tuple-element.37.after), channel_id=1, source_target_pairs={{0,1},{1,0},{2,3},{3,2},{4,5},{5,4},{6,7},{7,6},{8,9},{9,8},{10,11... | collective-permute-start | bytes 215048 | tf_op jit(solution)/shard_map/ppermute | solution.py:403
  8.7 6.3 %collective-permute-start.4 = (f32[24,2240]{1,0:T(8,128)S(1)}, f32[24,2240]{1,0:T(8,128)S(1)}, u32[]{:S(2)}, u32[]{:S(2)}) collective-permute-start(f32[24,2240]{1,0:T(8,128)S(1)} %get-tuple-element.45), channel_id=1, source_target_pairs={{0,1},{1,0},{2,3},{3,2},{4,5},{5,4},{6,7},{7,6},{8,9},{9,8},{10,11... | collective-permute-start | bytes 645128 | tf_op jit(solution)/shard_map/ppermute | solution.py:403
  9.3 8.2 %collective-permute-start.5 = (f32[24,2240]{1,0:T(8,128)S(1)}, f32[24,2240]{1,0:T(8,128)S(1)}, u32[]{:S(2)}, u32[]{:S(2)}) collective-permute-start(f32[24,2240]{1,0:T(8,128)S(1)} %get-tuple-element.46), channel_id=1, source_target_pairs={{0,15},{1,2},{2,1},{3,4},{4,3},{5,6},{6,5},{7,8},{8,7},{9,10},{10,... | collective-permute-start | bytes 645128 | tf_op jit(solution)/shard_map/ppermute | solution.py:403
  10.8 8.4 %collective-permute-start.2 = (f32[306,128]{1,0:T(8,128)S(1)}, f32[306,128]{1,0:T(8,128)S(1)}, u32[]{:S(2)}, u32[]{:S(2)}) collective-permute-start(f32[306,128]{1,0:T(8,128)S(1)} %get-tuple-element.42), channel_id=1, source_target_pairs={{0,15},{1,2},{2,1},{3,4},{4,3},{5,6},{6,5},{7,8},{8,7},{9,10},{10,... | collective-permute-start | bytes 470024 | tf_op jit(solution)/shard_map/ppermute | solution.py:403
  15.0 4.2 %collective-permute-start.3 = (f32[306,128]{1,0:T(8,128)S(1)}, f32[306,128]{1,0:T(8,128)S(1)}, u32[]{:S(2)}, u32[]{:S(2)}) collective-permute-start(f32[306,128]{1,0:T(8,128)S(1)} %get-tuple-element.43), channel_id=1, source_target_pairs={{0,1},{1,0},{2,3},{3,2},{4,5},{5,4},{6,7},{7,6},{8,9},{9,8},{10,11... | collective-permute-start | bytes 470024 | tf_op jit(solution)/shard_map/ppermute | solution.py:403
  20.7 6.7 %collective-permute-start.6 = (f32[162,128]{1,0:T(8,128)S(1)}, f32[162,128]{1,0:T(8,128)S(1)}, u32[]{:S(2)}, u32[]{:S(2)}) collective-permute-start(f32[162,128]{1,0:T(8,128)S(1)} %get-tuple-element.51), channel_id=1, source_target_pairs={{0,15},{1,2},{2,1},{3,4},{4,3},{5,6},{6,5},{7,8},{8,7},{9,10},{10,... | collective-permute-start | bytes 248840 | tf_op jit(solution)/shard_map/ppermute | solution.py:403
  24.0 3.4 %collective-permute-start.7 = (f32[162,128]{1,0:T(8,128)S(1)}, f32[162,128]{1,0:T(8,128)S(1)}, u32[]{:S(2)}, u32[]{:S(2)}) collective-permute-start(f32[162,128]{1,0:T(8,128)S(1)} %get-tuple-element.52), channel_id=1, source_target_pairs={{0,1},{1,0},{2,3},{3,2},{4,5},{5,4},{6,7},{7,6},{8,9},{9,8},{10,11... | collective-permute-start | bytes 248840 | tf_op jit(solution)/shard_map/ppermute | solution.py:403
